TPU v7x, 32 devices: a whole 2x2x4 slice. The times are simulated.
32 devices in a mesh: dp: 4 (over y, x), expert: 8 (over z, core).
Axes of the slice: x: 2, y: 2, z: 4, core: 2. Of those that a mesh axis runs over, the one named last changes fastest.
Arguments:
- tokens: bfloat16 [4, 1024, 2048], P('dp', 'expert'), may hold values from -6 to 6
- routes: int32 [4, 1024, 8], P('dp', 'expert'), may hold values from 0 to 15, all different within a row; in each aligned block of 128 rows (0 to 127, 128 to 255, ..., all dimensions but the last counted through in order) at most 128 rows name the same one
- grad_output: bfloat16 [4, 1024, 2048], P('dp', 'expert'), may hold values from -6 to 6
- w_query: bfloat16 [2048, 2048], P(('dp', 'expert')), may hold values from -0.125 to 0.125
- w_key: bfloat16 [2048, 2048], P(('dp', 'expert')), may hold values from -0.125 to 0.125
- w_value: bfloat16 [2048, 2048], P(('dp', 'expert')), may hold values from -0.125 to 0.125
- w_out: bfloat16 [2048, 2048], P(('dp', 'expert')), may hold values from -1 to 1
- w_router: bfloat16 [2048, 16], P(('dp', 'expert')), may hold values from -0.0625 to 0.0625
- gain_attn: bfloat16 [2048], P(('dp', 'expert')), may hold values from 0.5 to 1.5
- gain_query: bfloat16 [2048], P(('dp', 'expert')), may hold values from 0.5 to 1.5
- gain_key: bfloat16 [2048], P(('dp', 'expert')), may hold values from 0.5 to 1.5
- gain_ffn: bfloat16 [2048], P(('dp', 'expert')), may hold values from 0.5 to 1.5
- w_gate: bfloat16 [16, 2048, 1024], P('expert', 'dp'), may hold values from -0.125 to 0.125
- w_up: bfloat16 [16, 2048, 1024], P('expert', 'dp'), may hold values from -0.125 to 0.125
- w_down: bfloat16 [16, 1024, 2048], P('expert', 'dp'), may hold values from -1.5 to 1.5
Outputs:
- output: float32 [4, 1024, 2048], P('dp', 'expert')
- input_grad: float32 [4, 1024, 2048], P('dp', 'expert')
- grad_query: float32 [2048, 2048], P(('dp', 'expert'))
- grad_key: float32 [2048, 2048], P(('dp', 'expert'))
- grad_value: float32 [2048, 2048], P(('dp', 'expert'))
- grad_out: float32 [2048, 2048], P(('dp', 'expert'))
- grad_router: float32 [2048, 16], P(('dp', 'expert'))
- grad_gain_attn: float32 [2048], P(('dp', 'expert'))
- grad_gain_query: float32 [2048], P(('dp', 'expert'))
- grad_gain_key: float32 [2048], P(('dp', 'expert'))
- grad_gain_ffn: float32 [2048], P(('dp', 'expert'))
- grad_gate: float32 [16, 2048, 1024], P('expert', 'dp')
- grad_up: float32 [16, 2048, 1024], P('expert', 'dp')
- grad_down: float32 [16, 1024, 2048], P('expert', 'dp')
Inputs may be any that keep to these rules, and one draw needn't show every extreme that they name: `routes`: each token names 8 different experts; in the rows of one device no expert is named more than 128 times, a bound that some block reaches.
All inputs are finite; a program needn't handle non-finite values.
Results may differ from a plain program's by a relative error of at most 0.02.
Values may be sent and summed in bfloat16 or wider, within the bound.
A program may use at most 384 MiB of HBM per device.

v0:
```python
import math

import jax
import jax.numpy as jnp
from jax import lax
from jax.sharding import PartitionSpec as P

HEADS = 16
HEAD_DIM = 128


EPS = 1e-05
THETA = 10000.0
NEG = -1e30


def norm_rows(values, gain_vec):
    return values * lax.rsqrt(jnp.mean(values * values, axis=-1, keepdims=True) + EPS) * gain_vec


def rotary(values, positions):
    half_dim = values.shape[-1] // 2
    inv_freq = jnp.exp(
        jnp.arange(half_dim, dtype=jnp.float32) * (-2.0 * math.log(THETA) / values.shape[-1])
    )
    angles = positions.astype(jnp.float32)[:, None] * inv_freq[None, :]
    cosine = jnp.cos(angles)[:, None, :]
    sine_val = jnp.sin(angles)[:, None, :]
    front_half = values[..., :half_dim]
    back_half = values[..., half_dim:]
    return jnp.concatenate(
        [front_half * cosine - back_half * sine_val, back_half * cosine + front_half * sine_val],
        axis=-1,
    )


def project_heads(raw_proj, gain_vec, positions):
    normed = norm_rows(raw_proj, gain_vec).reshape(raw_proj.shape[0], HEADS, HEAD_DIM)
    return rotary(normed, positions)


def scores_of(queries, key_rows, query_pos, key_pos):
    raw_scores = jnp.einsum(
        "qd,kd->qk", queries, key_rows, preferred_element_type=jnp.float32
    ) * queries.shape[-1] ** (-0.5)
    return jnp.where(key_pos[None, :] <= query_pos[:, None], raw_scores, NEG)


def head_forward(queries, key_rows, value_rows, query_pos, key_pos):
    scores = scores_of(queries, key_rows, query_pos, key_pos)
    row_max = jnp.max(scores, axis=-1, keepdims=True)
    exp_terms = jnp.exp(scores - row_max)
    exp_sum = jnp.sum(exp_terms, axis=-1, keepdims=True)
    prob_low = (exp_terms / exp_sum).astype(jnp.bfloat16)
    result = jnp.dot(prob_low, value_rows, preferred_element_type=jnp.float32)
    return (result, (row_max + jnp.log(exp_sum))[:, 0])


def head_back(queries, key_rows, value_rows, grad_mix, log_norm, query_pos, key_pos):
    attn_prob = jnp.exp(scores_of(queries, key_rows, query_pos, key_pos) - log_norm[:, None])
    d_prob = jnp.einsum("qd,kd->qk", grad_mix, value_rows, preferred_element_type=jnp.float32)
    row_delta = jnp.sum(d_prob * attn_prob, axis=-1)
    d_score = (attn_prob * (d_prob - row_delta[:, None]) * queries.shape[-1] ** (-0.5)).astype(
        jnp.bfloat16
    )
    return (attn_prob, d_score, row_delta)


def left_product(left, right):
    return lax.dot_general(
        left, right, (((0,), (0,)), ((), ())), preferred_element_type=jnp.float32
    )


def right_product(left, right):
    return lax.dot_general(
        left, right, (((1,), (1,)), ((), ())), preferred_element_type=jnp.float32
    )


def shards(
    tokens,
    routes,
    grad_output,
    w_query,
    w_key,
    w_value,
    w_out,
    w_router,
    gain_attn,
    gain_query,
    gain_key,
    gain_ffn,
    w_gate,
    w_up,
    w_down,
):
    f32 = jnp.float32
    bf16 = jnp.bfloat16
    local_rows = tokens.shape[1]
    model_width = tokens.shape[2]
    top_count = routes.shape[2]
    groups = lax.axis_size("expert")
    device_pos = lax.axis_index("expert")
    local_experts = w_gate.shape[0]
    all_experts = local_experts * groups
    capacity = 2 * local_rows * top_count // all_experts
    query_pos = device_pos * local_rows + jnp.arange(local_rows, dtype=jnp.int32)
    key_pos = jnp.arange(local_rows * groups, dtype=jnp.int32)
    w_q, w_k, w_v, w_o, w_r, g_attn, g_query, g_key, g_ffn = (
        lax.all_gather(w_query, ("dp", "expert"), axis=0, tiled=True),
        lax.all_gather(w_key, ("dp", "expert"), axis=0, tiled=True),
        lax.all_gather(w_value, ("dp", "expert"), axis=0, tiled=True),
        lax.all_gather(w_out, ("dp", "expert"), axis=0, tiled=True),
        lax.all_gather(w_router, ("dp", "expert"), axis=0, tiled=True),
        lax.all_gather(gain_attn, ("dp", "expert"), axis=0, tiled=True),
        lax.all_gather(gain_query, ("dp", "expert"), axis=0, tiled=True),
        lax.all_gather(gain_key, ("dp", "expert"), axis=0, tiled=True),
        lax.all_gather(gain_ffn, ("dp", "expert"), axis=0, tiled=True),
    )
    g_attn = g_attn.astype(f32)
    g_query = g_query.astype(f32)
    g_key = g_key.astype(f32)
    g_ffn = g_ffn.astype(f32)
    x_in = tokens.reshape(local_rows, model_width).astype(f32)
    normed_in, norm1_back = jax.vjp(norm_rows, x_in, g_attn)
    normed_low = normed_in.astype(bf16)
    q_raw = jnp.dot(normed_low, w_q, preferred_element_type=f32)
    k_raw = jnp.dot(normed_low, w_k, preferred_element_type=f32)
    v_raw = jnp.dot(normed_low, w_v, preferred_element_type=f32)
    q_rot, query_back = jax.vjp(
        lambda raw_proj, gain_vec: project_heads(raw_proj, gain_vec, query_pos), q_raw, g_query
    )
    k_rot, key_back = jax.vjp(
        lambda raw_proj, gain_vec: project_heads(raw_proj, gain_vec, query_pos), k_raw, g_key
    )
    q_heads = q_rot.astype(bf16).transpose(1, 0, 2)
    k_heads = k_rot.astype(bf16).transpose(1, 0, 2)
    v_heads = v_raw.astype(bf16).reshape(local_rows, HEADS, HEAD_DIM).transpose(1, 0, 2)
    k_all, v_all = (
        lax.all_gather(k_heads, "expert", axis=1, tiled=True),
        lax.all_gather(v_heads, "expert", axis=1, tiled=True),
    )

    def forward_head(parts):
        return head_forward(parts[0], parts[1], parts[2], query_pos, key_pos)

    out_heads, log_norm = lax.map(forward_head, (q_heads, k_all, v_all))
    attn_mix = out_heads.transpose(1, 0, 2).reshape(local_rows, model_width).astype(bf16)
    after_attn = x_in + jnp.dot(attn_mix, w_o, preferred_element_type=f32)
    normed_ffn, norm2_back = jax.vjp(norm_rows, after_attn, g_ffn)
    ffn_low = normed_ffn.astype(bf16)
    router_prob = jax.nn.softmax(jnp.dot(ffn_low, w_r, preferred_element_type=f32), axis=-1)
    chosen = routes.reshape(local_rows, top_count)
    chosen_mask = (
        chosen[:, :, None] == jnp.arange(all_experts, dtype=jnp.int32)[None, None, :]
    ).astype(f32)
    route_weight = jnp.sum(chosen_mask * router_prob[:, None, :], axis=-1)
    flat_ids = chosen.reshape(local_rows * top_count)
    onehot = (flat_ids[:, None] == jnp.arange(all_experts, dtype=jnp.int32)[None, :]).astype(
        jnp.int32
    )
    slot_ids = jnp.sum(jnp.cumsum(onehot, axis=0) * onehot, axis=1) - 1
    dest_ids = flat_ids * capacity + slot_ids
    owner_tok = jnp.arange(local_rows * top_count, dtype=jnp.int32) // top_count
    send_buf = (
        jnp.zeros((all_experts * capacity, model_width), bf16).at[dest_ids].set(ffn_low[owner_tok])
    )
    arrived = lax.all_to_all(
        send_buf.reshape(groups, local_experts * capacity, model_width),
        "expert",
        split_axis=0,
        concat_axis=0,
        tiled=True,
    )
    arrived = arrived.reshape(groups, local_experts, capacity, model_width)
    wg_loc, wu_loc, wd_loc = (
        lax.all_gather(w_gate, "dp", axis=1, tiled=True),
        lax.all_gather(w_up, "dp", axis=1, tiled=True),
        lax.all_gather(w_down, "dp", axis=1, tiled=True),
    )
    gate_proj = jnp.einsum("secd,edf->secf", arrived, wg_loc, preferred_element_type=f32)
    up_proj = jnp.einsum("secd,edf->secf", arrived, wu_loc, preferred_element_type=f32)
    sigmoid_gate = jax.nn.sigmoid(gate_proj)
    silu_gate = gate_proj * sigmoid_gate
    hidden = (silu_gate * up_proj).astype(bf16)
    expert_out = jnp.einsum("secf,efd->secd", hidden, wd_loc, preferred_element_type=f32).astype(
        bf16
    )
    returned = lax.all_to_all(
        expert_out.reshape(groups, local_experts * capacity, model_width),
        "expert",
        split_axis=0,
        concat_axis=0,
        tiled=True,
    )
    row_vals = (
        returned.reshape(all_experts * capacity, model_width)[dest_ids]
        .astype(f32)
        .reshape(local_rows, top_count, model_width)
    )
    output = after_attn + jnp.sum(route_weight[:, :, None] * row_vals, axis=1)
    grad_rows = grad_output.reshape(local_rows, model_width).astype(f32)
    d_weight = jnp.sum(row_vals * grad_rows[:, None, :], axis=2)
    d_expert = (
        (route_weight[:, :, None] * grad_rows[:, None, :])
        .astype(bf16)
        .reshape(local_rows * top_count, model_width)
    )
    grad_send = jnp.zeros((all_experts * capacity, model_width), bf16).at[dest_ids].set(d_expert)
    grad_arrived = lax.all_to_all(
        grad_send.reshape(groups, local_experts * capacity, model_width),
        "expert",
        split_axis=0,
        concat_axis=0,
        tiled=True,
    )
    grad_arrived = grad_arrived.reshape(groups, local_experts, capacity, model_width)
    d_hidden = jnp.einsum("secd,efd->secf", grad_arrived, wd_loc, preferred_element_type=f32)
    d_down = jnp.einsum("secf,secd->efd", hidden, grad_arrived, preferred_element_type=f32)
    d_gate = (d_hidden * up_proj * sigmoid_gate * (1.0 + gate_proj * (1.0 - sigmoid_gate))).astype(
        bf16
    )
    d_up = (d_hidden * silu_gate).astype(bf16)
    d_gate_w = jnp.einsum("secd,secf->edf", arrived, d_gate, preferred_element_type=f32)
    d_up_w = jnp.einsum("secd,secf->edf", arrived, d_up, preferred_element_type=f32)
    d_inputs = jnp.einsum(
        "secf,edf->secd", d_gate, wg_loc, preferred_element_type=f32
    ) + jnp.einsum("secf,edf->secd", d_up, wu_loc, preferred_element_type=f32)
    d_returned = lax.all_to_all(
        d_inputs.reshape(groups, local_experts * capacity, model_width).astype(jnp.bfloat16),
        "expert",
        split_axis=0,
        concat_axis=0,
        tiled=True,
    ).astype(jnp.float32)
    d_rows = d_returned.reshape(all_experts * capacity, model_width)[dest_ids].reshape(
        local_rows, top_count, model_width
    )
    d_router_prob = jnp.sum(chosen_mask * d_weight[:, :, None], axis=1)
    d_logits = (
        router_prob * (d_router_prob - jnp.sum(d_router_prob * router_prob, axis=-1, keepdims=True))
    ).astype(bf16)
    d_router_w = left_product(ffn_low, d_logits)
    d_normed_ffn = jnp.sum(d_rows, axis=1) + right_product(d_logits, w_r)
    d_after_norm, d_gain_ffn = norm2_back(d_normed_ffn)
    d_after = grad_rows + d_after_norm
    d_after_low = d_after.astype(bf16)
    d_out_w = left_product(attn_mix, d_after_low)
    d_mix = right_product(d_after_low, w_o).astype(bf16)
    d_mix_heads = d_mix.reshape(local_rows, HEADS, HEAD_DIM).transpose(1, 0, 2)

    def back_head(parts):
        queries, key_rows, value_rows, grad_mix, norm_row = parts
        attn_prob, d_score, row_delta = head_back(
            queries, key_rows, value_rows, grad_mix, norm_row, query_pos, key_pos
        )
        d_queries = jnp.dot(d_score, key_rows, preferred_element_type=f32)
        d_keys = jnp.einsum("qk,qd->kd", d_score, queries, preferred_element_type=f32)
        d_values = jnp.einsum(
            "qk,qd->kd", attn_prob.astype(bf16), grad_mix, preferred_element_type=f32
        )
        return (d_queries, d_keys, d_values)

    dq_heads, dk_all, dv_all = lax.map(back_head, (q_heads, k_all, v_all, d_mix_heads, log_norm))
    dk_heads, dv_heads = (
        lax.psum_scatter(
            dk_all.astype(jnp.bfloat16), "expert", scatter_dimension=1, tiled=True
        ).astype(jnp.float32),
        lax.psum_scatter(
            dv_all.astype(jnp.bfloat16), "expert", scatter_dimension=1, tiled=True
        ).astype(jnp.float32),
    )
    d_q_raw, d_gain_query = query_back(dq_heads.transpose(1, 0, 2))
    d_k_raw, d_gain_key = key_back(dk_heads.transpose(1, 0, 2))
    dq_low = d_q_raw.astype(bf16)
    dk_low = d_k_raw.astype(bf16)
    dv_low = dv_heads.transpose(1, 0, 2).reshape(local_rows, model_width).astype(bf16)
    d_query_w = left_product(normed_low, dq_low)
    d_key_w = left_product(normed_low, dk_low)
    d_value_w = left_product(normed_low, dv_low)
    d_normed_in = (
        right_product(dq_low, w_q) + right_product(dk_low, w_k) + right_product(dv_low, w_v)
    )
    d_in_norm, d_gain_attn = norm1_back(d_normed_in)
    input_grad = d_after + d_in_norm
    owned = (
        lax.psum_scatter(d_query_w, ("dp", "expert"), scatter_dimension=0, tiled=True),
        lax.psum_scatter(d_key_w, ("dp", "expert"), scatter_dimension=0, tiled=True),
        lax.psum_scatter(d_value_w, ("dp", "expert"), scatter_dimension=0, tiled=True),
        lax.psum_scatter(d_out_w, ("dp", "expert"), scatter_dimension=0, tiled=True),
        lax.psum_scatter(d_router_w, ("dp", "expert"), scatter_dimension=0, tiled=True),
        lax.psum_scatter(d_gain_attn, ("dp", "expert"), scatter_dimension=0, tiled=True),
        lax.psum_scatter(d_gain_query, ("dp", "expert"), scatter_dimension=0, tiled=True),
        lax.psum_scatter(d_gain_key, ("dp", "expert"), scatter_dimension=0, tiled=True),
        lax.psum_scatter(d_gain_ffn, ("dp", "expert"), scatter_dimension=0, tiled=True),
    )
    expert_owned = (
        lax.psum_scatter(
            d_gate_w.astype(jnp.bfloat16), "dp", scatter_dimension=1, tiled=True
        ).astype(jnp.float32),
        lax.psum_scatter(d_up_w.astype(jnp.bfloat16), "dp", scatter_dimension=1, tiled=True).astype(
            jnp.float32
        ),
        lax.psum_scatter(d_down.astype(jnp.bfloat16), "dp", scatter_dimension=1, tiled=True).astype(
            jnp.float32
        ),
    )
    return (
        output.reshape(1, local_rows, model_width),
        input_grad.reshape(1, local_rows, model_width),
        owned[0],
        owned[1],
        owned[2],
        owned[3],
        owned[4],
        owned[5],
        owned[6],
        owned[7],
        owned[8],
        expert_owned[0],
        expert_owned[1],
        expert_owned[2],
    )


def solution(mesh):
    return jax.shard_map(
        shards,
        mesh=mesh,
        in_specs=(
            P("dp", "expert", None),
            P("dp", "expert", None),
            P("dp", "expert", None),
            P(("dp", "expert"), None),
            P(("dp", "expert"), None),
            P(("dp", "expert"), None),
            P(("dp", "expert"), None),
            P(("dp", "expert"), None),
            P(("dp", "expert")),
            P(("dp", "expert")),
            P(("dp", "expert")),
            P(("dp", "expert")),
            P("expert", "dp", None),
            P("expert", "dp", None),
            P("expert", "dp", None),
        ),
        out_specs=(
            P("dp", "expert", None),
            P("dp", "expert", None),
            P(("dp", "expert"), None),
            P(("dp", "expert"), None),
            P(("dp", "expert"), None),
            P(("dp", "expert"), None),
            P(("dp", "expert"), None),
            P(("dp", "expert")),
            P(("dp", "expert")),
            P(("dp", "expert")),
            P(("dp", "expert")),
            P("expert", "dp", None),
            P("expert", "dp", None),
            P("expert", "dp", None),
        ),
        check_vma=False,
    )
```

profile of v0, /device:TPU:5, one launch (start us, length us, event | category | flops | bytes accessed | tf_op | source)
XLA Modules:
  0.0 2721.0 jit_solution(14170477928927297422)
XLA Ops:
  12.8 40.4 %all-reduce.13 = (bf16[2048]{0:T(1024)(128)(2,1)S(1)}, bf16[2048]{0:T(1024)(128)(2,1)S(1)}, bf16[2048]{0:T(1024)(128)(2,1)S(1)}, bf16[2048]{0:T(1024)(128)(2,1)S(1)}) all-reduce(bf16[2048]{0:T(1024)(128)(2,1)S(1)} %dynamic-update-slice, bf16[2048]{0:T(1024)(128)(2,1)S(1)} %dynamic-update-slice.1, ...), channel_id=1, replica_groups=mesh['dp'=4,'expert'=8] {'dp','expert'}, use_global_device_ids=true, to_apply=%add.4 | all-reduce | flops 8192 | bytes 32768
  55.0 35.6 %all-gather.11.cloned.1.call-done = bf16[2048,2048]{1,0:T(8,128)(2,1)} async-done(((bf16[64,2048]{1,0:T(8,128)(2,1)}), bf16[2048,2048]{1,0:T(8,128)(2,1)}) %all-gather.11.cloned.1.call-update) | async-done | bytes 8388624 | tf_op jit(solution)/shard_map/all_gather | solution.py:111
  96.8 72.6 %all-gather.13.cloned.1.call-done = bf16[2048,2048]{1,0:T(8,128)(2,1)} async-done(((bf16[64,2048]{1,0:T(8,128)(2,1)}), bf16[2048,2048]{1,0:T(8,128)(2,1)}) %all-gather.13.cloned.1.call-update) | async-done | bytes 8388624 | tf_op jit(solution)/shard_map/all_gather | solution.py:112
  178.8 69.6 %all-gather.17.cloned.1.call-done = bf16[2048,2048]{1,0:T(8,128)(2,1)} async-done(((bf16[64,2048]{1,0:T(8,128)(2,1)}), bf16[2048,2048]{1,0:T(8,128)(2,1)}) %all-gather.17.cloned.1.call-update) | async-done | bytes 8388624 | tf_op jit(solution)/shard_map/all_gather | solution.py:113
  261.3 34.8 %all-gather.15.cloned.1.call-done = bf16[16,1024,128]{2,1,0:T(8,128)(2,1)} async-done(((bf16[16,128,128]{2,1,0:T(8,128)(2,1)}), bf16[16,1024,128]{2,1,0:T(8,128)(2,1)}) %all-gather.15.cloned.1.call-update) | async-done | bytes 4194320 | tf_op jit(solution)/shard_map/all_gather | solution.py:141
  296.1 48.4 %all-gather.19.cloned.1.call-done = bf16[16,1024,128]{2,1,0:T(8,128)(2,1)} async-done(((bf16[16,128,128]{2,1,0:T(8,128)(2,1)}), bf16[16,1024,128]{2,1,0:T(8,128)(2,1)}) %all-gather.19.cloned.1.call-update) | async-done | bytes 4194320 | tf_op jit(solution)/shard_map/all_gather | solution.py:142
  344.5 66.5 %while.28 = (s32[]{:T(128)}, bf16[16,128,128]{1,2,0:T(8,128)(2,1)S(1)}, f32[16,128]{1,0:T(8,128)}, bf16[16,128,128]{2,1,0:T(8,128)(2,1)S(1)}, bf16[16,1024,128]{...) while((s32[]{:T(128)}, ...), condition=%wide.region_6.7_spmd.clone, body=%wide.region_3.6_spmd.clone.sunk | while | flops 68288512 | bytes 2203749 | solution.py:148
  411.0 12.7 all-gather.21.cloned.1.call-done
  429.6 25.1 scatter_custom_fusion
  460.8 212.7 %all-gather = bf16[32,64,16]{1,2,0:T(8,128)(2,1)S(1)} all-gather(bf16[1,64,16]{1,2,0:T(8,128)(2,1)S(1)} %bitcast.394), channel_id=1, replica_groups=mesh['dp'=4,'expert'=8] {'dp','expert'}, dimensions={0}, use_global_device_ids=true | all-gather | bytes 67584 | tf_op jit(solution)/shard_map/all_gather | solution.py:115
  674.5 11.7 scatter_custom_fusion.1
  692.0 15.7 fusion.58
  707.6 15.6 fusion.54
  723.3 58.1 %all-gather.27.cloned.1.call-done = bf16[2,1024,2048]{2,1,0:T(8,128)(2,1)} async-done(((bf16[2,256,2048]{2,1,0:T(8,128)(2,1)}), bf16[2,1024,2048]{2,1,0:T(8,128)(2,1)}) %all-gather.27.cloned.1.call-update) | async-done | bytes 8388624 | tf_op jit(solution)/shard_map/all_gather | solution.py:180
  781.4 93.0 %all-to-all-done.2 = bf16[8,256,2048]{2,1,0:T(8,128)(2,1)} async-done(((bf16[8,256,2048]{2,1,0:T(8,128)(2,1)}), bf16[8,256,2048]{2,1,0:T(8,128)(2,1)}, u32[]{:S(2)}, u32[]{:S(2)}) %all-to-all-start.2) | async-done | bytes 8388640 | tf_op jit(solution)/shard_map/all_to_all | solution.py:211
  874.4 20.5 fusion.62
  894.9 15.5 convert_bitcast_fusion
  910.3 8.4 copy.144
  924.4 15.8 fusion.52
  940.2 17.0 fusion.51
  957.2 8.3 copy.147
  965.5 142.1 %all-to-all-done.1 = bf16[8,256,2048]{2,1,0:T(8,128)(2,1)} async-done(((bf16[8,256,2048]{2,1,0:T(8,128)(2,1)}), bf16[8,256,2048]{2,1,0:T(8,128)(2,1)}, u32[]{:S(2)}, u32[]{:S(2)}) %all-to-all-start.1) | async-done | bytes 8388640 | tf_op jit(solution)/shard_map/all_to_all | solution.py:190
  1113.5 13.6 gather_fusion
  1132.1 164.4 %all-to-all-done.3 = bf16[8,256,2048]{2,1,0:T(8,128)(2,1)} async-done(((bf16[8,256,2048]{2,1,0:T(8,128)(2,1)}), bf16[8,256,2048]{2,1,0:T(8,128)(2,1)}, u32[]{:S(2)}, u32[]{:S(2)}) %all-to-all-start.3) | async-done | bytes 8388640 | tf_op jit(solution)/shard_map/all_to_all | solution.py:230
  1296.6 11.3 bitcast_convert_fusion.3
  1307.8 14.7 gather_fusion.1
  1330.8 6.4 fusion.102
  1337.3 115.8 %while.29 = (s32[]{:T(128)}, f32[16,128,128]{2,1,0:T(8,128)S(1)}, bf16[16,1024,128]{2,1,0:T(8,128)(2,1)}, bf16[16,1024,128]{1,2,0:T(8,128)(2,1)}, bf16[16,128,12...) while((s32[]{:T(128)}, f32[16,128,128]{2,1,0:T(8,128)S(1)}, ...), condition=%wide.region_24.25_spmd.clone, body=%wide.region_22.24_spmd.clone.sunk | while | flops 169213952 | bytes 5972597 | solution.py:265
  1453.1 7.6 copy.166
  1460.8 6.4 copy.244
  1469.4 15.6 bitcast_convert_fusion
  1485.1 14.7 bitcast_convert_fusion.2
  1499.9 14.9 bitcast_convert_fusion.1
  1515.8 8.3 fusion.121
  1525.9 8.2 fusion.117
  1534.3 29.5 %reduce-scatter.15.cloned.1.call-done = bf16[16,128,128]{2,1,0:T(8,128)(2,1)} async-done(((bf16[16,1024,128]{2,1,0:T(8,128)(2,1)}), bf16[16,128,128]{2,1,0:T(8,128)(2,1)}) %reduce-scatter.15.cloned.1.call-update) | async-done | bytes 524304 | tf_op jit(solution)/shard_map/reduce_scatter | solution.py:267
  1570.3 8.2 fusion.133
  1584.6 8.2 fusion.135
  1592.9 103.2 %reduce-scatter.33.cloned.1.call-done = f32[64,16]{1,0:T(8,128)} async-done(((f32[2048,16]{1,0:T(8,128)}), f32[64,16]{1,0:T(8,128)}) %reduce-scatter.33.cloned.1.call-update) | async-done | bytes 4112
  1697.5 89.6 %reduce-scatter.29.cloned.1.call-done = bf16[2,256,2048]{2,1,0:T(8,128)(2,1)} async-done(((bf16[2,1024,2048]{2,1,0:T(8,128)(2,1)}), bf16[2,256,2048]{2,1,0:T(8,128)(2,1)}) %reduce-scatter.29.cloned.1.call-update) | async-done | bytes 2097168 | tf_op jit(solution)/shard_map/reduce_scatter | solution.py:305
  1791.2 85.2 %reduce-scatter.25.cloned.1.call-done = bf16[2,512,1024]{2,1,0:T(8,128)(2,1)} async-done(((bf16[2,2048,1024]{2,1,0:T(8,128)(2,1)}), bf16[2,512,1024]{2,1,0:T(8,128)(2,1)}) %reduce-scatter.25.cloned.1.call-update) | async-done | bytes 2097168 | tf_op jit(solution)/shard_map/reduce_scatter | solution.py:299
  1880.5 85.6 %reduce-scatter.27.cloned.1.call-done = bf16[2,512,1024]{2,1,0:T(8,128)(2,1)} async-done(((bf16[2,2048,1024]{2,1,0:T(8,128)(2,1)}), bf16[2,512,1024]{2,1,0:T(8,128)(2,1)}) %reduce-scatter.27.cloned.1.call-update) | async-done | bytes 2097168 | tf_op jit(solution)/shard_map/reduce_scatter | solution.py:302
  1970.3 6.4 fusion.146
  1982.9 42.0 %all-reduce.12 = (f32[2048]{0:T(1024)S(1)}, f32[2048]{0:T(1024)S(1)}, f32[2048]{0:T(1024)S(1)}, f32[2048]{0:T(1024)S(1)}) all-reduce(f32[2048]{0:T(1024)S(1)} %get-tuple-element.171, f32[2048]{0:T(1024)S(1)} %get-tuple-element.169, f32[2048]{0:T(1024)S(1)} %get-tuple-element.167, ...), channel_id=9, replica_groups=mesh['dp'=4,'expert'=8] {'dp','expert'}, use_global_device_ids=true, to_apply=%region_36.37.clone | all-reduce | flops 8192 | bytes 65536
  2028.6 124.1 %reduce-scatter.23.cloned.1.call-done = f32[64,2048]{1,0:T(8,128)} async-done(((f32[2048,2048]{1,0:T(8,128)}), f32[64,2048]{1,0:T(8,128)}) %reduce-scatter.23.cloned.1.call-update) | async-done | bytes 524304 | tf_op jit(solution)/shard_map/reduce_scatter | solution.py:291
  2152.7 187.1 %reduce-scatter.21.cloned.1.call-done = f32[64,2048]{1,0:T(8,128)} async-done(((f32[2048,2048]{1,0:T(8,128)}), f32[64,2048]{1,0:T(8,128)}) %reduce-scatter.21.cloned.1.call-update) | async-done | bytes 524304 | tf_op jit(solution)/shard_map/reduce_scatter | solution.py:290
  2339.8 187.1 %reduce-scatter.19.cloned.1.call-done = f32[64,2048]{1,0:T(8,128)} async-done(((f32[2048,2048]{1,0:T(8,128)}), f32[64,2048]{1,0:T(8,128)}) %reduce-scatter.19.cloned.1.call-update) | async-done | bytes 524304 | tf_op jit(solution)/shard_map/reduce_scatter | solution.py:289
  2526.9 187.3 %reduce-scatter.17.cloned.1.call-done = f32[64,2048]{1,0:T(8,128)} async-done(((f32[2048,2048]{1,0:T(8,128)}), f32[64,2048]{1,0:T(8,128)}) %reduce-scatter.17.cloned.1.call-update) | async-done | bytes 524304 | tf_op jit(solution)/shard_map/reduce_scatter | solution.py:288
  (515 shorter events, 301.2 us)
Async XLA Ops:
  7.2 83.4 %all-gather.11.cloned.1.call-start = ((), (), s32[]{:S(2)}) async-start(), calls=%async_computation.14 | async-start | bytes 8650752 | tf_op jit(solution)/shard_map/all_gather | solution.py:111
  7.9 161.5 %all-gather.13.cloned.1.call-start = ((), (), s32[]{:S(2)}) async-start(), calls=%async_computation.15 | async-start | bytes 8650752 | tf_op jit(solution)/shard_map/all_gather | solution.py:112
  8.7 239.8 %all-gather.17.cloned.1.call-start = ((), (), s32[]{:S(2)}) async-start(), calls=%async_computation.17 | async-start | bytes 8650752 | tf_op jit(solution)/shard_map/all_gather | solution.py:113
  9.4 286.7 %all-gather.15.cloned.1.call-start = ((), (), s32[]{:S(2)}) async-start(), calls=%async_computation.16 | async-start | bytes 4718592 | tf_op jit(solution)/shard_map/all_gather | solution.py:141
  53.3 195.2 %copy-start.20 = (f32[2048]{0:T(1024)}, f32[2048]{0:T(1024)S(1)}, u32[]{:S(2)}) copy-start(f32[2048]{0:T(1024)S(1)} %convert_element_type.171) | copy-start | bytes 24580
  53.3 42.2 %copy-start.35 = (f32[2048]{0:T(1024)}, f32[2048]{0:T(1024)S(1)}, u32[]{:S(2)}) copy-start(f32[2048]{0:T(1024)S(1)} %convert_element_type.173) | copy-start | bytes 24580
  53.3 120.9 %copy-start.37 = (f32[2048]{0:T(1024)}, f32[2048]{0:T(1024)S(1)}, u32[]{:S(2)}) copy-start(f32[2048]{0:T(1024)S(1)} %convert_element_type.175) | copy-start | bytes 24580
  54.6 40.9 %copy-start.61 = (f32[128]{0:T(128)}, f32[128]{0:T(128)S(1)}, u32[]{:S(2)}) copy-start(f32[128]{0:T(128)S(1)} %fusion.105) | copy-start | bytes 1540
  54.6 193.8 %copy-start.41 = (f32[128]{0:T(128)}, f32[128]{0:T(128)S(1)}, u32[]{:S(2)}) copy-start(f32[128]{0:T(128)S(1)} %fusion.129) | copy-start | bytes 1540
  54.9 121.3 %copy-start.25 = (f32[128,64]{1,0:T(8,128)}, f32[128,64]{1,0:T(8,128)S(1)}, u32[]{:S(2)}) copy-start(f32[128,64]{1,0:T(8,128)S(1)} %get-tuple-element.240) | copy-start | bytes 98308
  54.9 121.3 %copy-start.27 = (f32[128,64]{1,0:T(8,128)}, f32[128,64]{1,0:T(8,128)S(1)}, u32[]{:S(2)}) copy-start(f32[128,64]{1,0:T(8,128)S(1)} %get-tuple-element.241) | copy-start | bytes 98308
  55.0 114.5 %copy-start = (bf16[1,128,2048]{2,1,0:T(8,128)(2,1)S(1)}, bf16[1,128,2048]{2,1,0:T(8,128)(2,1)}, u32[]{:S(2)}) copy-start(bf16[1,128,2048]{2,1,0:T(8,128)(2,1)} %param.19) | copy-start | bytes 1572868
  95.5 78.7 %copy-start.63 = (f32[128]{0:T(128)}, f32[128]{0:T(128)S(1)}, u32[]{:S(2)}) copy-start(f32[128]{0:T(128)S(1)} %get-tuple-element.244) | copy-start | bytes 1540
  95.5 78.7 %copy-start.52 = (f32[128]{0:T(128)}, f32[128]{0:T(128)S(1)}, u32[]{:S(2)}) copy-start(f32[128]{0:T(128)S(1)} %fusion.130) | copy-start | bytes 1540
  178.8 76.7 %copy-start.43 = (s32[1,128,8]{1,2,0:T(8,128)S(1)}, s32[1,128,8]{1,2,0:T(8,128)}, u32[]{:S(2)}) copy-start(s32[1,128,8]{1,2,0:T(8,128)} %param.20) | copy-start | bytes 12292
  178.8 165.8 %all-gather.19.cloned.1.call-start = ((), (), s32[]{:S(2)}) async-start(), calls=%async_computation.18 | async-start | bytes 4718592 | tf_op jit(solution)/shard_map/all_gather | solution.py:142
  254.1 169.6 %all-gather.21.cloned.1.call-start = ((), (), s32[]{:S(2)}) async-start(), calls=%async_computation.19 | async-start | bytes 8650752 | tf_op jit(solution)/shard_map/all_gather | solution.py:114
  254.7 437.3 %all-gather.23.cloned.1.call-start = ((), (), s32[]{:S(2)}) async-start(), calls=%async_computation.20 | async-start | bytes 10485760 | tf_op jit(solution)/shard_map/all_gather | solution.py:178
  255.8 172.7 %copy-start.39 = (f32[2048]{0:T(1024)}, f32[2048]{0:T(1024)S(1)}, u32[]{:S(2)}) copy-start(f32[2048]{0:T(1024)S(1)} %convert_element_type.180) | copy-start | bytes 24580
  261.0 413.4 %copy-start.46 = (s32[1024,1]{0,1:T(1,128)}, s32[1024,1]{0,1:T(1,128)S(1)}, u32[]{:S(2)}) copy-start(s32[1024,1]{0,1:T(1,128)S(1)} %compare_select_fusion.1) | copy-start | bytes 12292
  428.5 26.3 copy-start.59
  429.6 244.3 %copy-start.10 = (bf16[128,2048]{1,0:T(8,128)(2,1)}, bf16[128,2048]{1,0:T(8,128)(2,1)S(1)}, u32[]{:S(2)}) copy-start(bf16[128,2048]{1,0:T(8,128)(2,1)S(1)} %multiply_convert_fusion.1) | copy-start | bytes 1572868
  454.8 219.0 %copy-start.22 = (bf16[1,128,2048]{2,1,0:T(8,128)(2,1)S(1)}, bf16[1,128,2048]{2,1,0:T(8,128)(2,1)}, u32[]{:S(2)}) copy-start(bf16[1,128,2048]{2,1,0:T(8,128)(2,1)} %param.21) | copy-start | bytes 1572868
  454.8 231.4 %all-to-all-start = ((bf16[8,256,2048]{2,1,0:T(8,128)(2,1)}), bf16[8,256,2048]{2,1,0:T(8,128)(2,1)}, u32[]{:S(2)}, u32[]{:S(2)}) async-start(bf16[8,256,2048]{2,1,0:T(8,128)(2,1)} %bitcast.369), calls=%async_computation | async-start | bytes 16777216 | tf_op jit(solution)/shard_map/all_to_all | solution.py:169
  460.0 247.6 %all-gather.25.cloned.1.call-start = ((), (), s32[]{:S(2)}) async-start(), calls=%async_computation.21 | async-start | bytes 10485760 | tf_op jit(solution)/shard_map/all_gather | solution.py:179
  686.2 188.1 %all-to-all-start.2 = ((bf16[8,256,2048]{2,1,0:T(8,128)(2,1)}), bf16[8,256,2048]{2,1,0:T(8,128)(2,1)}, u32[]{:S(2)}, u32[]{:S(2)}) async-start(bf16[8,256,2048]{2,1,0:T(8,128)(2,1)} %bitcast.370), calls=%async_computation.2 | async-start | bytes 16777216 | tf_op jit(solution)/shard_map/all_to_all | solution.py:211
  691.2 90.2 %all-gather.27.cloned.1.call-start = ((), (), s32[]{:S(2)}) async-start(), calls=%async_computation.22 | async-start | bytes 10485760 | tf_op jit(solution)/shard_map/all_gather | solution.py:180
  918.7 188.9 %all-to-all-start.1 = ((bf16[8,256,2048]{2,1,0:T(8,128)(2,1)}), bf16[8,256,2048]{2,1,0:T(8,128)(2,1)}, u32[]{:S(2)}, u32[]{:S(2)}) async-start(bf16[8,256,2048]{2,1,0:T(8,128)(2,1)} %bitcast.371), calls=%async_computation.1 | async-start | bytes 16777216 | tf_op jit(solution)/shard_map/all_to_all | solution.py:190
  1107.6 189.0 %all-to-all-start.3 = ((bf16[8,256,2048]{2,1,0:T(8,128)(2,1)}), bf16[8,256,2048]{2,1,0:T(8,128)(2,1)}, u32[]{:S(2)}, u32[]{:S(2)}) async-start(bf16[8,256,2048]{2,1,0:T(8,128)(2,1)} %bitcast.368), calls=%async_computation.3 | async-start | bytes 16777216 | tf_op jit(solution)/shard_map/all_to_all | solution.py:230
  1113.4 410.8 %reduce-scatter.31.cloned.1.call-start = ((), (), s32[]{:S(2)}) async-start(), calls=%async_computation.31 | async-start | bytes 4718592
  1467.2 96.6 %reduce-scatter.15.cloned.1.call-start = ((), (), s32[]{:S(2)}) async-start(), calls=%async_computation.23 | async-start | bytes 4718592 | tf_op jit(solution)/shard_map/reduce_scatter | solution.py:267
  1467.9 228.2 %reduce-scatter.33.cloned.1.call-start = ((), (), s32[]{:S(2)}) async-start(), calls=%async_computation.32 | async-start | bytes 1081344
  1469.4 317.7 %reduce-scatter.29.cloned.1.call-start = ((), (), s32[]{:S(2)}) async-start(), calls=%async_computation.30 | async-start | bytes 10485760 | tf_op jit(solution)/shard_map/reduce_scatter | solution.py:305
  1485.1 391.4 %reduce-scatter.25.cloned.1.call-start = ((), (), s32[]{:S(2)}) async-start(), calls=%async_computation.28 | async-start | bytes 10485760 | tf_op jit(solution)/shard_map/reduce_scatter | solution.py:299
  1499.9 466.2 %reduce-scatter.27.cloned.1.call-start = ((), (), s32[]{:S(2)}) async-start(), calls=%async_computation.29 | async-start | bytes 10485760 | tf_op jit(solution)/shard_map/reduce_scatter | solution.py:302
  1514.8 637.9 %reduce-scatter.23.cloned.1.call-start = ((), (), s32[]{:S(2)}) async-start(), calls=%async_computation.27 | async-start | bytes 17301504 | tf_op jit(solution)/shard_map/reduce_scatter | solution.py:291
  1524.2 815.7 %reduce-scatter.21.cloned.1.call-start = ((), (), s32[]{:S(2)}) async-start(), calls=%async_computation.26 | async-start | bytes 17301504 | tf_op jit(solution)/shard_map/reduce_scatter | solution.py:290
  1534.2 30.8 %copy-start.26 = (f32[128,64]{1,0:T(8,128)S(1)}, f32[128,64]{1,0:T(8,128)}, u32[]{:S(2)}) copy-start(f32[128,64]{1,0:T(8,128)} %copy-done.25) | copy-start | bytes 98308
  1534.2 30.8 %copy-start.28 = (f32[128,64]{1,0:T(8,128)S(1)}, f32[128,64]{1,0:T(8,128)}, u32[]{:S(2)}) copy-start(f32[128,64]{1,0:T(8,128)} %copy-done.27) | copy-start | bytes 98308
  1534.2 34.3 %copy-start.7 = (f32[128,2048]{1,0:T(8,128)S(1)}, f32[128,2048]{1,0:T(8,128)}, u32[]{:S(2)}) copy-start(f32[128,2048]{1,0:T(8,128)} %copy-done.6) | copy-start | bytes 3145732
  1534.2 34.3 %copy-start.38 = (f32[2048]{0:T(1024)S(1)}, f32[2048]{0:T(1024)}, u32[]{:S(2)}) copy-start(f32[2048]{0:T(1024)} %copy-done.37) | copy-start | bytes 24580
  1534.2 34.3 %copy-start.55 = (f32[128]{0:T(128)S(1)}, f32[128]{0:T(128)}, u32[]{:S(2)}) copy-start(f32[128]{0:T(128)} %copy-done.54) | copy-start | bytes 1540
  1534.2 34.8 %copy-start.66 = (f32[128]{0:T(128)S(1)}, f32[128]{0:T(128)}, u32[]{:S(2)}) copy-start(f32[128]{0:T(128)} %copy-done.65) | copy-start | bytes 1540
  1534.2 992.7 %reduce-scatter.19.cloned.1.call-start = ((), (), s32[]{:S(2)}) async-start(), calls=%async_computation.25 | async-start | bytes 17301504 | tf_op jit(solution)/shard_map/reduce_scatter | solution.py:289
  1578.6 1135.6 %reduce-scatter.17.cloned.1.call-start = ((), (), s32[]{:S(2)}) async-start(), calls=%async_computation.24 | async-start | bytes 17301504 | tf_op jit(solution)/shard_map/reduce_scatter | solution.py:288
  1697.5 272.8 %copy-start.13 = (bf16[128,2048]{1,0:T(8,128)(2,1)S(1)}, bf16[128,2048]{1,0:T(8,128)(2,1)}, u32[]{:S(2)}) copy-start(bf16[128,2048]{1,0:T(8,128)(2,1)} %copy-done.12) | copy-start | bytes 1572868
  1880.5 96.2 %copy-start.15 = (bf16[128,2048]{1,0:T(8,128)(2,1)S(1)}, bf16[128,2048]{1,0:T(8,128)(2,1)}, u32[]{:S(2)}) copy-start(bf16[128,2048]{1,0:T(8,128)(2,1)} %copy-done.14) | copy-start | bytes 1572868
  1979.7 47.6 %copy-start.62 = (f32[128]{0:T(128)S(1)}, f32[128]{0:T(128)}, u32[]{:S(2)}) copy-start(f32[128]{0:T(128)} %copy-done.61) | copy-start | bytes 1540
  (46 other events, 366.2 us)
Sparse Core Ops, SparseCore 0:
  11.0 79.4 all-gather.10
  93.5 75.8 all-gather.12
  172.4 75.9 all-gather.16
  250.5 45.5 all-gather.14
  298.1 46.3 all-gather.18
  347.4 76.3 all-gather.20
  425.6 85.8 all-gather.22
  513.3 87.6 all-gather.24
  693.9 87.4 all-gather.26
  1467.3 45.9 reduce-scatter.30
  1515.6 48.1 reduce-scatter.14
  1565.9 130.1 reduce-scatter.32
  1699.5 87.5 reduce-scatter.28
  1790.0 86.4 reduce-scatter.24
  1879.7 86.3 reduce-scatter.26
  1968.8 183.8 reduce-scatter.22
  2155.4 184.3 reduce-scatter.20
  2342.5 184.3 reduce-scatter.18
  2529.8 184.3 reduce-scatter.16
where the time goes:
time: 2740 us; the launch traced here: 2720 us
  waiting for transfers between devices  1820 us (66%)
  matrix products  362 us (13%)
  blocking collectives  295 us (11%)
  local copies, waits for them, and re-layouts  135 us (5%)
  other arithmetic  74.2 us (3%)
    all_gather x1, blocking collectives, shards(): lax.all_gather(w_router, ('dp', 'expert'), axis=0, tiled=True)  213 us
    reduce_scatter x1, waiting for transfers between devices, shards(): lax.psum_scatter(d_query_w, ('dp', 'expert'), scatter_dimension=0, tiled=...  187 us
    reduce_scatter x1, waiting for transfers between devices, shards(): lax.psum_scatter(d_key_w, ('dp', 'expert'), scatter_dimension=0, tiled=True)  187 us
    reduce_scatter x1, waiting for transfers between devices, shards(): lax.psum_scatter(d_value_w, ('dp', 'expert'), scatter_dimension=0, tiled=...  187 us
    all_to_all x1, waiting for transfers between devices, shards(): lax.all_to_all(d_inputs.reshape(groups, local_experts * capacity, model_w...  164 us
    all_to_all x1, waiting for transfers between devices, shards(): lax.all_to_all(expert_out.reshape(groups, local_experts * capacity, model...  142 us
    reduce_scatter x1, waiting for transfers between devices, shards(): lax.psum_scatter(d_out_w, ('dp', 'expert'), scatter_dimension=0, tiled=True)  124 us
    unnamed x21, waiting for transfers between devices  108 us
  transfers between devices with their start and end apart: 23, of which 19 were waited for; matrix products, arithmetic and copies ran while one was open for 13% of the time, Pallas kernels for 0%

commit v1 on v0

v1 whole, which is shorter than its diff:
```python
import math

import jax
import jax.numpy as jnp
from jax import lax
from jax.sharding import PartitionSpec as P

HEADS = 16
HEAD_DIM = 128

EPS = 1e-05
THETA = 10000.0
NEG = -1e30

F32 = jnp.float32
BF16 = jnp.bfloat16


def dot(left, right):
    return jnp.dot(left, right, preferred_element_type=F32)


def dot_tn(left, right):
    return lax.dot_general(left, right, (((0,), (0,)), ((), ())), preferred_element_type=F32)


def dot_nt(left, right):
    return lax.dot_general(left, right, (((1,), (1,)), ((), ())), preferred_element_type=F32)


def inv_rms(values):
    return lax.rsqrt(jnp.mean(values * values, axis=-1, keepdims=True) + EPS)


def norm_back(values, inv, gain_vec, grad):
    scaled = grad * gain_vec
    mean_dot = jnp.mean(scaled * values, axis=-1, keepdims=True)
    d_values = inv * scaled - values * (inv * inv * inv * mean_dot)
    d_gain = jnp.sum(grad * values * inv, axis=0)
    return d_values, d_gain


def rope_tables(length):
    half_dim = HEAD_DIM // 2
    inv_freq = jnp.exp(
        jnp.arange(half_dim, dtype=F32) * (-2.0 * math.log(THETA) / HEAD_DIM)
    )
    angles = jnp.arange(length, dtype=jnp.int32).astype(F32)[:, None] * inv_freq[None, :]
    cosine, sine = jnp.cos(angles), jnp.sin(angles)
    return (
        jnp.concatenate([cosine, cosine], axis=1)[:, None, :],
        jnp.concatenate([-sine, sine], axis=1)[:, None, :],
    )


def swap_halves(values):
    half_dim = HEAD_DIM // 2
    return jnp.concatenate([values[..., half_dim:], values[..., :half_dim]], axis=-1)


def rotary(values, tables):
    return values * tables[0] + swap_halves(values) * tables[1]


def rotary_back(grad, tables):
    return grad * tables[0] - swap_halves(grad) * tables[1]


def gather_expert(block, axis=0):
    return lax.all_gather(block, "expert", axis=axis, tiled=True)


def scatter_expert(partial):
    return lax.psum_scatter(partial.astype(BF16), "expert", scatter_dimension=0, tiled=True).astype(F32)


def shards(
    tokens, routes, grad_output, w_query, w_key, w_value, w_out, w_router,
    gain_attn, gain_query, gain_key, gain_ffn, w_gate, w_up, w_down,
):
    rows = tokens.shape[1]
    width = tokens.shape[2]
    groups = lax.axis_size("expert")
    seqs = lax.axis_size("dp")
    me = lax.axis_index("expert")
    length = rows * groups
    local_experts = w_gate.shape[0]
    all_experts = local_experts * groups
    block = w_query.shape[0]
    own = width // groups
    slab = max(own, HEAD_DIM)
    copies = slab // own
    heads = slab // HEAD_DIM
    share = 1.0 / copies
    offset = (me % copies) * own

    x_low = tokens.reshape(rows, width)
    g_low = grad_output.reshape(rows, width)

    small = jnp.concatenate(
        [w_router] + [g[:, None] for g in (gain_attn, gain_query, gain_key, gain_ffn)], axis=1
    )
    small_all = lax.all_gather(small, ("dp", "expert"), axis=0, tiled=True)
    w_r = small_all[:, :all_experts]
    gains = small_all[:, all_experts:].astype(F32)
    g_attn, g_ffn = gains[:, 0], gains[:, 3]
    slab_start = (me // copies) * slab
    g_query = lax.dynamic_slice(gains[:, 1], (slab_start,), (slab,))
    g_key = lax.dynamic_slice(gains[:, 2], (slab_start,), (slab,))

    qkv_send = jnp.stack([w_query, w_key, w_value], axis=1).reshape(block, 3, width // slab, slab)
    qkv_send = qkv_send.transpose(2, 0, 1, 3).reshape(width // slab, block, 3 * slab)
    qkv_send = jnp.repeat(qkv_send, copies, axis=0)
    qkv_got = lax.all_to_all(qkv_send, "expert", split_axis=0, concat_axis=0, tiled=True)
    w_qkv = lax.all_gather(qkv_got.reshape(groups * block, 3 * slab), "dp", axis=0, tiled=True)
    total = seqs * groups
    moves = [(b, (b % seqs) * groups + b // seqs) for b in range(total)]
    w_o = lax.ppermute(w_out, ("dp", "expert"), moves)
    w_o = lax.all_gather(w_o, "dp", axis=0, tiled=True)
    if copies > 1:
        sets = [[c * copies + i for i in range(copies)] for c in range(groups // copies)]
        w_o = lax.all_gather(w_o, "expert", axis_index_groups=sets, axis=0, tiled=True)

    x_in = x_low.astype(F32)
    inv_attn = inv_rms(x_in)
    normed_low = (x_in * inv_attn * g_attn).astype(BF16)
    normed_all = gather_expert(normed_low)
    g_all = gather_expert(g_low)

    raw = dot(normed_all, w_qkv)
    q_raw, k_raw, v_raw = raw[:, :slab], raw[:, slab : 2 * slab], raw[:, 2 * slab :]
    squares = jnp.stack([jnp.sum(q_raw * q_raw, axis=1), jnp.sum(k_raw * k_raw, axis=1)], axis=0)
    squares = lax.psum(squares * share, "expert")
    inv_qk = lax.rsqrt(squares / width + EPS)
    inv_q, inv_k = inv_qk[0][:, None], inv_qk[1][:, None]
    tables = rope_tables(length)

    def to_heads(values):
        return values.reshape(length, heads, HEAD_DIM)

    queries = rotary(to_heads(q_raw * inv_q * g_query), tables).astype(BF16).transpose(1, 0, 2)
    keys = rotary(to_heads(k_raw * inv_k * g_key), tables).astype(BF16).transpose(1, 0, 2)
    values = to_heads(v_raw).astype(BF16).transpose(1, 0, 2)
    positions = jnp.arange(length, dtype=jnp.int32)
    scale = HEAD_DIM ** (-0.5)

    def head_probs(q, k):
        scores = dot_nt(q, k) * scale
        scores = jnp.where(positions[None, :] <= positions[:, None], scores, NEG)
        exp_terms = jnp.exp(scores - jnp.max(scores, axis=-1, keepdims=True))
        return exp_terms / jnp.sum(exp_terms, axis=-1, keepdims=True)

    mixes = []
    for h in range(heads):
        mixes.append(dot(head_probs(queries[h], keys[h]).astype(BF16), values[h]).astype(BF16))
    mix = jnp.concatenate(mixes, axis=1)
    after_attn = x_in + scatter_expert(dot(mix, w_o) * share)

    inv_ffn = inv_rms(after_attn)
    ffn_low = (after_attn * inv_ffn * g_ffn).astype(BF16)
    ffn_all = gather_expert(ffn_low)
    router_prob = jax.nn.softmax(dot(ffn_low, w_r), axis=-1)
    chosen = routes.reshape(rows, routes.shape[2])
    chosen_mask = jnp.sum(
        (chosen[:, :, None] == jnp.arange(all_experts, dtype=jnp.int32)[None, None, :]).astype(F32),
        axis=1,
    )
    route_dense = router_prob * chosen_mask
    route_all = gather_expert(route_dense)
    route_mine = lax.dynamic_slice(route_all, (0, me * local_experts), (length, local_experts))

    wg, wu, wd = (
        lax.all_gather(w_gate, "dp", axis=1, tiled=True),
        lax.all_gather(w_up, "dp", axis=1, tiled=True),
        lax.all_gather(w_down, "dp", axis=1, tiled=True),
    )
    y_part = 0.0
    dx_part = 0.0
    d_down, d_gate_w, d_up_w, d_weights = [], [], [], []
    for i in range(local_experts):
        weight = route_mine[:, i : i + 1]
        gate = dot(ffn_all, wg[i])
        up = dot(ffn_all, wu[i])
        d_hid = dot_nt(g_all, wd[i])
        sig = jax.nn.sigmoid(gate)
        silu = gate * sig
        hidden = silu * up
        d_weights.append(jnp.sum(hidden * d_hid, axis=1))
        hidden_w = (hidden * weight).astype(BF16)
        d_hid = d_hid * weight
        d_gate = (d_hid * up * sig * (1.0 + gate * (1.0 - sig))).astype(BF16)
        d_up = (d_hid * silu).astype(BF16)
        y_part = y_part + dot(hidden_w, wd[i])
        d_down.append(dot_tn(hidden_w, g_all).astype(BF16))
        d_gate_w.append(dot_tn(ffn_all, d_gate).astype(BF16))
        d_up_w.append(dot_tn(ffn_all, d_up).astype(BF16))
        dx_part = dx_part + dot_nt(d_gate, wg[i]) + dot_nt(d_up, wu[i])
    d_down, d_gate_w, d_up_w = jnp.stack(d_down), jnp.stack(d_gate_w), jnp.stack(d_up_w)

    output = after_attn + scatter_expert(y_part)
    d_rows = scatter_expert(dx_part)
    d_weight = lax.all_to_all(
        jnp.stack(d_weights, axis=0).reshape(local_experts, groups, rows).transpose(1, 0, 2),
        "expert", split_axis=0, concat_axis=0, tiled=True,
    )
    d_router_prob = d_weight.reshape(all_experts, rows).T * chosen_mask

    d_logits = (
        router_prob * (d_router_prob - jnp.sum(d_router_prob * router_prob, axis=-1, keepdims=True))
    ).astype(BF16)
    d_router_w = dot_tn(ffn_low, d_logits)
    d_normed_ffn = d_rows + dot_nt(d_logits, w_r)
    d_after_norm, d_gain_ffn = norm_back(after_attn, inv_ffn, g_ffn, d_normed_ffn)
    d_after = g_low.astype(F32) + d_after_norm
    d_after_all = gather_expert(d_after.astype(BF16))

    d_out_w = dot_tn(mix, d_after_all)
    d_mix = dot_nt(d_after_all, w_o).astype(BF16)
    dqs, dks, dvs = [], [], []
    for h in range(heads):
        prob = head_probs(queries[h], keys[h])
        d_m = d_mix[:, h * HEAD_DIM : (h + 1) * HEAD_DIM]
        d_prob = dot_nt(d_m, values[h])
        row_delta = jnp.sum(d_prob * prob, axis=-1, keepdims=True)
        d_score = (prob * (d_prob - row_delta) * scale).astype(BF16)
        dqs.append(dot(d_score, keys[h]))
        dks.append(dot_tn(d_score, queries[h]))
        dvs.append(dot_tn(prob.astype(BF16), d_m))
    dq_n = rotary_back(jnp.stack(dqs, axis=1), tables).reshape(length, slab)
    dk_n = rotary_back(jnp.stack(dks, axis=1), tables).reshape(length, slab)
    dv_low = jnp.concatenate(dvs, axis=1).astype(BF16)
    dots = jnp.stack(
        [jnp.sum(dq_n * g_query * q_raw, axis=1), jnp.sum(dk_n * g_key * k_raw, axis=1)], axis=0
    )
    dots = lax.psum(dots * share, "expert") / width
    d_gain_query = jnp.sum(dq_n * q_raw * inv_q, axis=0)
    d_gain_key = jnp.sum(dk_n * k_raw * inv_k, axis=0)
    dq_low = (inv_q * dq_n * g_query - q_raw * (inv_q**3 * dots[0][:, None])).astype(BF16)
    dk_low = (inv_k * dk_n * g_key - k_raw * (inv_k**3 * dots[1][:, None])).astype(BF16)
    d_raw = jnp.concatenate([dq_low, dk_low, dv_low], axis=1)
    d_qkv_w = dot_tn(normed_all, d_raw).astype(BF16)
    d_normed_in = scatter_expert(dot_nt(d_raw, w_qkv) * share)
    d_in_norm, d_gain_attn = norm_back(x_in, inv_attn, g_attn, d_normed_in)
    input_grad = d_after + d_in_norm

    d_qkv_w = d_qkv_w.reshape(width, 3, slab)
    d_qkv_w = lax.dynamic_slice(d_qkv_w, (0, 0, offset), (width, 3, own))
    d_qkv_w = lax.psum_scatter(
        d_qkv_w.reshape(width, 3 * own), "dp", scatter_dimension=0, tiled=True
    )
    d_qkv_w = lax.all_to_all(
        d_qkv_w.reshape(groups, block, 3 * own), "expert", split_axis=0, concat_axis=0, tiled=True
    ).reshape(groups, block, 3, own)
    d_qkv_w = d_qkv_w.transpose(2, 1, 0, 3).reshape(3, block, width).astype(F32)
    d_out_w = lax.dynamic_slice(d_out_w.astype(BF16), (offset, 0), (own, width))
    d_out_w = lax.psum_scatter(d_out_w, "dp", scatter_dimension=0, tiled=True)
    d_out_w = lax.ppermute(d_out_w, ("dp", "expert"), [(b, a) for a, b in moves]).astype(F32)

    spread = jnp.zeros((2, width), F32)
    spread = lax.dynamic_update_slice(
        spread, jnp.stack([d_gain_query, d_gain_key]) * share, (0, slab_start)
    )
    small_grad = jnp.concatenate(
        [d_router_w, d_gain_attn[:, None], spread.T, d_gain_ffn[:, None]], axis=1
    )
    small_grad = lax.psum_scatter(small_grad, ("dp", "expert"), scatter_dimension=0, tiled=True)

    expert_owned = [
        lax.psum_scatter(d, "dp", scatter_dimension=1, tiled=True).astype(F32)
        for d in (d_gate_w, d_up_w, d_down)
    ]
    return (
        output.reshape(1, rows, width),
        input_grad.reshape(1, rows, width),
        d_qkv_w[0],
        d_qkv_w[1],
        d_qkv_w[2],
        d_out_w,
        small_grad[:, :all_experts],
        small_grad[:, all_experts],
        small_grad[:, all_experts + 1],
        small_grad[:, all_experts + 2],
        small_grad[:, all_experts + 3],
        *expert_owned,
    )


def solution(mesh):
    tok = P("dp", "expert", None)
    mat = P(("dp", "expert"), None)
    vec = P(("dp", "expert"))
    exp = P("expert", "dp", None)
    return jax.shard_map(
        shards,
        mesh=mesh,
        in_specs=(tok, tok, tok, mat, mat, mat, mat, mat, vec, vec, vec, vec, exp, exp, exp),
        out_specs=(tok, tok, mat, mat, mat, mat, mat, vec, vec, vec, vec, exp, exp, exp),
        check_vma=False,
    )
```

time: 2740 us -> 1400 us (0.51)
  waiting for transfers between devices: 1820 us -> 951 us
  blocking collectives: 295 us -> 118 us
  matrix products: 362 us -> 198 us
  local copies, waits for them, and re-layouts: 135 us -> 29.5 us
    reduce_scatter x8 -> x9, waiting for transfers between devices: 976 us -> 408 us  [the longest x3 239 us: shards(): lax.psum_scatter(d, 'dp', scatter_dimension=1, tiled=True).astype(F32)]
    all_to_all x4 -> x1, waiting for transfers between devices: 399 us -> 0.01 us  [shards(): lax.all_to_all(d_qkv_w.reshape(groups, block, 3 * own), 'expert', split_a...]
    dot_general x135 -> x39, matrix products: 360 us -> 198 us  [the longest x13 71.2 us: dot_nt(): lax.dot_general(left, right, (((1,), (1,)), ((), ())), preferred_element_...]
    all_gather x1 -> x2, blocking collectives: 213 us -> 55.1 us  [the longest x1 40.6 us: shards(): small_all = lax.all_gather(small, ('dp', 'expert'), axis=0, tiled=True)]
    all_gather x6, waiting for transfers between devices: 274 us -> 187 us  [the longest x4 187 us: gather_expert(): return lax.all_gather(block, 'expert', axis=axis, tiled=True)]
    unnamed x2 -> x0, blocking collectives: 82.4 us -> none
    all_gather x1, waiting for transfers between devices: 0.02 us -> 71.2 us  [shards(): lax.all_gather(w_gate, 'dp', axis=1, tiled=True)]
    all_gather x1, waiting for transfers between devices: 0.01 us -> 58.2 us  [shards(): lax.all_gather(w_up, 'dp', axis=1, tiled=True)]
  transfers between devices with their start and end apart: 23 -> 22, of which waited for: 19 -> 16; matrix products, arithmetic and copies ran while one was open for 13% -> 12% of each run, Pallas kernels for 0% -> 0%
where the time goes in v1:
time: 1400 us; the launch traced here: 1380 us
  waiting for transfers between devices  951 us (68%)
  matrix products  198 us (14%)
  blocking collectives  118 us (8%)
  other arithmetic  55.3 us (4%)
  local copies, waits for them, and re-layouts  29.5 us (2%)
  between operations  15.9 us (1%)
  starting transfers between devices  14.6 us (1%)
    reduce_scatter x3, waiting for transfers between devices, shards(): lax.psum_scatter(d, 'dp', scatter_dimension=1, tiled=True).astype(F32)  239 us
    all_gather x4, waiting for transfers between devices, gather_expert(): return lax.all_gather(block, 'expert', axis=axis, tiled=True)  187 us
    reduce_scatter x4, waiting for transfers between devices, scatter_expert(): lax.psum_scatter(partial.astype(BF16), 'expert', scatter_dimension=0, til...  169 us
    unnamed x20, waiting for transfers between devices  132 us
    all_gather x1, waiting for transfers between devices, shards(): lax.all_gather(w_down, 'dp', axis=1, tiled=True)  87.6 us
    dot_general x13, matrix products, dot_nt(): lax.dot_general(left, right, (((1,), (1,)), ((), ())), preferred_element_...  71.2 us
    all_gather x1, waiting for transfers between devices, shards(): lax.all_gather(w_gate, 'dp', axis=1, tiled=True)  71.2 us
    dot_general x13, matrix products, dot(): return jnp.dot(left, right, preferred_element_type=F32)  71.1 us
  transfers between devices with their start and end apart: 22, of which 16 were waited for; matrix products, arithmetic and copies ran while one was open for 12% of the time, Pallas kernels for 0%

profile of v1, /device:TPU:5, one launch (start us, length us, event | category | flops | bytes accessed | tf_op | source)
XLA Modules:
  0.0 1382.4 jit_solution(10244016583605328332)
XLA Ops:
  14.3 25.4 %all_to_all.15 = bf16[8,64,768]{2,1,0:T(8,128)(2,1)} all-to-all(bf16[8,64,768]{2,1,0:T(8,128)(2,1)S(1)} %reshape_broadcast_in_dim_reshape.3), channel_id=1, replica_groups=mesh['dp'=4,'expert'=8] {'expert'}, dimensions={0} | all-to-all | bytes 1572864 | tf_op jit(solution)/shard_map/all_to_all | solution.py:114
  39.9 40.6 %all-gather.1 = bf16[32,64,20]{1,2,0:T(8,128)(2,1)S(1)} all-gather(bf16[1,64,20]{1,2,0:T(8,128)(2,1)S(1)} %bitcast.315), channel_id=1, replica_groups=mesh['dp'=4,'expert'=8] {'dp','expert'}, dimensions={0}, use_global_device_ids=true | all-gather | bytes 84480 | tf_op jit(solution)/shard_map/all_gather | solution.py:103
  85.7 7.4 collective-permute-done
  93.9 45.0 %all-gather.12.cloned.1.call-done = bf16[1024,2048]{1,0:T(8,128)(2,1)} async-done(((bf16[128,2048]{1,0:T(8,128)(2,1)}), bf16[1024,2048]{1,0:T(8,128)(2,1)}) %all-gather.12.cloned.1.call-update) | async-done | bytes 4194320 | tf_op jit(solution)/shard_map/all_gather | solution.py:70
  139.0 6.2 fusion.106
  147.1 13.6 psum.14
  176.4 45.1 %reduce-scatter.13.cloned.1.call-done = bf16[128,2048]{1,0:T(8,128)(2,1)} async-done(((bf16[1024,2048]{1,0:T(8,128)(2,1)}), bf16[128,2048]{1,0:T(8,128)(2,1)}) %reduce-scatter.13.cloned.1.call-update) | async-done | bytes 524304 | tf_op jit(solution)/shard_map/reduce_scatter | solution.py:74
  226.1 44.7 %all-gather.28.cloned.1.call-done = bf16[1,1024,2048]{2,1,0:T(8,128)(2,1)} async-done(((bf16[1,128,2048]{2,1,0:T(8,128)(2,1)}), bf16[1,1024,2048]{2,1,0:T(8,128)(2,1)}) %all-gather.28.cloned.1.call-update) | async-done | bytes 4194320 | tf_op jit(solution)/shard_map/all_gather | solution.py:70
  270.9 87.6 %all-gather.24.cloned.1.call-done = bf16[2,1024,2048]{2,1,0:T(8,128)(2,1)} async-done(((bf16[2,256,2048]{2,1,0:T(8,128)(2,1)}), bf16[2,1024,2048]{2,1,0:T(8,128)(2,1)}) %all-gather.24.cloned.1.call-update) | async-done | bytes 8388624 | tf_op jit(solution)/shard_map/all_gather | solution.py:175
  358.5 10.4 fusion.4
  368.9 6.1 fusion.6
  375.4 14.5 %all_gather.40 = f32[1024,16]{0,1:T(8,128)S(1)} all-gather(f32[128,16]{0,1:T(8,128)S(1)} %fusion.92), channel_id=1, replica_groups=mesh['dp'=4,'expert'=8] {'expert'}, dimensions={0}, use_global_device_ids=true | all-gather | bytes 73728 | tf_op jit(solution)/shard_map/all_gather | solution.py:70
  389.9 58.2 %all-gather.22.cloned.1.call-done = bf16[2,2048,1024]{2,1,0:T(8,128)(2,1)} async-done(((bf16[2,512,1024]{2,1,0:T(8,128)(2,1)}), bf16[2,2048,1024]{2,1,0:T(8,128)(2,1)}) %all-gather.22.cloned.1.call-update) | async-done | bytes 8388624 | tf_op jit(solution)/shard_map/all_gather | solution.py:174
  448.0 49.8 %all-gather.18.cloned.1.call-done = bf16[1024,2048]{1,0:T(8,128)(2,1)} async-done(((bf16[128,2048]{1,0:T(8,128)(2,1)}), bf16[1024,2048]{1,0:T(8,128)(2,1)}) %all-gather.18.cloned.1.call-update) | async-done | bytes 4194320 | tf_op jit(solution)/shard_map/all_gather | solution.py:70
  497.8 10.3 fusion.25
  508.1 6.3 fusion.21
  514.4 71.2 %all-gather.20.cloned.1.call-done = bf16[2,2048,1024]{2,1,0:T(8,128)(2,1)} async-done(((bf16[2,512,1024]{2,1,0:T(8,128)(2,1)}), bf16[2,2048,1024]{2,1,0:T(8,128)(2,1)}) %all-gather.20.cloned.1.call-update) | async-done | bytes 8388624 | tf_op jit(solution)/shard_map/all_gather | solution.py:173
  585.6 13.1 multiply_convert_fusion.3
  598.7 6.9 fusion.23
  605.6 12.7 multiply_convert_fusion.5
  618.3 10.5 fusion.18
  628.8 6.9 fusion.20
  635.8 13.5 add_convert_fusion
  649.3 10.5 all_to_all.16
  659.9 37.4 %reduce-scatter.17.cloned.1.call-done = bf16[128,2048]{1,0:T(8,128)(2,1)} async-done(((bf16[1024,2048]{1,0:T(8,128)(2,1)}), bf16[128,2048]{1,0:T(8,128)(2,1)}) %reduce-scatter.17.cloned.1.call-update) | async-done | bytes 524304 | tf_op jit(solution)/shard_map/reduce_scatter | solution.py:74
  702.2 47.5 %all-gather.26.cloned.1.call-done = bf16[1024,2048]{1,0:T(8,128)(2,1)} async-done(((bf16[128,2048]{1,0:T(8,128)(2,1)}), bf16[1024,2048]{1,0:T(8,128)(2,1)}) %all-gather.26.cloned.1.call-update) | async-done | bytes 4194320 | tf_op jit(solution)/shard_map/all_gather | solution.py:70
  767.4 13.6 psum.15
  784.2 4.9 convolution_convert_fusion.2
  793.8 7.7 convert_bitcast_fusion.4
  801.6 6.3 convert_bitcast_fusion.5
  807.9 6.3 pad_maximum_fusion
  815.8 7.2 convert_bitcast_fusion.2
  823.1 6.3 convert_bitcast_fusion.3
  829.4 6.3 pad_maximum_fusion.1
  835.8 7.5 convert_bitcast_fusion
  843.3 6.1 convert_bitcast_fusion.1
  849.4 6.3 pad_maximum_fusion.2
  856.8 7.7 convolution_convert_fusion.1
  864.6 6.6 fusion.22
  871.3 8.6 add_convert_fusion.1
  880.0 4.9 all-to-all-start.2
  884.9 5.8 collective-permute-start.1
  890.9 67.7 %reduce-scatter.25.cloned.1.call-done = bf16[2,512,1024]{2,1,0:T(8,128)(2,1)} async-done(((bf16[2,2048,1024]{2,1,0:T(8,128)(2,1)}), bf16[2,512,1024]{2,1,0:T(8,128)(2,1)}) %reduce-scatter.25.cloned.1.call-update) | async-done | bytes 2097168 | tf_op jit(solution)/shard_map/reduce_scatter | solution.py:269
  962.7 85.2 %reduce-scatter.27.cloned.1.call-done = bf16[2,512,1024]{2,1,0:T(8,128)(2,1)} async-done(((bf16[2,2048,1024]{2,1,0:T(8,128)(2,1)}), bf16[2,512,1024]{2,1,0:T(8,128)(2,1)}) %reduce-scatter.27.cloned.1.call-update) | async-done | bytes 2097168 | tf_op jit(solution)/shard_map/reduce_scatter | solution.py:269
  1052.0 85.6 %reduce-scatter.29.cloned.1.call-done = bf16[2,256,2048]{2,1,0:T(8,128)(2,1)} async-done(((bf16[2,1024,2048]{2,1,0:T(8,128)(2,1)}), bf16[2,256,2048]{2,1,0:T(8,128)(2,1)}) %reduce-scatter.29.cloned.1.call-update) | async-done | bytes 2097168 | tf_op jit(solution)/shard_map/reduce_scatter | solution.py:269
  1148.8 38.9 %reduce-scatter.19.cloned.1.call-done = bf16[128,2048]{1,0:T(8,128)(2,1)} async-done(((bf16[1024,2048]{1,0:T(8,128)(2,1)}), bf16[128,2048]{1,0:T(8,128)(2,1)}) %reduce-scatter.19.cloned.1.call-update) | async-done | bytes 524304 | tf_op jit(solution)/shard_map/reduce_scatter | solution.py:74
  1190.6 47.5 %reduce-scatter.15.cloned.1.call-done = bf16[128,2048]{1,0:T(8,128)(2,1)} async-done(((bf16[1024,2048]{1,0:T(8,128)(2,1)}), bf16[128,2048]{1,0:T(8,128)(2,1)}) %reduce-scatter.15.cloned.1.call-update) | async-done | bytes 524304 | tf_op jit(solution)/shard_map/reduce_scatter | solution.py:74
  1241.3 129.2 %reduce-scatter.31.cloned.1.call-done = f32[64,20]{1,0:T(8,128)} async-done(((f32[2048,20]{1,0:T(8,128)}), f32[64,20]{1,0:T(8,128)}) %reduce-scatter.31.cloned.1.call-update) | async-done | bytes 5136
  (323 shorter events, 98.6 us)
Async XLA Ops:
  7.2 86.8 %all-gather.14.cloned.1.call-start = ((), (), s32[]{:S(2)}) async-start(), calls=%async_computation.14 | async-start | bytes 3932160 | tf_op jit(solution)/shard_map/all_gather | solution.py:115
  11.1 69.6 %copy-start = (bf16[1,128,2048]{2,1,0:T(8,128)(2,1)S(1)}, bf16[1,128,2048]{2,1,0:T(8,128)(2,1)}, u32[]{:S(2)}) copy-start(bf16[1,128,2048]{2,1,0:T(8,128)(2,1)} %param.15) | copy-start | bytes 1572868
  13.4 69.2 %copy-start.74 = (bf16[64,2048]{1,0:T(8,128)(2,1)S(1)}, bf16[64,2048]{1,0:T(8,128)(2,1)}, u32[]{:S(2)}) copy-start(bf16[64,2048]{1,0:T(8,128)(2,1)} %param.21) | copy-start | bytes 786436
  39.8 99.2 %all-gather.12.cloned.1.call-start = ((), (), s32[]{:S(2)}) async-start(), calls=%async_computation.13 | async-start | bytes 4718592 | tf_op jit(solution)/shard_map/all_gather | solution.py:70
  81.5 63.7 %copy-start.51 = (f32[128]{0:T(128)}, f32[128]{0:T(128)S(1)}, u32[]{:S(2)}) copy-start(f32[128]{0:T(128)S(1)} %add_rsqrt_fusion.2) | copy-start | bytes 1540
  81.5 63.7 %copy-start.38 = (f32[2048,1]{0,1:T(1,128)}, f32[2048,1]{0,1:T(1,128)S(1)}, u32[]{:S(2)}) copy-start(f32[2048,1]{0,1:T(1,128)S(1)} %get-tuple-element.66) | copy-start | bytes 24580
  81.5 618.1 %copy-start.36 = (f32[2048,1]{0,1:T(1,128)}, f32[2048,1]{0,1:T(1,128)S(1)}, u32[]{:S(2)}) copy-start(f32[2048,1]{0,1:T(1,128)S(1)} %get-tuple-element.63) | copy-start | bytes 24580
  82.5 87.2 %all-gather.16.cloned.1.call-start = ((), (), s32[]{:S(2)}) async-start(), calls=%async_computation.15 | async-start | bytes 1310720 | tf_op jit(solution)/shard_map/all_gather | solution.py:119
  82.6 10.5 collective-permute-start
  85.6 75.3 %copy-start.45 = (f32[256,1]{0,1:T(1,128)}, f32[256,1]{0,1:T(1,128)S(1)}, u32[]{:S(2)}) copy-start(f32[256,1]{0,1:T(1,128)S(1)} %get-tuple-element.85) | copy-start | bytes 3076
  85.6 75.3 %copy-start.47 = (f32[256,1]{0,1:T(1,128)}, f32[256,1]{0,1:T(1,128)S(1)}, u32[]{:S(2)}) copy-start(f32[256,1]{0,1:T(1,128)S(1)} %get-tuple-element.86) | copy-start | bytes 3076
  85.7 77.2 %copy-start.16 = (f32[1024,128]{0,1:T(8,128)}, f32[1024,128]{0,1:T(8,128)S(1)}, u32[]{:S(2)}) copy-start(f32[1024,128]{0,1:T(8,128)S(1)} %get-tuple-element.87) | copy-start | bytes 1572868
  85.7 77.2 %copy-start.18 = (f32[1024,128]{0,1:T(8,128)}, f32[1024,128]{0,1:T(8,128)S(1)}, u32[]{:S(2)}) copy-start(f32[1024,128]{0,1:T(8,128)S(1)} %get-tuple-element.88) | copy-start | bytes 1572868
  93.9 127.7 %reduce-scatter.13.cloned.1.call-start = ((), (), s32[]{:S(2)}) async-start(), calls=%async_computation.16 | async-start | bytes 4718592 | tf_op jit(solution)/shard_map/reduce_scatter | solution.py:74
  174.4 96.5 %all-gather.28.cloned.1.call-start = ((), (), s32[]{:S(2)}) async-start(), calls=%async_computation.30 | async-start | bytes 4718592 | tf_op jit(solution)/shard_map/all_gather | solution.py:70
  175.0 183.5 %all-gather.24.cloned.1.call-start = ((), (), s32[]{:S(2)}) async-start(), calls=%async_computation.20 | async-start | bytes 10485760 | tf_op jit(solution)/shard_map/all_gather | solution.py:175
  175.6 50.5 %copy-start.56 = (s32[1,128,8]{1,2,0:T(8,128)S(1)}, s32[1,128,8]{1,2,0:T(8,128)}, u32[]{:S(2)}) copy-start(s32[1,128,8]{1,2,0:T(8,128)} %param.16) | copy-start | bytes 12292
  175.6 272.4 %all-gather.22.cloned.1.call-start = ((), (), s32[]{:S(2)}) async-start(), calls=%async_computation.19 | async-start | bytes 10485760 | tf_op jit(solution)/shard_map/all_gather | solution.py:174
  176.4 321.4 %all-gather.18.cloned.1.call-start = ((), (), s32[]{:S(2)}) async-start(), calls=%async_computation.17 | async-start | bytes 4718592 | tf_op jit(solution)/shard_map/all_gather | solution.py:70
  222.8 476.8 %copy-start.49 = (f32[128]{0:T(128)}, f32[128]{0:T(128)S(1)}, u32[]{:S(2)}) copy-start(f32[128]{0:T(128)S(1)} %add_rsqrt_fusion.1) | copy-start | bytes 1540
  224.9 360.7 %all-gather.20.cloned.1.call-start = ((), (), s32[]{:S(2)}) async-start(), calls=%async_computation.18 | async-start | bytes 10485760 | tf_op jit(solution)/shard_map/all_gather | solution.py:173
  225.6 471.7 %reduce-scatter.17.cloned.1.call-start = ((), (), s32[]{:S(2)}) async-start(), calls=%async_computation.22 | async-start | bytes 4718592 | tf_op jit(solution)/shard_map/reduce_scatter | solution.py:74
  649.2 48.1 %copy-start.8 = (bf16[128,2048]{1,0:T(8,128)(2,1)S(1)}, bf16[128,2048]{1,0:T(8,128)(2,1)}, u32[]{:S(2)}) copy-start(bf16[128,2048]{1,0:T(8,128)(2,1)} %reduce-scatter.13.cloned.1.call-done) | copy-start | bytes 1572868
  649.2 51.3 %copy-start.20 = (bf16[1,128,2048]{2,1,0:T(8,128)(2,1)S(1)}, bf16[1,128,2048]{2,1,0:T(8,128)(2,1)}, u32[]{:S(2)}) copy-start(bf16[1,128,2048]{2,1,0:T(8,128)(2,1)} %param.17) | copy-start | bytes 1572868
  649.2 100.5 %copy-start.26 = (bf16[256,2048]{1,0:T(8,128)(2,1)S(1)}, bf16[256,2048]{1,0:T(8,128)(2,1)}, u32[]{:S(2)}) copy-start(bf16[256,2048]{1,0:T(8,128)(2,1)} %all-gather.16.cloned.1.call-done) | copy-start | bytes 3145732
  649.3 100.5 %all-gather.26.cloned.1.call-start = ((), (), s32[]{:S(2)}) async-start(), calls=%async_computation.23 | async-start | bytes 4718592 | tf_op jit(solution)/shard_map/all_gather | solution.py:70
  699.6 53.8 %copy-start.57 = (f32[128]{0:T(128)}, f32[128]{0:T(128)S(1)}, u32[]{:S(2)}) copy-start(f32[128]{0:T(128)S(1)} %fusion.86) | copy-start | bytes 1540
  701.8 178.2 %reduce-scatter.21.cloned.1.call-start = ((), (), s32[]{:S(2)}) async-start(), calls=%async_computation.25 | async-start | bytes 3932160 | tf_op jit(solution)/shard_map/reduce_scatter | solution.py:248
  789.1 95.8 %reduce-scatter.23.cloned.1.call-start = ((), (), s32[]{:S(2)}) async-start(), calls=%async_computation.26 | async-start | bytes 1310720 | tf_op jit(solution)/shard_map/reduce_scatter | solution.py:256
  793.7 164.9 %reduce-scatter.25.cloned.1.call-start = ((), (), s32[]{:S(2)}) async-start(), calls=%async_computation.27 | async-start | bytes 10485760 | tf_op jit(solution)/shard_map/reduce_scatter | solution.py:269
  814.2 233.7 %reduce-scatter.27.cloned.1.call-start = ((), (), s32[]{:S(2)}) async-start(), calls=%async_computation.28 | async-start | bytes 10485760 | tf_op jit(solution)/shard_map/reduce_scatter | solution.py:269
  835.7 301.9 %reduce-scatter.29.cloned.1.call-start = ((), (), s32[]{:S(2)}) async-start(), calls=%async_computation.29 | async-start | bytes 10485760 | tf_op jit(solution)/shard_map/reduce_scatter | solution.py:269
  855.7 332.1 %reduce-scatter.19.cloned.1.call-start = ((), (), s32[]{:S(2)}) async-start(), calls=%async_computation.24 | async-start | bytes 4718592 | tf_op jit(solution)/shard_map/reduce_scatter | solution.py:74
  864.6 373.5 %reduce-scatter.15.cloned.1.call-start = ((), (), s32[]{:S(2)}) async-start(), calls=%async_computation.21 | async-start | bytes 4718592 | tf_op jit(solution)/shard_map/reduce_scatter | solution.py:74
  880.0 262.6 %all-to-all-start.2 = ((bf16[8,64,768]{2,1,0:T(8,128)(2,1)}), bf16[8,64,768]{2,1,0:T(8,128)(2,1)S(1)}, u32[]{:S(2)}, u32[]{:S(2)}) async-start(bf16[8,64,768]{2,1,0:T(8,128)(2,1)} %bitcast.285), calls=%async_computation.7 | async-start | bytes 1572864 | tf_op jit(solution)/shard_map/all_to_all | solution.py:251
  884.9 485.7 %reduce-scatter.31.cloned.1.call-start = ((), (), s32[]{:S(2)}) async-start(), calls=%async_computation.31 | async-start | bytes 1081344
  884.9 256.9 %collective-permute-start.1 = (bf16[64,2048]{1,0:T(8,128)(2,1)}, bf16[64,2048]{1,0:T(8,128)(2,1)S(1)}, u32[]{:S(2)}, u32[]{:S(2)}) collective-permute-start(bf16[64,2048]{1,0:T(8,128)(2,1)} %reduce-scatter.23.cloned.1.call-done), channel_id=1, source_target_pairs={{0,0},{8,1},{16,2},{24,3},{1,4},{9,5},{17,6},{25,7},{2,8},{10,9},{... | collective-permute-start | bytes 786440 | tf_op jit(solution)/shard_map/ppermute | solution.py:257
  1143.4 44.3 %copy-start.1 = (bf16[1,128,2048]{2,1,0:T(8,128)(2,1)S(1)}, bf16[1,128,2048]{2,1,0:T(8,128)(2,1)}, u32[]{:S(2)}) copy-start(bf16[1,128,2048]{2,1,0:T(8,128)(2,1)} %param.15) | copy-start | bytes 1572868
  1143.5 44.3 %copy-start.39 = (f32[2048,1]{0,1:T(1,128)S(1)}, f32[2048,1]{0,1:T(1,128)}, u32[]{:S(2)}) copy-start(f32[2048,1]{0,1:T(1,128)} %copy-done.38) | copy-start | bytes 24580
  1143.5 44.3 %copy-start.52 = (f32[128]{0:T(128)S(1)}, f32[128]{0:T(128)}, u32[]{:S(2)}) copy-start(f32[128]{0:T(128)} %copy-done.51) | copy-start | bytes 1540
  1145.0 44.2 %copy-start.44 = (f32[2048]{0:T(1024)S(1)}, f32[2048]{0:T(1024)}, u32[]{:S(2)}) copy-start(f32[2048]{0:T(1024)} %get-tuple-element.22) | copy-start | bytes 24580
  1145.3 45.3 %copy-start.60 = (f32[128]{0:T(128)S(1)}, f32[128]{0:T(128)}, u32[]{:S(2)}) copy-start(f32[128]{0:T(128)} %copy-done.59) | copy-start | bytes 1540
  1146.3 91.8 %copy-start.9 = (bf16[128,2048]{1,0:T(8,128)(2,1)S(1)}, bf16[128,2048]{1,0:T(8,128)(2,1)}, u32[]{:S(2)}) copy-start(bf16[128,2048]{1,0:T(8,128)(2,1)} %reduce-scatter.13.cloned.1.call-done) | copy-start | bytes 1572868
  1146.3 91.8 %copy-start.13 = (f32[128,2048]{1,0:T(8,128)S(1)}, f32[128,2048]{1,0:T(8,128)}, u32[]{:S(2)}) copy-start(f32[128,2048]{1,0:T(8,128)} %copy-done.12) | copy-start | bytes 3145732
  1146.3 91.8 %copy-start.21 = (bf16[1,128,2048]{2,1,0:T(8,128)(2,1)S(1)}, bf16[1,128,2048]{2,1,0:T(8,128)(2,1)}, u32[]{:S(2)}) copy-start(bf16[1,128,2048]{2,1,0:T(8,128)(2,1)} %param.17) | copy-start | bytes 1572868
  1146.3 91.8 %copy-start.37 = (f32[2048,1]{0,1:T(1,128)S(1)}, f32[2048,1]{0,1:T(1,128)}, u32[]{:S(2)}) copy-start(f32[2048,1]{0,1:T(1,128)} %copy-done.36) | copy-start | bytes 24580
  1146.3 91.8 %copy-start.50 = (f32[128]{0:T(128)S(1)}, f32[128]{0:T(128)}, u32[]{:S(2)}) copy-start(f32[128]{0:T(128)} %copy-done.49) | copy-start | bytes 1540
  1146.3 91.8 %copy-start.58 = (f32[128]{0:T(128)S(1)}, f32[128]{0:T(128)}, u32[]{:S(2)}) copy-start(f32[128]{0:T(128)} %copy-done.57) | copy-start | bytes 1540
  (63 other events, 475.6 us)
Sparse Core Ops, SparseCore 0:
  39.9 43.7 all-gather.13
  85.9 53.0 all-gather.11
  141.4 24.9 all-gather.15
  174.5 46.9 reduce-scatter.12
  223.0 47.8 all-gather.27
  272.6 85.9 all-gather.23
  360.4 87.5 all-gather.21
  450.2 47.5 all-gather.17
  499.6 85.8 all-gather.19
  649.4 47.9 reduce-scatter.16
  701.9 47.8 all-gather.25
  789.2 42.9 reduce-scatter.20
  835.7 27.7 reduce-scatter.22
  866.7 91.8 reduce-scatter.24
  961.5 86.3 reduce-scatter.26
  1051.2 86.4 reduce-scatter.28
  1139.7 47.9 reduce-scatter.18
  1189.9 48.1 reduce-scatter.14
  1240.3 130.1 reduce-scatter.30

commit v2 on v1

v2 whole, which is shorter than its diff:
```python
import functools
import math

import jax
import jax.numpy as jnp
from jax import lax
from jax.experimental import pallas as pl
from jax.experimental.pallas import tpu as pltpu
from jax.sharding import PartitionSpec as P

HEADS = 16
HEAD_DIM = 128

EPS = 1e-05
THETA = 10000.0
NEG = -1e30

F32 = jnp.float32
BF16 = jnp.bfloat16


def dot(left, right):
    return jnp.dot(left, right, preferred_element_type=F32)


def dot_tn(left, right):
    return lax.dot_general(left, right, (((0,), (0,)), ((), ())), preferred_element_type=F32)


def dot_nt(left, right):
    return lax.dot_general(left, right, (((1,), (1,)), ((), ())), preferred_element_type=F32)


def inv_rms(values):
    return lax.rsqrt(jnp.mean(values * values, axis=-1, keepdims=True) + EPS)


def norm_back(values, inv, gain_vec, grad):
    scaled = grad * gain_vec
    mean_dot = jnp.mean(scaled * values, axis=-1, keepdims=True)
    d_values = inv * scaled - values * (inv * inv * inv * mean_dot)
    d_gain = jnp.sum(grad * values * inv, axis=0)
    return d_values, d_gain


def rope_tables(length):
    half_dim = HEAD_DIM // 2
    inv_freq = jnp.exp(
        jnp.arange(half_dim, dtype=F32) * (-2.0 * math.log(THETA) / HEAD_DIM)
    )
    angles = jnp.arange(length, dtype=jnp.int32).astype(F32)[:, None] * inv_freq[None, :]
    cosine, sine = jnp.cos(angles), jnp.sin(angles)
    return (
        jnp.concatenate([cosine, cosine], axis=1)[:, None, :],
        jnp.concatenate([-sine, sine], axis=1)[:, None, :],
    )


def swap_halves(values):
    half_dim = HEAD_DIM // 2
    return jnp.concatenate([values[..., half_dim:], values[..., :half_dim]], axis=-1)


def rotary(values, tables):
    return values * tables[0] + swap_halves(values) * tables[1]


def rotary_back(grad, tables):
    return grad * tables[0] - swap_halves(grad) * tables[1]


MESH = pl.DeviceIdType.MESH
VMEM_LIMIT = 56 * 1024 * 1024


def cost_of(micros):
    return pl.CostEstimate(flops=0, bytes_accessed=int(micros * 3.0e6), transcendentals=0)


def flipped(dp, flip):
    return dp + flip - 2 * flip * ((dp // flip) % 2)


class Plane:
    def __init__(self, sends, later, sources, targets, send, recv):
        self.me, self.dp = lax.axis_index("expert"), lax.axis_index("dp")
        self.sends, self.later = sends, later
        self.sources, self.targets, self.send, self.recv = sources, targets, send, recv

    def busy(self):
        return len(self.sends) > 0

    def greet(self, barrier):
        if self.busy():
            for flip in (1, 2):
                pl.semaphore_signal(
                    barrier, inc=1, device_id=(flipped(self.dp, flip), self.me), device_id_type=MESH
                )

    def copy(self, i):
        first = len(self.sends)
        if i < first:
            source, start, size, flip = self.sends[i]
            ref = self.sources[source]
        else:
            source, start, size, flip = self.later[i - first]
            ref = self.targets[source]
        return pltpu.make_async_remote_copy(
            src_ref=ref.at[pl.ds(start, size)],
            dst_ref=self.targets[i],
            send_sem=self.send.at[i],
            recv_sem=self.recv.at[i],
            device_id=(flipped(self.dp, flip), self.me),
            device_id_type=MESH,
        )

    def start(self):
        for i in range(len(self.sends)):
            self.copy(i).start()

    def start_later(self):
        first = len(self.sends)
        for source in sorted({l[0] for l in self.later}):
            self.copy(source).wait_recv()
        for i in range(len(self.later)):
            self.copy(first + i).start()

    def finish(self):
        waited = {l[0] for l in self.later}
        for i in range(len(self.sends) + len(self.later)):
            self.copy(i).wait_send()
            if i not in waited:
                self.copy(i).wait_recv()


def line_greet(me, dp, chip, chips, plane):
    barrier = pltpu.get_barrier_semaphore()
    sibling = chip * 2 + 1 - me % 2
    extra = 2 if plane.busy() else 0
    pl.semaphore_signal(barrier, inc=1, device_id=(dp, sibling), device_id_type=MESH)
    plane.greet(barrier)

    @pl.when(chip > 0)
    def _():
        pl.semaphore_signal(barrier, inc=1, device_id=(dp, me - 2), device_id_type=MESH)

    @pl.when(chip < chips - 1)
    def _():
        pl.semaphore_signal(barrier, inc=1, device_id=(dp, me + 2), device_id_type=MESH)

    @pl.when((chip > 0) & (chip < chips - 1))
    def _():
        pl.semaphore_wait(barrier, 3 + extra)

    @pl.when((chip == 0) | (chip == chips - 1))
    def _():
        pl.semaphore_wait(barrier, 2 + extra)


def gather_body(groups, rows, parts, plane, x_ref, o_ref, own_sem, send, recv, pair_send, pair_recv):
    chips = groups // 2
    me, dp = lax.axis_index("expert"), lax.axis_index("dp")
    chip = me // 2
    sibling = chip * 2 + 1 - me % 2
    part = rows // parts
    line_greet(me, dp, chip, chips, plane)
    keep = pltpu.make_async_copy(x_ref, o_ref.at[pl.ds(pl.multiple_of(me * rows, rows), rows)], own_sem)

    def copy(origin, u, target, send_sem, recv_sem, first):
        place = pl.ds(pl.multiple_of(origin * rows + u * part, part), part)
        return pltpu.make_async_remote_copy(
            src_ref=x_ref.at[pl.ds(u * part, part)] if first else o_ref.at[place],
            dst_ref=o_ref.at[place],
            send_sem=send_sem,
            recv_sem=recv_sem,
            device_id=(dp, target),
            device_id_type=MESH,
        )

    def right(k, u):
        return copy(me - 2 * k, u, me + 2, send.at[0, k, u], recv.at[0, k, u], k == 0)

    def left(k, u):
        return copy(me + 2 * k, u, me - 2, send.at[1, k, u], recv.at[1, k, u], k == 0)

    def pair(side, k, u):
        origin = me - 2 * k if side == 0 else me + 2 * k
        return copy(origin, u, sibling, pair_send.at[side, k, u], pair_recv.at[side, k, u], k == 0)

    sides = lambda k: (
        (0, chip - k >= 0, chip < chips - 1),
        (1, chip + k <= chips - 1, chip > 0),
    )
    for k in range(chips):
        if k == chips - 1:
            plane.start_later()
        for u in range(parts):
            for side, has, send_on in sides(k):
                step = right if side == 0 else left

                @pl.when(has)
                def _(k=k, u=u, side=side, send_on=send_on, step=step):
                    if k > 0:
                        step(k - 1, u).wait_recv()
                    if k < chips - 1:

                        @pl.when(send_on)
                        def _():
                            step(k, u).start()

                    if k > 0:
                        pair(side, k, u).start()

            if k == 0:
                pair(0, 0, u).start()
        if k == 0:
            plane.start()
            keep.start()

    keep.wait()
    for k in range(chips):
        for u in range(parts):
            if k == 0:
                pair(0, 0, u).wait()
            for side, has, send_on in sides(k):
                step = right if side == 0 else left

                @pl.when(has)
                def _(k=k, u=u, side=side, send_on=send_on, step=step):
                    if k < chips - 1:

                        @pl.when(send_on)
                        def _():
                            step(k, u).wait_send()

                    if k > 0:
                        pair(side, k, u).wait()

    plane.finish()


def reduce_body(
    groups, rows, parts, plane, p_ref, o_ref, own, pair, inbox, load_sem, pair_send, pair_recv, send, recv
):
    chips = groups // 2
    me, dp = lax.axis_index("expert"), lax.axis_index("dp")
    chip, core = me // 2, me % 2
    sibling = chip * 2 + 1 - core
    part = rows // parts
    step_rows = 16
    line_greet(me, dp, chip, chips, plane)

    def pair_copy(d):
        place = pl.ds(pl.multiple_of((2 * d + 1 - core) * rows, rows), rows)
        return pltpu.make_async_remote_copy(
            src_ref=p_ref.at[place],
            dst_ref=pair.at[d],
            send_sem=pair_send.at[d],
            recv_sem=pair_recv.at[d],
            device_id=(dp, sibling),
            device_id_type=MESH,
        )

    def own_copy(d):
        place = pl.ds(pl.multiple_of((2 * d + core) * rows, rows), rows)
        return pltpu.make_async_copy(p_ref.at[place], own.at[d], load_sem.at[d])

    order = []
    for j in range((chips + 1) // 2):
        order += [chips - 1 - j] + ([j] if j != chips - 1 - j else [])
    for d in order:
        pair_copy(d).start()
        own_copy(d).start()
    plane.start()

    def hop(d, u, side):
        place = pl.ds(u * part, part)
        target = me + 2 if side == 0 else me - 2
        slot = d if side == 0 else chips + d
        return pltpu.make_async_remote_copy(
            src_ref=own.at[d, place],
            dst_ref=inbox.at[slot, place],
            send_sem=send.at[d, u],
            recv_sem=recv.at[slot, u],
            device_id=(dp, target),
            device_id_type=MESH,
        )

    def add(d, u, slots, store):
        def body(i, carry):
            at = pl.ds(pl.multiple_of(u * part + i * step_rows, step_rows), step_rows)
            value = own[d, at].astype(F32) + pair[d, at].astype(F32)
            for slot in slots:
                value = value + inbox[slot, at].astype(F32)
            store(at, value)
            return carry

        lax.fori_loop(0, part // step_rows, body, 0)

    def forward(d, side):
        pair_copy(d).wait_recv()
        own_copy(d).wait()

        def store(at, value):
            own[d, at] = value.astype(BF16)

        end = chip == (0 if side == 0 else chips - 1)
        for u in range(parts):

            @pl.when(end)
            def _(u=u):
                add(d, u, (), store)

            @pl.when(jnp.logical_not(end))
            def _(u=u):
                hop(d, u, side).wait_recv()
                add(d, u, (d if side == 0 else chips + d,), store)

            hop(d, u, side).start()

    for j in range(chips - 1):
        far, near = chips - 1 - j, j

        @pl.when(far > chip)
        def _(far=far):
            forward(far, 0)

        @pl.when(near < chip)
        def _(near=near):
            forward(near, 1)

        if j == chips - 2:
            plane.start_later()

    pair_copy(chip).wait_recv()
    own_copy(chip).wait()

    def finish(at, value):
        o_ref[at] = value

    for u in range(parts):

        @pl.when(chip == 0)
        def _(u=u):
            hop(chip, u, 1).wait_recv()
            add(chip, u, (chips + chip,), finish)

        @pl.when(chip == chips - 1)
        def _(u=u):
            hop(chip, u, 0).wait_recv()
            add(chip, u, (chip,), finish)

        @pl.when((chip > 0) & (chip < chips - 1))
        def _(u=u):
            hop(chip, u, 0).wait_recv()
            hop(chip, u, 1).wait_recv()
            add(chip, u, (chip, chips + chip), finish)

    for d in range(chips):
        pair_copy(d).wait_send()
        for u in range(parts):

            @pl.when(d > chip)
            def _(d=d, u=u):
                hop(d, u, 0).wait_send()

            @pl.when(d < chip)
            def _(d=d, u=u):
                hop(d, u, 1).wait_send()

    plane.finish()


def exchange_body(count, spread, same, reduce, plane, x_ref, o_ref, box, send, recv):
    me, dp = lax.axis_index("expert"), lax.axis_index("dp")
    groups = lax.axis_size("expert")
    mine = dp * groups + me if spread else me

    def device(index):
        return (index // groups, index % groups) if spread else (dp, index)

    barrier = pltpu.get_barrier_semaphore()

    def hello(s, carry):
        pl.semaphore_signal(
            barrier, inc=1, device_id=device((mine + s) % count), device_id_type=MESH
        )
        return carry

    lax.fori_loop(1, count, hello, 0)
    plane.greet(barrier)
    pl.semaphore_wait(barrier, count - 1 + (2 if plane.busy() else 0))

    def copy(s):
        target = (mine + s) % count
        return pltpu.make_async_remote_copy(
            src_ref=x_ref.at[0] if same else x_ref.at[target],
            dst_ref=box.at[mine],
            send_sem=send.at[s],
            recv_sem=recv.at[s],
            device_id=device(target),
            device_id_type=MESH,
        )

    def start(s, carry):
        copy(s).start()
        return carry

    def wait(s, carry):
        copy(s).wait()
        return carry

    lax.fori_loop(1, count, start, 0)
    plane.start()
    box[mine] = x_ref[0] if same else x_ref[mine]
    lax.fori_loop(1, count, wait, 0)
    if reduce:

        def add(s, total):
            return total + box[s]

        o_ref[...] = lax.fori_loop(1, count, add, box[0])
    else:
        o_ref[...] = box[...]
    plane.start_later()
    plane.finish()


def run(body, name, micros, collective_id, x, x_space, out, out_space, scratch, sends, later):
    arrays, specs = [], []
    for array, start, size, flip in sends:
        found = [i for i, a in enumerate(arrays) if a is array]
        if not found:
            arrays.append(array)
            found = [len(arrays) - 1]
        specs.append((found[0], start, size, flip))
    targets = [jax.ShapeDtypeStruct((s[2],) + s[0].shape[1:], s[0].dtype) for s in sends]
    for source, start, size, flip in later:
        targets.append(jax.ShapeDtypeStruct((size,) + targets[source].shape[1:], targets[source].dtype))
    n_in, n_out = len(arrays), len(targets)

    def kernel(*refs):
        x_ref, sources = refs[0], refs[1 : 1 + n_in]
        o_ref, dests = refs[1 + n_in], refs[2 + n_in : 2 + n_in + n_out]
        rest = refs[2 + n_in + n_out :]
        plane = Plane(specs, later, sources, dests, *rest[:2])
        body(plane, x_ref, o_ref, *rest[2:])

    anywhere = pl.BlockSpec(memory_space=pl.ANY)
    got = pl.pallas_call(
        kernel,
        out_shape=[out] + targets,
        in_specs=[pl.BlockSpec(memory_space=x_space)] + [anywhere] * n_in,
        out_specs=[pl.BlockSpec(memory_space=out_space)] + [anywhere] * n_out,
        scratch_shapes=[pltpu.SemaphoreType.DMA((max(n_out, 1),))] * 2 + scratch,
        compiler_params=pltpu.CompilerParams(
            collective_id=collective_id, has_side_effects=True, vmem_limit_bytes=VMEM_LIMIT
        ),
        cost_estimate=cost_of(micros),
        name=name,
    )(x, *arrays)
    return got if n_out else got[0]


def line_gather(x, collective_id, sends=(), later=(), parts=2):
    rows, width = x.shape
    groups = lax.axis_size("expert")
    shape = (2, groups // 2, parts)
    return run(
        functools.partial(gather_body, groups, rows, parts), "line_gather", 40, collective_id,
        x, pl.ANY, jax.ShapeDtypeStruct((groups * rows, width), x.dtype), pl.ANY,
        [pltpu.SemaphoreType.DMA] + [pltpu.SemaphoreType.DMA(shape)] * 4, sends, later,
    )


def line_reduce(partial, collective_id, sends=(), later=(), parts=2):
    groups = lax.axis_size("expert")
    chips = groups // 2
    rows, width = partial.shape[0] // groups, partial.shape[1]
    return run(
        functools.partial(reduce_body, groups, rows, parts), "line_reduce", 40, collective_id,
        partial.astype(BF16), pl.ANY, jax.ShapeDtypeStruct((rows, width), F32), pltpu.VMEM,
        [
            pltpu.VMEM((chips, rows, width), BF16),
            pltpu.VMEM((chips, rows, width), BF16),
            pltpu.VMEM((2 * chips, rows, width), BF16),
            pltpu.SemaphoreType.DMA((chips,)),
            pltpu.SemaphoreType.DMA((chips,)),
            pltpu.SemaphoreType.DMA((chips,)),
            pltpu.SemaphoreType.DMA((chips, parts)),
            pltpu.SemaphoreType.DMA((2 * chips, parts)),
        ],
        sends, later,
    )


def exchange(x, collective_id, spread=False, same=False, reduce=False, sends=(), later=()):
    count = lax.axis_size("expert") * (lax.axis_size("dp") if spread else 1)
    block = x.shape[1:]
    return run(
        functools.partial(exchange_body, count, spread, same, reduce), "exchange", 8, collective_id,
        x, pltpu.VMEM, jax.ShapeDtypeStruct(block if reduce else (count,) + block, x.dtype), pltpu.VMEM,
        [
            pltpu.VMEM((count,) + block, x.dtype),
            pltpu.SemaphoreType.DMA((count,)),
            pltpu.SemaphoreType.DMA((count,)),
        ],
        sends, later,
    )


def both(array, start=0, size=None):
    size = array.shape[0] if size is None else size
    return [(array, start, size, 1), (array, start, size, 2)]


def swap_dp(block, flip):
    seqs = lax.axis_size("dp")
    return lax.ppermute(block, "dp", [(i, i ^ flip) for i in range(seqs)])


def tie(value, *deps):
    return lax.optimization_barrier((value,) + deps)[0]


def near_dp(block):
    return block, swap_dp(block, 1), swap_dp(block, 2)


def far_dp(near, *deps):
    block, near_x, near_y = near
    half = block.shape[0] // 2
    via_x, via_y = lax.optimization_barrier((near_y[:half], near_x[half:]) + deps)[:2]
    far = jnp.concatenate([swap_dp(via_x, 1), swap_dp(via_y, 2)], axis=0)
    return [block, near_x, near_y, far]


def halves(block):
    half = block.shape[0] // 2
    return [(block, 0, half, 1), (block, half, half, 2)]


def relay(blocks, from_x, from_y):
    _, to_x, to_y, _ = blocks
    half = to_x.shape[0] // 2
    to_x = jnp.concatenate(
        [to_x[:half], (to_x[half:].astype(F32) + from_y.astype(F32)).astype(BF16)], axis=0
    )
    to_y = jnp.concatenate(
        [(to_y[:half].astype(F32) + from_x.astype(F32)).astype(BF16), to_y[half:]], axis=0
    )
    return to_x, to_y


def settle(blocks, from_x, from_y):
    return blocks[0].astype(F32) + from_x.astype(F32) + from_y.astype(F32)


def send_halves(blocks):
    half = blocks[3].shape[0] // 2
    return swap_dp(blocks[3][:half], 1), swap_dp(blocks[3][half:], 2)


def in_order(pieces, index, axis):
    low = (index % 2) == 1
    high = (index // 2) == 1
    a, b, c, d = pieces
    a, b, c, d = (
        jnp.where(low, b, a), jnp.where(low, a, b), jnp.where(low, d, c), jnp.where(low, c, d)
    )
    return jnp.concatenate(
        [jnp.where(high, c, a), jnp.where(high, d, b), jnp.where(high, a, c), jnp.where(high, b, d)],
        axis=axis,
    )


def own_order(array, index, axis):
    return in_order(jnp.split(array, 4, axis=axis), index, axis)


def shards(
    tokens, routes, grad_output, w_query, w_key, w_value, w_out, w_router,
    gain_attn, gain_query, gain_key, gain_ffn, w_gate, w_up, w_down,
):
    rows = tokens.shape[1]
    width = tokens.shape[2]
    groups = lax.axis_size("expert")
    seqs = lax.axis_size("dp")
    me = lax.axis_index("expert")
    length = rows * groups
    local_experts = w_gate.shape[0]
    all_experts = local_experts * groups
    block = w_query.shape[0]
    own = width // groups
    slab = max(own, HEAD_DIM)
    copies = slab // own
    heads = slab // HEAD_DIM
    share = 1.0 / copies
    offset = (me % copies) * own

    x_low = tokens.reshape(rows, width)
    g_low = grad_output.reshape(rows, width)

    my_dp = lax.axis_index("dp")
    small_size = block * (all_experts + 4)
    small_rows = -(-small_size // (16 * 128)) * 16
    small = jnp.concatenate(
        [w_router.reshape(-1), gain_attn, gain_query, gain_key, gain_ffn,
         jnp.zeros((small_rows * 128 - small_size,), BF16)]
    )
    small_all = exchange(small.reshape(1, small_rows, 128), 1, spread=True, same=True)
    small_all = small_all.reshape(seqs * groups, small_rows * 128)
    split = block * all_experts
    w_r = small_all[:, :split].reshape(width, all_experts)
    gains = [
        small_all[:, split + i * block : split + (i + 1) * block].reshape(width).astype(F32)
        for i in range(4)
    ]
    g_attn, g_ffn = gains[0], gains[3]
    slab_start = (me // copies) * slab
    g_query = lax.dynamic_slice(gains[1], (slab_start,), (slab,))
    g_key = lax.dynamic_slice(gains[2], (slab_start,), (slab,))

    qkv_send = jnp.stack([w_query, w_key, w_value], axis=1).reshape(block, 3, width // slab, slab)
    qkv_send = qkv_send.transpose(2, 0, 1, 3).reshape(width // slab, block, 3 * slab)
    qkv_send = jnp.repeat(qkv_send, copies, axis=0)
    qkv_got, gate0_x, gate0_y = exchange(
        tie(qkv_send, small_all), 2, sends=both(w_gate, 0, 1)
    )
    qkv_got = qkv_got.reshape(groups * block, 3 * slab)
    total = seqs * groups
    moves = [(b, (b % seqs) * groups + b // seqs) for b in range(total)]
    o_own = lax.ppermute(tie(w_out, small_all), ("dp", "expert"), moves)

    x_in = x_low.astype(F32)
    inv_attn = inv_rms(x_in)
    normed_low = (x_in * inv_attn * g_attn).astype(BF16)
    half_q, half_o = qkv_got.shape[0] // 2, block // 2
    normed_all, q_x, q_y, o_x, o_y, q_f0, q_f1, o_f0, o_f1 = line_gather(
        tie(normed_low, qkv_got), 3,
        sends=both(qkv_got) + both(o_own),
        later=[(1, 0, half_q, 1), (0, half_q, half_q, 2), (3, 0, half_o, 1), (2, half_o, half_o, 2)],
    )
    w_qkv = in_order([qkv_got, q_x, q_y, jnp.concatenate([q_f0, q_f1], axis=0)], my_dp, 0)
    w_o = in_order([o_own, o_x, o_y, jnp.concatenate([o_f0, o_f1], axis=0)], my_dp, 0)
    if copies > 1:
        sets = [[c * copies + i for i in range(copies)] for c in range(groups // copies)]
        w_o = lax.all_gather(w_o, "expert", axis_index_groups=sets, axis=0, tiled=True)

    gate1 = tie(w_gate[1:2], normed_all)
    gate1_x, gate1_y = swap_dp(gate1, 1), swap_dp(gate1, 2)
    g_all = lax.all_gather(tie(g_low, normed_all), "expert", axis=0, tiled=True)

    raw = dot(normed_all, w_qkv)
    q_raw, k_raw, v_raw = raw[:, :slab], raw[:, slab : 2 * slab], raw[:, 2 * slab :]
    squares = jnp.stack([jnp.sum(q_raw * q_raw, axis=1), jnp.sum(k_raw * k_raw, axis=1)], axis=0)
    squares = exchange(
        (squares * share).reshape(1, 2 * length // 128, 128), 4, same=True, reduce=True
    ).reshape(2, length)
    inv_qk = lax.rsqrt(squares / width + EPS)
    inv_q, inv_k = inv_qk[0][:, None], inv_qk[1][:, None]
    tables = rope_tables(length)

    def to_heads(values):
        return values.reshape(length, heads, HEAD_DIM)

    queries = rotary(to_heads(q_raw * inv_q * g_query), tables).astype(BF16).transpose(1, 0, 2)
    keys = rotary(to_heads(k_raw * inv_k * g_key), tables).astype(BF16).transpose(1, 0, 2)
    values = to_heads(v_raw).astype(BF16).transpose(1, 0, 2)
    positions = jnp.arange(length, dtype=jnp.int32)
    scale = HEAD_DIM ** (-0.5)

    def head_probs(q, k):
        scores = dot_nt(q, k) * scale
        scores = jnp.where(positions[None, :] <= positions[:, None], scores, NEG)
        exp_terms = jnp.exp(scores - jnp.max(scores, axis=-1, keepdims=True))
        return exp_terms / jnp.sum(exp_terms, axis=-1, keepdims=True)

    mixes = []
    for h in range(heads):
        mixes.append(dot(head_probs(queries[h], keys[h]).astype(BF16), values[h]).astype(BF16))
    mix = jnp.concatenate(mixes, axis=1)
    o_sum, gate0_f, gate1_f, up0_x, up0_y = line_reduce(
        dot(mix, w_o) * share, 5,
        sends=[(gate0_y, 0, 1, 1), (gate1_x, 0, 1, 2)] + both(w_up, 0, 1),
    )
    after_attn = x_in + o_sum

    inv_ffn = inv_rms(after_attn)
    ffn_low = (after_attn * inv_ffn * g_ffn).astype(BF16)
    ffn_all, up1_x, up1_y, up0_f, up1_f = line_gather(
        own_order(ffn_low, my_dp, 1), 9,
        sends=both(w_up, 1, 1) + [(up0_y, 0, 1, 1)], later=[(0, 0, 1, 2)],
    )
    router_prob = jax.nn.softmax(dot(ffn_low, w_r), axis=-1)
    chosen = routes.reshape(rows, routes.shape[2])
    chosen_mask = jnp.sum(
        (chosen[:, :, None] == jnp.arange(all_experts, dtype=jnp.int32)[None, None, :]).astype(F32),
        axis=1,
    )
    route_dense = router_prob * chosen_mask
    pad = -local_experts % 8
    route_send = route_dense.T.reshape(groups, local_experts, rows)
    route_send = jnp.pad(route_send, ((0, 0), (0, pad), (0, 0)))
    route_mine = exchange(route_send, 6)[:, :local_experts].transpose(0, 2, 1)
    route_mine = route_mine.reshape(length, local_experts)

    near_down = near_dp(tie(w_down, ffn_all))
    wd = in_order(far_dp(near_down), my_dp, 1)
    wg = [
        jnp.concatenate([own[0], x[0], y[0], f[0]], axis=0)
        for own, x, y, f in (
            (w_gate[0:1], gate0_x, gate0_y, gate0_f), (w_gate[1:2], gate1_x, gate1_y, gate1_f)
        )
    ]
    wu = [
        jnp.concatenate([own[0], x[0], y[0], f[0]], axis=0)
        for own, x, y, f in ((w_up[0:1], up0_x, up0_y, up0_f), (w_up[1:2], up1_x, up1_y, up1_f))
    ]
    cols = jnp.split(ffn_all, 4, axis=1)
    gates, ups, hidden_ws, d_weights, d_gates, d_ups = [], [], [], [], [], []
    d_down, d_gate_w, d_up_w = [], [], []
    for i in range(local_experts):
        gate, up = dot(ffn_all, wg[i]), dot(ffn_all, wu[i])
        gates.append(gate)
        ups.append(up)
        hidden = gate * jax.nn.sigmoid(gate) * up
        hidden_ws.append((hidden * route_mine[:, i : i + 1]).astype(BF16))
        mine = own_order(hidden_ws[i], my_dp, 1)
        d_down.append([dot_tn(h, g_all).astype(BF16) for h in jnp.split(mine, 4, axis=1)])
    d_down = [jnp.stack(b) for b in zip(*d_down)]
    down_x, down_y = send_halves(d_down)
    for i in range(local_experts):
        gate, up = gates[i], ups[i]
        d_hid = dot_nt(g_all, tie(wd, *d_down)[i])
        sig = jax.nn.sigmoid(gate)
        silu = gate * sig
        d_weights.append(jnp.sum(silu * up * d_hid, axis=1))
        d_hid = d_hid * route_mine[:, i : i + 1]
        d_gates.append((d_hid * up * sig * (1.0 + gate * (1.0 - sig))).astype(BF16))
        d_ups.append((d_hid * silu).astype(BF16))
        d_gate_w.append([dot_tn(f, d_gates[i]).astype(BF16) for f in cols])
    d_gate_w = [jnp.stack(b) for b in zip(*d_gate_w)]
    gate_x, gate_y = send_halves(d_gate_w)
    d_gates = [tie(d, *d_gate_w) for d in d_gates]
    dx_part = 0.0
    for i in range(local_experts):
        dx_part = dx_part + dot_nt(d_gates[i], wg[i]) + dot_nt(d_ups[i], wu[i])
    dx_part = dx_part.astype(BF16)
    down_to_x, down_to_y = relay(d_down, down_x, down_y)
    down_fx, down_fy = swap_dp(down_to_x, 1), swap_dp(down_to_y, 2)
    gate_to_x, gate_to_y = relay(d_gate_w, gate_x, gate_y)
    d_rows, gate_fx, gate_fy = line_reduce(
        tie(dx_part, down_to_x, down_to_y), 10,
        sends=[(gate_to_x, 0, 2, 1), (gate_to_y, 0, 2, 2)],
    )
    d_rows = own_order(d_rows, my_dp, 1)
    d_ups = [tie(d, d_rows) for d in d_ups]
    for i in range(local_experts):
        d_up_w.append([dot_tn(f, d_ups[i]).astype(BF16) for f in cols])
    d_up_w = [jnp.stack(b) for b in zip(*d_up_w)]
    y_part = 0.0
    for i in range(local_experts):
        y_part = y_part + dot(tie(hidden_ws[i], d_rows), wd[i])
    y_sum = lax.psum_scatter(y_part.astype(BF16), "expert", scatter_dimension=0, tiled=True)
    output = after_attn + y_sum.astype(F32)
    d_weight = jnp.stack(d_weights, axis=0).reshape(local_experts, groups, rows).transpose(1, 0, 2)
    d_weight = exchange(jnp.pad(d_weight, ((0, 0), (0, pad), (0, 0))), 6)[:, :local_experts]
    d_router_prob = d_weight.reshape(all_experts, rows).T * chosen_mask

    d_logits = (
        router_prob * (d_router_prob - jnp.sum(d_router_prob * router_prob, axis=-1, keepdims=True))
    ).astype(BF16)
    d_router_w = dot_tn(ffn_low, d_logits)
    d_normed_ffn = d_rows + dot_nt(d_logits, w_r)
    d_after_norm, d_gain_ffn = norm_back(after_attn, inv_ffn, g_ffn, d_normed_ffn)
    d_after = g_low.astype(F32) + d_after_norm
    d_after_all, up_x, up_y = line_gather(
        d_after.astype(BF16), 11, sends=halves(d_up_w[3])
    )
    up_to_x, up_to_y = relay(d_up_w, up_x, up_y)
    up_fx, up_fy = swap_dp(up_to_x, 1), swap_dp(up_to_y, 2)

    d_out_w = dot_tn(mix, d_after_all)
    d_mix = dot_nt(d_after_all, w_o).astype(BF16)
    dqs, dks, dvs = [], [], []
    for h in range(heads):
        prob = head_probs(queries[h], keys[h])
        d_m = d_mix[:, h * HEAD_DIM : (h + 1) * HEAD_DIM]
        d_prob = dot_nt(d_m, values[h])
        row_delta = jnp.sum(d_prob * prob, axis=-1, keepdims=True)
        d_score = (prob * (d_prob - row_delta) * scale).astype(BF16)
        dqs.append(dot(d_score, keys[h]))
        dks.append(dot_tn(d_score, queries[h]))
        dvs.append(dot_tn(prob.astype(BF16), d_m))
    dq_n = rotary_back(jnp.stack(dqs, axis=1), tables).reshape(length, slab)
    dk_n = rotary_back(jnp.stack(dks, axis=1), tables).reshape(length, slab)
    dv_low = jnp.concatenate(dvs, axis=1).astype(BF16)
    dots = jnp.stack(
        [jnp.sum(dq_n * g_query * q_raw, axis=1), jnp.sum(dk_n * g_key * k_raw, axis=1)], axis=0
    )
    dots = exchange(
        (dots * share).reshape(1, 2 * length // 128, 128), 4, same=True, reduce=True
    ).reshape(2, length) / width
    d_gain_query = jnp.sum(dq_n * q_raw * inv_q, axis=0)
    d_gain_key = jnp.sum(dk_n * k_raw * inv_k, axis=0)
    dq_low = (inv_q * dq_n * g_query - q_raw * (inv_q**3 * dots[0][:, None])).astype(BF16)
    dk_low = (inv_k * dk_n * g_key - k_raw * (inv_k**3 * dots[1][:, None])).astype(BF16)
    d_raw = jnp.concatenate([dq_low, dk_low, dv_low], axis=1)
    d_qkv_w = dot_tn(normed_all, d_raw).astype(BF16)
    d_qkv_w = d_qkv_w.reshape(width, 3, slab)
    d_qkv_w = lax.dynamic_slice(d_qkv_w, (0, 0, offset), (width, 3, own))
    d_qkv_w = jnp.split(own_order(d_qkv_w.reshape(width, 3 * own), my_dp, 0), 4, axis=0)
    d_out_w = lax.dynamic_slice(d_out_w.astype(BF16), (offset, 0), (own, width))
    d_out_w = jnp.split(own_order(d_out_w, my_dp, 0), 4, axis=0)
    d_normed_in, qkv_x, qkv_y, out_x, out_y = line_reduce(
        dot_nt(d_raw, w_qkv) * share, 12, sends=halves(d_qkv_w[3]) + halves(d_out_w[3])
    )
    d_in_norm, d_gain_attn = norm_back(x_in, inv_attn, g_attn, d_normed_in)
    input_grad = d_after + d_in_norm

    spread = jnp.zeros((2, width), F32)
    spread = lax.dynamic_update_slice(
        spread, jnp.stack([d_gain_query, d_gain_key]) * share, (0, slab_start)
    )
    total = seqs * groups
    small_grad = jnp.concatenate(
        [d_router_w.reshape(total, split)]
        + [v.reshape(total, block) for v in (d_gain_attn, spread[0], spread[1], d_gain_ffn)]
        + [jnp.zeros((total, small_rows * 128 - small_size), F32)],
        axis=1,
    )
    qkv_to_x, qkv_to_y = relay(d_qkv_w, qkv_x, qkv_y)
    out_to_x, out_to_y = relay(d_out_w, out_x, out_y)
    small_grad, qkv_x, qkv_y, out_x, out_y = exchange(
        small_grad.reshape(total, small_rows, 128), 8, spread=True, reduce=True,
        sends=[
            (qkv_to_x, 0, qkv_to_x.shape[0], 1), (qkv_to_y, 0, qkv_to_y.shape[0], 2),
            (out_to_x, 0, out_to_x.shape[0], 1), (out_to_y, 0, out_to_y.shape[0], 2),
        ],
    )
    small_grad = small_grad.reshape(-1)
    d_qkv_w = settle(d_qkv_w, qkv_x, qkv_y).astype(BF16)
    d_qkv_w = exchange(d_qkv_w.reshape(groups, block, 3 * own), 7).reshape(groups, block, 3, own)
    d_qkv_w = d_qkv_w.transpose(2, 1, 0, 3).reshape(3, block, width).astype(F32)
    d_out_w = settle(d_out_w, out_x, out_y).astype(BF16)
    d_out_w = lax.ppermute(d_out_w, ("dp", "expert"), [(b, a) for a, b in moves]).astype(F32)
    expert_owned = [
        settle(d_gate_w, gate_fx, gate_fy),
        settle(d_up_w, up_fx, up_fy),
        settle(d_down, down_fx, down_fy),
    ]

    return (
        output.reshape(1, rows, width),
        input_grad.reshape(1, rows, width),
        d_qkv_w[0],
        d_qkv_w[1],
        d_qkv_w[2],
        d_out_w,
        small_grad[:split].reshape(block, all_experts),
        small_grad[split : split + block],
        small_grad[split + block : split + 2 * block],
        small_grad[split + 2 * block : split + 3 * block],
        small_grad[split + 3 * block : split + 4 * block],
        *expert_owned,
    )


def solution(mesh):
    tok = P("dp", "expert", None)
    mat = P(("dp", "expert"), None)
    vec = P(("dp", "expert"))
    exp = P("expert", "dp", None)
    return jax.shard_map(
        shards,
        mesh=mesh,
        in_specs=(tok, tok, tok, mat, mat, mat, mat, mat, vec, vec, vec, vec, exp, exp, exp),
        out_specs=(tok, tok, mat, mat, mat, mat, mat, vec, vec, vec, vec, exp, exp, exp),
        check_vma=False,
    )
```

time: 1400 us -> 924 us (0.66)
  waiting for transfers between devices: 951 us -> 38.7 us
  Pallas kernels: 0 us -> 479 us
  blocking collectives: 118 us -> 0 us
  local copies, waits for them, and re-layouts: 29.5 us -> 63.6 us
  other arithmetic: 55.3 us -> 79.9 us
  matrix products: 198 us -> 218 us
    pallas_call x0 -> x14, Pallas kernels: none -> 479 us  [run(): pl.pallas_call(kernel, out_shape=[out] + targets, in_specs=[pl.BlockSpec(...]
    reduce_scatter x9 -> x1, waiting for transfers between devices: 408 us -> 0.01 us  [shards(): lax.psum_scatter(y_part.astype(BF16), 'expert', scatter_dimension=0, tile...]
    all_gather x9 -> x1, waiting for transfers between devices: 404 us -> 0.01 us  [shards(): g_all = lax.all_gather(tie(g_low, normed_all), 'expert', axis=0, tiled=True)]
    unnamed x20 -> x2, waiting for transfers between devices: 132 us -> 0.03 us
    all_gather x2 -> x0, blocking collectives: 55.1 us -> none  [the longest x1 40.6 us: shards(): small_all = lax.all_gather(small, ('dp', 'expert'), axis=0, tiled=True)]
    all_to_all x2 -> x0, blocking collectives: 35.9 us -> none  [the longest x1 25.4 us: shards(): lax.all_to_all(qkv_send, 'expert', split_axis=0, concat_axis=0, tiled=True)]
    ppermute x1 -> x15, waiting for transfers between devices: 7.41 us -> 38.7 us  [the longest x14 38.7 us: swap_dp(): return lax.ppermute(block, 'dp', [(i, i ^ flip) for i in range(seqs)])]
    psum x2 -> x0, blocking collectives: 27.3 us -> none  [the longest x1 13.6 us: shards(): squares = lax.psum(squares * share, 'expert')]
  transfers between devices with their start and end apart: 22 -> 18, of which waited for: 16 -> 2; matrix products, arithmetic and copies ran while one was open for 12% -> 31% of each run, Pallas kernels for 0% -> 47%
where the time goes in v2:
time: 924 us; the launch traced here: 916 us
  Pallas kernels  479 us (52%)
  matrix products  218 us (24%)
  other arithmetic  79.9 us (9%)
  local copies, waits for them, and re-layouts  63.6 us (7%)
  waiting for transfers between devices  38.7 us (4%)
  starting transfers between devices  20.6 us (2%)
  between operations  16.5 us (2%)
    pallas_call x14, Pallas kernels, run(): pl.pallas_call(kernel, out_shape=[out] + targets, in_specs=[pl.BlockSpec(...  479 us
    dot_general x13, matrix products, dot_nt(): lax.dot_general(left, right, (((1,), (1,)), ((), ())), preferred_element_...  80 us
    dot_general x31, matrix products, dot_tn(): lax.dot_general(left, right, (((0,), (0,)), ((), ())), preferred_element_...  75.9 us
    dot_general x13, matrix products, dot(): return jnp.dot(left, right, preferred_element_type=F32)  62.2 us
    ppermute x14, waiting for transfers between devices, swap_dp(): return lax.ppermute(block, 'dp', [(i, i ^ flip) for i in range(seqs)])  38.7 us
    unnamed x373, local copies, waits for them, and re-layouts  27 us
  transfers between devices with their start and end apart: 18, of which 2 were waited for; matrix products, arithmetic and copies ran while one was open for 31% of the time, Pallas kernels for 47%

profile of v2, /device:TPU:5, one launch (start us, length us, event | category | flops | bytes accessed | tf_op | source)
XLA Modules:
  0.0 916.0 jit_solution(13703469590204076402)
XLA Ops:
  11.4 11.2 %exchange.8 = bf16[32,16,128]{2,1,0:T(8,128)(2,1)} custom-call(bf16[1,16,128]{2,1,0:T(8,128)(2,1)} %bitcast.374), custom_call_target="tpu_custom_call" | custom-call | bytes 24000000 | tf_op jit(solution)/shard_map/exchange/pallas_call | solution.py:450
  23.6 5.2 collective-permute-start
  37.7 3.5 reshape_broadcast_in_dim_reshape.3.refs_0_
  42.2 28.4 %exchange.9 = (bf16[8,64,768]{2,1,0:T(8,128)(2,1)}, bf16[1,512,1024]{2,1,0:T(8,128)(2,1)}, bf16[1,512,1024]{2,1,0:T(8,128)(2,1)}) custom-call(bf16[8,64,768]{2,1,0:T(8,128)(2,1)} %reshape_broadcast_in_dim_reshape.3.refs_0_, bf16[2,512,1024]{2,1,0:T(8,128)(2,1)} %refs_1_.2), custom_call_target="tpu_custom_call" | custom-call | bytes 24000000 | tf_op jit(solution)/shard_map/exchange/pallas_call | solution.py:450
  75.3 39.9 %line_gather.3 = (bf16[1024,2048]{1,0:T(8,128)(2,1)}, bf16[512,768]{1,0:T(8,128)(2,1)}, bf16[512,768]{1,0:T(8,128)(2,1)}, bf16[64,2048]{1,0:T(8,128)(2,1)}, bf16...) custom-call(bf16[128,2048]{1,0:T(8,128)(2,1)} %fusion.50.refs_0_, ...), custom_call_target="tpu_custom_call" | custom-call | bytes 120000000 | tf_op jit(solution)/shard_map/line_gather/pallas_call | solution.py:450
  120.5 3.5 fusion.104
  126.0 7.3 exchange.10
  152.6 66.2 %line_reduce.3 = (f32[128,2048]{1,0:T(8,128)}, bf16[1,512,1024]{2,1,0:T(8,128)(2,1)}, bf16[1,512,1024]{2,1,0:T(8,128)(2,1)}, bf16[1,512,1024]{2,1,0:T(8,128)(2,1)}, bf16[1,512,1024]{2,1,0:T(8,128)(2,1)}) custom-call(bf16[1024,2048]{1,0:T(8,128)(2,1)} %convolution_convert_fusion.refs_0_, bf16[1,512,1024]{2,1,0:T(8,128)(2,1)} %get-tuple-element.81.refs_1_, ...), custom_call_target="tpu_custom_call" | custom-call | bytes 120000000 | tf_op jit(solution)/shard_map/line_reduce/pallas_call | solution.py:450
  222.3 53.1 %line_gather.4 = (bf16[1024,2048]{1,0:T(8,128)(2,1)}, bf16[1,512,1024]{2,1,0:T(8,128)(2,1)}, bf16[1,512,1024]{2,1,0:T(8,128)(2,1)}, bf16[1,512,1024]{2,1,0:T(8,128)(2,1)}, bf16[1,512,1024]{2,1,0:T(8,128)(2,1)}) custom-call(bf16[128,2048]{1,0:T(8,128)(2,1)} %pad_maximum_fusion.38.refs_0_, bf16[2,512,1024]{2,1,0:T(8,128)(2,1)} %refs_1_.3, ...), custom_call_target="tpu_custom_call" | custom-call | bytes 120000000 | tf_op jit(solution)/shard_map/line_gather/pallas_call | solution.py:450
  278.5 9.6 %fusion.83 = f32[1024,1024]{0,1:T(8,128)} fusion(bf16[1024,2048]{1,0:T(8,128)(2,1)} %get-tuple-element.85, bf16[512,1024]{1,0:T(8,128)(2,1)S(1)} %bitcast.385, bf16[512,1024]{1,0:T(8,128)(2,1)} %bitcast.40, bf16[512,1024]{1,0:T(8,128)(2,1)} %bitcast.39, bf16[512,1024]{1,0:T(8,128)(2,1)S(1)} %copy-done.47), kind=kOutput, calls=%fused_computation.243 | convolution fusion | flops 4311744512 | bytes 12582912 | tf_op jit(solution)/shard_map/dot_general | solution.py:23
  288.1 32.8 %collective-permute-done.3 = bf16[2,256,2048]{2,1,0:T(8,128)(2,1)} collective-permute-done((bf16[2,256,2048]{2,1,0:T(8,128)(2,1)}, bf16[2,256,2048]{2,1,0:T(8,128)(2,1)}, u32[]{:S(2)}, u32[]{:S(2)}) %collective-permute-start.3) | collective-permute-done | bytes 2097184 | tf_op jit(solution)/shard_map/ppermute | solution.py:519
  323.8 6.4 fusion.87
  331.2 13.7 %exchange.11 = f32[8,8,128]{2,1,0:T(8,128)} custom-call(f32[8,8,128]{2,1,0:T(8,128)} %pad.7.refs_0_), custom_call_target="tpu_custom_call" | custom-call | bytes 24000000 | tf_op jit(solution)/shard_map/exchange/pallas_call | solution.py:450
  345.8 5.8 collective-permute-done.5
  354.9 3.9 pad_maximum_fusion
  358.9 10.1 %fusion.2 = f32[1024,1024]{0,1:T(8,128)} fusion(bf16[1024,2048]{1,0:T(8,128)(2,1)} %all-gather.2.cloned.1.call-done, bf16[2,1024,2048]{2,1,0:T(8,128)(2,1)} %pad_maximum_fusion), kind=kOutput, calls=%fused_computation.11 | convolution fusion | flops 4294967296 | bytes 12582912 | tf_op jit(solution)/shard_map/dot_general | solution.py:31
  369.0 10.1 %multiply_reduce_fusion.2 = (f32[1024]{0:T(1024)S(1)}, bf16[1024,1024]{0,1:T(8,128)(2,1)S(1)}, bf16[1024,1024]{0,1:T(8,128)(2,1)}, bf16[1024,1024]{0,1:T(8,128)(2,1)}) fusion(f32[1024,1024]{0,1:T(8,128)} %fusion.2, f32[1024,1024]{0,1:T(8,128)} %fusion.83, f32[1024]{0:T(1024)S(1)} %bitcast.381, bf16[1024,2048]{1,0:T(8,128)(2,1)S(1)} %copy-done.136, ...), kind=kOutput, calls=%fused_computation.22 | convolution fusion | flops 4331666432 | bytes 23076864 | tf_op jit(solution)/shard_map/dot_general | solution.py:23
  387.6 6.1 fusion.4
  393.7 10.8 %multiply_reduce_fusion.3 = (f32[1024]{0:T(1024)S(1)}, bf16[1024,1024]{0,1:T(8,128)(2,1)}, bf16[1024,1024]{0,1:T(8,128)(2,1)}, bf16[1024,1024]{0,1:T(8,128)(2,1)}) fusion(f32[1024,1024]{0,1:T(8,128)} %fusion.4, f32[1024,1024]{0,1:T(8,128)} %fusion.87, f32[1024]{0:T(1024)S(1)} %bitcast.379, bf16[1024,2048]{1,0:T(8,128)(2,1)S(1)} %copy-done.136, ...), kind=kOutput, calls=%fused_computation.23 | convolution fusion | flops 4331666432 | bytes 23076864 | tf_op jit(solution)/shard_map/dot_general | solution.py:23
  404.5 4.0 fusion.34
  414.7 3.9 fusion.21
  420.0 9.9 %fusion.81 = f32[1024,2048]{1,0:T(8,128)} fusion(bf16[1024,1024]{0,1:T(8,128)(2,1)S(1)} %copy-done.170, bf16[512,1024]{1,0:T(8,128)(2,1)S(1)} %bitcast.398, bf16[512,1024]{1,0:T(8,128)(2,1)S(1)} %bitcast.396, bf16[512,1024]{1,0:T(8,128)(2,1)S(1)} %bitcast.394, bf16[512,1024]{1,0:T(8,128)(2,1)S(1)} %copy-done.58), kind=kOutput, calls=%fused_computation.241 | convolution fusion | flops 4311744512 | bytes 14680064 | tf_op jit(solution)/shard_map/dot_general | solution.py:31
  430.6 13.2 %exchange.12 = f32[8,8,128]{2,1,0:T(8,128)} custom-call(f32[8,8,128]{2,1,0:T(8,128)} %pad.8.refs_0_), custom_call_target="tpu_custom_call" | custom-call | bytes 24000000 | tf_op jit(solution)/shard_map/exchange/pallas_call | solution.py:450
  446.2 4.3 fusion.24
  451.3 10.1 %fusion.84 = f32[1024,2048]{1,0:T(8,128)} fusion(bf16[1024,1024]{0,1:T(8,128)(2,1)S(1)} %copy-done.173, bf16[512,1024]{1,0:T(8,128)(2,1)S(1)} %bitcast.392, bf16[512,1024]{1,0:T(8,128)(2,1)S(1)} %bitcast.347, bf16[512,1024]{1,0:T(8,128)(2,1)S(1)} %bitcast.390, bf16[512,1024]{1,0:T(8,128)(2,1)S(1)} %copy-done.57), kind=kOutput, calls=%fused_computation.244 | convolution fusion | flops 4311744512 | bytes 14680064 | tf_op jit(solution)/shard_map/dot_general | solution.py:31
  470.2 3.5 add_convert_fusion.3
  475.3 3.6 add_convert_fusion.2
  484.7 10.2 %fusion.86 = f32[1024,2048]{1,0:T(8,128)} fusion(bf16[1024,1024]{0,1:T(8,128)(2,1)S(1)} %copy-done.163, bf16[512,1024]{1,0:T(8,128)(2,1)S(1)} %bitcast.388, bf16[512,1024]{1,0:T(8,128)(2,1)S(1)} %bitcast.354, bf16[512,1024]{1,0:T(8,128)(2,1)S(1)} %bitcast.384, bf16[512,1024]{1,0:T(8,128)(2,1)S(1)} %copy-done.49), kind=kOutput, calls=%fused_computation.246 | convolution fusion | flops 4311744512 | bytes 14680064 | tf_op jit(solution)/shard_map/dot_general | solution.py:31
  499.7 14.1 %add_convert_fusion.1.refs_0_ = bf16[1024,2048]{1,0:T(8,128)(2,1)} fusion(f32[1024,2048]{1,0:T(8,128)} %fusion.81, f32[1024,2048]{1,0:T(8,128)} %fusion.86, f32[1024,2048]{1,0:T(8,128)} %fusion.84, bf16[1024,1024]{0,1:T(8,128)(2,1)} %copy-done.160, bf16[512,1024]{1,0:T(8,128)(2,1)S(1)} %bitcast.386, bf16[512,1024]{1,0:T(8,128)(2,1)} %bitcast.40, ...), kind=kOutput, calls=%fused_computation.2 | convolution fusion | flops 4320133120 | bytes 35651584 | tf_op jit(solution)/shard_map/dot_general | solution.py:31
  513.8 77.9 %line_reduce.4 = (f32[128,2048]{1,0:T(8,128)}, bf16[2,512,1024]{2,1,0:T(8,128)(2,1)}, bf16[2,512,1024]{2,1,0:T(8,128)(2,1)}) custom-call(bf16[1024,2048]{1,0:T(8,128)(2,1)} %add_convert_fusion.1.refs_0_, bf16[2,512,1024]{2,1,0:T(8,128)(2,1)} %pad_maximum_fusion.6, bf16[2,512,1024]{2,1,0:T(8,128)(2,1)} %pad_maximum_fusion.8), custom_call_target="tpu_custom_call" | custom-call | bytes 120000000 | tf_op jit(solution)/shard_map/line_reduce/pallas_call | solution.py:450
  594.2 4.3 fusion.43
  606.5 40.1 %line_gather.5 = (bf16[1024,2048]{1,0:T(8,128)(2,1)}, bf16[1,512,1024]{2,1,0:T(8,128)(2,1)}, bf16[1,512,1024]{2,1,0:T(8,128)(2,1)}) custom-call(bf16[128,2048]{1,0:T(8,128)(2,1)} %fusion.161.refs_0_, bf16[2,512,1024]{2,1,0:T(8,128)(2,1)} %pad_maximum_fusion.15.refs_1_), custom_call_target="tpu_custom_call" | custom-call | bytes 120000000 | tf_op jit(solution)/shard_map/line_gather/pallas_call | solution.py:450
  646.6 3.6 convolution_convert_fusion.28
  663.7 3.6 fusion.26
  684.1 7.3 exchange.13
  696.1 7.2 fusion
  703.4 8.6 add_convert_fusion
  715.0 3.8 convolution_convert_fusion.2
  722.6 7.8 convolution_convert_fusion.1.refs_0_
  730.5 61.9 %line_reduce.5 = (f32[128,2048]{1,0:T(8,128)}, bf16[256,768]{1,0:T(8,128)(2,1)}, bf16[256,768]{1,0:T(8,128)(2,1)}, bf16[32,2048]{1,0:T(8,128)(2,1)}, bf16[32,2048]{1,0:T(8,128)(2,1)}) custom-call(bf16[1024,2048]{1,0:T(8,128)(2,1)} %convolution_convert_fusion.1.refs_0_, bf16[512,768]{1,0:T(8,128)(2,1)} %get-tuple-element.209.refs_1_, ...), custom_call_target="tpu_custom_call" | custom-call | bytes 120000000 | tf_op jit(solution)/shard_map/line_reduce/pallas_call | solution.py:450
  802.3 39.3 %exchange.14 = (f32[16,128]{1,0:T(8,128)}, bf16[512,768]{1,0:T(8,128)(2,1)}, bf16[512,768]{1,0:T(8,128)(2,1)}, bf16[64,2048]{1,0:T(8,128)(2,1)}, bf16[64,2048]{1,0:T(8,128)(2,1)}) custom-call(f32[32,16,128]{2,1,0:T(8,128)} %bitcast.348, bf16[512,768]{1,0:T(8,128)(2,1)} %pad_maximum_fusion.23.refs_1_, bf16[512,768]{1,0:T(8,128)(2,1)} %pad_maximum_fusion.24.refs_2_, ...), custom_call_target="tpu_custom_call" | custom-call | bytes 24000000 | tf_op jit(solution)/shard_map/exchange/pallas_call | solution.py:450
  845.7 19.2 %exchange.15 = bf16[8,64,768]{2,1,0:T(8,128)(2,1)} custom-call(bf16[8,64,768]{2,1,0:T(8,128)(2,1)} %bitcast.342), custom_call_target="tpu_custom_call" | custom-call | bytes 24000000 | tf_op jit(solution)/shard_map/exchange/pallas_call | solution.py:450
  865.0 6.1 collective-permute-start.11
  875.9 4.3 fusion.39
  880.3 3.6 fusion.38
  884.0 3.4 convert_add_fusion.2
  894.4 5.8 convert_add_fusion.1
  900.3 5.5 convert_add_fusion
  (559 shorter events, 181.6 us)
Async XLA Ops:
  7.2 351.6 %all-gather.2.cloned.1.call-start = ((), (), s32[]{:S(2)}) async-start(), calls=%async_computation.1 | async-start | bytes 4718592 | tf_op jit(solution)/shard_map/all_gather | solution.py:652
  23.6 51.0 %collective-permute-start = (bf16[64,2048]{1,0:T(8,128)(2,1)}, bf16[64,2048]{1,0:T(8,128)(2,1)S(1)}, u32[]{:S(2)}, u32[]{:S(2)}) collective-permute-start(bf16[64,2048]{1,0:T(8,128)(2,1)} %param.21), channel_id=1, source_target_pairs={{0,0},{1,8},{2,16},{3,24},{4,1},{5,9},{6,17},{7,25},{8,2},{9,10},{... | collective-permute-start | bytes 786440 | tf_op jit(solution)/shard_map/ppermute | solution.py:633
  30.2 190.1 %copy-start.90 = (f32[2048]{0:T(1024)}, f32[2048]{0:T(1024)S(1)}, u32[]{:S(2)}) copy-start(f32[2048]{0:T(1024)S(1)} %reshape.328) | copy-start | bytes 24580
  30.5 103.5 %copy-start.114 = (f32[256]{0:T(256)}, f32[256]{0:T(256)S(1)}, u32[]{:S(2)}) copy-start(f32[256]{0:T(256)S(1)} %dynamic_slice.9) | copy-start | bytes 3076
  30.6 103.4 %copy-start.116 = (f32[256]{0:T(256)}, f32[256]{0:T(256)S(1)}, u32[]{:S(2)}) copy-start(f32[256]{0:T(256)S(1)} %dynamic_slice.8) | copy-start | bytes 3076
  72.7 46.2 %copy-start.32 = (bf16[8,64,768]{2,1,0:T(8,128)(2,1)S(1)}, bf16[8,64,768]{2,1,0:T(8,128)(2,1)}, u32[]{:S(2)}) copy-start(bf16[8,64,768]{2,1,0:T(8,128)(2,1)} %get-tuple-element.69) | copy-start | bytes 2359300
  115.2 162.4 %collective-permute-start.6 = (bf16[1,512,1024]{2,1,0:T(8,128)(2,1)}, bf16[1,512,1024]{2,1,0:T(8,128)(2,1)}, u32[]{:S(2)}, u32[]{:S(2)}) collective-permute-start(bf16[1,512,1024]{2,1,0:T(8,128)(2,1)} %get-tuple-element.82), channel_id=1, source_target_pairs={{0,16},{8,24},{16,0},{24,8},{1,17},{9,25},{17,1},{25,9},{2,18},{10... | collective-permute-start | bytes 3145736 | tf_op jit(solution)/shard_map/ppermute | solution.py:519
  115.6 37.0 %collective-permute-start.1 = (bf16[1,512,1024]{2,1,0:T(8,128)(2,1)}, bf16[1,512,1024]{2,1,0:T(8,128)(2,1)}, u32[]{:S(2)}, u32[]{:S(2)}) collective-permute-start(bf16[1,512,1024]{2,1,0:T(8,128)(2,1)} %get-tuple-element.82), channel_id=1, source_target_pairs={{0,8},{8,0},{16,24},{24,16},{1,9},{9,1},{17,25},{25,17},{2,10},{10... | collective-permute-start | bytes 3145736 | tf_op jit(solution)/shard_map/ppermute | solution.py:519
  141.5 764.3 %reduce-scatter.2.cloned.1.call-start = ((), (), s32[]{:S(2)}) async-start(), calls=%async_computation.2 | async-start | bytes 4718592 | tf_op jit(solution)/shard_map/reduce_scatter | solution.py:765
  149.2 69.6 %copy-start.168 = (bf16[1024,128]{0,1:T(8,128)(2,1)}, bf16[1024,128]{0,1:T(8,128)(2,1)S(1)}, u32[]{:S(2)}) copy-start(bf16[1024,128]{0,1:T(8,128)(2,1)S(1)} %convolution_convert_fusion.30) | copy-start | bytes 786436
  152.6 66.2 %copy-start.11 = (bf16[1,128,2048]{2,1,0:T(8,128)(2,1)S(1)}, bf16[1,128,2048]{2,1,0:T(8,128)(2,1)}, u32[]{:S(2)}) copy-start(bf16[1,128,2048]{2,1,0:T(8,128)(2,1)} %param.15) | copy-start | bytes 1572868
  220.3 57.4 %copy-start.131 = (f32[128]{0:T(128)}, f32[128]{0:T(128)S(1)}, u32[]{:S(2)}) copy-start(f32[128]{0:T(128)S(1)} %get-tuple-element.194) | copy-start | bytes 1540
  220.3 55.8 %copy-start.125 = (s32[1,128,8]{1,2,0:T(8,128)S(1)}, s32[1,128,8]{1,2,0:T(8,128)}, u32[]{:S(2)}) copy-start(s32[1,128,8]{1,2,0:T(8,128)} %param.16) | copy-start | bytes 12292
  220.3 55.8 %copy-start.2 = (bf16[2,512,1024]{2,1,0:T(8,128)(2,1)S(1)}, bf16[2,512,1024]{2,1,0:T(8,128)(2,1)}, u32[]{:S(2)}) copy-start(bf16[2,512,1024]{2,1,0:T(8,128)(2,1)} %refs_1_.3) | copy-start | bytes 6291460
  220.3 55.3 %copy-start.121 = (f32[128]{0:T(128)}, f32[128]{0:T(128)S(1)}, u32[]{:S(2)}) copy-start(f32[128]{0:T(128)S(1)} %add_rsqrt_fusion.1) | copy-start | bytes 1540
  275.4 45.5 %collective-permute-start.3 = (bf16[2,256,2048]{2,1,0:T(8,128)(2,1)}, bf16[2,256,2048]{2,1,0:T(8,128)(2,1)}, u32[]{:S(2)}, u32[]{:S(2)}) collective-permute-start(bf16[2,256,2048]{2,1,0:T(8,128)(2,1)} %param.29), channel_id=1, source_target_pairs={{0,8},{8,0},{16,24},{24,16},{1,9},{9,1},{17,25},{25,17},{2,10},{10... | collective-permute-start | bytes 6291464 | tf_op jit(solution)/shard_map/ppermute | solution.py:519
  275.5 46.8 %collective-permute-start.2 = (bf16[2,256,2048]{2,1,0:T(8,128)(2,1)}, bf16[2,256,2048]{2,1,0:T(8,128)(2,1)}, u32[]{:S(2)}, u32[]{:S(2)}) collective-permute-start(bf16[2,256,2048]{2,1,0:T(8,128)(2,1)} %param.29), channel_id=1, source_target_pairs={{0,16},{8,24},{16,0},{24,8},{1,17},{9,25},{17,1},{25,9},{2,18},{10... | collective-permute-start | bytes 6291464 | tf_op jit(solution)/shard_map/ppermute | solution.py:519
  276.0 54.2 %copy-start.35 = (bf16[2048,16]{1,0:T(8,128)(2,1)}, bf16[2048,16]{1,0:T(8,128)(2,1)S(1)}, u32[]{:S(2)}) copy-start(bf16[2048,16]{1,0:T(8,128)(2,1)S(1)} %reshape.309) | copy-start | bytes 196612
  278.5 45.2 %copy-start.135 = (bf16[1024,2048]{1,0:T(8,128)(2,1)S(1)}, bf16[1024,2048]{1,0:T(8,128)(2,1)}, u32[]{:S(2)}) copy-start(bf16[1024,2048]{1,0:T(8,128)(2,1)} %get-tuple-element.85) | copy-start | bytes 12582916
  288.1 35.6 %copy-start.65 = (bf16[1,512,1024]{2,1,0:T(8,128)(2,1)S(1)}, bf16[1,512,1024]{2,1,0:T(8,128)(2,1)}, u32[]{:S(2)}) copy-start(bf16[1,512,1024]{2,1,0:T(8,128)(2,1)} %get-tuple-element.81.refs_1_) | copy-start | bytes 3145732
  288.1 35.6 %copy-start.143 = (bf16[1,512,1024]{2,1,0:T(8,128)(2,1)S(1)}, bf16[1,512,1024]{2,1,0:T(8,128)(2,1)}, u32[]{:S(2)}) copy-start(bf16[1,512,1024]{2,1,0:T(8,128)(2,1)} %get-tuple-element.86) | copy-start | bytes 3145732
  288.1 35.6 %copy-start.147 = (bf16[1,512,1024]{2,1,0:T(8,128)(2,1)S(1)}, bf16[1,512,1024]{2,1,0:T(8,128)(2,1)}, u32[]{:S(2)}) copy-start(bf16[1,512,1024]{2,1,0:T(8,128)(2,1)} %get-tuple-element.87) | copy-start | bytes 3145732
  323.6 22.0 %collective-permute-start.4 = (bf16[1,256,2048]{2,1,0:T(8,128)(2,1)S(1)}, bf16[1,256,2048]{2,1,0:T(8,128)(2,1)S(1)}, u32[]{:S(2)}, u32[]{:S(2)}) collective-permute-start(bf16[1,256,2048]{2,1,0:T(8,128)(2,1)S(1)} %slice.284), channel_id=1, source_target_pairs={{0,8},{8,0},{16,24},{24,16},{1,9},{9,1},{17,25},{25,17},{2,10},{10... | collective-permute-start | bytes 3145736 | tf_op jit(solution)/shard_map/ppermute | solution.py:519
  330.2 21.4 %collective-permute-start.5 = (bf16[1,256,2048]{2,1,0:T(8,128)(2,1)S(1)}, bf16[1,256,2048]{2,1,0:T(8,128)(2,1)S(1)}, u32[]{:S(2)}, u32[]{:S(2)}) collective-permute-start(bf16[1,256,2048]{2,1,0:T(8,128)(2,1)S(1)} %slice.285), channel_id=1, source_target_pairs={{0,16},{8,24},{16,0},{24,8},{1,17},{9,25},{17,1},{25,9},{2,18},{10... | collective-permute-start | bytes 3145736 | tf_op jit(solution)/shard_map/ppermute | solution.py:519
  413.1 55.6 %collective-permute-start.9 = (bf16[1,512,1024]{2,1,0:T(8,128)(2,1)}, bf16[1,512,1024]{2,1,0:T(8,128)(2,1)}, u32[]{:S(2)}, u32[]{:S(2)}) collective-permute-start(bf16[1,512,1024]{2,1,0:T(8,128)(2,1)} %fusion.35), channel_id=1, source_target_pairs={{0,16},{8,24},{16,0},{24,8},{1,17},{9,25},{17,1},{25,9},{2,18},{10... | collective-permute-start | bytes 3145736 | tf_op jit(solution)/shard_map/ppermute | solution.py:519
  413.1 62.1 %collective-permute-start.10 = (bf16[1,512,1024]{2,1,0:T(8,128)(2,1)}, bf16[1,512,1024]{2,1,0:T(8,128)(2,1)}, u32[]{:S(2)}, u32[]{:S(2)}) collective-permute-start(bf16[1,512,1024]{2,1,0:T(8,128)(2,1)} %fusion.34), channel_id=1, source_target_pairs={{0,8},{8,0},{16,24},{24,16},{1,9},{9,1},{17,25},{25,17},{2,10},{10... | collective-permute-start | bytes 3145736 | tf_op jit(solution)/shard_map/ppermute | solution.py:519
  418.6 76.3 %collective-permute-start.7 = (bf16[1,256,2048]{2,1,0:T(8,128)(2,1)}, bf16[1,256,2048]{2,1,0:T(8,128)(2,1)}, u32[]{:S(2)}, u32[]{:S(2)}) collective-permute-start(bf16[1,256,2048]{2,1,0:T(8,128)(2,1)} %fusion.21), channel_id=1, source_target_pairs={{0,16},{8,24},{16,0},{24,8},{1,17},{9,25},{17,1},{25,9},{2,18},{10... | collective-permute-start | bytes 3145736 | tf_op jit(solution)/shard_map/ppermute | solution.py:519
  450.5 29.9 %collective-permute-start.8 = (bf16[1,256,2048]{2,1,0:T(8,128)(2,1)S(1)}, bf16[1,256,2048]{2,1,0:T(8,128)(2,1)S(1)}, u32[]{:S(2)}, u32[]{:S(2)}) collective-permute-start(bf16[1,256,2048]{2,1,0:T(8,128)(2,1)S(1)} %fusion.24), channel_id=1, source_target_pairs={{0,8},{8,0},{16,24},{24,16},{1,9},{9,1},{17,25},{25,17},{2,10},{10... | collective-permute-start | bytes 3145736 | tf_op jit(solution)/shard_map/ppermute | solution.py:519
  483.2 417.0 %collective-permute-start.15 = (bf16[2,256,2048]{2,1,0:T(8,128)(2,1)}, bf16[2,256,2048]{2,1,0:T(8,128)(2,1)}, u32[]{:S(2)}, u32[]{:S(2)}) collective-permute-start(bf16[2,256,2048]{2,1,0:T(8,128)(2,1)} %pad_maximum_fusion.14), channel_id=1, source_target_pairs={{0,16},{8,24},{16,0},{24,8},{1,17},{9,25},{17,1},{25,9},{2,18},{10... | collective-permute-start | bytes 6291464 | tf_op jit(solution)/shard_map/ppermute | solution.py:519
  499.0 401.3 %collective-permute-start.14 = (bf16[2,256,2048]{2,1,0:T(8,128)(2,1)}, bf16[2,256,2048]{2,1,0:T(8,128)(2,1)}, u32[]{:S(2)}, u32[]{:S(2)}) collective-permute-start(bf16[2,256,2048]{2,1,0:T(8,128)(2,1)} %pad_maximum_fusion.13), channel_id=1, source_target_pairs={{0,8},{8,0},{16,24},{24,16},{1,9},{9,1},{17,25},{25,17},{2,10},{10... | collective-permute-start | bytes 6291464 | tf_op jit(solution)/shard_map/ppermute | solution.py:519
  513.8 79.4 %copy-start.4 = (f32[128,2048]{1,0:T(8,128)S(1)}, f32[128,2048]{1,0:T(8,128)}, u32[]{:S(2)}) copy-start(f32[128,2048]{1,0:T(8,128)} %copy-done.3) | copy-start | bytes 3145732
  513.8 79.4 %copy-start.36 = (bf16[2048,16]{1,0:T(8,128)(2,1)S(1)}, bf16[2048,16]{1,0:T(8,128)(2,1)}, u32[]{:S(2)}) copy-start(bf16[2048,16]{1,0:T(8,128)(2,1)} %copy-done.35) | copy-start | bytes 196612
  513.8 79.4 %copy-start.91 = (f32[2048]{0:T(1024)S(1)}, f32[2048]{0:T(1024)}, u32[]{:S(2)}) copy-start(f32[2048]{0:T(1024)} %copy-done.90) | copy-start | bytes 24580
  513.8 79.4 %copy-start.122 = (f32[128]{0:T(128)S(1)}, f32[128]{0:T(128)}, u32[]{:S(2)}) copy-start(f32[128]{0:T(128)} %copy-done.121) | copy-start | bytes 1540
  603.8 42.8 %copy-start.126 = (f32[128]{0:T(128)}, f32[128]{0:T(128)S(1)}, u32[]{:S(2)}) copy-start(f32[128]{0:T(128)S(1)} %fusion.144) | copy-start | bytes 1540
  605.0 41.6 %copy-start.81 = (bf16[64,2048]{1,0:T(8,128)(2,1)S(1)}, bf16[64,2048]{1,0:T(8,128)(2,1)}, u32[]{:S(2)}) copy-start(bf16[64,2048]{1,0:T(8,128)(2,1)} %copy-done.80) | copy-start | bytes 786436
  605.0 41.6 %copy-start.83 = (bf16[64,2048]{1,0:T(8,128)(2,1)S(1)}, bf16[64,2048]{1,0:T(8,128)(2,1)}, u32[]{:S(2)}) copy-start(bf16[64,2048]{1,0:T(8,128)(2,1)} %copy-done.82) | copy-start | bytes 786436
  605.0 41.6 %copy-start.85 = (bf16[64,2048]{1,0:T(8,128)(2,1)S(1)}, bf16[64,2048]{1,0:T(8,128)(2,1)}, u32[]{:S(2)}) copy-start(bf16[64,2048]{1,0:T(8,128)(2,1)} %copy-done.84) | copy-start | bytes 786436
  605.0 41.6 %copy-start.87 = (bf16[64,2048]{1,0:T(8,128)(2,1)S(1)}, bf16[64,2048]{1,0:T(8,128)(2,1)}, u32[]{:S(2)}) copy-start(bf16[64,2048]{1,0:T(8,128)(2,1)} %copy-done.86) | copy-start | bytes 786436
  674.2 220.2 %collective-permute-start.13 = (bf16[2,512,1024]{2,1,0:T(8,128)(2,1)}, bf16[2,512,1024]{2,1,0:T(8,128)(2,1)}, u32[]{:S(2)}, u32[]{:S(2)}) collective-permute-start(bf16[2,512,1024]{2,1,0:T(8,128)(2,1)} %pad_maximum_fusion.17), channel_id=1, source_target_pairs={{0,16},{8,24},{16,0},{24,8},{1,17},{9,25},{17,1},{25,9},{2,18},{10... | collective-permute-start | bytes 6291464 | tf_op jit(solution)/shard_map/ppermute | solution.py:519
  676.8 217.6 %collective-permute-start.12 = (bf16[2,512,1024]{2,1,0:T(8,128)(2,1)}, bf16[2,512,1024]{2,1,0:T(8,128)(2,1)}, u32[]{:S(2)}, u32[]{:S(2)}) collective-permute-start(bf16[2,512,1024]{2,1,0:T(8,128)(2,1)} %pad_maximum_fusion.16), channel_id=1, source_target_pairs={{0,8},{8,0},{16,24},{24,16},{1,9},{9,1},{17,25},{25,17},{2,10},{10... | collective-permute-start | bytes 6291464 | tf_op jit(solution)/shard_map/ppermute | solution.py:519
  730.5 61.9 %copy-start.12 = (bf16[1,128,2048]{2,1,0:T(8,128)(2,1)S(1)}, bf16[1,128,2048]{2,1,0:T(8,128)(2,1)}, u32[]{:S(2)}) copy-start(bf16[1,128,2048]{2,1,0:T(8,128)(2,1)} %param.15) | copy-start | bytes 1572868
  730.5 62.0 %copy-start.93 = (f32[2048]{0:T(1024)S(1)}, f32[2048]{0:T(1024)}, u32[]{:S(2)}) copy-start(f32[2048]{0:T(1024)} %copy-done.92) | copy-start | bytes 24580
  730.5 62.0 %copy-start.119 = (f32[128]{0:T(128)S(1)}, f32[128]{0:T(128)}, u32[]{:S(2)}) copy-start(f32[128]{0:T(128)} %copy-done.118) | copy-start | bytes 1540
  730.5 65.4 %copy-start.75 = (f32[32,1024]{1,0:T(8,128)S(1)}, f32[32,1024]{1,0:T(8,128)}, u32[]{:S(2)}) copy-start(f32[32,1024]{1,0:T(8,128)} %reshape.317) | copy-start | bytes 393220
  798.8 42.8 %copy-start.31 = (bf16[256,2048]{1,0:T(8,128)(2,1)S(1)}, bf16[256,2048]{1,0:T(8,128)(2,1)}, u32[]{:S(2)}) copy-start(bf16[256,2048]{1,0:T(8,128)(2,1)} %copy-done.30) | copy-start | bytes 3145732
  799.7 43.2 %copy-start.14 = (bf16[2048,768]{1,0:T(8,128)(2,1)S(1)}, bf16[2048,768]{1,0:T(8,128)(2,1)}, u32[]{:S(2)}) copy-start(bf16[2048,768]{1,0:T(8,128)(2,1)} %copy-done.13) | copy-start | bytes 9437188
  865.0 27.7 %collective-permute-start.11 = (bf16[64,2048]{1,0:T(8,128)(2,1)S(1)}, bf16[64,2048]{1,0:T(8,128)(2,1)}, u32[]{:S(2)}, u32[]{:S(2)}) collective-permute-start(bf16[64,2048]{1,0:T(8,128)(2,1)S(1)} %add_convert_fusion.9), channel_id=1, source_target_pairs={{0,0},{8,1},{16,2},{24,3},{1,4},{9,5},{17,6},{25,7},{2,8},{10,9},{... | collective-permute-start | bytes 786440 | tf_op jit(solution)/shard_map/ppermute | solution.py:847
  (150 other events, 754.6 us)
Sparse Core Ops, SparseCore 0:
  141.6 69.1 all-gather.1
  712.1 67.6 reduce-scatter.1

commit v3 on v2

--- a/solution.py
+++ b/solution.py
@@ -426,7 +426,9 @@
     plane.finish()
 
 
-def run(body, name, micros, collective_id, x, x_space, out, out_space, scratch, sends, later):
+def run(
+    body, name, micros, collective_id, x, x_space, out, out_space, scratch, sends, later, carry=(), after=()
+):
     arrays, specs = [], []
     for array, start, size, flip in sends:
         found = [i for i, a in enumerate(arrays) if a is array]
@@ -437,43 +439,45 @@
     targets = [jax.ShapeDtypeStruct((s[2],) + s[0].shape[1:], s[0].dtype) for s in sends]
     for source, start, size, flip in later:
         targets.append(jax.ShapeDtypeStruct((size,) + targets[source].shape[1:], targets[source].dtype))
-    n_in, n_out = len(arrays), len(targets)
+    n_in, n_out, held = len(arrays), len(targets), len(carry)
 
     def kernel(*refs):
         x_ref, sources = refs[0], refs[1 : 1 + n_in]
-        o_ref, dests = refs[1 + n_in], refs[2 + n_in : 2 + n_in + n_out]
-        rest = refs[2 + n_in + n_out :]
+        refs = refs[1 + n_in + held + len(after) :]
+        o_ref, dests = refs[0], refs[1 : 1 + n_out]
+        rest = refs[1 + n_out + held :]
         plane = Plane(specs, later, sources, dests, *rest[:2])
         body(plane, x_ref, o_ref, *rest[2:])
 
     anywhere = pl.BlockSpec(memory_space=pl.ANY)
     got = pl.pallas_call(
         kernel,
-        out_shape=[out] + targets,
-        in_specs=[pl.BlockSpec(memory_space=x_space)] + [anywhere] * n_in,
-        out_specs=[pl.BlockSpec(memory_space=out_space)] + [anywhere] * n_out,
+        out_shape=[out] + targets + [jax.ShapeDtypeStruct(c.shape, c.dtype) for c in carry],
+        in_specs=[pl.BlockSpec(memory_space=x_space)] + [anywhere] * (n_in + held + len(after)),
+        out_specs=[pl.BlockSpec(memory_space=out_space)] + [anywhere] * (n_out + held),
+        input_output_aliases={1 + n_in + i: 1 + n_out + i for i in range(held)},
         scratch_shapes=[pltpu.SemaphoreType.DMA((max(n_out, 1),))] * 2 + scratch,
         compiler_params=pltpu.CompilerParams(
             collective_id=collective_id, has_side_effects=True, vmem_limit_bytes=VMEM_LIMIT
         ),
         cost_estimate=cost_of(micros),
         name=name,
-    )(x, *arrays)
-    return got if n_out else got[0]
-
-
-def line_gather(x, collective_id, sends=(), later=(), parts=2):
+    )(x, *arrays, *carry, *after)
+    return got if n_out + held else got[0]
+
+
+def line_gather(x, collective_id, sends=(), later=(), after=(), parts=2):
     rows, width = x.shape
     groups = lax.axis_size("expert")
     shape = (2, groups // 2, parts)
     return run(
         functools.partial(gather_body, groups, rows, parts), "line_gather", 40, collective_id,
         x, pl.ANY, jax.ShapeDtypeStruct((groups * rows, width), x.dtype), pl.ANY,
-        [pltpu.SemaphoreType.DMA] + [pltpu.SemaphoreType.DMA(shape)] * 4, sends, later,
-    )
-
-
-def line_reduce(partial, collective_id, sends=(), later=(), parts=2):
+        [pltpu.SemaphoreType.DMA] + [pltpu.SemaphoreType.DMA(shape)] * 4, sends, later, (), after,
+    )
+
+
+def line_reduce(partial, collective_id, sends=(), later=(), after=(), parts=2):
     groups = lax.axis_size("expert")
     chips = groups // 2
     rows, width = partial.shape[0] // groups, partial.shape[1]
@@ -490,11 +494,13 @@
             pltpu.SemaphoreType.DMA((chips, parts)),
             pltpu.SemaphoreType.DMA((2 * chips, parts)),
         ],
-        sends, later,
-    )
-
-
-def exchange(x, collective_id, spread=False, same=False, reduce=False, sends=(), later=()):
+        sends, later, (), after,
+    )
+
+
+def exchange(
+    x, collective_id, spread=False, same=False, reduce=False, sends=(), later=(), carry=()
+):
     count = lax.axis_size("expert") * (lax.axis_size("dp") if spread else 1)
     block = x.shape[1:]
     return run(
@@ -505,8 +511,668 @@
             pltpu.SemaphoreType.DMA((count,)),
             pltpu.SemaphoreType.DMA((count,)),
         ],
-        sends, later,
-    )
+        sends, later, carry,
+    )
+
+
+LANES = 128
+TILE = 512
+
+
+def expert_first_body(
+    groups, seqs, rows, width, ff, experts, parts,
+    x_ref, g_ref, gate_ref, up_ref, down_ref, near_refs,
+    f_out, hid_out, sg_out, su_out, tail_out, down_out,
+    f_buf, g_buf, wg, wu, wd, hid, sg, su, tail_buf, tail_sum,
+    line_send, line_recv, side_send, side_recv, own_sem, f_sem, w_sem, d_sem, g_sem, out_sem, tail_sem,
+    plane_send, plane_recv,
+):
+    chips = groups // 2
+    me, dp = lax.axis_index("expert"), lax.axis_index("dp")
+    chip, core = me // 2, me % 2
+    sibling = chip * 2 + 1 - core
+    chunk = 2 * rows
+    part = rows // parts
+    depth, wide_ff = width // seqs, ff // seqs
+
+    def remote(src, dst, send_sem, recv_sem, device):
+        return pltpu.make_async_remote_copy(
+            src_ref=src, dst_ref=dst, send_sem=send_sem, recv_sem=recv_sem,
+            device_id=device, device_id_type=MESH,
+        )
+
+    def at(index, size):
+        return pl.ds(pl.multiple_of(index * size, size), size)
+
+    def neighbour(flip):
+        return (flipped(dp, flip), me)
+
+    barrier = pltpu.get_barrier_semaphore()
+    pl.semaphore_signal(barrier, inc=1, device_id=(dp, sibling), device_id_type=MESH)
+    for flip in (1, 2):
+        pl.semaphore_signal(barrier, inc=1, device_id=neighbour(flip), device_id_type=MESH)
+
+    @pl.when(chip > 0)
+    def _():
+        pl.semaphore_signal(barrier, inc=1, device_id=(dp, me - 2), device_id_type=MESH)
+
+    @pl.when(chip < chips - 1)
+    def _():
+        pl.semaphore_signal(barrier, inc=1, device_id=(dp, me + 2), device_id_type=MESH)
+
+    @pl.when((chip > 0) & (chip < chips - 1))
+    def _():
+        pl.semaphore_wait(barrier, 5)
+
+    @pl.when((chip == 0) | (chip == chips - 1))
+    def _():
+        pl.semaphore_wait(barrier, 4)
+
+    def row_copy(origin, u, target, send_sem, recv_sem, first):
+        place = pl.ds(pl.multiple_of(origin * rows + u * part, part), part)
+        return remote(
+            x_ref.at[pl.ds(u * part, part)] if first else f_buf.at[place], f_buf.at[place],
+            send_sem, recv_sem, (dp, target),
+        )
+
+    def step(side, k, u):
+        origin, target = (me - 2 * k, me + 2) if side == 0 else (me + 2 * k, me - 2)
+        return row_copy(origin, u, target, line_send.at[side, k, u], line_recv.at[side, k, u], k == 0)
+
+    def aside(side, k, u):
+        origin = me - 2 * k if side == 0 else me + 2 * k
+        return row_copy(origin, u, sibling, side_send.at[side, k, u], side_recv.at[side, k, u], k == 0)
+
+    def sides(k):
+        return (
+            (0, chip - k >= 0, chip < chips - 1),
+            (1, chip + k <= chips - 1, chip > 0),
+        )
+
+    keep = pltpu.make_async_copy(x_ref, f_buf.at[at(me, rows)], own_sem)
+
+    def rows_out(c):
+        return pltpu.make_async_copy(
+            f_buf.at[at(c, chunk), pl.ds(0, width)], f_out.at[at(c, chunk)], f_sem.at[c]
+        )
+
+    def plane_copy(i):
+        e, flip = (i // 2, i % 2 + 1) if i < 4 else (i - 4, i - 3)
+        if i < 4:
+            src, dst = down_ref.at[e], wd.at[e, at(dp, wide_ff)]
+        else:
+            src = wd.at[e, at(flipped(dp, 3 - flip), wide_ff)]
+            dst = src
+        return remote(src, dst, plane_send.at[i], plane_recv.at[i], neighbour(flip))
+
+    owners = (dp, flipped(dp, 1), flipped(dp, 2), flipped(flipped(dp, 1), 2))
+
+    def weight_copies():
+        copies = []
+        for m, (own, buf) in enumerate(((gate_ref, wg), (up_ref, wu))):
+            for e in range(experts):
+                near = near_refs[4 * m : 4 * m + 4]
+                pieces = [own.at[e], near[0].at[e], near[1].at[e], near[2 + e].at[0]]
+                for q, piece in enumerate(pieces):
+                    copies.append(
+                        pltpu.make_async_copy(
+                            piece, buf.at[at(owners[q], depth), pl.ds(e * ff, ff)],
+                            w_sem.at[m, e, q],
+                        )
+                    )
+        return copies
+
+    def down_copies():
+        return [
+            pltpu.make_async_copy(down_ref.at[e], wd.at[e, at(dp, wide_ff)], d_sem.at[e])
+            for e in range(experts)
+        ]
+
+    def grad_rows(r):
+        return pltpu.make_async_copy(
+            g_ref.at[pl.ds((r % chips) * chunk, chunk)], g_buf.at[r % 2], g_sem.at[r % 2]
+        )
+
+    def first_layer(c):
+        place = at(c, chunk)
+
+        def tile(t, carry):
+            cols = at(t, TILE)
+            gate = dot(f_buf[place, pl.ds(0, width)], wg[:, cols])
+            up = dot(f_buf[place, pl.ds(0, width)], wu[:, cols])
+            sig = 1.0 / (1.0 + jnp.exp(-gate))
+            silu = gate * sig
+            hid[place, cols] = (silu * up).astype(BF16)
+            sg[place, cols] = (up * sig * (1.0 + gate * (1.0 - sig))).astype(BF16)
+            su[place, cols] = silu.astype(BF16)
+            return carry
+
+        lax.fori_loop(0, experts * ff // TILE, tile, 0)
+
+    def ready(k):
+        for u in range(parts):
+            if k == 0:
+                aside(0, 0, u).wait_recv()
+            else:
+                for side, has, _ in sides(k):
+
+                    @pl.when(has)
+                    def _(side=side, u=u):
+                        aside(side, k, u).wait_recv()
+
+        if k == 0:
+            rows_out(chip).start()
+            first_layer(chip)
+        else:
+            for side, has, _ in sides(k):
+                c = chip - k if side == 0 else chip + k
+
+                @pl.when(has)
+                def _(c=c):
+                    rows_out(c).start()
+                    first_layer(c)
+
+    for k in range(chips):
+        for u in range(parts):
+            for side, has, send_on in sides(k):
+
+                @pl.when(has)
+                def _(k=k, u=u, side=side, send_on=send_on):
+                    if k > 0:
+                        step(side, k - 1, u).wait_recv()
+                    if k < chips - 1:
+
+                        @pl.when(send_on)
+                        def _():
+                            step(side, k, u).start()
+
+                    if k > 0:
+                        aside(side, k, u).start()
+
+            if k == 0:
+                aside(0, 0, u).start()
+        if k == 0:
+            for i in range(4):
+                plane_copy(i).start()
+            keep.start()
+            for copy in weight_copies():
+                copy.start()
+            for copy in down_copies():
+                copy.start()
+            grad_rows(0).start()
+            keep.wait()
+            for copy in weight_copies():
+                copy.wait()
+        if k > 0:
+            ready(k - 1)
+    plane_copy(1).wait_recv()
+    plane_copy(4).start()
+    ready(chips - 1)
+    plane_copy(2).wait_recv()
+    plane_copy(5).start()
+
+    for copy in down_copies():
+        copy.wait()
+    for i in (0, 3):
+        plane_copy(i).wait_recv()
+
+    def outs(r):
+        place = pl.ds(r * chunk, chunk)
+        return [
+            pltpu.make_async_copy(buf.at[place], out.at[place], out_sem.at[i, r])
+            for i, (buf, out) in enumerate(((hid, hid_out), (sg, sg_out), (su, su_out)))
+        ]
+
+    lane = lax.broadcasted_iota(jnp.int32, (chunk, LANES), 1)
+
+    def back(r, first, last):
+        place = pl.ds(r * chunk, chunk)
+        extra = f_buf[place, pl.ds(width, LANES)].astype(F32)
+        tail = jnp.zeros((chunk, LANES), F32) if first == 0 else tail_sum[place, :]
+        for e in range(experts):
+            which = me * experts + e
+            low = which + LANES // 2
+            weight = jnp.sum(
+                jnp.where((lane == which) | (lane == low), extra, 0.0), axis=1, keepdims=True
+            )
+            for owner in owners[first:last]:
+                d_hid = dot_nt(g_buf[r % 2], wd[e, at(owner, wide_ff), :])
+                cols = pl.ds(pl.multiple_of(e * ff + owner * wide_ff, wide_ff), wide_ff)
+                hidden = hid[place, cols].astype(F32)
+                d_weight = jnp.sum(hidden * d_hid, axis=1, keepdims=True)
+                tail = tail + jnp.where(lane == which, d_weight, 0.0)
+                d_hid = d_hid * weight
+                hid[place, cols] = (hidden * weight).astype(BF16)
+                sg[place, cols] = (d_hid * sg[place, cols].astype(F32)).astype(BF16)
+                su[place, cols] = (d_hid * su[place, cols].astype(F32)).astype(BF16)
+        if last < len(owners):
+            tail_sum[place, :] = tail
+        else:
+            high = tail.astype(BF16).astype(F32)
+            tail_buf[place, :] = (high + pltpu.roll(tail - high, LANES // 2, 1)).astype(BF16)
+
+    for r in range(chips):
+        grad_rows(r + 1 if r + 1 < chips else chips).start()
+        grad_rows(r).wait()
+        back(r, 0, 3)
+    for i in (4, 5):
+        plane_copy(i).wait_recv()
+    keep_down = pltpu.make_async_copy(wd, down_out, d_sem.at[experts])
+    keep_down.start()
+    for r in range(chips):
+        if r + 1 < chips:
+            grad_rows(chips + r + 1).start()
+        grad_rows(chips + r).wait()
+        back(r, 3, 4)
+        for copy in outs(r):
+            copy.start()
+    keep_tail = pltpu.make_async_copy(tail_buf, tail_out, tail_sem)
+    keep_tail.start()
+    keep_tail.wait()
+    keep_down.wait()
+    for k in range(chips):
+        for u in range(parts):
+            if k == 0:
+                aside(0, 0, u).wait_send()
+            for side, has, send_on in sides(k):
+
+                @pl.when(has)
+                def _(k=k, u=u, side=side, send_on=send_on):
+                    if k < chips - 1:
+
+                        @pl.when(send_on)
+                        def _():
+                            step(side, k, u).wait_send()
+
+                    if k > 0:
+                        aside(side, k, u).wait_send()
+
+    for i in range(6):
+        plane_copy(i).wait_send()
+    for d in range(chips):
+        rows_out(d).wait()
+        for copy in outs(d):
+            copy.wait()
+
+
+def expert_first(x, g_all, w_gate, w_up, w_down, near, collective_id, parts=2):
+    groups, seqs = lax.axis_size("expert"), lax.axis_size("dp")
+    chips = groups // 2
+    rows, wide = x.shape
+    length, width = g_all.shape
+    experts, _, ff = w_gate.shape
+    n = len(near)
+
+    def kernel(*refs):
+        expert_first_body(
+            groups, seqs, rows, width, ff, experts, parts, *refs[:5], refs[5 : 5 + n], *refs[5 + n :]
+        )
+
+    anywhere = pl.BlockSpec(memory_space=pl.ANY)
+    dma = pltpu.SemaphoreType.DMA
+    flat = jax.ShapeDtypeStruct((length, experts * ff), BF16)
+    return pl.pallas_call(
+        kernel,
+        out_shape=[
+            jax.ShapeDtypeStruct((length, width), BF16), flat, flat, flat,
+            jax.ShapeDtypeStruct((length, LANES), BF16),
+            jax.ShapeDtypeStruct((experts, ff, width), BF16),
+        ],
+        in_specs=[anywhere] * (5 + n),
+        out_specs=[anywhere] * 6,
+        scratch_shapes=[
+            pltpu.VMEM((length, wide), BF16),
+            pltpu.VMEM((2, 2 * rows, width), BF16),
+            pltpu.VMEM((width, experts * ff), BF16),
+            pltpu.VMEM((width, experts * ff), BF16),
+            pltpu.VMEM((experts, ff, width), BF16),
+            pltpu.VMEM((length, experts * ff), BF16),
+            pltpu.VMEM((length, experts * ff), BF16),
+            pltpu.VMEM((length, experts * ff), BF16),
+            pltpu.VMEM((length, LANES), BF16),
+            pltpu.VMEM((length, LANES), F32),
+            dma((2, chips, parts)), dma((2, chips, parts)), dma((2, chips, parts)), dma((2, chips, parts)),
+            dma, dma((chips,)), dma((2, experts, 4)), dma((experts + 1,)), dma((2,)), dma((3, chips)), dma,
+            dma((6,)), dma((6,)),
+        ],
+        compiler_params=pltpu.CompilerParams(
+            collective_id=collective_id, has_side_effects=True, vmem_limit_bytes=VMEM_LIMIT
+        ),
+        cost_estimate=cost_of(70),
+        name="expert_first",
+    )(x, g_all, w_gate, w_up, w_down, *near)
+
+
+def expert_second_body(
+    groups, seqs, rows, width, ff, experts, parts,
+    hid_ref, sg_ref, su_ref, tail_ref, down_ref, gate_ref, up_ref, near_refs, y_out, o_ref,
+    wg, wu, wd, hid, sg, su, tail_buf, acc, pair_in, inbox, last, y_buf,
+    in_sem, w_sem, y_sem, pair_send, pair_recv, hop_send, hop_recv, last_recv,
+):
+    chips = groups // 2
+    me, dp = lax.axis_index("expert"), lax.axis_index("dp")
+    chip, core = me // 2, me % 2
+    sibling = chip * 2 + 1 - core
+    chunk = 2 * rows
+    part = rows // parts
+    depth = width // seqs
+
+    def remote(src, dst, send_sem, recv_sem, device):
+        return pltpu.make_async_remote_copy(
+            src_ref=src, dst_ref=dst, send_sem=send_sem, recv_sem=recv_sem,
+            device_id=device, device_id_type=MESH,
+        )
+
+    def at(index, size):
+        return pl.ds(pl.multiple_of(index * size, size), size)
+
+    owners = (dp, flipped(dp, 1), flipped(dp, 2), flipped(flipped(dp, 1), 2))
+    loads = [
+        pltpu.make_async_copy(src, dst, in_sem.at[i])
+        for i, (src, dst) in enumerate(
+            ((sg_ref, sg), (su_ref, su), (tail_ref, tail_buf), (hid_ref, hid), (down_ref, wd))
+        )
+    ]
+    weights = []
+    for m, (own, buf) in enumerate(((gate_ref, wg), (up_ref, wu))):
+        for e in range(experts):
+            near = near_refs[4 * m : 4 * m + 4]
+            pieces = [own.at[e], near[0].at[e], near[1].at[e], near[2 + e].at[0]]
+            for q, piece in enumerate(pieces):
+                weights.append(
+                    pltpu.make_async_copy(
+                        piece, buf.at[at(owners[q], depth), pl.ds(e * ff, ff)], w_sem.at[m, e, q]
+                    )
+                )
+    for copy in loads[:3] + weights + loads[3:]:
+        copy.start()
+    line_greet(me, dp, chip, chips, Plane((), (), (), (), None, None))
+    for copy in loads[:3] + weights:
+        copy.wait()
+    for r in range(chips):
+        for half in range(2):
+            acc[r, half, :, pl.ds(width, LANES)] = tail_buf[pl.ds(r * chunk + half * rows, rows), :]
+
+    out_tile = 256
+
+    def row_grads(d):
+        place = at(d, chunk)
+
+        def tile(t, carry):
+            cols = at(t, out_tile)
+            value = dot_nt(sg[place, :], wg[cols, :]) + dot_nt(su[place, :], wu[cols, :])
+            value = value.astype(BF16)
+            acc[d, 0, :, cols] = value[:rows]
+            acc[d, 1, :, cols] = value[rows:]
+            return carry
+
+        lax.fori_loop(0, width // out_tile, tile, 0)
+
+    def pair_copy(d):
+        return remote(acc.at[d, 1 - core], pair_in.at[d], pair_send.at[d], pair_recv.at[d], (dp, sibling))
+
+    def hop(d, u, kind):
+        place = pl.ds(u * part, part)
+        if kind == 0:
+            return remote(
+                acc.at[d, core, place], inbox.at[d, place], hop_send.at[d, u], hop_recv.at[d, u],
+                (dp, me + 2),
+            )
+        if kind == 1:
+            return remote(
+                acc.at[d, core, place], inbox.at[d, place], hop_send.at[d, u], hop_recv.at[d, u],
+                (dp, me - 2),
+            )
+        return remote(
+            acc.at[d, core, place], last.at[place], hop_send.at[d, u], last_recv.at[u], (dp, me - 2)
+        )
+
+    step_rows = 16
+
+    def add(d, u, more, store):
+        def body(i, carry):
+            here = pl.ds(pl.multiple_of(u * part + i * step_rows, step_rows), step_rows)
+            value = acc[d, core, here].astype(F32) + pair_in[d, here].astype(F32)
+            for ref in more:
+                value = value + ref[here].astype(F32)
+            store(here, value)
+            return carry
+
+        lax.fori_loop(0, part // step_rows, body, 0)
+
+    def forward(d):
+        pair_copy(d).wait_recv()
+
+        def store(here, value):
+            acc[d, core, here] = value.astype(BF16)
+
+        source = ((d > chip) & (chip == 0)) | ((d < chip) & (chip == chips - 1))
+        for u in range(parts):
+
+            @pl.when(source)
+            def _(u=u):
+                add(d, u, (), store)
+
+            @pl.when(jnp.logical_not(source))
+            def _(u=u):
+                hop(d, u, 0).wait_recv()
+                add(d, u, (inbox.at[d],), store)
+
+            @pl.when(d > chip)
+            def _(u=u):
+                hop(d, u, 0).start()
+
+            @pl.when((d < chip) & (d != chip - 1))
+            def _(u=u):
+                hop(d, u, 1).start()
+
+            @pl.when((d < chip) & (d == chip - 1))
+            def _(u=u):
+                hop(d, u, 2).start()
+
+    upper = chip // (chips // 2)
+    mirrored = chip + upper * (chips - 1 - 2 * chip)
+
+    def goal(j):
+        turn = (j + mirrored) // (chips - 1)
+        d = (1 - turn) * (chips - 1 - j) + turn * (j + mirrored - (chips - 1))
+        return d + upper * (chips - 1 - 2 * d)
+
+    edge = (chip == 0) | (chip == chips - 1)
+
+    def mix_copy(r):
+        return pltpu.make_async_copy(y_buf.at[r % 2], y_out.at[pl.ds(r * chunk, chunk)], y_sem.at[r % 2])
+
+    def mix(r):
+        if r >= 2:
+            mix_copy(r - 2).wait()
+
+        def tile(t, carry):
+            cols = at(t, TILE)
+            value = jnp.zeros((chunk, TILE), F32)
+            for e in range(experts):
+                value = value + dot(hid[pl.ds(r * chunk, chunk), pl.ds(e * ff, ff)], wd[e, :, cols])
+            y_buf[r % 2, :, cols] = value.astype(BF16)
+            return carry
+
+        lax.fori_loop(0, width // TILE, tile, 0)
+        mix_copy(r).start()
+
+    for j in range(chips):
+        row_grads(goal(j))
+        pair_copy(goal(j)).start()
+        if j > 0:
+
+            @pl.when(edge)
+            def _(j=j):
+                forward(goal(j - 1))
+
+    for copy in loads[3:]:
+        copy.wait()
+    for j in range(chips):
+        if j < chips - 1:
+
+            @pl.when(jnp.logical_not(edge))
+            def _(j=j):
+                forward(goal(j))
+
+        mix(j)
+
+    pair_copy(chip).wait_recv()
+
+    def finish(here, value):
+        o_ref[here] = value
+
+    for u in range(parts):
+
+        @pl.when(chip == 0)
+        def _(u=u):
+            hop(chip, u, 2).wait_recv()
+            add(chip, u, (last,), finish)
+
+        @pl.when(chip == chips - 1)
+        def _(u=u):
+            hop(chip, u, 0).wait_recv()
+            add(chip, u, (inbox.at[chip],), finish)
+
+        @pl.when((chip > 0) & (chip < chips - 1))
+        def _(u=u):
+            hop(chip, u, 0).wait_recv()
+            hop(chip, u, 2).wait_recv()
+            add(chip, u, (inbox.at[chip], last), finish)
+
+    for d in range(chips):
+        pair_copy(d).wait_send()
+        for u in range(parts):
+
+            @pl.when(d != chip)
+            def _(d=d, u=u):
+                hop(d, u, 0).wait_send()
+
+    for r in range(max(chips - 2, 0), chips):
+        mix_copy(r).wait()
+
+
+def expert_second(hid, sg, su, tail, w_down, w_gate, w_up, near, before, collective_id, parts=2):
+    groups, seqs = lax.axis_size("expert"), lax.axis_size("dp")
+    chips = groups // 2
+    length = hid.shape[0]
+    rows = length // groups
+    experts, ff, width = w_down.shape
+    wide = width + LANES
+    n = len(near)
+
+    def kernel(*refs):
+        expert_second_body(
+            groups, seqs, rows, width, ff, experts, parts, *refs[:7], refs[7 : 7 + n],
+            *refs[8 + n : 10 + n], *refs[11 + n :],
+        )
+
+    anywhere = pl.BlockSpec(memory_space=pl.ANY)
+    dma = pltpu.SemaphoreType.DMA
+    return pl.pallas_call(
+        kernel,
+        out_shape=[
+            jax.ShapeDtypeStruct((length, width), BF16),
+            jax.ShapeDtypeStruct((rows, wide), F32),
+            jax.ShapeDtypeStruct(sg.shape, BF16),
+        ],
+        in_specs=[anywhere] * (8 + n),
+        out_specs=[anywhere, pl.BlockSpec(memory_space=pltpu.VMEM), anywhere],
+        input_output_aliases={1: 2},
+        scratch_shapes=[
+            pltpu.VMEM((width, experts * ff), BF16),
+            pltpu.VMEM((width, experts * ff), BF16),
+            pltpu.VMEM((experts, ff, width), BF16),
+            pltpu.VMEM((length, experts * ff), BF16),
+            pltpu.VMEM((length, experts * ff), BF16),
+            pltpu.VMEM((length, experts * ff), BF16),
+            pltpu.VMEM((length, LANES), BF16),
+            pltpu.VMEM((chips, 2, rows, wide), BF16),
+            pltpu.VMEM((chips, rows, wide), BF16),
+            pltpu.VMEM((chips, rows, wide), BF16),
+            pltpu.VMEM((rows, wide), BF16),
+            pltpu.VMEM((2, 2 * rows, width), BF16),
+            dma((5,)), dma((2, experts, 4)), dma((2,)), dma((chips,)), dma((chips,)),
+            dma((chips, parts)), dma((chips, parts)), dma((parts,)),
+        ],
+        compiler_params=pltpu.CompilerParams(
+            collective_id=collective_id, has_side_effects=True, vmem_limit_bytes=VMEM_LIMIT
+        ),
+        cost_estimate=cost_of(60),
+        name="expert_second",
+    )(hid, sg, su, tail, w_down, w_gate, w_up, *near, before)
+
+
+def spread_body(groups, copies, slab, plane, q_ref, k_ref, v_ref, o_ref, own_sem, send, recv):
+    me, dp = lax.axis_index("expert"), lax.axis_index("dp")
+    block = q_ref.shape[0]
+    barrier = pltpu.get_barrier_semaphore()
+    for s in range(1, groups):
+        pl.semaphore_signal(
+            barrier, inc=1, device_id=(dp, (me + s) % groups), device_id_type=MESH
+        )
+    plane.greet(barrier)
+    pl.semaphore_wait(barrier, groups - 1 + (2 if plane.busy() else 0))
+    half = groups // 2
+    place = pl.ds(pl.multiple_of((me % half) * block, block), block)
+    copies_out = []
+    for s in range(1, groups):
+        peer = (me + s) % groups
+        for m, ref in enumerate((q_ref, k_ref, v_ref)):
+            cols = pl.ds(pl.multiple_of((peer // copies) * slab, slab), slab)
+            copies_out.append(
+                pltpu.make_async_remote_copy(
+                    src_ref=ref.at[:, cols],
+                    dst_ref=o_ref.at[me // half, m, place],
+                    send_sem=send.at[s, m],
+                    recv_sem=recv.at[s, m],
+                    device_id=(dp, peer),
+                    device_id_type=MESH,
+                )
+            )
+    for copy in copies_out:
+        copy.start()
+    plane.start()
+    own = []
+    for m, ref in enumerate((q_ref, k_ref, v_ref)):
+        cols = pl.ds(pl.multiple_of((me // copies) * slab, slab), slab)
+        own.append(
+            pltpu.make_async_copy(ref.at[:, cols], o_ref.at[me // half, m, place], own_sem.at[m])
+        )
+    for copy in own:
+        copy.start()
+    for copy in own + copies_out:
+        copy.wait()
+    plane.finish()
+
+
+def spread_columns(w_query, w_key, w_value, copies, slab, collective_id, sends):
+    groups = lax.axis_size("expert")
+    block = w_query.shape[0]
+    arrays, specs = [], []
+    for array, start, size, flip in sends:
+        arrays.append(array)
+        specs.append((len(arrays) - 1, start, size, flip))
+    targets = [jax.ShapeDtypeStruct((s[2],) + s[0].shape[1:], s[0].dtype) for s in sends]
+    n = len(sends)
+
+    def kernel(q_ref, k_ref, v_ref, *refs):
+        plane = Plane(specs, (), refs[:n], refs[n + 1 : 2 * n + 1], *refs[2 * n + 1 : 2 * n + 3])
+        spread_body(groups, copies, slab, plane, q_ref, k_ref, v_ref, refs[n], *refs[2 * n + 3 :])
+
+    anywhere = pl.BlockSpec(memory_space=pl.ANY)
+    dma = pltpu.SemaphoreType.DMA
+    return pl.pallas_call(
+        kernel,
+        out_shape=[jax.ShapeDtypeStruct((2, 3, groups // 2 * block, slab), BF16)] + targets,
+        in_specs=[anywhere] * (3 + n),
+        out_specs=[anywhere] * (1 + n),
+        scratch_shapes=[dma((max(n, 1),)), dma((max(n, 1),)), dma((3,)), dma((groups, 3)), dma((groups, 3))],
+        compiler_params=pltpu.CompilerParams(collective_id=collective_id, has_side_effects=True),
+        cost_estimate=cost_of(20),
+        name="spread_columns",
+    )(w_query, w_key, w_value, *arrays)
 
 
 def both(array, start=0, size=None):
@@ -621,13 +1287,9 @@
     g_query = lax.dynamic_slice(gains[1], (slab_start,), (slab,))
     g_key = lax.dynamic_slice(gains[2], (slab_start,), (slab,))
 
-    qkv_send = jnp.stack([w_query, w_key, w_value], axis=1).reshape(block, 3, width // slab, slab)
-    qkv_send = qkv_send.transpose(2, 0, 1, 3).reshape(width // slab, block, 3 * slab)
-    qkv_send = jnp.repeat(qkv_send, copies, axis=0)
-    qkv_got, gate0_x, gate0_y = exchange(
-        tie(qkv_send, small_all), 2, sends=both(w_gate, 0, 1)
-    )
-    qkv_got = qkv_got.reshape(groups * block, 3 * slab)
+    near_gate = tie(w_gate, small_all)
+    gate_x, gate_y = swap_dp(near_gate, 1), swap_dp(near_gate, 2)
+    (qkv_got,) = spread_columns(tie(w_query, small_all), w_key, w_value, copies, slab, 2, ())
     total = seqs * groups
     moves = [(b, (b % seqs) * groups + b // seqs) for b in range(total)]
     o_own = lax.ppermute(tie(w_out, small_all), ("dp", "expert"), moves)
@@ -635,21 +1297,24 @@
     x_in = x_low.astype(F32)
     inv_attn = inv_rms(x_in)
     normed_low = (x_in * inv_attn * g_attn).astype(BF16)
-    half_q, half_o = qkv_got.shape[0] // 2, block // 2
+    half_o = block // 2
     normed_all, q_x, q_y, o_x, o_y, q_f0, q_f1, o_f0, o_f1 = line_gather(
         tie(normed_low, qkv_got), 3,
         sends=both(qkv_got) + both(o_own),
-        later=[(1, 0, half_q, 1), (0, half_q, half_q, 2), (3, 0, half_o, 1), (2, half_o, half_o, 2)],
-    )
-    w_qkv = in_order([qkv_got, q_x, q_y, jnp.concatenate([q_f0, q_f1], axis=0)], my_dp, 0)
+        later=[(1, 0, 1, 1), (0, 1, 1, 2), (3, 0, half_o, 1), (2, half_o, half_o, 2)],
+    )
+    qkv_pieces = [qkv_got, q_x, q_y, jnp.concatenate([q_f0, q_f1], axis=0)]
+    w_qkv = jnp.concatenate(
+        [in_order([p[:, m].reshape(-1, slab) for p in qkv_pieces], my_dp, 0) for m in range(3)], axis=1
+    )
     w_o = in_order([o_own, o_x, o_y, jnp.concatenate([o_f0, o_f1], axis=0)], my_dp, 0)
     if copies > 1:
         sets = [[c * copies + i for i in range(copies)] for c in range(groups // copies)]
         w_o = lax.all_gather(w_o, "expert", axis_index_groups=sets, axis=0, tiled=True)
 
-    gate1 = tie(w_gate[1:2], normed_all)
-    gate1_x, gate1_y = swap_dp(gate1, 1), swap_dp(gate1, 2)
-    g_all = lax.all_gather(tie(g_low, normed_all), "expert", axis=0, tiled=True)
+    near_up = tie(w_up, normed_all)
+    up_x, up_y = swap_dp(near_up, 1), swap_dp(near_up, 2)
+    g_all = lax.all_gather(g_low, "expert", axis=0, tiled=True)
 
     raw = dot(normed_all, w_qkv)
     q_raw, k_raw, v_raw = raw[:, :slab], raw[:, slab : 2 * slab], raw[:, 2 * slab :]
@@ -680,18 +1345,14 @@
     for h in range(heads):
         mixes.append(dot(head_probs(queries[h], keys[h]).astype(BF16), values[h]).astype(BF16))
     mix = jnp.concatenate(mixes, axis=1)
-    o_sum, gate0_f, gate1_f, up0_x, up0_y = line_reduce(
+    o_sum, gate0_f, gate1_f, up0_f, up1_f = line_reduce(
         dot(mix, w_o) * share, 5,
-        sends=[(gate0_y, 0, 1, 1), (gate1_x, 0, 1, 2)] + both(w_up, 0, 1),
+        sends=[(gate_y, 0, 1, 1), (gate_x, 1, 1, 2), (up_y, 0, 1, 1), (up_x, 1, 1, 2)],
     )
     after_attn = x_in + o_sum
 
     inv_ffn = inv_rms(after_attn)
     ffn_low = (after_attn * inv_ffn * g_ffn).astype(BF16)
-    ffn_all, up1_x, up1_y, up0_f, up1_f = line_gather(
-        own_order(ffn_low, my_dp, 1), 9,
-        sends=both(w_up, 1, 1) + [(up0_y, 0, 1, 1)], later=[(0, 0, 1, 2)],
-    )
     router_prob = jax.nn.softmax(dot(ffn_low, w_r), axis=-1)
     chosen = routes.reshape(rows, routes.shape[2])
     chosen_mask = jnp.sum(
@@ -699,74 +1360,74 @@
         axis=1,
     )
     route_dense = router_prob * chosen_mask
-    pad = -local_experts % 8
-    route_send = route_dense.T.reshape(groups, local_experts, rows)
-    route_send = jnp.pad(route_send, ((0, 0), (0, pad), (0, 0)))
-    route_mine = exchange(route_send, 6)[:, :local_experts].transpose(0, 2, 1)
-    route_mine = route_mine.reshape(length, local_experts)
-
-    near_down = near_dp(tie(w_down, ffn_all))
-    wd = in_order(far_dp(near_down), my_dp, 1)
-    wg = [
-        jnp.concatenate([own[0], x[0], y[0], f[0]], axis=0)
-        for own, x, y, f in (
-            (w_gate[0:1], gate0_x, gate0_y, gate0_f), (w_gate[1:2], gate1_x, gate1_y, gate1_f)
-        )
-    ]
-    wu = [
-        jnp.concatenate([own[0], x[0], y[0], f[0]], axis=0)
-        for own, x, y, f in ((w_up[0:1], up0_x, up0_y, up0_f), (w_up[1:2], up1_x, up1_y, up1_f))
-    ]
-    cols = jnp.split(ffn_all, 4, axis=1)
-    gates, ups, hidden_ws, d_weights, d_gates, d_ups = [], [], [], [], [], []
-    d_down, d_gate_w, d_up_w = [], [], []
-    for i in range(local_experts):
-        gate, up = dot(ffn_all, wg[i]), dot(ffn_all, wu[i])
-        gates.append(gate)
-        ups.append(up)
-        hidden = gate * jax.nn.sigmoid(gate) * up
-        hidden_ws.append((hidden * route_mine[:, i : i + 1]).astype(BF16))
-        mine = own_order(hidden_ws[i], my_dp, 1)
-        d_down.append([dot_tn(h, g_all).astype(BF16) for h in jnp.split(mine, 4, axis=1)])
-    d_down = [jnp.stack(b) for b in zip(*d_down)]
-    down_x, down_y = send_halves(d_down)
-    for i in range(local_experts):
-        gate, up = gates[i], ups[i]
-        d_hid = dot_nt(g_all, tie(wd, *d_down)[i])
-        sig = jax.nn.sigmoid(gate)
-        silu = gate * sig
-        d_weights.append(jnp.sum(silu * up * d_hid, axis=1))
-        d_hid = d_hid * route_mine[:, i : i + 1]
-        d_gates.append((d_hid * up * sig * (1.0 + gate * (1.0 - sig))).astype(BF16))
-        d_ups.append((d_hid * silu).astype(BF16))
-        d_gate_w.append([dot_tn(f, d_gates[i]).astype(BF16) for f in cols])
-    d_gate_w = [jnp.stack(b) for b in zip(*d_gate_w)]
-    gate_x, gate_y = send_halves(d_gate_w)
-    d_gates = [tie(d, *d_gate_w) for d in d_gates]
-    dx_part = 0.0
-    for i in range(local_experts):
-        dx_part = dx_part + dot_nt(d_gates[i], wg[i]) + dot_nt(d_ups[i], wu[i])
-    dx_part = dx_part.astype(BF16)
-    down_to_x, down_to_y = relay(d_down, down_x, down_y)
-    down_fx, down_fy = swap_dp(down_to_x, 1), swap_dp(down_to_y, 2)
-    gate_to_x, gate_to_y = relay(d_gate_w, gate_x, gate_y)
-    d_rows, gate_fx, gate_fy = line_reduce(
-        tie(dx_part, down_to_x, down_to_y), 10,
-        sends=[(gate_to_x, 0, 2, 1), (gate_to_y, 0, 2, 2)],
-    )
-    d_rows = own_order(d_rows, my_dp, 1)
-    d_ups = [tie(d, d_rows) for d in d_ups]
-    for i in range(local_experts):
-        d_up_w.append([dot_tn(f, d_ups[i]).astype(BF16) for f in cols])
-    d_up_w = [jnp.stack(b) for b in zip(*d_up_w)]
-    y_part = 0.0
-    for i in range(local_experts):
-        y_part = y_part + dot(tie(hidden_ws[i], d_rows), wd[i])
-    y_sum = lax.psum_scatter(y_part.astype(BF16), "expert", scatter_dimension=0, tiled=True)
-    output = after_attn + y_sum.astype(F32)
-    d_weight = jnp.stack(d_weights, axis=0).reshape(local_experts, groups, rows).transpose(1, 0, 2)
-    d_weight = exchange(jnp.pad(d_weight, ((0, 0), (0, pad), (0, 0))), 6)[:, :local_experts]
-    d_router_prob = d_weight.reshape(all_experts, rows).T * chosen_mask
+    gate_near = [gate_x, gate_y, gate0_f, gate1_f]
+    up_near = [up_x, up_y, up0_f, up1_f]
+    ff = w_gate.shape[2]
+    if copies == 1 and length * width <= 1 << 21:
+        high = lax.reduce_precision(route_dense, 8, 7)
+        space = jnp.zeros((rows, LANES // 2 - all_experts), F32)
+        extra = jnp.concatenate([high, space, route_dense - high, space], axis=1).astype(BF16)
+        ffn_all, hidden_w, d_gate, d_up, tail, wd = expert_first(
+            jnp.concatenate([ffn_low, extra], axis=1), g_all, w_gate, w_up, w_down,
+            gate_near + up_near, 9,
+        )
+        d_down = dot_tn(hidden_w, g_all).astype(BF16)
+        y_part, d_rows, d_gate = expert_second(
+            hidden_w, d_gate, d_up, tail, wd, w_gate, w_up, gate_near + up_near, d_down, 13
+        )
+        d_weight = d_rows[:, width : width + LANES]
+        d_weight = d_weight[:, :all_experts] + d_weight[:, LANES // 2 : LANES // 2 + all_experts]
+        d_rows = d_rows[:, :width]
+    else:
+        ffn_all = line_gather(ffn_low, 3)
+        pad = -local_experts % 8
+        route_send = route_dense.T.reshape(groups, local_experts, rows)
+        route_send = jnp.pad(route_send, ((0, 0), (0, pad), (0, 0)))
+        route_mine = exchange(route_send, 6)[:, :local_experts].transpose(0, 2, 1)
+        route_mine = route_mine.reshape(length, local_experts)
+        near_down = near_dp(tie(w_down, ffn_all))
+        wd = in_order(far_dp(near_down), my_dp, 1)
+        hidden_w, d_gate, d_up, d_weights = [], [], [], []
+        y_part, dx_part = 0.0, 0.0
+        for i in range(local_experts):
+            wg, wu = (
+                in_order([own[i], near[0][i], near[1][i], near[2 + i][0]], my_dp, 0)
+                for own, near in ((w_gate, gate_near), (w_up, up_near))
+            )
+            weight = route_mine[:, i : i + 1]
+            gate, up = dot(ffn_all, wg), dot(ffn_all, wu)
+            d_hid = dot_nt(g_all, wd[i])
+            sig = jax.nn.sigmoid(gate)
+            silu = gate * sig
+            d_weights.append(jnp.sum(silu * up * d_hid, axis=1))
+            hidden_w.append((silu * up * weight).astype(BF16))
+            d_hid = d_hid * weight
+            d_gate.append((d_hid * up * sig * (1.0 + gate * (1.0 - sig))).astype(BF16))
+            d_up.append((d_hid * silu).astype(BF16))
+            y_part = y_part + dot(hidden_w[i], wd[i])
+            dx_part = dx_part + dot_nt(d_gate[i], wg) + dot_nt(d_up[i], wu)
+            (ffn_all, y_part, dx_part) = lax.optimization_barrier((ffn_all, y_part, dx_part))
+        hidden_w, d_gate, d_up = (jnp.concatenate(a, axis=1) for a in (hidden_w, d_gate, d_up))
+        y_part = y_part.astype(BF16)
+        d_down = dot_tn(hidden_w, g_all).astype(BF16)
+        d_rows = line_reduce(dx_part, 10)
+        d_weight = jnp.stack(d_weights, axis=0).reshape(local_experts, groups, rows)
+        d_weight = jnp.pad(d_weight.transpose(1, 0, 2), ((0, 0), (0, pad), (0, 0)))
+        d_weight = exchange(d_weight, 6)[:, :local_experts].reshape(all_experts, rows).T
+
+    own_down = lax.psum_scatter(
+        d_down.reshape(local_experts, ff, width), "dp", scatter_dimension=1, tiled=True
+    )
+
+    def in_grad(grad):
+        product = dot_tn(ffn_all, grad).astype(BF16)
+        return product, lax.psum_scatter(product, "dp", scatter_dimension=0, tiled=True)
+
+    def to_experts(own_grad):
+        return jnp.stack([own_grad[:, i * ff : (i + 1) * ff] for i in range(local_experts)]).astype(F32)
+
+    d_gate_w, own_gate = in_grad(d_gate)
+    d_router_prob = d_weight * chosen_mask
 
     d_logits = (
         router_prob * (d_router_prob - jnp.sum(d_router_prob * router_prob, axis=-1, keepdims=True))
@@ -775,12 +1436,7 @@
     d_normed_ffn = d_rows + dot_nt(d_logits, w_r)
     d_after_norm, d_gain_ffn = norm_back(after_attn, inv_ffn, g_ffn, d_normed_ffn)
     d_after = g_low.astype(F32) + d_after_norm
-    d_after_all, up_x, up_y = line_gather(
-        d_after.astype(BF16), 11, sends=halves(d_up_w[3])
-    )
-    up_to_x, up_to_y = relay(d_up_w, up_x, up_y)
-    up_fx, up_fy = swap_dp(up_to_x, 1), swap_dp(up_to_y, 2)
-
+    d_after_all = line_gather(d_after.astype(BF16), 11, after=[own_down, d_gate_w])
     d_out_w = dot_tn(mix, d_after_all)
     d_mix = dot_nt(d_after_all, w_o).astype(BF16)
     dqs, dks, dvs = [], [], []
@@ -799,9 +1455,11 @@
     dots = jnp.stack(
         [jnp.sum(dq_n * g_query * q_raw, axis=1), jnp.sum(dk_n * g_key * k_raw, axis=1)], axis=0
     )
-    dots = exchange(
-        (dots * share).reshape(1, 2 * length // 128, 128), 4, same=True, reduce=True
-    ).reshape(2, length) / width
+    dots, d_up = exchange(
+        (dots * share).reshape(1, 2 * length // 128, 128), 14, same=True, reduce=True, carry=[d_up]
+    )
+    dots = dots.reshape(2, length) / width
+    d_up_w, own_up = in_grad(d_up)
     d_gain_query = jnp.sum(dq_n * q_raw * inv_q, axis=0)
     d_gain_key = jnp.sum(dk_n * k_raw * inv_k, axis=0)
     dq_low = (inv_q * dq_n * g_query - q_raw * (inv_q**3 * dots[0][:, None])).astype(BF16)
@@ -814,7 +1472,8 @@
     d_out_w = lax.dynamic_slice(d_out_w.astype(BF16), (offset, 0), (own, width))
     d_out_w = jnp.split(own_order(d_out_w, my_dp, 0), 4, axis=0)
     d_normed_in, qkv_x, qkv_y, out_x, out_y = line_reduce(
-        dot_nt(d_raw, w_qkv) * share, 12, sends=halves(d_qkv_w[3]) + halves(d_out_w[3])
+        dot_nt(d_raw, w_qkv) * share, 12, sends=halves(d_qkv_w[3]) + halves(d_out_w[3]),
+        after=[own_gate, d_up_w],
     )
     d_in_norm, d_gain_attn = norm_back(x_in, inv_attn, g_attn, d_normed_in)
     input_grad = d_after + d_in_norm
@@ -832,25 +1491,22 @@
     )
     qkv_to_x, qkv_to_y = relay(d_qkv_w, qkv_x, qkv_y)
     out_to_x, out_to_y = relay(d_out_w, out_x, out_y)
-    small_grad, qkv_x, qkv_y, out_x, out_y = exchange(
-        small_grad.reshape(total, small_rows, 128), 8, spread=True, reduce=True,
+    y_sum, qkv_x, qkv_y, out_x, out_y = line_reduce(
+        tie(y_part, d_normed_in), 15,
         sends=[
             (qkv_to_x, 0, qkv_to_x.shape[0], 1), (qkv_to_y, 0, qkv_to_y.shape[0], 2),
             (out_to_x, 0, out_to_x.shape[0], 1), (out_to_y, 0, out_to_y.shape[0], 2),
         ],
     )
+    output = after_attn + y_sum
+    small_grad = exchange(small_grad.reshape(total, small_rows, 128), 8, spread=True, reduce=True)
     small_grad = small_grad.reshape(-1)
     d_qkv_w = settle(d_qkv_w, qkv_x, qkv_y).astype(BF16)
     d_qkv_w = exchange(d_qkv_w.reshape(groups, block, 3 * own), 7).reshape(groups, block, 3, own)
     d_qkv_w = d_qkv_w.transpose(2, 1, 0, 3).reshape(3, block, width).astype(F32)
     d_out_w = settle(d_out_w, out_x, out_y).astype(BF16)
     d_out_w = lax.ppermute(d_out_w, ("dp", "expert"), [(b, a) for a, b in moves]).astype(F32)
-    expert_owned = [
-        settle(d_gate_w, gate_fx, gate_fy),
-        settle(d_up_w, up_fx, up_fy),
-        settle(d_down, down_fx, down_fy),
-    ]
-
+    expert_owned = [to_experts(own_gate), to_experts(own_up), own_down.astype(F32)]
     return (
         output.reshape(1, rows, width),
         input_grad.reshape(1, rows, width),

time: 924 us -> 762 us (0.82)
  matrix products: 218 us -> 78 us
  local copies, waits for them, and re-layouts: 63.6 us -> 48 us
    dot_general x13 -> x7, matrix products: 80 us -> 14.3 us  [dot_nt(): lax.dot_general(left, right, (((1,), (1,)), ((), ())), preferred_element_...]
    dot_general x13 -> x7, matrix products: 62.2 us -> 9.6 us  [dot(): return jnp.dot(left, right, preferred_element_type=F32)]
    concatenate x2 -> x1, other arithmetic: 4.77 us -> 29.1 us  [shards(): jnp.concatenate([in_order([p[:, m].reshape(-1, slab) for p in qkv_pieces]...]
    dot_general x31 -> x10, matrix products: 75.9 us -> 54.1 us  [dot_tn(): lax.dot_general(left, right, (((0,), (0,)), ((), ())), preferred_element_...]
    add x3 -> x0, other arithmetic: 14.7 us -> none  [settle(): return blocks[0].astype(F32) + from_x.astype(F32) + from_y.astype(F32)]
    reduce_scatter x1 -> x3, waiting for transfers between devices: 0.01 us -> 13.9 us  [the longest x1 13.9 us: shards(): lax.psum_scatter(d_down.reshape(local_experts, ff, width), 'dp', scatter_...]
    ppermute x14 -> x4, waiting for transfers between devices: 38.7 us -> 27 us  [swap_dp(): return lax.ppermute(block, 'dp', [(i, i ^ flip) for i in range(seqs)])]
    unnamed x373 -> x173, local copies, waits for them, and re-layouts: 27 us -> 18.5 us
  transfers between devices with their start and end apart: 18 -> 10, of which waited for: 2 -> 3; matrix products, arithmetic and copies ran while one was open for 31% -> 22% of each run, Pallas kernels for 47% -> 52%
where the time goes in v3:
time: 762 us; the launch traced here: 755 us
  Pallas kernels  485 us (64%)
  matrix products  78 us (10%)
  other arithmetic  74.7 us (10%)
  local copies, waits for them, and re-layouts  48 us (6%)
  waiting for transfers between devices  41 us (5%)
  between operations  15.4 us (2%)
  starting transfers between devices  13.3 us (2%)
    pallas_call x10, Pallas kernels, run(): pl.pallas_call(kernel, out_shape=[out] + targets + [jax.ShapeDtypeStruct(...  320 us
    pallas_call x1, Pallas kernels, expert_first(): pl.pallas_call(kernel, out_shape=[jax.ShapeDtypeStruct((length, width), B...  82.2 us
    pallas_call x1, Pallas kernels, expert_second(): pl.pallas_call(kernel, out_shape=[jax.ShapeDtypeStruct((length, width), B...  56.3 us
    dot_general x10, matrix products, dot_tn(): lax.dot_general(left, right, (((0,), (0,)), ((), ())), preferred_element_...  54.1 us
    concatenate x1, other arithmetic, shards(): jnp.concatenate([in_order([p[:, m].reshape(-1, slab) for p in qkv_pieces]...  29.1 us
    ppermute x4, waiting for transfers between devices, swap_dp(): return lax.ppermute(block, 'dp', [(i, i ^ flip) for i in range(seqs)])  27 us
    pallas_call x1, Pallas kernels, spread_columns(): pl.pallas_call(kernel, out_shape=[jax.ShapeDtypeStruct((2, 3, groups // 2...  26.2 us
    unnamed x173, local copies, waits for them, and re-layouts  18.5 us
  transfers between devices with their start and end apart: 10, of which 3 were waited for; matrix products, arithmetic and copies ran while one was open for 22% of the time, Pallas kernels for 52%

profile of v3, /device:TPU:5, one launch (start us, length us, event | category | flops | bytes accessed | tf_op | source)
XLA Modules:
  0.0 755.3 jit_solution(16345878966231152863)
XLA Ops:
  8.1 3.3 concatenate.72
  11.5 11.2 %exchange.5 = bf16[32,16,128]{2,1,0:T(8,128)(2,1)} custom-call(bf16[1,16,128]{2,1,0:T(8,128)(2,1)} %bitcast.231), custom_call_target="tpu_custom_call" | custom-call | bytes 24000000 | tf_op jit(solution)/shard_map/exchange/pallas_call | solution.py:453
  25.7 5.0 collective-permute-start
  32.2 2.0 fusion.12.refs_0_
  34.2 26.2 %spread_columns.1.refs_1_ = bf16[2,3,256,256]{3,2,1,0:T(8,128)(2,1)} custom-call(bf16[64,2048]{1,0:T(8,128)(2,1)} %q_ref, bf16[64,2048]{1,0:T(8,128)(2,1)} %k_ref.1, bf16[64,2048]{1,0:T(8,128)(2,1)} %v_ref.1), custom_call_target="tpu_custom_call" | custom-call | bytes 60000000 | tf_op jit(solution)/shard_map/spread_columns/pallas_call | solution.py:1166
  65.0 68.7 %line_gather.2 = (bf16[1024,2048]{1,0:T(8,128)(2,1)}, bf16[2,3,256,256]{3,2,1,0:T(8,128)(2,1)}, bf16[2,3,256,256]{3,2,1,0:T(8,128)(2,1)}, bf16[64,2048]{1,0:T(8,...) custom-call(bf16[128,2048]{1,0:T(8,128)(2,1)} %fusion.12.refs_0_, ...), custom_call_target="tpu_custom_call" | custom-call | bytes 120000000 | tf_op jit(solution)/shard_map/line_gather/pallas_call | solution.py:453
  139.3 29.1 %maximum_maximum_fusion = bf16[2048,768]{1,0:T(8,128)(2,1)S(1)} fusion(bf16[512,256]{1,0:T(8,128)(2,1)S(1)} %bitcast.215, bf16[512,256]{1,0:T(8,128)(2,1)S(1)} %bitcast.214, bf16[512,256]{1,0:T(8,128)(2,1)S(1)} %bitcast.213, bf16[512,256]{1,0:T(8,128)(2,1)S(1)} %bitcast.212, bf16[512,256]{1,0:T(8,128)(2,1)S(1)} %bitcast.211, ...), kind=kLoop, calls=%fused_computation.19 | loop fusion | flops 37748736 | bytes 6291456 | tf_op jit(solution)/shard_map/concatenate | solution.py:1307
  168.4 3.6 fusion.80
  175.5 7.5 exchange.6
  190.8 3.3 convolution_convert_fusion.3.refs_0_
  194.1 26.4 %collective-permute-done.3.refs_3_.refs_10_.refs_12_ = bf16[2,512,1024]{2,1,0:T(8,128)(2,1)} collective-permute-done((bf16[2,512,1024]{2,1,0:T(8,128)(2,1)}, bf16[2,512,1024]{2,1,0:T(8,128)(2,1)}, u32[]{:S(2)}, u32[]{:S(2)}) %collective-permute-start.3) | collective-permute-done | bytes 2097184 | tf_op jit(solution)/shard_map/ppermute | solution.py:1185
  221.2 48.6 %line_reduce.3 = (f32[128,2048]{1,0:T(8,128)}, bf16[1,512,1024]{2,1,0:T(8,128)(2,1)}, bf16[1,512,1024]{2,1,0:T(8,128)(2,1)}, bf16[1,512,1024]{2,1,0:T(8,128)(2,1)}, bf16[1,512,1024]{2,1,0:T(8,128)(2,1)}) custom-call(bf16[1024,2048]{1,0:T(8,128)(2,1)} %convolution_convert_fusion.3.refs_0_, ...), custom_call_target="tpu_custom_call" | custom-call | bytes 120000000 | tf_op jit(solution)/shard_map/line_reduce/pallas_call | solution.py:453
  269.8 1.5 multiply_reduce_fusion.4
  273.2 82.2 %expert_first.1 = (bf16[1024,2048]{1,0:T(8,128)(2,1)}, bf16[1024,2048]{1,0:T(8,128)(2,1)}, bf16[1024,2048]{1,0:T(8,128)(2,1)}, bf16[1024,2048]{1,0:T(8,128)(2,1)...) custom-call(bf16[128,2176]{1,0:T(8,128)(2,1)} %concatenate.85.refs_0_, bf16[1024,2048]{1,0:T(8,128)(2,1)} %bitcast.197, ...), custom_call_target="tpu_custom_call" | custom-call | bytes 210000000 | tf_op jit(solution)/shard_map/expert_first/pallas_call | solution.py:814
  355.4 13.7 %convolution_convert_fusion.2.refs_15_ = bf16[2048,2048]{1,0:T(8,128)(2,1)} fusion(bf16[1024,2048]{1,0:T(8,128)(2,1)} %get-tuple-element.74.refs_0_, bf16[1,1024,2048]{2,1,0:T(8,128)(2,1)S(1)} %copy-done.25), kind=kOutput, calls=%fused_computation.2 | convolution fusion | flops 8594128896 | bytes 16777216 | tf_op jit(solution)/shard_map/dot_general | solution.py:27
  369.2 56.3 %expert_second.1 = (bf16[1024,2048]{1,0:T(8,128)(2,1)}, f32[128,2176]{1,0:T(8,128)}, bf16[1024,2048]{1,0:T(8,128)(2,1)}) custom-call(bf16[1024,2048]{1,0:T(8,128)(2,1)} %get-tuple-element.74.refs_0_, bf16[1024,2048]{1,0:T(8,128)(2,1)} %get-tuple-element.75.refs_1_, ...), custom_call_target="tpu_custom_call", output_to_operand_aliasing={{2}: (1, {})} | custom-call | bytes 180000000 | tf_op jit(solution)/shard_map/expert_second/pallas_call | solution.py:1073
  425.5 13.4 %convolution_convert_fusion.1.refs_2_ = bf16[2048,2048]{1,0:T(8,128)(2,1)} fusion(bf16[1024,2048]{1,0:T(8,128)(2,1)S(1)} %copy-done.76, bf16[1024,2048]{1,0:T(8,128)(2,1)} %get-tuple-element.82), kind=kOutput, calls=%fused_computation.1 | convolution fusion | flops 8594128896 | bytes 16777216 | tf_op jit(solution)/shard_map/dot_general | solution.py:27
  440.1 1.9 multiply_reduce_fusion.2
  442.0 2.8 fusion.73
  444.8 13.9 %reduce-scatter.4.cloned.1.call-done.refs_1_ = bf16[2,256,2048]{2,1,0:T(8,128)(2,1)} async-done(((bf16[2,1024,2048]{2,1,0:T(8,128)(2,1)}), bf16[2,256,2048]{2,1,0:T(8,128)(2,1)}) %reduce-scatter.4.cloned.1.call-update) | async-done | bytes 2097168 | tf_op jit(solution)/shard_map/reduce_scatter | solution.py:1418
  458.7 40.5 %line_gather.3 = bf16[1024,2048]{1,0:T(8,128)(2,1)} custom-call(bf16[128,2048]{1,0:T(8,128)(2,1)} %get-tuple-element.180.refs_0_, bf16[2,256,2048]{2,1,0:T(8,128)(2,1)} %reduce-scatter.4.cloned.1.call-done.refs_1_, bf16[2048,2048]{1,0:T(8,128)(2,1)} %convolution_convert_fusion.1.refs_2_), custom_call_target="tpu_custom_call" | custom-call | bytes 120000000 | tf_op jit(solution)/shard_map/line_gather/pallas_call | solution.py:453
  499.3 3.9 convolution_convert_fusion.7
  514.2 7.0 exchange.7
  521.3 13.6 %convolution_convert_fusion.refs_4_ = bf16[2048,2048]{1,0:T(8,128)(2,1)} fusion(bf16[1024,2048]{1,0:T(8,128)(2,1)S(1)} %copy-done.77, bf16[1024,2048]{1,0:T(8,128)(2,1)} %get-tuple-element.84), kind=kOutput, calls=%fused_computation | convolution fusion | flops 8594128896 | bytes 16777216 | tf_op jit(solution)/shard_map/dot_general | solution.py:27
  534.9 2.5 fusion.79
  537.4 1.8 reshape.330
  539.9 3.7 convolution_convert_fusion.6
  548.3 1.4 copy-done.5
  551.9 3.8 convolution_convert_fusion.5
  555.7 1.7 copy-done.11
  558.5 1.6 copy-done.28
  560.1 5.2 convolution_convert_fusion.4.refs_0_
  565.3 42.7 %line_reduce.4 = (f32[128,2048]{1,0:T(8,128)}, bf16[256,768]{1,0:T(8,128)(2,1)}, bf16[256,768]{1,0:T(8,128)(2,1)}, bf16[32,2048]{1,0:T(8,128)(2,1)}, bf16[32,2048]{1,0:T(8,128)(2,1)}) custom-call(bf16[1024,2048]{1,0:T(8,128)(2,1)} %convolution_convert_fusion.4.refs_0_, bf16[512,768]{1,0:T(8,128)(2,1)} %get-tuple-element.186.refs_1_, ...), custom_call_target="tpu_custom_call" | custom-call | bytes 120000000 | tf_op jit(solution)/shard_map/line_reduce/pallas_call | solution.py:453
  613.7 55.5 %line_reduce.5 = (f32[128,2048]{1,0:T(8,128)}, bf16[512,768]{1,0:T(8,128)(2,1)}, bf16[512,768]{1,0:T(8,128)(2,1)}, bf16[64,2048]{1,0:T(8,128)(2,1)}, bf16[64,2048]{1,0:T(8,128)(2,1)}) custom-call(bf16[1024,2048]{1,0:T(8,128)(2,1)} %get-tuple-element.86.refs_0_, bf16[512,768]{1,0:T(8,128)(2,1)} %pad_maximum_fusion.4.refs_1_, ...), custom_call_target="tpu_custom_call" | custom-call | bytes 120000000 | tf_op jit(solution)/shard_map/line_reduce/pallas_call | solution.py:453
  670.5 4.6 collective-permute-start.5
  675.2 2.9 add_convert_fusion
  678.1 21.3 %exchange.8 = bf16[8,64,768]{2,1,0:T(8,128)(2,1)} custom-call(bf16[8,64,768]{2,1,0:T(8,128)(2,1)} %bitcast.198), custom_call_target="tpu_custom_call" | custom-call | bytes 24000000 | tf_op jit(solution)/shard_map/exchange/pallas_call | solution.py:453
  699.5 3.6 reshape.341
  703.4 1.7 slice_bitcast_fusion.3
  705.2 2.4 maximum_convert_fusion
  707.6 2.4 fusion.74
  714.3 17.1 %exchange.9 = f32[16,128]{1,0:T(8,128)} custom-call(f32[32,16,128]{2,1,0:T(8,128)} %bitcast.203), custom_call_target="tpu_custom_call" | custom-call | bytes 24000000 | tf_op jit(solution)/shard_map/exchange/pallas_call | solution.py:453
  732.8 1.3 copy.64
  738.7 2.5 convert_element_type.275
  741.3 1.4 fusion.77
  742.7 1.8 convert_element_type.272
  744.5 1.7 slice_bitcast_fusion.1
  746.2 2.3 maximum_convert_fusion.1
  (291 shorter events, 67.2 us)
Async XLA Ops:
  7.2 54.9 %copy-start.71 = (s32[1,128,8]{1,2,0:T(8,128)S(1)}, s32[1,128,8]{1,2,0:T(8,128)}, u32[]{:S(2)}) copy-start(s32[1,128,8]{1,2,0:T(8,128)} %param.16) | copy-start | bytes 12292
  7.2 266.0 %all-gather.3.cloned.1.call-start = ((), (), s32[]{:S(2)}) async-start(), calls=%async_computation.6 | async-start | bytes 4718592 | tf_op jit(solution)/shard_map/all_gather | solution.py:1317
  23.6 170.6 %collective-permute-start.1 = (bf16[2,512,1024]{2,1,0:T(8,128)(2,1)}, bf16[2,512,1024]{2,1,0:T(8,128)(2,1)}, u32[]{:S(2)}, u32[]{:S(2)}) collective-permute-start(bf16[2,512,1024]{2,1,0:T(8,128)(2,1)} %refs_5_.1), channel_id=1, source_target_pairs={{0,16},{8,24},{16,0},{24,8},{1,17},{9,25},{17,1},{25,9},{2,18},{10... | collective-permute-start | bytes 6291464 | tf_op jit(solution)/shard_map/ppermute | solution.py:1185
  24.7 169.5 %collective-permute-start.2 = (bf16[2,512,1024]{2,1,0:T(8,128)(2,1)}, bf16[2,512,1024]{2,1,0:T(8,128)(2,1)}, u32[]{:S(2)}, u32[]{:S(2)}) collective-permute-start(bf16[2,512,1024]{2,1,0:T(8,128)(2,1)} %refs_5_.1), channel_id=1, source_target_pairs={{0,8},{8,0},{16,24},{24,16},{1,9},{9,1},{17,25},{25,17},{2,10},{10... | collective-permute-start | bytes 6291464 | tf_op jit(solution)/shard_map/ppermute | solution.py:1185
  25.7 38.6 %collective-permute-start = (bf16[64,2048]{1,0:T(8,128)(2,1)}, bf16[64,2048]{1,0:T(8,128)(2,1)S(1)}, u32[]{:S(2)}, u32[]{:S(2)}) collective-permute-start(bf16[64,2048]{1,0:T(8,128)(2,1)} %param.21), channel_id=1, source_target_pairs={{0,0},{1,8},{2,16},{3,24},{4,1},{5,9},{6,17},{7,25},{8,2},{9,10},{... | collective-permute-start | bytes 786440 | tf_op jit(solution)/shard_map/ppermute | solution.py:1295
  30.7 428.0 %reduce-scatter.4.cloned.1.call-start = ((), (), s32[]{:S(2)}) async-start(), calls=%async_computation.3 | async-start | bytes 10485760 | tf_op jit(solution)/shard_map/reduce_scatter | solution.py:1418
  32.2 102.5 %copy-start.72 = (f32[128]{0:T(128)}, f32[128]{0:T(128)S(1)}, u32[]{:S(2)}) copy-start(f32[128]{0:T(128)S(1)} %fusion.10) | copy-start | bytes 1540
  32.2 29.9 %copy-start.66 = (f32[128]{0:T(128)}, f32[128]{0:T(128)S(1)}, u32[]{:S(2)}) copy-start(f32[128]{0:T(128)S(1)} %add_rsqrt_fusion.2) | copy-start | bytes 1540
  60.5 75.3 %copy-start.15 = (bf16[2,3,256,256]{3,2,1,0:T(8,128)(2,1)S(1)}, bf16[2,3,256,256]{3,2,1,0:T(8,128)(2,1)}, u32[]{:S(2)}) copy-start(bf16[2,3,256,256]{3,2,1,0:T(8,128)(2,1)} %spread_columns.1.refs_1_) | copy-start | bytes 2359300
  60.7 123.1 %copy-start.61 = (f32[256]{0:T(256)}, f32[256]{0:T(256)S(1)}, u32[]{:S(2)}) copy-start(f32[256]{0:T(256)S(1)} %dynamic_slice.8) | copy-start | bytes 3076
  60.8 123.0 %copy-start.63 = (f32[256]{0:T(256)}, f32[256]{0:T(256)S(1)}, u32[]{:S(2)}) copy-start(f32[256]{0:T(256)S(1)} %dynamic_slice.9) | copy-start | bytes 3076
  138.0 30.4 %copy-start.74 = (bf16[1024,2048]{1,0:T(8,128)(2,1)S(1)}, bf16[1024,2048]{1,0:T(8,128)(2,1)}, u32[]{:S(2)}) copy-start(bf16[1024,2048]{1,0:T(8,128)(2,1)} %get-tuple-element.58) | copy-start | bytes 12582916
  168.4 15.3 %copy-start.56 = (bf16[32,2048]{1,0:T(8,128)(2,1)S(1)}, bf16[32,2048]{1,0:T(8,128)(2,1)}, u32[]{:S(2)}) copy-start(bf16[32,2048]{1,0:T(8,128)(2,1)} %get-tuple-element.63) | copy-start | bytes 393220
  168.4 15.4 %copy-start.55 = (bf16[32,2048]{1,0:T(8,128)(2,1)S(1)}, bf16[32,2048]{1,0:T(8,128)(2,1)}, u32[]{:S(2)}) copy-start(bf16[32,2048]{1,0:T(8,128)(2,1)} %get-tuple-element.64) | copy-start | bytes 393220
  172.1 12.3 %copy-start = (f32[1024,768]{0,1:T(8,128)}, f32[1024,768]{0,1:T(8,128)S(1)}, u32[]{:S(2)}) copy-start(f32[1024,768]{0,1:T(8,128)S(1)} %fusion.80) | copy-start | bytes 9437188
  173.4 47.1 %collective-permute-start.3 = (bf16[2,512,1024]{2,1,0:T(8,128)(2,1)}, bf16[2,512,1024]{2,1,0:T(8,128)(2,1)}, u32[]{:S(2)}, u32[]{:S(2)}) collective-permute-start(bf16[2,512,1024]{2,1,0:T(8,128)(2,1)} %refs_6_.1), channel_id=1, source_target_pairs={{0,16},{8,24},{16,0},{24,8},{1,17},{9,25},{17,1},{25,9},{2,18},{10... | collective-permute-start | bytes 6291464 | tf_op jit(solution)/shard_map/ppermute | solution.py:1185
  174.4 46.8 %collective-permute-start.4 = (bf16[2,512,1024]{2,1,0:T(8,128)(2,1)}, bf16[2,512,1024]{2,1,0:T(8,128)(2,1)}, u32[]{:S(2)}, u32[]{:S(2)}) collective-permute-start(bf16[2,512,1024]{2,1,0:T(8,128)(2,1)} %refs_6_.1), channel_id=1, source_target_pairs={{0,8},{8,0},{16,24},{24,16},{1,9},{9,1},{17,25},{25,17},{2,10},{10... | collective-permute-start | bytes 6291464 | tf_op jit(solution)/shard_map/ppermute | solution.py:1185
  194.1 75.6 %copy-start.9 = (bf16[1,128,2048]{2,1,0:T(8,128)(2,1)S(1)}, bf16[1,128,2048]{2,1,0:T(8,128)(2,1)}, u32[]{:S(2)}) copy-start(bf16[1,128,2048]{2,1,0:T(8,128)(2,1)} %param.15) | copy-start | bytes 1572868
  271.5 83.9 %copy-start.13 = (bf16[128,2048]{1,0:T(8,128)(2,1)}, bf16[128,2048]{1,0:T(8,128)(2,1)S(1)}, u32[]{:S(2)}) copy-start(bf16[128,2048]{1,0:T(8,128)(2,1)S(1)} %multiply_convert_fusion.2) | copy-start | bytes 1572868
  273.2 82.2 %copy-start.25 = (bf16[1,1024,2048]{2,1,0:T(8,128)(2,1)S(1)}, bf16[1,1024,2048]{2,1,0:T(8,128)(2,1)}, u32[]{:S(2)}) copy-start(bf16[1,1024,2048]{2,1,0:T(8,128)(2,1)} %all-gather.3.cloned.1.call-done) | copy-start | bytes 12582916
  369.1 196.2 %reduce-scatter.6.cloned.1.call-start = ((), (), s32[]{:S(2)}) async-start(), calls=%async_computation.4 | async-start | bytes 10485760 | tf_op jit(solution)/shard_map/reduce_scatter | solution.py:1424
  369.1 56.4 %copy-start.76 = (bf16[1024,2048]{1,0:T(8,128)(2,1)S(1)}, bf16[1024,2048]{1,0:T(8,128)(2,1)}, u32[]{:S(2)}) copy-start(bf16[1024,2048]{1,0:T(8,128)(2,1)} %get-tuple-element.81) | copy-start | bytes 12582916
  438.9 305.5 %reduce-scatter.8.cloned.1.call-start = ((), (), s32[]{:S(2)}) async-start(), calls=%async_computation.5 | async-start | bytes 10485760 | tf_op jit(solution)/shard_map/reduce_scatter | solution.py:1424
  458.7 40.5 %copy-start.42 = (bf16[64,2048]{1,0:T(8,128)(2,1)S(1)}, bf16[64,2048]{1,0:T(8,128)(2,1)}, u32[]{:S(2)}) copy-start(bf16[64,2048]{1,0:T(8,128)(2,1)} %copy-done.41) | copy-start | bytes 786436
  458.7 40.5 %copy-start.44 = (bf16[64,2048]{1,0:T(8,128)(2,1)S(1)}, bf16[64,2048]{1,0:T(8,128)(2,1)}, u32[]{:S(2)}) copy-start(bf16[64,2048]{1,0:T(8,128)(2,1)} %copy-done.43) | copy-start | bytes 786436
  458.7 40.6 %copy-start.46 = (bf16[64,2048]{1,0:T(8,128)(2,1)S(1)}, bf16[64,2048]{1,0:T(8,128)(2,1)}, u32[]{:S(2)}) copy-start(bf16[64,2048]{1,0:T(8,128)(2,1)} %copy-done.45) | copy-start | bytes 786436
  458.7 40.6 %copy-start.48 = (bf16[64,2048]{1,0:T(8,128)(2,1)S(1)}, bf16[64,2048]{1,0:T(8,128)(2,1)}, u32[]{:S(2)}) copy-start(bf16[64,2048]{1,0:T(8,128)(2,1)} %copy-done.47) | copy-start | bytes 786436
  499.3 3.9 copy-start.4
  514.2 7.0 copy-start.77
  539.9 6.9 copy-start.65
  539.9 6.9 copy-start.2
  608.0 4.2 copy-start.34
  608.0 4.2 copy-start.54
  608.0 4.2 copy-start.40
  608.0 4.9 copy-start.32
  608.0 4.9 copy-start.53
  608.0 5.0 copy-start.39
  612.2 57.0 %copy-start.23 = (bf16[256,2048]{1,0:T(8,128)(2,1)S(1)}, bf16[256,2048]{1,0:T(8,128)(2,1)}, u32[]{:S(2)}) copy-start(bf16[256,2048]{1,0:T(8,128)(2,1)} %copy-done.22) | copy-start | bytes 3145732
  613.7 61.4 %copy-start.12 = (bf16[2048,768]{1,0:T(8,128)(2,1)S(1)}, bf16[2048,768]{1,0:T(8,128)(2,1)}, u32[]{:S(2)}) copy-start(bf16[2048,768]{1,0:T(8,128)(2,1)} %copy-done.11) | copy-start | bytes 9437188
  670.5 72.2 %collective-permute-start.5 = (bf16[64,2048]{1,0:T(8,128)(2,1)S(1)}, bf16[64,2048]{1,0:T(8,128)(2,1)}, u32[]{:S(2)}, u32[]{:S(2)}) collective-permute-start(bf16[64,2048]{1,0:T(8,128)(2,1)S(1)} %add_convert_fusion.3), channel_id=1, source_target_pairs={{0,0},{8,1},{16,2},{24,3},{1,4},{9,5},{17,6},{25,7},{2,8},{10,9},{... | collective-permute-start | bytes 786440 | tf_op jit(solution)/shard_map/ppermute | solution.py:1508
  675.1 27.9 %copy-start.69 = (f32[256]{0:T(256)S(1)}, f32[256]{0:T(256)}, u32[]{:S(2)}) copy-start(f32[256]{0:T(256)} %get-tuple-element.166) | copy-start | bytes 3076
  675.1 27.9 %copy-start.70 = (f32[256]{0:T(256)S(1)}, f32[256]{0:T(256)}, u32[]{:S(2)}) copy-start(f32[256]{0:T(256)} %get-tuple-element.173) | copy-start | bytes 3076
  675.2 27.9 %copy-start.10 = (bf16[1,128,2048]{2,1,0:T(8,128)(2,1)S(1)}, bf16[1,128,2048]{2,1,0:T(8,128)(2,1)}, u32[]{:S(2)}) copy-start(bf16[1,128,2048]{2,1,0:T(8,128)(2,1)} %param.15) | copy-start | bytes 1572868
  675.2 27.9 %copy-start.24 = (f32[128,2048]{1,0:T(8,128)S(1)}, f32[128,2048]{1,0:T(8,128)}, u32[]{:S(2)}) copy-start(f32[128,2048]{1,0:T(8,128)} %get-tuple-element.85) | copy-start | bytes 3145732
  675.2 27.9 %copy-start.52 = (f32[2048]{0:T(1024)S(1)}, f32[2048]{0:T(1024)}, u32[]{:S(2)}) copy-start(f32[2048]{0:T(1024)} %copy-done.51) | copy-start | bytes 24580
  675.2 27.9 %copy-start.67 = (f32[128]{0:T(128)S(1)}, f32[128]{0:T(128)}, u32[]{:S(2)}) copy-start(f32[128]{0:T(128)} %copy-done.66) | copy-start | bytes 1540
  705.1 4.8 copy-start.30
  712.4 26.4 %copy-start.14 = (bf16[2,256,2048]{2,1,0:T(8,128)(2,1)S(1)}, bf16[2,256,2048]{2,1,0:T(8,128)(2,1)}, u32[]{:S(2)}) copy-start(bf16[2,256,2048]{2,1,0:T(8,128)(2,1)} %reduce-scatter.4.cloned.1.call-done.refs_1_) | copy-start | bytes 6291460
  (44 other events, 92.1 us)
Sparse Core Ops, SparseCore 0:
  30.8 57.2 all-gather.2
  369.2 89.4 reduce-scatter.3
  462.1 86.4 reduce-scatter.5
  551.5 118.8 reduce-scatter.7

commit v4 on v3

--- a/solution.py
+++ b/solution.py
@@ -81,14 +81,61 @@
     return dp + flip - 2 * flip * ((dp // flip) % 2)
 
 
+class Whole:
+    def __init__(self, source, target, own_sem, send, recv):
+        self.me, self.dp = lax.axis_index("expert"), lax.axis_index("dp")
+        self.source, self.target = source, target
+        self.own_sem, self.send, self.recv = own_sem, send, recv
+        self.rows = source.shape[0]
+        half = self.rows // 2
+        self.split = (half, half) if half % 16 == 0 else (self.rows, 0)
+
+    def place(self, owner, start, size):
+        return self.target.at[pl.ds(pl.multiple_of(owner * self.rows, self.rows) + start, size)]
+
+    def keep(self):
+        return pltpu.make_async_copy(self.source, self.place(self.dp, 0, self.rows), self.own_sem)
+
+    def copy(self, i):
+        flip = i % 2 + 1
+        if i < 2:
+            src, dst = self.source, self.place(self.dp, 0, self.rows)
+        else:
+            start = 0 if i == 2 else self.split[0]
+            src = dst = self.place(flipped(self.dp, 3 - flip), start, self.split[i - 2])
+        return pltpu.make_async_remote_copy(
+            src_ref=src, dst_ref=dst, send_sem=self.send.at[i], recv_sem=self.recv.at[i],
+            device_id=(flipped(self.dp, flip), self.me), device_id_type=MESH,
+        )
+
+    def start(self):
+        self.copy(0).start()
+        self.copy(1).start()
+        self.keep().start()
+
+    def start_later(self):
+        self.copy(1).wait_recv()
+        self.copy(2).start()
+        self.copy(0).wait_recv()
+        if self.split[1]:
+            self.copy(3).start()
+
+    def finish(self):
+        self.keep().wait()
+        for i in range(4 if self.split[1] else 3):
+            self.copy(i).wait_send()
+            if i >= 2:
+                self.copy(i).wait_recv()
+
+
 class Plane:
-    def __init__(self, sends, later, sources, targets, send, recv):
+    def __init__(self, sends, later, sources, targets, send, recv, wholes=()):
         self.me, self.dp = lax.axis_index("expert"), lax.axis_index("dp")
-        self.sends, self.later = sends, later
+        self.sends, self.later, self.wholes = sends, later, wholes
         self.sources, self.targets, self.send, self.recv = sources, targets, send, recv
 
     def busy(self):
-        return len(self.sends) > 0
+        return len(self.sends) + len(self.wholes) > 0
 
     def greet(self, barrier):
         if self.busy():
@@ -115,6 +162,8 @@
         )
 
     def start(self):
+        for whole in self.wholes:
+            whole.start()
         for i in range(len(self.sends)):
             self.copy(i).start()
 
@@ -124,8 +173,12 @@
             self.copy(source).wait_recv()
         for i in range(len(self.later)):
             self.copy(first + i).start()
+        for whole in self.wholes:
+            whole.start_later()
 
     def finish(self):
+        for whole in self.wholes:
+            whole.finish()
         waited = {l[0] for l in self.later}
         for i in range(len(self.sends) + len(self.later)):
             self.copy(i).wait_send()
@@ -157,13 +210,17 @@
         pl.semaphore_wait(barrier, 2 + extra)
 
 
-def gather_body(groups, rows, parts, plane, x_ref, o_ref, own_sem, send, recv, pair_send, pair_recv):
+def gather_body(
+    groups, rows, parts, plane, x_ref, o_ref, own_sem, send, recv, pair_send, pair_recv,
+    greet=True, work=None,
+):
     chips = groups // 2
     me, dp = lax.axis_index("expert"), lax.axis_index("dp")
     chip = me // 2
     sibling = chip * 2 + 1 - me % 2
     part = rows // parts
-    line_greet(me, dp, chip, chips, plane)
+    if greet:
+        line_greet(me, dp, chip, chips, plane)
     keep = pltpu.make_async_copy(x_ref, o_ref.at[pl.ds(pl.multiple_of(me * rows, rows), rows)], own_sem)
 
     def copy(origin, u, target, send_sem, recv_sem, first):
@@ -192,6 +249,8 @@
         (1, chip + k <= chips - 1, chip > 0),
     )
     for k in range(chips):
+        if k == 1 and not greet:
+            plane.start_mid()
         if k == chips - 1:
             plane.start_later()
         for u in range(parts):
@@ -216,6 +275,8 @@
         if k == 0:
             plane.start()
             keep.start()
+        if work is not None:
+            work(k)
 
     keep.wait()
     for k in range(chips):
@@ -371,6 +432,402 @@
     plane.finish()
 
 
+def joint_body(
+    groups, rows, parts, plane, p_refs, o_refs, own, pair, inbox, load_sem, pair_send, pair_recv, send, recv
+):
+    kinds = range(len(p_refs))
+    chips = groups // 2
+    me, dp = lax.axis_index("expert"), lax.axis_index("dp")
+    chip, core = me // 2, me % 2
+    sibling = chip * 2 + 1 - core
+    part = rows // parts
+    step_rows = 16
+    line_greet(me, dp, chip, chips, plane)
+
+    def pair_copy(a, d):
+        place = pl.ds(pl.multiple_of((2 * d + 1 - core) * rows, rows), rows)
+        return pltpu.make_async_remote_copy(
+            src_ref=p_refs[a].at[place],
+            dst_ref=pair.at[a, d],
+            send_sem=pair_send.at[a, d],
+            recv_sem=pair_recv.at[a, d],
+            device_id=(dp, sibling),
+            device_id_type=MESH,
+        )
+
+    def own_copy(a, d):
+        place = pl.ds(pl.multiple_of((2 * d + core) * rows, rows), rows)
+        return pltpu.make_async_copy(p_refs[a].at[place], own.at[a, d], load_sem.at[a, d])
+
+    order = []
+    for j in range((chips + 1) // 2):
+        order += [chips - 1 - j] + ([j] if j != chips - 1 - j else [])
+    for a in kinds:
+        for d in order:
+            pair_copy(a, d).start()
+            own_copy(a, d).start()
+    plane.start()
+
+    def hop(a, d, u, side):
+        place = pl.ds(u * part, part)
+        target = me + 2 if side == 0 else me - 2
+        slot = d if side == 0 else chips + d
+        return pltpu.make_async_remote_copy(
+            src_ref=own.at[a, d, place],
+            dst_ref=inbox.at[a, slot, place],
+            send_sem=send.at[a, d, u],
+            recv_sem=recv.at[a, slot, u],
+            device_id=(dp, target),
+            device_id_type=MESH,
+        )
+
+    def add(a, d, u, slots, store):
+        def body(i, carry):
+            at = pl.ds(pl.multiple_of(u * part + i * step_rows, step_rows), step_rows)
+            value = own[a, d, at].astype(F32) + pair[a, d, at].astype(F32)
+            for slot in slots:
+                value = value + inbox[a, slot, at].astype(F32)
+            store(at, value)
+            return carry
+
+        lax.fori_loop(0, part // step_rows, body, 0)
+
+    def forward(a, d, side):
+        pair_copy(a, d).wait_recv()
+        own_copy(a, d).wait()
+
+        def store(at, value):
+            own[a, d, at] = value.astype(BF16)
+
+        end = chip == (0 if side == 0 else chips - 1)
+        for u in range(parts):
+
+            @pl.when(end)
+            def _(u=u):
+                add(a, d, u, (), store)
+
+            @pl.when(jnp.logical_not(end))
+            def _(u=u):
+                hop(a, d, u, side).wait_recv()
+                add(a, d, u, (d if side == 0 else chips + d,), store)
+
+            hop(a, d, u, side).start()
+
+    def finish(a):
+        pair_copy(a, chip).wait_recv()
+        own_copy(a, chip).wait()
+
+        def store(at, value):
+            o_refs[a][at] = value
+
+        for u in range(parts):
+
+            @pl.when(chip == 0)
+            def _(u=u):
+                hop(a, chip, u, 1).wait_recv()
+                add(a, chip, u, (chips + chip,), store)
+
+            @pl.when(chip == chips - 1)
+            def _(u=u):
+                hop(a, chip, u, 0).wait_recv()
+                add(a, chip, u, (chip,), store)
+
+            @pl.when((chip > 0) & (chip < chips - 1))
+            def _(u=u):
+                hop(a, chip, u, 0).wait_recv()
+                hop(a, chip, u, 1).wait_recv()
+                add(a, chip, u, (chip, chips + chip), store)
+
+    for a in kinds:
+        for j in range(chips - 1):
+            far, near = chips - 1 - j, j
+
+            @pl.when(far > chip)
+            def _(a=a, far=far):
+                forward(a, far, 0)
+
+            @pl.when(near < chip)
+            def _(a=a, near=near):
+                forward(a, near, 1)
+
+            if a == 0 and j == (chips - 1) // 2:
+                plane.start_later()
+
+        finish(a)
+
+    for a in kinds:
+        for d in range(chips):
+            pair_copy(a, d).wait_send()
+            for u in range(parts):
+
+                @pl.when(d > chip)
+                def _(a=a, d=d, u=u):
+                    hop(a, d, u, 0).wait_send()
+
+                @pl.when(d < chip)
+                def _(a=a, d=d, u=u):
+                    hop(a, d, u, 1).wait_send()
+
+    plane.finish()
+
+
+class PlaneSum:
+    def __init__(self, parts):
+        self.me, self.dp = lax.axis_index("expert"), lax.axis_index("dp")
+        self.parts = parts
+        self.owners = (
+            self.dp, flipped(self.dp, 1), flipped(self.dp, 2), flipped(flipped(self.dp, 1), 2)
+        )
+
+    def busy(self):
+        return True
+
+    greet = Plane.greet
+
+    def remote(self, src, dst, send, recv, flip):
+        return pltpu.make_async_remote_copy(
+            src_ref=src, dst_ref=dst, send_sem=send, recv_sem=recv,
+            device_id=(flipped(self.dp, flip), self.me), device_id_type=MESH,
+        )
+
+    def sizes(self, p):
+        rows = p["out"].shape[0]
+        half = rows // 2
+        return rows, ((half, half) if half % 16 == 0 else (rows, 0))
+
+    def rows_of(self, p, q, start, size):
+        rows, _ = self.sizes(p)
+        return pl.ds(pl.multiple_of(self.owners[q] * rows, rows) + start, size)
+
+    def load(self, p):
+        return pltpu.make_async_copy(p["ref"], p["buf"], p["load"])
+
+    def early(self, p, i):
+        _, split = self.sizes(p)
+        start = 0 if i == 0 else split[0]
+        return self.remote(
+            p["ref"].at[self.rows_of(p, 3, start, split[i])], p["first"].at[pl.ds(start, split[i])],
+            p["send"].at[i], p["recv"].at[i], i + 1,
+        )
+
+    def late(self, p, i):
+        rows, _ = self.sizes(p)
+        return self.remote(
+            p["buf"].at[self.rows_of(p, i + 1, 0, rows)], p["second"].at[i],
+            p["send"].at[2 + i], p["recv"].at[2 + i], i + 1,
+        )
+
+    def counts(self, p):
+        return 2 if self.sizes(p)[1][1] else 1
+
+    def start(self):
+        for p in self.parts:
+            for i in range(self.counts(p)):
+                self.early(p, i).start()
+            self.load(p).start()
+
+    def start_later(self):
+        for p in self.parts:
+            rows, split = self.sizes(p)
+            self.load(p).wait()
+            for i in range(self.counts(p)):
+                self.early(p, i).wait_recv()
+                start = 0 if i == 0 else split[0]
+                step = 16
+                base = pl.multiple_of(self.owners[2 - i] * rows, rows) + start
+
+                def body(t, carry, p=p, start=start, base=base, step=step):
+                    here = pl.ds(pl.multiple_of(base + t * step, step), step)
+                    there = pl.ds(pl.multiple_of(start + t * step, step), step)
+                    value = p["buf"][here].astype(F32) + p["first"][there].astype(F32)
+                    p["buf"][here] = value.astype(BF16)
+                    return carry
+
+                lax.fori_loop(0, split[i] // step, body, 0)
+            for i in range(2):
+                self.late(p, i).start()
+
+    def finish(self):
+        for p in self.parts:
+            rows, _ = self.sizes(p)
+            for i in range(2):
+                self.late(p, i).wait()
+            for i in range(self.counts(p)):
+                self.early(p, i).wait_send()
+            step = 16
+            base = pl.multiple_of(self.dp * rows, rows)
+
+            def body(t, carry, p=p, base=base, step=step):
+                here = pl.ds(pl.multiple_of(base + t * step, step), step)
+                there = pl.ds(pl.multiple_of(t * step, step), step)
+                value = p["buf"][here].astype(F32) + p["second"][0, there].astype(F32)
+                value = value + p["second"][1, there].astype(F32)
+                p["out"][there] = value.astype(BF16)
+                return carry
+
+            lax.fori_loop(0, rows // step, body, 0)
+
+
+def joint_reduce(partials, sums, after, collective_id, parts=4):
+    groups, seqs = lax.axis_size("expert"), lax.axis_size("dp")
+    chips = groups // 2
+    rows, width = partials[0].shape[0] // groups, partials[0].shape[1]
+    n, m, extra = len(partials), len(sums), len(after)
+
+    def kernel(*refs):
+        p_refs, s_refs = refs[:n], refs[n : n + m]
+        refs = refs[n + m + extra :]
+        o_refs, outs, rest = refs[:n], refs[n : n + m], refs[n + m :]
+        names = ("buf", "first", "second", "load", "send", "recv")
+        made = [
+            dict(zip(names, rest[len(names) * i : len(names) * (i + 1)]), ref=s_refs[i], out=outs[i])
+            for i in range(m)
+        ]
+        joint_body(groups, rows, parts, PlaneSum(made), p_refs, o_refs, *rest[len(names) * m :])
+
+    anywhere, vmem = pl.BlockSpec(memory_space=pl.ANY), pl.BlockSpec(memory_space=pltpu.VMEM)
+    dma = pltpu.SemaphoreType.DMA
+    scratch = []
+    for s in sums:
+        own_rows = s.shape[0] // seqs
+        scratch += [
+            pltpu.VMEM(s.shape, BF16), pltpu.VMEM((own_rows,) + s.shape[1:], BF16),
+            pltpu.VMEM((2, own_rows) + s.shape[1:], BF16), dma, dma((4,)), dma((4,)),
+        ]
+    return pl.pallas_call(
+        kernel,
+        out_shape=[jax.ShapeDtypeStruct((rows, width), F32)] * n
+        + [jax.ShapeDtypeStruct((s.shape[0] // seqs,) + s.shape[1:], BF16) for s in sums],
+        in_specs=[anywhere] * (n + m + extra),
+        out_specs=[vmem] * (n + m),
+        scratch_shapes=scratch + [
+            pltpu.VMEM((n, chips, rows, width), BF16),
+            pltpu.VMEM((n, chips, rows, width), BF16),
+            pltpu.VMEM((n, 2 * chips, rows, width), BF16),
+            dma((n, chips)), dma((n, chips)), dma((n, chips)),
+            dma((n, chips, parts)), dma((n, 2 * chips, parts)),
+        ],
+        compiler_params=pltpu.CompilerParams(
+            collective_id=collective_id, has_side_effects=True, vmem_limit_bytes=VMEM_LIMIT
+        ),
+        cost_estimate=cost_of(70),
+        name="joint_reduce",
+    )(*partials, *sums, *after)
+
+
+def last_body(
+    groups, seqs, small_ref, qkv_ref, out_ref, small_to, q_to, k_to, v_to, o_to,
+    box, qkv_box, out_box, send, recv, qkv_send, qkv_recv, out_sem,
+):
+    me, dp = lax.axis_index("expert"), lax.axis_index("dp")
+    total = groups * seqs
+    mine = dp * groups + me
+    block, width = o_to.shape
+    own = width // groups
+    barrier = pltpu.get_barrier_semaphore()
+
+    def device(index):
+        return (index // groups, index % groups)
+
+    def hello(s, carry):
+        pl.semaphore_signal(
+            barrier, inc=1, device_id=device((mine + s) % total), device_id_type=MESH
+        )
+        return carry
+
+    lax.fori_loop(1, total, hello, 0)
+    pl.semaphore_wait(barrier, total - 1)
+
+    def qkv_copy(s):
+        peer = (me + s) % groups
+        return pltpu.make_async_remote_copy(
+            src_ref=qkv_ref.at[pl.ds(pl.multiple_of(peer * block, block), block)],
+            dst_ref=qkv_box.at[me],
+            send_sem=qkv_send.at[s], recv_sem=qkv_recv.at[s],
+            device_id=(dp, peer), device_id_type=MESH,
+        )
+
+    def small_copy(s):
+        target = (mine + s) % total
+        return pltpu.make_async_remote_copy(
+            src_ref=small_ref.at[target], dst_ref=box.at[mine],
+            send_sem=send.at[s], recv_sem=recv.at[s],
+            device_id=device(target), device_id_type=MESH,
+        )
+
+    owner = me * seqs + dp
+    out_copy = pltpu.make_async_remote_copy(
+        src_ref=out_ref, dst_ref=out_box, send_sem=out_sem.at[0], recv_sem=out_sem.at[1],
+        device_id=device(owner), device_id_type=MESH,
+    )
+
+    def start(s, carry):
+        small_copy(s).start()
+        return carry
+
+    def wait(s, carry):
+        small_copy(s).wait()
+        return carry
+
+    lax.fori_loop(1, total, start, 0)
+    for s in range(1, groups):
+        qkv_copy(s).start()
+
+    @pl.when(owner != mine)
+    def _():
+        out_copy.start()
+
+    box[mine] = small_ref[mine]
+    qkv_box[me] = qkv_ref[pl.ds(pl.multiple_of(me * block, block), block)]
+    lax.fori_loop(1, total, wait, 0)
+
+    def add(s, value):
+        return value + box[s]
+
+    small_to[...] = lax.fori_loop(1, total, add, box[0])
+
+    @pl.when(owner != mine)
+    def _():
+        out_copy.wait()
+        o_to[...] = out_box[...].astype(F32)
+
+    @pl.when(owner == mine)
+    def _():
+        o_to[...] = out_ref[...].astype(F32)
+
+    for s in range(1, groups):
+        qkv_copy(s).wait()
+    for e in range(groups):
+        for m, to in enumerate((q_to, k_to, v_to)):
+            to[:, e * own : (e + 1) * own] = qkv_box[e, :, m * own : (m + 1) * own].astype(F32)
+
+
+def last_exchange(small, qkv, out, collective_id):
+    groups, seqs = lax.axis_size("expert"), lax.axis_size("dp")
+    total = groups * seqs
+    block, width = out.shape
+    vmem = pl.BlockSpec(memory_space=pltpu.VMEM)
+    dma = pltpu.SemaphoreType.DMA
+    matrix = jax.ShapeDtypeStruct((block, width), F32)
+    return pl.pallas_call(
+        functools.partial(last_body, groups, seqs),
+        out_shape=[jax.ShapeDtypeStruct(small.shape[1:], F32)] + [matrix] * 4,
+        in_specs=[vmem] * 3,
+        out_specs=[vmem] * 5,
+        scratch_shapes=[
+            pltpu.VMEM(small.shape, F32),
+            pltpu.VMEM((groups, block, qkv.shape[1]), BF16),
+            pltpu.VMEM((block, width), BF16),
+            dma((total,)), dma((total,)), dma((groups,)), dma((groups,)), dma((2,)),
+        ],
+        compiler_params=pltpu.CompilerParams(
+            collective_id=collective_id, has_side_effects=True, vmem_limit_bytes=VMEM_LIMIT
+        ),
+        cost_estimate=cost_of(25),
+        name="last_exchange",
+    )(small, qkv, out)
+
+
 def exchange_body(count, spread, same, reduce, plane, x_ref, o_ref, box, send, recv):
     me, dp = lax.axis_index("expert"), lax.axis_index("dp")
     groups = lax.axis_size("expert")
@@ -427,7 +884,8 @@
 
 
 def run(
-    body, name, micros, collective_id, x, x_space, out, out_space, scratch, sends, later, carry=(), after=()
+    body, name, micros, collective_id, x, x_space, out, out_space, scratch, sends, later,
+    carry=(), after=(), wholes=(),
 ):
     arrays, specs = [], []
     for array, start, size, flip in sends:
@@ -439,45 +897,56 @@
     targets = [jax.ShapeDtypeStruct((s[2],) + s[0].shape[1:], s[0].dtype) for s in sends]
     for source, start, size, flip in later:
         targets.append(jax.ShapeDtypeStruct((size,) + targets[source].shape[1:], targets[source].dtype))
-    n_in, n_out, held = len(arrays), len(targets), len(carry)
+    seqs = lax.axis_size("dp")
+    whole_out = [jax.ShapeDtypeStruct((seqs * w.shape[0],) + w.shape[1:], w.dtype) for w in wholes]
+    n_in, n_out, held, n_whole = len(arrays), len(targets), len(carry), len(wholes)
 
     def kernel(*refs):
-        x_ref, sources = refs[0], refs[1 : 1 + n_in]
-        refs = refs[1 + n_in + held + len(after) :]
-        o_ref, dests = refs[0], refs[1 : 1 + n_out]
-        rest = refs[1 + n_out + held :]
-        plane = Plane(specs, later, sources, dests, *rest[:2])
-        body(plane, x_ref, o_ref, *rest[2:])
+        x_ref, sources, whole_in = refs[0], refs[1 : 1 + n_in], refs[1 + n_in : 1 + n_in + n_whole]
+        refs = refs[1 + n_in + n_whole + held + len(after) :]
+        o_ref, dests, whole_to = refs[0], refs[1 : 1 + n_out], refs[1 + n_out : 1 + n_out + n_whole]
+        rest = refs[1 + n_out + n_whole + held :]
+        made = [
+            Whole(a, b, rest[2].at[i], rest[3].at[i], rest[4].at[i])
+            for i, (a, b) in enumerate(zip(whole_in, whole_to))
+        ]
+        plane = Plane(specs, later, sources, dests, *rest[:2], made)
+        body(plane, x_ref, o_ref, *rest[5 if n_whole else 2 :])
 
     anywhere = pl.BlockSpec(memory_space=pl.ANY)
+    dma = pltpu.SemaphoreType.DMA
+    first, second = 1 + n_in + n_whole, 1 + n_out + n_whole
     got = pl.pallas_call(
         kernel,
-        out_shape=[out] + targets + [jax.ShapeDtypeStruct(c.shape, c.dtype) for c in carry],
-        in_specs=[pl.BlockSpec(memory_space=x_space)] + [anywhere] * (n_in + held + len(after)),
-        out_specs=[pl.BlockSpec(memory_space=out_space)] + [anywhere] * (n_out + held),
-        input_output_aliases={1 + n_in + i: 1 + n_out + i for i in range(held)},
-        scratch_shapes=[pltpu.SemaphoreType.DMA((max(n_out, 1),))] * 2 + scratch,
+        out_shape=[out] + targets + whole_out + [jax.ShapeDtypeStruct(c.shape, c.dtype) for c in carry],
+        in_specs=[pl.BlockSpec(memory_space=x_space)] + [anywhere] * (n_in + n_whole + held + len(after)),
+        out_specs=[pl.BlockSpec(memory_space=out_space)] + [anywhere] * (n_out + n_whole + held),
+        input_output_aliases={first + i: second + i for i in range(held)},
+        scratch_shapes=[dma((max(n_out, 1),))] * 2
+        + ([dma((n_whole,)), dma((n_whole, 4)), dma((n_whole, 4))] if n_whole else [])
+        + scratch,
         compiler_params=pltpu.CompilerParams(
             collective_id=collective_id, has_side_effects=True, vmem_limit_bytes=VMEM_LIMIT
         ),
         cost_estimate=cost_of(micros),
         name=name,
-    )(x, *arrays, *carry, *after)
-    return got if n_out + held else got[0]
-
-
-def line_gather(x, collective_id, sends=(), later=(), after=(), parts=2):
+    )(x, *arrays, *wholes, *carry, *after)
+    return got if n_out + n_whole + held else got[0]
+
+
+def line_gather(x, collective_id, sends=(), later=(), carry=(), after=(), wholes=(), parts=4):
     rows, width = x.shape
     groups = lax.axis_size("expert")
     shape = (2, groups // 2, parts)
     return run(
         functools.partial(gather_body, groups, rows, parts), "line_gather", 40, collective_id,
         x, pl.ANY, jax.ShapeDtypeStruct((groups * rows, width), x.dtype), pl.ANY,
-        [pltpu.SemaphoreType.DMA] + [pltpu.SemaphoreType.DMA(shape)] * 4, sends, later, (), after,
-    )
-
-
-def line_reduce(partial, collective_id, sends=(), later=(), after=(), parts=2):
+        [pltpu.SemaphoreType.DMA] + [pltpu.SemaphoreType.DMA(shape)] * 4,
+        sends, later, carry, after, wholes,
+    )
+
+
+def line_reduce(partial, collective_id, sends=(), later=(), after=(), parts=4):
     groups = lax.axis_size("expert")
     chips = groups // 2
     rows, width = partial.shape[0] // groups, partial.shape[1]
@@ -522,10 +991,10 @@
 def expert_first_body(
     groups, seqs, rows, width, ff, experts, parts,
     x_ref, g_ref, gate_ref, up_ref, down_ref, near_refs,
-    f_out, hid_out, sg_out, su_out, tail_out, down_out,
-    f_buf, g_buf, wg, wu, wd, hid, sg, su, tail_buf, tail_sum,
+    f_out, hid_out, sg_out, su_out, tail_out, down_out, grad_out,
+    f_buf, g_buf, wg, wu, wd, hid, sg, su, tail_buf, tail_sum, stage,
     line_send, line_recv, side_send, side_recv, own_sem, f_sem, w_sem, d_sem, g_sem, out_sem, tail_sem,
-    plane_send, plane_recv,
+    plane_send, plane_recv, stage_sem,
 ):
     chips = groups // 2
     me, dp = lax.axis_index("expert"), lax.axis_index("dp")
@@ -611,8 +1080,8 @@
         copies = []
         for m, (own, buf) in enumerate(((gate_ref, wg), (up_ref, wu))):
             for e in range(experts):
-                near = near_refs[4 * m : 4 * m + 4]
-                pieces = [own.at[e], near[0].at[e], near[1].at[e], near[2 + e].at[0]]
+                near = [near_refs[6 * m + 2 * q + e] for q in range(3)]
+                pieces = [own.at[e]] + [ref.at[index] for ref, index in near]
                 for q, piece in enumerate(pieces):
                     copies.append(
                         pltpu.make_async_copy(
@@ -628,10 +1097,12 @@
             for e in range(experts)
         ]
 
-    def grad_rows(r):
-        return pltpu.make_async_copy(
-            g_ref.at[pl.ds((r % chips) * chunk, chunk)], g_buf.at[r % 2], g_sem.at[r % 2]
-        )
+    grad_rows = [
+        pltpu.make_async_copy(
+            g_ref.at[pl.ds(r * chunk, chunk)], g_buf.at[pl.ds(r * chunk, chunk)], g_sem.at[r]
+        )
+        for r in range(chips)
+    ]
 
     def first_layer(c):
         place = at(c, chunk)
@@ -699,7 +1170,8 @@
                 copy.start()
             for copy in down_copies():
                 copy.start()
-            grad_rows(0).start()
+            for copy in grad_rows:
+                copy.start()
             keep.wait()
             for copy in weight_copies():
                 copy.wait()
@@ -707,9 +1179,9 @@
             ready(k - 1)
     plane_copy(1).wait_recv()
     plane_copy(4).start()
-    ready(chips - 1)
     plane_copy(2).wait_recv()
     plane_copy(5).start()
+    ready(chips - 1)
 
     for copy in down_copies():
         copy.wait()
@@ -736,7 +1208,7 @@
                 jnp.where((lane == which) | (lane == low), extra, 0.0), axis=1, keepdims=True
             )
             for owner in owners[first:last]:
-                d_hid = dot_nt(g_buf[r % 2], wd[e, at(owner, wide_ff), :])
+                d_hid = dot_nt(g_buf[place, :], wd[e, at(owner, wide_ff), :])
                 cols = pl.ds(pl.multiple_of(e * ff + owner * wide_ff, wide_ff), wide_ff)
                 hidden = hid[place, cols].astype(F32)
                 d_weight = jnp.sum(hidden * d_hid, axis=1, keepdims=True)
@@ -751,21 +1223,41 @@
             high = tail.astype(BF16).astype(F32)
             tail_buf[place, :] = (high + pltpu.roll(tail - high, LANES // 2, 1)).astype(BF16)
 
+    tiles = [(e, q) for q in range(len(owners)) for e in range(experts)]
+
+    def grad_place(t):
+        e, q = tiles[t]
+        return pl.ds(pl.multiple_of(e * ff + owners[q] * wide_ff, wide_ff), wide_ff)
+
+    def grad_copy(t):
+        return pltpu.make_async_copy(stage.at[t % 2], grad_out.at[grad_place(t)], stage_sem.at[t % 2])
+
+    def grad_tile(t):
+        if t >= 2:
+            grad_copy(t - 2).wait()
+        for n in range(width // (2 * TILE)):
+            cols = pl.ds(n * 2 * TILE, 2 * TILE)
+            stage[t % 2, :, cols] = dot_tn(hid[:, grad_place(t)], g_buf[:, cols]).astype(BF16)
+        grad_copy(t).start()
+
+    for copy in grad_rows:
+        copy.wait()
     for r in range(chips):
-        grad_rows(r + 1 if r + 1 < chips else chips).start()
-        grad_rows(r).wait()
         back(r, 0, 3)
+    for t in range(3 * experts):
+        grad_tile(t)
     for i in (4, 5):
         plane_copy(i).wait_recv()
     keep_down = pltpu.make_async_copy(wd, down_out, d_sem.at[experts])
     keep_down.start()
     for r in range(chips):
-        if r + 1 < chips:
-            grad_rows(chips + r + 1).start()
-        grad_rows(chips + r).wait()
         back(r, 3, 4)
         for copy in outs(r):
             copy.start()
+    for t in range(3 * experts, 4 * experts):
+        grad_tile(t)
+    for t in range(4 * experts - 2, 4 * experts):
+        grad_copy(t).wait()
     keep_tail = pltpu.make_async_copy(tail_buf, tail_out, tail_sem)
     keep_tail.start()
     keep_tail.wait()
@@ -795,17 +1287,20 @@
             copy.wait()
 
 
-def expert_first(x, g_all, w_gate, w_up, w_down, near, collective_id, parts=2):
+def expert_first(x, g_all, w_gate, w_up, w_down, near, collective_id, parts=4):
     groups, seqs = lax.axis_size("expert"), lax.axis_size("dp")
     chips = groups // 2
     rows, wide = x.shape
     length, width = g_all.shape
     experts, _, ff = w_gate.shape
+    where = [index for _, index in near]
+    near = [array for array, _ in near]
     n = len(near)
 
     def kernel(*refs):
         expert_first_body(
-            groups, seqs, rows, width, ff, experts, parts, *refs[:5], refs[5 : 5 + n], *refs[5 + n :]
+            groups, seqs, rows, width, ff, experts, parts, *refs[:5],
+            list(zip(refs[5 : 5 + n], where)), *refs[5 + n :],
         )
 
     anywhere = pl.BlockSpec(memory_space=pl.ANY)
@@ -817,12 +1312,13 @@
             jax.ShapeDtypeStruct((length, width), BF16), flat, flat, flat,
             jax.ShapeDtypeStruct((length, LANES), BF16),
             jax.ShapeDtypeStruct((experts, ff, width), BF16),
+            jax.ShapeDtypeStruct((experts * ff, width), BF16),
         ],
         in_specs=[anywhere] * (5 + n),
-        out_specs=[anywhere] * 6,
+        out_specs=[anywhere] * 7,
         scratch_shapes=[
             pltpu.VMEM((length, wide), BF16),
-            pltpu.VMEM((2, 2 * rows, width), BF16),
+            pltpu.VMEM((length, width), BF16),
             pltpu.VMEM((width, experts * ff), BF16),
             pltpu.VMEM((width, experts * ff), BF16),
             pltpu.VMEM((experts, ff, width), BF16),
@@ -831,9 +1327,10 @@
             pltpu.VMEM((length, experts * ff), BF16),
             pltpu.VMEM((length, LANES), BF16),
             pltpu.VMEM((length, LANES), F32),
+            pltpu.VMEM((2, ff // seqs, width), BF16),
             dma((2, chips, parts)), dma((2, chips, parts)), dma((2, chips, parts)), dma((2, chips, parts)),
-            dma, dma((chips,)), dma((2, experts, 4)), dma((experts + 1,)), dma((2,)), dma((3, chips)), dma,
-            dma((6,)), dma((6,)),
+            dma, dma((chips,)), dma((2, experts, 4)), dma((experts + 1,)), dma((chips,)), dma((3, chips)), dma,
+            dma((6,)), dma((6,)), dma((2,)),
         ],
         compiler_params=pltpu.CompilerParams(
             collective_id=collective_id, has_side_effects=True, vmem_limit_bytes=VMEM_LIMIT
@@ -843,11 +1340,101 @@
     )(x, g_all, w_gate, w_up, w_down, *near)
 
 
+class ExpertSum:
+    def __init__(self, size, ref, out, first, mid, own, near, load, send, recv):
+        self.me, self.dp = lax.axis_index("expert"), lax.axis_index("dp")
+        self.size, self.ref, self.out = size, ref, out
+        self.first, self.mid, self.own, self.near = first, mid, own, near
+        self.load_sem, self.send, self.recv = load, send, recv
+        x, y = flipped(self.dp, 1), flipped(self.dp, 2)
+        self.owners = (self.dp, x, y, flipped(x, 2))
+        self.stride = ref.shape[0] // 2
+
+    def busy(self):
+        return True
+
+    greet = Plane.greet
+
+    def piece(self, e, q):
+        return self.ref.at[
+            pl.ds(pl.multiple_of(e * self.stride + self.owners[q] * self.size, self.size), self.size)
+        ]
+
+    def copy(self, i):
+        src, dst, flip = (
+            (self.piece(0, 3), self.first.at[0], 1),
+            (self.piece(1, 3), self.first.at[1], 2),
+            (self.piece(0, 1), self.near.at[0, 0], 1),
+            (self.piece(1, 2), self.near.at[1, 1], 2),
+            (self.mid.at[1], self.near.at[0, 1], 1),
+            (self.mid.at[0], self.near.at[1, 0], 2),
+        )[i]
+        return pltpu.make_async_remote_copy(
+            src_ref=src, dst_ref=dst, send_sem=self.send.at[i], recv_sem=self.recv.at[i],
+            device_id=(flipped(self.dp, flip), self.me), device_id_type=MESH,
+        )
+
+    def loads(self):
+        return [
+            pltpu.make_async_copy(src, dst, self.load_sem.at[i])
+            for i, (src, dst) in enumerate(
+                (
+                    (self.piece(0, 2), self.mid.at[0]), (self.piece(1, 1), self.mid.at[1]),
+                    (self.piece(0, 0), self.own.at[0]), (self.piece(1, 0), self.own.at[1]),
+                )
+            )
+        ]
+
+    def start(self):
+        for i in range(4):
+            self.copy(i).start()
+        for copy in self.loads():
+            copy.start()
+
+    def relay(self):
+        for copy in self.loads():
+            copy.wait()
+        for i in range(2):
+            self.copy(i).wait_recv()
+
+            def body(t, carry, i=i):
+                here = pl.ds(pl.multiple_of(t * 16, 16), 16)
+                value = self.mid[i, here].astype(F32) + self.first[i, here].astype(F32)
+                self.mid[i, here] = value.astype(BF16)
+                return carry
+
+            lax.fori_loop(0, self.size // 16, body, 0)
+        for i in (4, 5):
+            self.copy(i).start()
+
+    def finish(self):
+        for i in range(2, 6):
+            self.copy(i).wait_recv()
+        for e in range(2):
+
+            def body(t, carry, e=e):
+                here = pl.ds(pl.multiple_of(t * 16, 16), 16)
+                value = self.own[e, here].astype(F32)
+                for side in range(2):
+                    value = value + self.near[side, e, here].astype(F32)
+                self.own[e, here] = value.astype(BF16)
+                return carry
+
+            lax.fori_loop(0, self.size // 16, body, 0)
+        keep = pltpu.make_async_copy(self.own, self.out, self.load_sem.at[0])
+        keep.start()
+        for i in range(6):
+            self.copy(i).wait_send()
+        keep.wait()
+
+
 def expert_second_body(
     groups, seqs, rows, width, ff, experts, parts,
-    hid_ref, sg_ref, su_ref, tail_ref, down_ref, gate_ref, up_ref, near_refs, y_out, o_ref,
-    wg, wu, wd, hid, sg, su, tail_buf, acc, pair_in, inbox, last, y_buf,
-    in_sem, w_sem, y_sem, pair_send, pair_recv, hop_send, hop_recv, last_recv,
+    sg_ref, su_ref, tail_ref, f_ref, gate_ref, up_ref, down_ref, near_refs, grad_out, down_out, o_ref,
+    wg, wu, sg, su, tail_buf, f_buf, stage, acc, pair_in, inbox, last,
+    first, mid, own_block, near_buf,
+    in_sem, w_sem, stage_sem, pair_send, pair_recv, hop_send, hop_recv, last_recv,
+    sum_load, sum_send, sum_recv,
 ):
     chips = groups // 2
     me, dp = lax.axis_index("expert"), lax.axis_index("dp")
@@ -870,14 +1457,14 @@
     loads = [
         pltpu.make_async_copy(src, dst, in_sem.at[i])
         for i, (src, dst) in enumerate(
-            ((sg_ref, sg), (su_ref, su), (tail_ref, tail_buf), (hid_ref, hid), (down_ref, wd))
+            ((sg_ref, sg), (su_ref, su), (tail_ref, tail_buf), (f_ref, f_buf))
         )
     ]
     weights = []
     for m, (own, buf) in enumerate(((gate_ref, wg), (up_ref, wu))):
         for e in range(experts):
-            near = near_refs[4 * m : 4 * m + 4]
-            pieces = [own.at[e], near[0].at[e], near[1].at[e], near[2 + e].at[0]]
+            near = [near_refs[6 * m + 2 * q + e] for q in range(3)]
+            pieces = [own.at[e]] + [ref.at[index] for ref, index in near]
             for q, piece in enumerate(pieces):
                 weights.append(
                     pltpu.make_async_copy(
@@ -886,8 +1473,12 @@
                 )
     for copy in loads[:3] + weights + loads[3:]:
         copy.start()
-    line_greet(me, dp, chip, chips, Plane((), (), (), (), None, None))
-    for copy in loads[:3] + weights:
+    total = ExpertSum(
+        ff // seqs, down_ref, down_out, first, mid, own_block, near_buf, sum_load, sum_send, sum_recv
+    )
+    line_greet(me, dp, chip, chips, total)
+    total.start()
+    for copy in loads[:3]:
         copy.wait()
     for r in range(chips):
         for half in range(2):
@@ -895,8 +1486,9 @@
 
     out_tile = 256
 
-    def row_grads(d):
+    def row_grads(d, first=False):
         place = at(d, chunk)
+        per = depth // out_tile
 
         def tile(t, carry):
             cols = at(t, out_tile)
@@ -906,7 +1498,13 @@
             acc[d, 1, :, cols] = value[rows:]
             return carry
 
-        lax.fori_loop(0, width // out_tile, tile, 0)
+        if not first:
+            lax.fori_loop(0, width // out_tile, tile, 0)
+            return
+        for q, owner in enumerate(owners):
+            for copy in weights[q :: len(owners)]:
+                copy.wait()
+            lax.fori_loop(owner * per, owner * per + per, tile, 0)
 
     def pair_copy(d):
         return remote(acc.at[d, 1 - core], pair_in.at[d], pair_send.at[d], pair_recv.at[d], (dp, sibling))
@@ -980,26 +1578,24 @@
 
     edge = (chip == 0) | (chip == chips - 1)
 
-    def mix_copy(r):
-        return pltpu.make_async_copy(y_buf.at[r % 2], y_out.at[pl.ds(r * chunk, chunk)], y_sem.at[r % 2])
-
-    def mix(r):
-        if r >= 2:
-            mix_copy(r - 2).wait()
-
-        def tile(t, carry):
-            cols = at(t, TILE)
-            value = jnp.zeros((chunk, TILE), F32)
-            for e in range(experts):
-                value = value + dot(hid[pl.ds(r * chunk, chunk), pl.ds(e * ff, ff)], wd[e, :, cols])
-            y_buf[r % 2, :, cols] = value.astype(BF16)
-            return carry
-
-        lax.fori_loop(0, width // TILE, tile, 0)
-        mix_copy(r).start()
-
+    def grad_copy(t):
+        return pltpu.make_async_copy(
+            stage.at[t % 2], grad_out.at[pl.ds(t * out_tile, out_tile)], stage_sem.at[t % 2]
+        )
+
+    def grad_tile(t):
+        if t >= 2:
+            grad_copy(t - 2).wait()
+        for n in range(experts * ff // (2 * TILE)):
+            cols = pl.ds(n * 2 * TILE, 2 * TILE)
+            stage[t % 2, :, cols] = dot_tn(
+                f_buf[:, pl.ds(t * out_tile, out_tile)], sg[:, cols]
+            ).astype(BF16)
+        grad_copy(t).start()
+
+    tiles = width // out_tile
     for j in range(chips):
-        row_grads(goal(j))
+        row_grads(goal(j), j == 0)
         pair_copy(goal(j)).start()
         if j > 0:
 
@@ -1016,7 +1612,10 @@
             def _(j=j):
                 forward(goal(j))
 
-        mix(j)
+        if j == min(1, chips - 1):
+            total.relay()
+        for t in range(j * tiles // chips, (j + 1) * tiles // chips):
+            grad_tile(t)
 
     pair_copy(chip).wait_recv()
 
@@ -1049,130 +1648,321 @@
             def _(d=d, u=u):
                 hop(d, u, 0).wait_send()
 
-    for r in range(max(chips - 2, 0), chips):
-        mix_copy(r).wait()
-
-
-def expert_second(hid, sg, su, tail, w_down, w_gate, w_up, near, before, collective_id, parts=2):
+    for t in range(tiles - 2, tiles):
+        grad_copy(t).wait()
+    total.finish()
+
+
+def expert_second(sg, su, tail, ffn_all, d_down, w_gate, w_up, near, collective_id, parts=4):
     groups, seqs = lax.axis_size("expert"), lax.axis_size("dp")
     chips = groups // 2
-    length = hid.shape[0]
+    length, width = ffn_all.shape
     rows = length // groups
-    experts, ff, width = w_down.shape
+    experts, _, ff = w_gate.shape
     wide = width + LANES
+    size = ff // seqs
+    where = [index for _, index in near]
+    near = [array for array, _ in near]
     n = len(near)
 
     def kernel(*refs):
         expert_second_body(
-            groups, seqs, rows, width, ff, experts, parts, *refs[:7], refs[7 : 7 + n],
-            *refs[8 + n : 10 + n], *refs[11 + n :],
+            groups, seqs, rows, width, ff, experts, parts, *refs[:7], list(zip(refs[7 : 7 + n], where)),
+            *refs[7 + n :],
         )
 
     anywhere = pl.BlockSpec(memory_space=pl.ANY)
     dma = pltpu.SemaphoreType.DMA
+    flat = pltpu.VMEM((length, experts * ff), BF16)
+    block = pltpu.VMEM((2, size, width), BF16)
     return pl.pallas_call(
         kernel,
         out_shape=[
-            jax.ShapeDtypeStruct((length, width), BF16),
+            jax.ShapeDtypeStruct((width, experts * ff), BF16),
+            jax.ShapeDtypeStruct((2, size, width), BF16),
             jax.ShapeDtypeStruct((rows, wide), F32),
-            jax.ShapeDtypeStruct(sg.shape, BF16),
         ],
-        in_specs=[anywhere] * (8 + n),
-        out_specs=[anywhere, pl.BlockSpec(memory_space=pltpu.VMEM), anywhere],
-        input_output_aliases={1: 2},
+        in_specs=[anywhere] * (7 + n),
+        out_specs=[anywhere, anywhere, pl.BlockSpec(memory_space=pltpu.VMEM)],
         scratch_shapes=[
             pltpu.VMEM((width, experts * ff), BF16),
             pltpu.VMEM((width, experts * ff), BF16),
-            pltpu.VMEM((experts, ff, width), BF16),
-            pltpu.VMEM((length, experts * ff), BF16),
-            pltpu.VMEM((length, experts * ff), BF16),
-            pltpu.VMEM((length, experts * ff), BF16),
+            flat, flat,
             pltpu.VMEM((length, LANES), BF16),
+            pltpu.VMEM((length, width), BF16),
+            pltpu.VMEM((2, 256, experts * ff), BF16),
             pltpu.VMEM((chips, 2, rows, wide), BF16),
             pltpu.VMEM((chips, rows, wide), BF16),
             pltpu.VMEM((chips, rows, wide), BF16),
             pltpu.VMEM((rows, wide), BF16),
-            pltpu.VMEM((2, 2 * rows, width), BF16),
-            dma((5,)), dma((2, experts, 4)), dma((2,)), dma((chips,)), dma((chips,)),
+            block, block, block, pltpu.VMEM((2, 2, size, width), BF16),
+            dma((4,)), dma((2, experts, 4)), dma((2,)), dma((chips,)), dma((chips,)),
             dma((chips, parts)), dma((chips, parts)), dma((parts,)),
+            dma((4,)), dma((6,)), dma((6,)),
+        ],
+        compiler_params=pltpu.CompilerParams(
+            collective_id=collective_id, has_side_effects=True, vmem_limit_bytes=60 * 1024 * 1024
+        ),
+        cost_estimate=cost_of(65),
+        name="expert_second",
+    )(sg, su, tail, ffn_all, w_gate, w_up, d_down, *near)
+
+
+def gather_fill_body(
+    groups, rows, parts, x_ref, f_ref, su_ref, hid_ref, wd_ref, o_ref, grad_out, y_out,
+    f_buf, su, hid, wd, stage, in_sem, stage_sem, own_sem, send, recv, pair_send, pair_recv,
+):
+    chips = groups // 2
+    length, width = f_buf.shape
+    hidden = su.shape[1]
+    size = stage.shape[1]
+    loads = [
+        pltpu.make_async_copy(src, dst, in_sem.at[i])
+        for i, (src, dst) in enumerate(((f_ref, f_buf), (su_ref, su), (hid_ref, hid), (wd_ref, wd)))
+    ]
+    for copy in loads:
+        copy.start()
+    grads, mixes = width // size, length // size
+    total = grads + mixes
+
+    def place(t):
+        return pl.ds((t if t < grads else t - grads) * size, size)
+
+    def out_copy(t):
+        to = grad_out if t < grads else y_out
+        return pltpu.make_async_copy(stage.at[t % 2], to.at[place(t)], stage_sem.at[t % 2])
+
+    def tile(t):
+        if t == 0:
+            loads[0].wait()
+            loads[1].wait()
+        if t == grads:
+            loads[2].wait()
+            loads[3].wait()
+        if t >= 2:
+            out_copy(t - 2).wait()
+        for n in range(hidden // (2 * TILE)):
+            cols = pl.ds(n * 2 * TILE, 2 * TILE)
+            if t < grads:
+                value = dot_tn(f_buf[:, place(t)], su[:, cols])
+            else:
+                value = dot(hid[place(t), :], wd[:, cols])
+            stage[t % 2, :, cols] = value.astype(BF16)
+        out_copy(t).start()
+
+    turns = max(chips - 1, 1)
+
+    def work(k):
+        if k < turns:
+            for t in range(k * total // turns, (k + 1) * total // turns):
+                tile(t)
+
+    gather_body(
+        groups, rows, parts, Plane((), (), (), (), None, None), x_ref, o_ref,
+        own_sem, send, recv, pair_send, pair_recv, work=work,
+    )
+    for t in range(total - 2, total):
+        out_copy(t).wait()
+
+
+def gather_fill(x, ffn_all, su, hid, wd, collective_id, parts=4):
+    groups = lax.axis_size("expert")
+    rows, width = x.shape
+    length, hidden = su.shape
+    anywhere = pl.BlockSpec(memory_space=pl.ANY)
+    dma = pltpu.SemaphoreType.DMA
+    line = dma((2, groups // 2, parts))
+    tokens = jax.ShapeDtypeStruct((length, width), BF16)
+    return pl.pallas_call(
+        functools.partial(gather_fill_body, groups, rows, parts),
+        out_shape=[tokens, jax.ShapeDtypeStruct((width, hidden), BF16), tokens],
+        in_specs=[anywhere] * 5,
+        out_specs=[anywhere] * 3,
+        scratch_shapes=[
+            pltpu.VMEM((length, width), BF16),
+            pltpu.VMEM((length, hidden), BF16),
+            pltpu.VMEM((length, hidden), BF16),
+            pltpu.VMEM((hidden, width), BF16),
+            pltpu.VMEM((2, 256, max(hidden, width)), BF16),
+            dma((4,)), dma((2,)), dma, line, line, line, line,
         ],
         compiler_params=pltpu.CompilerParams(
             collective_id=collective_id, has_side_effects=True, vmem_limit_bytes=VMEM_LIMIT
         ),
-        cost_estimate=cost_of(60),
-        name="expert_second",
-    )(hid, sg, su, tail, w_down, w_gate, w_up, *near, before)
-
-
-def spread_body(groups, copies, slab, plane, q_ref, k_ref, v_ref, o_ref, own_sem, send, recv):
+        cost_estimate=cost_of(45),
+        name="gather_fill",
+    )(x, ffn_all, su, hid, wd)
+
+
+class Opening:
+    def __init__(self, sends, arrived, wholes):
+        self.sends, self.arrived, self.wholes = sends, arrived, wholes
+
+    def start(self):
+        for i in (0, 1):
+            self.sends.copy(i).start()
+
+    def start_mid(self):
+        self.arrived()
+        for whole in self.wholes:
+            whole.start()
+        for i in (2, 3):
+            self.sends.copy(i).start()
+
+    def start_later(self):
+        for whole in self.wholes:
+            whole.start_later()
+
+    def finish(self):
+        for whole in self.wholes:
+            whole.finish()
+        self.sends.finish()
+
+
+def opening_body(
+    groups, seqs, copies, slab, rows, parts, gate_refs, x_ref, small_ref, out_ref, q_ref, k_ref, v_ref, gate_ref,
+    x_to, small_to, qkv_to, wo_to, out_to, spread_to,
+    box, send, recv, out_sem, own_sem, qkv_send, qkv_recv, small_sem, plane_send, plane_recv,
+    whole_own, whole_send, whole_recv, keep_sem, line_send, line_recv, pair_send, pair_recv,
+):
     me, dp = lax.axis_index("expert"), lax.axis_index("dp")
+    total = groups * seqs
+    mine = dp * groups + me
     block = q_ref.shape[0]
     barrier = pltpu.get_barrier_semaphore()
-    for s in range(1, groups):
+
+    def device(index):
+        return (index // groups, index % groups)
+
+    def hello(s, carry):
         pl.semaphore_signal(
-            barrier, inc=1, device_id=(dp, (me + s) % groups), device_id_type=MESH
-        )
-    plane.greet(barrier)
-    pl.semaphore_wait(barrier, groups - 1 + (2 if plane.busy() else 0))
-    half = groups // 2
-    place = pl.ds(pl.multiple_of((me % half) * block, block), block)
-    copies_out = []
-    for s in range(1, groups):
-        peer = (me + s) % groups
-        for m, ref in enumerate((q_ref, k_ref, v_ref)):
+            barrier, inc=1, device_id=device((mine + s) % total), device_id_type=MESH
+        )
+        return carry
+
+    lax.fori_loop(1, total, hello, 0)
+    pl.semaphore_wait(barrier, total - 1)
+
+    def small_copy(s):
+        return pltpu.make_async_remote_copy(
+            src_ref=small_ref, dst_ref=box.at[mine], send_sem=send.at[s], recv_sem=recv.at[s],
+            device_id=device((mine + s) % total), device_id_type=MESH,
+        )
+
+    def start(s, carry):
+        small_copy(s).start()
+        return carry
+
+    def wait(s, carry):
+        small_copy(s).wait()
+        return carry
+
+    lax.fori_loop(1, total, start, 0)
+    place = pl.ds(pl.multiple_of(me * block, block), block)
+    spread, own = [], []
+    for m, ref in enumerate((q_ref, k_ref, v_ref)):
+        cols = pl.ds(pl.multiple_of((me // copies) * slab, slab), slab)
+        dst = spread_to.at[place, pl.ds(m * slab, slab)]
+        own.append(pltpu.make_async_copy(ref.at[:, cols], dst, own_sem.at[m]))
+        for s in range(1, groups):
+            peer = (me + s) % groups
             cols = pl.ds(pl.multiple_of((peer // copies) * slab, slab), slab)
-            copies_out.append(
+            spread.append(
                 pltpu.make_async_remote_copy(
-                    src_ref=ref.at[:, cols],
-                    dst_ref=o_ref.at[me // half, m, place],
-                    send_sem=send.at[s, m],
-                    recv_sem=recv.at[s, m],
-                    device_id=(dp, peer),
-                    device_id_type=MESH,
+                    src_ref=ref.at[:, cols], dst_ref=dst,
+                    send_sem=qkv_send.at[s, m], recv_sem=qkv_recv.at[s, m],
+                    device_id=(dp, peer), device_id_type=MESH,
                 )
             )
-    for copy in copies_out:
+    moved = (mine % seqs) * groups + mine // seqs
+    away = pltpu.make_async_remote_copy(
+        src_ref=out_ref, dst_ref=out_to, send_sem=out_sem.at[0], recv_sem=out_sem.at[1],
+        device_id=device(moved), device_id_type=MESH,
+    )
+    stay = pltpu.make_async_copy(out_ref, out_to, out_sem.at[0])
+    for copy in spread:
         copy.start()
-    plane.start()
-    own = []
-    for m, ref in enumerate((q_ref, k_ref, v_ref)):
-        cols = pl.ds(pl.multiple_of((me // copies) * slab, slab), slab)
-        own.append(
-            pltpu.make_async_copy(ref.at[:, cols], o_ref.at[me // half, m, place], own_sem.at[m])
-        )
+
+    @pl.when(moved != mine)
+    def _():
+        away.start()
+
+    @pl.when(moved == mine)
+    def _():
+        stay.start()
+
     for copy in own:
         copy.start()
-    for copy in own + copies_out:
-        copy.wait()
-    plane.finish()
-
-
-def spread_columns(w_query, w_key, w_value, copies, slab, collective_id, sends):
-    groups = lax.axis_size("expert")
-    block = w_query.shape[0]
-    arrays, specs = [], []
-    for array, start, size, flip in sends:
-        arrays.append(array)
-        specs.append((len(arrays) - 1, start, size, flip))
-    targets = [jax.ShapeDtypeStruct((s[2],) + s[0].shape[1:], s[0].dtype) for s in sends]
-    n = len(sends)
-
-    def kernel(q_ref, k_ref, v_ref, *refs):
-        plane = Plane(specs, (), refs[:n], refs[n + 1 : 2 * n + 1], *refs[2 * n + 1 : 2 * n + 3])
-        spread_body(groups, copies, slab, plane, q_ref, k_ref, v_ref, refs[n], *refs[2 * n + 3 :])
-
-    anywhere = pl.BlockSpec(memory_space=pl.ANY)
+    box[mine] = small_ref[...]
+    out_small = pltpu.make_async_copy(box, small_to, small_sem)
+
+    def arrived():
+        lax.fori_loop(1, total, wait, 0)
+        out_small.start()
+        for copy in own + spread:
+            copy.wait()
+
+        @pl.when(moved != mine)
+        def _():
+            away.wait()
+
+        @pl.when(moved == mine)
+        def _():
+            stay.wait()
+
+    sends = Plane(
+        [(0, 0, 1, 1), (0, 0, 1, 2), (0, 1, 1, 1), (0, 1, 1, 2)], (), [gate_ref], gate_refs,
+        plane_send, plane_recv,
+    )
+    wholes = [
+        Whole(a, b, whole_own.at[i], whole_send.at[i], whole_recv.at[i])
+        for i, (a, b) in enumerate(((spread_to, qkv_to), (out_to, wo_to)))
+    ]
+    gather_body(
+        groups, rows, parts, Opening(sends, arrived, wholes), x_ref, x_to,
+        keep_sem, line_send, line_recv, pair_send, pair_recv, greet=False,
+    )
+    out_small.wait()
+
+
+def opening(x, small, w_out, w_query, w_key, w_value, w_gate, copies, slab, carry, collective_id, parts=4):
+    groups, seqs = lax.axis_size("expert"), lax.axis_size("dp")
+    total = groups * seqs
+    block, width = w_query.shape
+    rows = x.shape[0]
+    gate = jax.ShapeDtypeStruct((1,) + w_gate.shape[1:], BF16)
+
+    def kernel(*refs):
+        ins, refs = refs[:7], refs[8:]
+        outs, gates, rest = refs[:6], refs[6:10], refs[11:]
+        opening_body(groups, seqs, copies, slab, rows, parts, gates, *ins, *outs, *rest)
+
+    vmem, anywhere = pl.BlockSpec(memory_space=pltpu.VMEM), pl.BlockSpec(memory_space=pl.ANY)
     dma = pltpu.SemaphoreType.DMA
+    line = dma((2, groups // 2, parts))
     return pl.pallas_call(
         kernel,
-        out_shape=[jax.ShapeDtypeStruct((2, 3, groups // 2 * block, slab), BF16)] + targets,
-        in_specs=[anywhere] * (3 + n),
-        out_specs=[anywhere] * (1 + n),
-        scratch_shapes=[dma((max(n, 1),)), dma((max(n, 1),)), dma((3,)), dma((groups, 3)), dma((groups, 3))],
+        out_shape=[
+            jax.ShapeDtypeStruct((groups * rows, width), x.dtype),
+            jax.ShapeDtypeStruct((total,) + small.shape, small.dtype),
+            jax.ShapeDtypeStruct((seqs * groups * block, 3 * slab), BF16),
+            jax.ShapeDtypeStruct((seqs * block, width), BF16),
+            jax.ShapeDtypeStruct((block, width), BF16),
+            jax.ShapeDtypeStruct((groups * block, 3 * slab), BF16),
+        ]
+        + [gate] * 4
+        + [jax.ShapeDtypeStruct(carry.shape, carry.dtype)],
+        in_specs=[anywhere, vmem] + [anywhere] * 6,
+        out_specs=[anywhere] * 11,
+        input_output_aliases={7: 10},
+        scratch_shapes=[pltpu.VMEM((total,) + small.shape, small.dtype)]
+        + [dma((total,)), dma((total,)), dma((2,)), dma((3,)), dma((groups, 3)), dma((groups, 3)), dma]
+        + [dma((4,)), dma((4,)), dma((2,)), dma((2, 4)), dma((2, 4))]
+        + [dma] + [line] * 4,
         compiler_params=pltpu.CompilerParams(collective_id=collective_id, has_side_effects=True),
-        cost_estimate=cost_of(20),
-        name="spread_columns",
-    )(w_query, w_key, w_value, *arrays)
+        cost_estimate=cost_of(80),
+        name="opening",
+    )(x, small, w_out, w_query, w_key, w_value, w_gate, carry)
 
 
 def both(array, start=0, size=None):
@@ -1274,7 +2064,10 @@
         [w_router.reshape(-1), gain_attn, gain_query, gain_key, gain_ffn,
          jnp.zeros((small_rows * 128 - small_size,), BF16)]
     )
-    small_all = exchange(small.reshape(1, small_rows, 128), 1, spread=True, same=True)
+    x_all, small_all, w_qkv, w_o, _, _, gate0_x, gate0_y, gate1_x, gate1_y, g_low = opening(
+        x_low, small.reshape(small_rows, 128), w_out, w_query, w_key, w_value, w_gate, copies, slab,
+        g_low, 1,
+    )
     small_all = small_all.reshape(seqs * groups, small_rows * 128)
     split = block * all_experts
     w_r = small_all[:, :split].reshape(width, all_experts)
@@ -1287,32 +2080,18 @@
     g_query = lax.dynamic_slice(gains[1], (slab_start,), (slab,))
     g_key = lax.dynamic_slice(gains[2], (slab_start,), (slab,))
 
-    near_gate = tie(w_gate, small_all)
-    gate_x, gate_y = swap_dp(near_gate, 1), swap_dp(near_gate, 2)
-    (qkv_got,) = spread_columns(tie(w_query, small_all), w_key, w_value, copies, slab, 2, ())
     total = seqs * groups
     moves = [(b, (b % seqs) * groups + b // seqs) for b in range(total)]
-    o_own = lax.ppermute(tie(w_out, small_all), ("dp", "expert"), moves)
 
     x_in = x_low.astype(F32)
     inv_attn = inv_rms(x_in)
-    normed_low = (x_in * inv_attn * g_attn).astype(BF16)
-    half_o = block // 2
-    normed_all, q_x, q_y, o_x, o_y, q_f0, q_f1, o_f0, o_f1 = line_gather(
-        tie(normed_low, qkv_got), 3,
-        sends=both(qkv_got) + both(o_own),
-        later=[(1, 0, 1, 1), (0, 1, 1, 2), (3, 0, half_o, 1), (2, half_o, half_o, 2)],
-    )
-    qkv_pieces = [qkv_got, q_x, q_y, jnp.concatenate([q_f0, q_f1], axis=0)]
-    w_qkv = jnp.concatenate(
-        [in_order([p[:, m].reshape(-1, slab) for p in qkv_pieces], my_dp, 0) for m in range(3)], axis=1
-    )
-    w_o = in_order([o_own, o_x, o_y, jnp.concatenate([o_f0, o_f1], axis=0)], my_dp, 0)
+    x_wide = x_all.astype(F32)
+    normed_all = (x_wide * inv_rms(x_wide) * g_attn).astype(BF16)
     if copies > 1:
         sets = [[c * copies + i for i in range(copies)] for c in range(groups // copies)]
         w_o = lax.all_gather(w_o, "expert", axis_index_groups=sets, axis=0, tiled=True)
 
-    near_up = tie(w_up, normed_all)
+    near_up = tie(w_up, x_all)
     up_x, up_y = swap_dp(near_up, 1), swap_dp(near_up, 2)
     g_all = lax.all_gather(g_low, "expert", axis=0, tiled=True)
 
@@ -1347,7 +2126,7 @@
     mix = jnp.concatenate(mixes, axis=1)
     o_sum, gate0_f, gate1_f, up0_f, up1_f = line_reduce(
         dot(mix, w_o) * share, 5,
-        sends=[(gate_y, 0, 1, 1), (gate_x, 1, 1, 2), (up_y, 0, 1, 1), (up_x, 1, 1, 2)],
+        sends=[(gate0_y, 0, 1, 1), (gate1_x, 0, 1, 2), (up_y, 0, 1, 1), (up_x, 1, 1, 2)],
     )
     after_attn = x_in + o_sum
 
@@ -1360,20 +2139,19 @@
         axis=1,
     )
     route_dense = router_prob * chosen_mask
-    gate_near = [gate_x, gate_y, gate0_f, gate1_f]
-    up_near = [up_x, up_y, up0_f, up1_f]
+    gate_near = [(gate0_x, 0), (gate1_x, 0), (gate0_y, 0), (gate1_y, 0), (gate0_f, 0), (gate1_f, 0)]
+    up_near = [(up_x, 0), (up_x, 1), (up_y, 0), (up_y, 1), (up0_f, 0), (up1_f, 0)]
     ff = w_gate.shape[2]
     if copies == 1 and length * width <= 1 << 21:
         high = lax.reduce_precision(route_dense, 8, 7)
         space = jnp.zeros((rows, LANES // 2 - all_experts), F32)
         extra = jnp.concatenate([high, space, route_dense - high, space], axis=1).astype(BF16)
-        ffn_all, hidden_w, d_gate, d_up, tail, wd = expert_first(
+        ffn_all, hidden_w, d_gate, d_up, tail, wd, d_down = expert_first(
             jnp.concatenate([ffn_low, extra], axis=1), g_all, w_gate, w_up, w_down,
             gate_near + up_near, 9,
         )
-        d_down = dot_tn(hidden_w, g_all).astype(BF16)
-        y_part, d_rows, d_gate = expert_second(
-            hidden_w, d_gate, d_up, tail, wd, w_gate, w_up, gate_near + up_near, d_down, 13
+        d_gate_w, own_down, d_rows = expert_second(
+            d_gate, d_up, tail, ffn_all, d_down, w_gate, w_up, gate_near + up_near, 13
         )
         d_weight = d_rows[:, width : width + LANES]
         d_weight = d_weight[:, :all_experts] + d_weight[:, LANES // 2 : LANES // 2 + all_experts]
@@ -1391,7 +2169,7 @@
         y_part, dx_part = 0.0, 0.0
         for i in range(local_experts):
             wg, wu = (
-                in_order([own[i], near[0][i], near[1][i], near[2 + i][0]], my_dp, 0)
+                in_order([own[i]] + [near[2 * q + i][0][near[2 * q + i][1]] for q in range(3)], my_dp, 0)
                 for own, near in ((w_gate, gate_near), (w_up, up_near))
             )
             weight = route_mine[:, i : i + 1]
@@ -1409,24 +2187,24 @@
             (ffn_all, y_part, dx_part) = lax.optimization_barrier((ffn_all, y_part, dx_part))
         hidden_w, d_gate, d_up = (jnp.concatenate(a, axis=1) for a in (hidden_w, d_gate, d_up))
         y_part = y_part.astype(BF16)
-        d_down = dot_tn(hidden_w, g_all).astype(BF16)
+        d_down = dot_tn(hidden_w, g_all).astype(BF16).reshape(local_experts, ff, width)
         d_rows = line_reduce(dx_part, 10)
         d_weight = jnp.stack(d_weights, axis=0).reshape(local_experts, groups, rows)
         d_weight = jnp.pad(d_weight.transpose(1, 0, 2), ((0, 0), (0, pad), (0, 0)))
         d_weight = exchange(d_weight, 6)[:, :local_experts].reshape(all_experts, rows).T
 
-    own_down = lax.psum_scatter(
-        d_down.reshape(local_experts, ff, width), "dp", scatter_dimension=1, tiled=True
-    )
-
-    def in_grad(grad):
-        product = dot_tn(ffn_all, grad).astype(BF16)
-        return product, lax.psum_scatter(product, "dp", scatter_dimension=0, tiled=True)
+    fused = copies == 1 and length * width <= 1 << 21
+
+    def scatter_in(product):
+        return lax.psum_scatter(product, "dp", scatter_dimension=0, tiled=True)
 
     def to_experts(own_grad):
         return jnp.stack([own_grad[:, i * ff : (i + 1) * ff] for i in range(local_experts)]).astype(F32)
 
-    d_gate_w, own_gate = in_grad(d_gate)
+    if not fused:
+        own_down = lax.psum_scatter(d_down, "dp", scatter_dimension=1, tiled=True)
+        d_gate_w = dot_tn(ffn_all, d_gate).astype(BF16)
+    own_gate = scatter_in(d_gate_w)
     d_router_prob = d_weight * chosen_mask
 
     d_logits = (
@@ -1436,7 +2214,14 @@
     d_normed_ffn = d_rows + dot_nt(d_logits, w_r)
     d_after_norm, d_gain_ffn = norm_back(after_attn, inv_ffn, g_ffn, d_normed_ffn)
     d_after = g_low.astype(F32) + d_after_norm
-    d_after_all = line_gather(d_after.astype(BF16), 11, after=[own_down, d_gate_w])
+    if fused:
+        d_after_all, d_up_w, y_part = gather_fill(
+            d_after.astype(BF16), ffn_all, d_up, hidden_w, wd.reshape(local_experts * ff, width), 11
+        )
+    else:
+        d_after_all = line_gather(d_after.astype(BF16), 16)
+        d_up_w = dot_tn(ffn_all, d_up).astype(BF16)
+    own_up = scatter_in(d_up_w)
     d_out_w = dot_tn(mix, d_after_all)
     d_mix = dot_nt(d_after_all, w_o).astype(BF16)
     dqs, dks, dvs = [], [], []
@@ -1455,11 +2240,9 @@
     dots = jnp.stack(
         [jnp.sum(dq_n * g_query * q_raw, axis=1), jnp.sum(dk_n * g_key * k_raw, axis=1)], axis=0
     )
-    dots, d_up = exchange(
-        (dots * share).reshape(1, 2 * length // 128, 128), 14, same=True, reduce=True, carry=[d_up]
-    )
-    dots = dots.reshape(2, length) / width
-    d_up_w, own_up = in_grad(d_up)
+    dots = exchange(
+        (dots * share).reshape(1, 2 * length // 128, 128), 4, same=True, reduce=True
+    ).reshape(2, length) / width
     d_gain_query = jnp.sum(dq_n * q_raw * inv_q, axis=0)
     d_gain_key = jnp.sum(dk_n * k_raw * inv_k, axis=0)
     dq_low = (inv_q * dq_n * g_query - q_raw * (inv_q**3 * dots[0][:, None])).astype(BF16)
@@ -1468,13 +2251,19 @@
     d_qkv_w = dot_tn(normed_all, d_raw).astype(BF16)
     d_qkv_w = d_qkv_w.reshape(width, 3, slab)
     d_qkv_w = lax.dynamic_slice(d_qkv_w, (0, 0, offset), (width, 3, own))
-    d_qkv_w = jnp.split(own_order(d_qkv_w.reshape(width, 3 * own), my_dp, 0), 4, axis=0)
+    d_qkv_w = d_qkv_w.reshape(width, 3 * own)
     d_out_w = lax.dynamic_slice(d_out_w.astype(BF16), (offset, 0), (own, width))
-    d_out_w = jnp.split(own_order(d_out_w, my_dp, 0), 4, axis=0)
-    d_normed_in, qkv_x, qkv_y, out_x, out_y = line_reduce(
-        dot_nt(d_raw, w_qkv) * share, 12, sends=halves(d_qkv_w[3]) + halves(d_out_w[3]),
-        after=[own_gate, d_up_w],
-    )
+    dx_in = (dot_nt(d_raw, w_qkv) * share).astype(BF16)
+    if length * width <= 1 << 21:
+        d_normed_in, y_sum, own_qkv, own_out = joint_reduce(
+            [dx_in, y_part], [d_qkv_w, d_out_w], [own_gate], 12
+        )
+    else:
+        d_normed_in, own_qkv, own_out = joint_reduce(
+            [dx_in], [d_qkv_w, d_out_w], [own_gate], 12
+        )
+        y_sum = line_reduce(y_part, 15)
+    output = after_attn + y_sum
     d_in_norm, d_gain_attn = norm_back(x_in, inv_attn, g_attn, d_normed_in)
     input_grad = d_after + d_in_norm
 
@@ -1489,31 +2278,21 @@
         + [jnp.zeros((total, small_rows * 128 - small_size), F32)],
         axis=1,
     )
-    qkv_to_x, qkv_to_y = relay(d_qkv_w, qkv_x, qkv_y)
-    out_to_x, out_to_y = relay(d_out_w, out_x, out_y)
-    y_sum, qkv_x, qkv_y, out_x, out_y = line_reduce(
-        tie(y_part, d_normed_in), 15,
-        sends=[
-            (qkv_to_x, 0, qkv_to_x.shape[0], 1), (qkv_to_y, 0, qkv_to_y.shape[0], 2),
-            (out_to_x, 0, out_to_x.shape[0], 1), (out_to_y, 0, out_to_y.shape[0], 2),
-        ],
-    )
-    output = after_attn + y_sum
-    small_grad = exchange(small_grad.reshape(total, small_rows, 128), 8, spread=True, reduce=True)
+    small_grad = small_grad.reshape(total, small_rows, 128)
+    if own % 128 == 0:
+        small_grad, *matrices = last_exchange(small_grad, own_qkv, own_out, 8)
+    else:
+        small_grad = exchange(small_grad, 8, spread=True, reduce=True)
+        own_qkv = exchange(own_qkv.reshape(groups, block, 3 * own), 7)
+        own_qkv = own_qkv.reshape(groups, block, 3, own).transpose(2, 1, 0, 3)
+        own_out = lax.ppermute(own_out, ("dp", "expert"), [(b, a) for a, b in moves])
+        matrices = [*own_qkv.reshape(3, block, width).astype(F32), own_out.astype(F32)]
     small_grad = small_grad.reshape(-1)
-    d_qkv_w = settle(d_qkv_w, qkv_x, qkv_y).astype(BF16)
-    d_qkv_w = exchange(d_qkv_w.reshape(groups, block, 3 * own), 7).reshape(groups, block, 3, own)
-    d_qkv_w = d_qkv_w.transpose(2, 1, 0, 3).reshape(3, block, width).astype(F32)
-    d_out_w = settle(d_out_w, out_x, out_y).astype(BF16)
-    d_out_w = lax.ppermute(d_out_w, ("dp", "expert"), [(b, a) for a, b in moves]).astype(F32)
     expert_owned = [to_experts(own_gate), to_experts(own_up), own_down.astype(F32)]
     return (
         output.reshape(1, rows, width),
         input_grad.reshape(1, rows, width),
-        d_qkv_w[0],
-        d_qkv_w[1],
-        d_qkv_w[2],
-        d_out_w,
+        *matrices,
         small_grad[:split].reshape(block, all_experts),
         small_grad[split : split + block],
         small_grad[split + block : split + 2 * block],

time: 762 us -> 638 us (0.84)
  other arithmetic: 74.7 us -> 34.3 us
  matrix products: 78 us -> 41.2 us
  waiting for transfers between devices: 41 us -> 11.2 us
  local copies, waits for them, and re-layouts: 48 us -> 36.2 us
    dot_general x10 -> x7, matrix products: 54.1 us -> 13.9 us  [dot_tn(): lax.dot_general(left, right, (((0,), (0,)), ((), ())), preferred_element_...]
    concatenate x5 -> x0, other arithmetic: 32.4 us -> none  [the longest x1 29.1 us: shards(): jnp.concatenate([in_order([p[:, m].reshape(-1, slab) for p in qkv_pieces]...]
    ppermute x4 -> x2, waiting for transfers between devices: 27 us -> 11.1 us  [swap_dp(): return lax.ppermute(block, 'dp', [(i, i ^ flip) for i in range(seqs)])]
    reduce_scatter x3 -> x2, waiting for transfers between devices: 13.9 us -> 0.01 us  [scatter_in(): return lax.psum_scatter(product, 'dp', scatter_dimension=0, tiled=True)]
    convert_element_type x8 -> x0, other arithmetic: 10.3 us -> none  [the longest x1 2.95 us: shards(): d_qkv_w = settle(d_qkv_w, qkv_x, qkv_y).astype(BF16)]
    ppermute x2 -> x0, starting transfers between devices: 9.61 us -> none  [the longest x1 4.96 us: shards(): o_own = lax.ppermute(tie(w_out, small_all), ('dp', 'expert'), moves)]
    unnamed x173 -> x167, local copies, waits for them, and re-layouts: 18.5 us -> 17.3 us
    pallas_call x12 -> x8, Pallas kernels: 403 us -> 401 us  [the longest x1 95.9 us: opening(): pl.pallas_call(kernel, out_shape=[jax.ShapeDtypeStruct((groups * rows, wi...]
  transfers between devices with their start and end apart: 10 -> 5, of which waited for: 3 -> 2; matrix products, arithmetic and copies ran while one was open for 22% -> 13% of each run, Pallas kernels for 52% -> 37%
where the time goes in v4:
time: 638 us; the launch traced here: 627 us
  Pallas kernels  482 us (76%)
  matrix products  41.2 us (6%)
  local copies, waits for them, and re-layouts  36.2 us (6%)
  other arithmetic  34.3 us (5%)
  between operations  15 us (2%)
  waiting for transfers between devices  11.2 us (2%)
  starting transfers between devices  7.27 us (1%)
    pallas_call x1, Pallas kernels, opening(): pl.pallas_call(kernel, out_shape=[jax.ShapeDtypeStruct((groups * rows, wi...  95.9 us
    pallas_call x1, Pallas kernels, expert_first(): pl.pallas_call(kernel, out_shape=[jax.ShapeDtypeStruct((length, width), B...  80.4 us
    pallas_call x1, Pallas kernels, expert_second(): pl.pallas_call(kernel, out_shape=[jax.ShapeDtypeStruct((width, experts *...  76.5 us
    pallas_call x1, Pallas kernels, joint_reduce(): pl.pallas_call(kernel, out_shape=[jax.ShapeDtypeStruct((rows, width), F32...  75.4 us
    pallas_call x3, Pallas kernels, run(): pl.pallas_call(kernel, out_shape=[out] + targets + whole_out + [jax.Shape...  63.9 us
    pallas_call x1, Pallas kernels, last_exchange(): pl.pallas_call(functools.partial(last_body, groups, seqs), out_shape=[jax...  48.9 us
    pallas_call x1, Pallas kernels, gather_fill(): pl.pallas_call(functools.partial(gather_fill_body, groups, rows, parts),...  40.8 us
    unnamed x167, local copies, waits for them, and re-layouts  17.3 us
  transfers between devices with their start and end apart: 5, of which 2 were waited for; matrix products, arithmetic and copies ran while one was open for 13% of the time, Pallas kernels for 37%

profile of v4, /device:TPU:5, one launch (start us, length us, event | category | flops | bytes accessed | tf_op | source)
XLA Modules:
  0.0 627.0 jit_solution(12824470116184094447)
XLA Ops:
  7.2 1.9 copy.63
  10.0 3.3 concatenate.39
  13.3 95.9 %opening.1 = (bf16[1024,2048]{1,0:T(8,128)(2,1)}, bf16[32,16,128]{2,1,0:T(8,128)(2,1)}, bf16[2048,768]{1,0:T(8,128)(2,1)}, bf16[256,2048]{1,0:T(8,128)(2,1)}, bf...) custom-call(bf16[128,2048]{1,0:T(8,128)(2,1)} %bitcast.160, ...), custom_call_target="tpu_custom_call", output_to_operand_aliasing={{10}: (7, {})} | custom-call | bytes 240000000 | tf_op jit(solution)/shard_map/opening/pallas_call | solution.py:1943
  109.2 5.2 collective-permute-start
  114.5 1.9 collective-permute-start.1
  116.5 3.1 fusion
  119.8 6.8 %fusion.10 = f32[1024,768]{0,1:T(8,128)S(1)} fusion(bf16[2048,768]{1,0:T(8,128)(2,1)} %get-tuple-element.53, bf16[1024,2048]{1,0:T(8,128)(2,1)} %get-tuple-element.51, f32[2048]{0:T(1024)S(1)} %reshape.281, f32[1024]{0:T(1024)S(1)} %add_rsqrt_fusion.1), kind=kOutput, calls=%fused_computation.47 | convolution fusion | flops 3229614080 | bytes 10498048 | tf_op jit(solution)/shard_map/dot_general | solution.py:23
  129.2 7.0 %exchange.2 = f32[16,128]{1,0:T(8,128)} custom-call(f32[1,16,128]{2,1,0:T(8,128)} %reshape.267.refs_0_), custom_call_target="tpu_custom_call" | custom-call | bytes 24000000 | tf_op jit(solution)/shard_map/exchange/pallas_call | solution.py:919
  139.0 1.8 multiply_multiply_fusion
  147.2 3.3 convolution_convert_fusion.refs_0_
  150.5 8.6 %collective-permute-done.refs_3_.refs_13_.refs_14_.refs_15_.refs_16_ = bf16[2,512,1024]{2,1,0:T(8,128)(2,1)S(1)} collective-permute-done((bf16[2,512,1024]{2,1,0:T(8,128)(2,1)}, bf16[2,512,1024]{2,1,0:T(8,128)(2,1)S(1)}, u32[]{:S(2)}, u32[]{:S(2)}) %collective-permute-start) | collective-permute-done | bytes 2097184 | tf_op jit(solution)/shard_map/ppermute | solution.py:1975
  159.1 2.5 collective-permute-done.1.refs_4_.refs_11_.refs_12_.refs_13_.refs_14_
  161.6 50.3 %line_reduce.1 = (f32[128,2048]{1,0:T(8,128)}, bf16[1,512,1024]{2,1,0:T(8,128)(2,1)}, bf16[1,512,1024]{2,1,0:T(8,128)(2,1)}, bf16[1,512,1024]{2,1,0:T(8,128)(2,1)}, bf16[1,512,1024]{2,1,0:T(8,128)(2,1)}) custom-call(bf16[1024,2048]{1,0:T(8,128)(2,1)} %convolution_convert_fusion.refs_0_, bf16[1,512,1024]{2,1,0:T(8,128)(2,1)} %get-tuple-element.55.refs_1_.refs_7_.refs_9_, ...), custom_call_target="tpu_custom_call" | custom-call | bytes 120000000 | tf_op jit(solution)/shard_map/line_reduce/pallas_call | solution.py:919
  211.9 2.0 multiply_reduce_fusion.4
  215.8 80.4 %expert_first.1 = (bf16[1024,2048]{1,0:T(8,128)(2,1)}, bf16[1024,2048]{1,0:T(8,128)(2,1)}, bf16[1024,2048]{1,0:T(8,128)(2,1)}, bf16[1024,2048]{1,0:T(8,128)(2,1)...) custom-call(bf16[128,2176]{1,0:T(8,128)(2,1)} %concatenate.45.refs_0_, ...), custom_call_target="tpu_custom_call" | custom-call | bytes 210000000 | tf_op jit(solution)/shard_map/expert_first/pallas_call | solution.py:1309
  296.2 76.5 %expert_second.1 = (bf16[2048,2048]{1,0:T(8,128)(2,1)}, bf16[2,256,2048]{2,1,0:T(8,128)(2,1)}, f32[128,2176]{1,0:T(8,128)}) custom-call(bf16[1024,2048]{1,0:T(8,128)(2,1)} %get-tuple-element.66.refs_0_, bf16[1024,2048]{1,0:T(8,128)(2,1)} %get-tuple-element.67.refs_1_.su_ref, bf16[1024,128]{1,0:T(8,128)(2,1)} %get-tuple-element.68.refs_2_, ...), custom_call_target="tpu_custom_call" | custom-call | bytes 195000000 | tf_op jit(solution)/shard_map/expert_second/pallas_call | solution.py:1678
  372.8 1.1 multiply_reduce_fusion.7
  373.9 2.5 multiply_reduce_fusion.2
  376.4 2.8 fusion.75
  379.1 40.8 %gather_fill.1 = (bf16[1024,2048]{1,0:T(8,128)(2,1)}, bf16[2048,2048]{1,0:T(8,128)(2,1)}, bf16[1024,2048]{1,0:T(8,128)(2,1)}) custom-call(bf16[128,2048]{1,0:T(8,128)(2,1)} %get-tuple-element.158.x_ref, bf16[1024,2048]{1,0:T(8,128)(2,1)} %get-tuple-element.69.refs_3_.f_ref, bf16[1024,2048]{1,0:T(8,128)(2,1)} %get-tuple-element.67.refs_1_.su_ref, ...), custom_call_target="tpu_custom_call" | custom-call | bytes 135000000 | tf_op jit(solution)/shard_map/gather_fill/pallas_call | solution.py:1776
  421.2 3.6 convolution_convert_fusion.4
  425.9 1.1 multiply_convert_fusion
  429.3 1.1 multiply_convert_fusion.1
  433.0 1.8 copy-done.2
  434.8 1.1 fusion.40
  436.6 1.4 reshape_squeeze.6
  438.6 2.6 fusion.80
  441.2 2.2 reshape.275
  443.4 1.3 pad_maximum_fusion.11
  444.7 1.3 reshape.272.refs_0_
  446.0 6.7 %exchange.3 = f32[16,128]{1,0:T(8,128)} custom-call(f32[1,16,128]{2,1,0:T(8,128)} %reshape.272.refs_0_), custom_call_target="tpu_custom_call" | custom-call | bytes 24000000 | tf_op jit(solution)/shard_map/exchange/pallas_call | solution.py:919
  452.7 1.4 reshape.277
  454.1 4.3 convert_element_type.166
  459.3 1.3 copy-done.75
  460.7 2.3 convolution_convert_fusion.3.refs_3_
  464.1 1.3 copy-done.6
  466.3 1.0 copy-done.76
  467.3 5.0 convolution_convert_fusion.1.refs_0_
  472.4 5.7 convolution_convert_fusion.2.refs_2_
  478.1 75.4 %joint_reduce.1 = (f32[128,2048]{1,0:T(8,128)}, f32[128,2048]{1,0:T(8,128)}, bf16[512,768]{1,0:T(8,128)(2,1)}, bf16[64,2048]{1,0:T(8,128)(2,1)}) custom-call(bf16[1024,2048]{1,0:T(8,128)(2,1)} %convolution_convert_fusion.1.refs_0_, bf16[1024,2048]{1,0:T(8,128)(2,1)} %get-tuple-element.75.refs_1_, bf16[2048,768]{1,0:T(8,128)(2,1)} %convolution_convert_fusion.2.refs_2_, ...), custom_call_target="tpu_custom_call" | custom-call | bytes 210000000 | tf_op jit(solution)/shard_map/joint_reduce/pallas_call | solution.py:697
  553.6 1.6 fusion.22
  556.1 48.9 %last_exchange.1 = (f32[16,128]{1,0:T(8,128)}, f32[64,2048]{1,0:T(8,128)}, f32[64,2048]{1,0:T(8,128)}, f32[64,2048]{1,0:T(8,128)}, f32[64,2048]{1,0:T(8,128)}) custom-call(f32[32,16,128]{2,1,0:T(8,128)} %bitcast.162, bf16[512,768]{1,0:T(8,128)(2,1)} %get-tuple-element.79.qkv_ref, bf16[64,2048]{1,0:T(8,128)(2,1)} %get-tuple-element.80.out_ref), custom_call_target="tpu_custom_call" | custom-call | bytes 75000000 | tf_op jit(solution)/shard_map/last_exchange/pallas_call | solution.py:812
  606.5 1.4 fusion.78
  607.9 1.1 add_bitcast_fusion
  608.9 1.7 slice_bitcast_fusion.1
  610.7 2.3 maximum_convert_fusion.1
  613.3 2.4 maximum_convert_fusion
  615.7 1.3 fusion.20
  (238 shorter events, 31.9 us)
Async XLA Ops:
  7.2 208.6 %all-gather.2.cloned.1.call-start = ((), (), s32[]{:S(2)}) async-start(), calls=%async_computation.2 | async-start | bytes 4718592 | tf_op jit(solution)/shard_map/all_gather | solution.py:2096
  109.2 10.3 %copy-start.35 = (bf16[32,16,128]{2,1,0:T(8,128)(2,1)S(1)}, bf16[32,16,128]{2,1,0:T(8,128)(2,1)}, u32[]{:S(2)}) copy-start(bf16[32,16,128]{2,1,0:T(8,128)(2,1)} %get-tuple-element.52) | copy-start | bytes 393220
  109.2 49.8 %collective-permute-start = (bf16[2,512,1024]{2,1,0:T(8,128)(2,1)}, bf16[2,512,1024]{2,1,0:T(8,128)(2,1)S(1)}, u32[]{:S(2)}, u32[]{:S(2)}) collective-permute-start(bf16[2,512,1024]{2,1,0:T(8,128)(2,1)} %refs_5_.3), channel_id=1, source_target_pairs={{0,16},{8,24},{16,0},{24,8},{1,17},{9,25},{17,1},{25,9},{2,18},{10... | collective-permute-start | bytes 6291464 | tf_op jit(solution)/shard_map/ppermute | solution.py:1975
  114.5 47.1 %collective-permute-start.1 = (bf16[2,512,1024]{2,1,0:T(8,128)(2,1)}, bf16[2,512,1024]{2,1,0:T(8,128)(2,1)}, u32[]{:S(2)}, u32[]{:S(2)}) collective-permute-start(bf16[2,512,1024]{2,1,0:T(8,128)(2,1)} %refs_5_.3), channel_id=1, source_target_pairs={{0,8},{8,0},{16,24},{24,16},{1,9},{9,1},{17,25},{25,17},{2,10},{10... | collective-permute-start | bytes 6291464 | tf_op jit(solution)/shard_map/ppermute | solution.py:1975
  116.4 361.6 %reduce-scatter.3.cloned.1.call-start = ((), (), s32[]{:S(2)}) async-start(), calls=%async_computation.3 | async-start | bytes 10485760 | tf_op jit(solution)/shard_map/reduce_scatter | solution.py:2199
  119.8 6.8 %copy-start.70 = (f32[1024]{0:T(1024)}, f32[1024]{0:T(1024)S(1)}, u32[]{:S(2)}) copy-start(f32[1024]{0:T(1024)S(1)} %add_rsqrt_fusion.1) | copy-start | bytes 12292
  119.8 17.2 %copy-start.69 = (s32[1,128,8]{1,2,0:T(8,128)S(1)}, s32[1,128,8]{1,2,0:T(8,128)}, u32[]{:S(2)}) copy-start(s32[1,128,8]{1,2,0:T(8,128)} %param.16) | copy-start | bytes 12292
  136.4 4.6 copy-start.61
  136.5 4.5 copy-start.64
  138.3 2.8 copy-start.15
  138.3 2.8 copy-start.17
  143.3 2.6 copy-start.4
  143.3 2.6 copy-start.49
  146.7 14.9 %copy-start.33 = (bf16[1024,128]{0,1:T(8,128)(2,1)}, bf16[1024,128]{0,1:T(8,128)(2,1)S(1)}, u32[]{:S(2)}) copy-start(bf16[1024,128]{0,1:T(8,128)(2,1)S(1)} %convolution_convert_fusion.5) | copy-start | bytes 786436
  161.6 50.3 %copy-start.13 = (bf16[1,128,2048]{2,1,0:T(8,128)(2,1)S(1)}, bf16[1,128,2048]{2,1,0:T(8,128)(2,1)}, u32[]{:S(2)}) copy-start(bf16[1,128,2048]{2,1,0:T(8,128)(2,1)} %param.15) | copy-start | bytes 1572868
  214.1 82.1 %copy-start.12 = (bf16[128,2048]{1,0:T(8,128)(2,1)}, bf16[128,2048]{1,0:T(8,128)(2,1)S(1)}, u32[]{:S(2)}) copy-start(bf16[128,2048]{1,0:T(8,128)(2,1)S(1)} %multiply_convert_fusion.2) | copy-start | bytes 1572868
  214.4 159.5 %copy-start.48 = (f32[128]{0:T(128)}, f32[128]{0:T(128)S(1)}, u32[]{:S(2)}) copy-start(f32[128]{0:T(128)S(1)} %get-tuple-element.204) | copy-start | bytes 1540
  214.7 159.2 %copy-start.67 = (f32[128]{0:T(128)}, f32[128]{0:T(128)S(1)}, u32[]{:S(2)}) copy-start(f32[128]{0:T(128)S(1)} %fusion.62) | copy-start | bytes 1540
  372.7 3.7 copy-start.11
  372.7 236.2 %reduce-scatter.5.cloned.1.call-start = ((), (), s32[]{:S(2)}) async-start(), calls=%async_computation.4 | async-start | bytes 10485760 | tf_op jit(solution)/shard_map/reduce_scatter | solution.py:2199
  373.9 46.1 %copy-start.68 = (f32[128]{0:T(128)}, f32[128]{0:T(128)S(1)}, u32[]{:S(2)}) copy-start(f32[128]{0:T(128)S(1)} %multiply_reduce_fusion.7) | copy-start | bytes 1540
  421.2 3.7 copy-start.5
  421.2 3.7 copy-start.28
  421.2 3.7 copy-start.50
  421.2 3.7 copy-start.56
  424.9 2.9 copy-start.77
  432.3 2.6 copy-start.2
  441.2 17.1 %copy-start.37 = (f32[16,128]{1,0:T(8,128)S(1)}, f32[16,128]{1,0:T(8,128)}, u32[]{:S(2)}) copy-start(f32[16,128]{1,0:T(8,128)} %copy-done.36) | copy-start | bytes 24580
  454.0 4.3 copy-start.47
  454.0 4.3 copy-start.3
  454.0 4.4 copy-start.43
  454.0 4.4 copy-start.46
  454.0 4.4 copy-start.63
  454.1 4.4 copy-start.66
  460.7 2.6 copy-start.78
  467.3 5.0 copy-start.19
  467.3 5.0 copy-start.71
  478.1 75.5 %copy-start.14 = (bf16[1,128,2048]{2,1,0:T(8,128)(2,1)S(1)}, bf16[1,128,2048]{2,1,0:T(8,128)(2,1)}, u32[]{:S(2)}) copy-start(bf16[1,128,2048]{2,1,0:T(8,128)(2,1)} %param.15) | copy-start | bytes 1572868
  478.1 75.5 %copy-start.72 = (f32[128]{0:T(128)S(1)}, f32[128]{0:T(128)}, u32[]{:S(2)}) copy-start(f32[128]{0:T(128)} %add_rsqrt_fusion.2) | copy-start | bytes 1540
  478.1 77.2 %copy-start.38 = (f32[32,64]{1,0:T(8,128)S(1)}, f32[32,64]{1,0:T(8,128)}, u32[]{:S(2)}) copy-start(f32[32,64]{1,0:T(8,128)} %reshape_squeeze.6) | copy-start | bytes 24580
  478.1 77.2 %copy-start.39 = (f32[32,64]{1,0:T(8,128)S(1)}, f32[32,64]{1,0:T(8,128)}, u32[]{:S(2)}) copy-start(f32[32,64]{1,0:T(8,128)} %reshape_squeeze.7) | copy-start | bytes 24580
  478.1 77.2 %copy-start.40 = (f32[32,64]{1,0:T(8,128)S(1)}, f32[32,64]{1,0:T(8,128)}, u32[]{:S(2)}) copy-start(f32[32,64]{1,0:T(8,128)} %reshape.277) | copy-start | bytes 24580
  553.5 52.9 %copy-start.74 = (f32[128]{0:T(128)S(1)}, f32[128]{0:T(128)}, u32[]{:S(2)}) copy-start(f32[128]{0:T(128)} %get-tuple-element.182) | copy-start | bytes 1540
  553.5 54.3 %copy-start.26 = (f32[128,2048]{1,0:T(8,128)S(1)}, f32[128,2048]{1,0:T(8,128)}, u32[]{:S(2)}) copy-start(f32[128,2048]{1,0:T(8,128)} %get-tuple-element.77) | copy-start | bytes 3145732
  613.3 3.7 copy-start.32
  613.3 4.5 copy-start.31
  615.7 2.9 copy-start.30
  615.7 3.7 copy-start.29
  (36 other events, 70.9 us)
Sparse Core Ops, SparseCore 0:
  116.5 47.0 all-gather.1
  372.8 85.8 reduce-scatter.2
  462.1 122.8 reduce-scatter.4

commit v5 on v4

--- a/solution.py
+++ b/solution.py
@@ -550,9 +550,21 @@
             def _(a=a, near=near):
                 forward(a, near, 1)
 
-            if a == 0 and j == (chips - 1) // 2:
+        if a == 0 and len(p_refs) > 1:
+
+            @pl.when((chip > 0) & (chip < chips - 1))
+            def _():
                 plane.start_later()
 
+    if len(p_refs) > 1:
+
+        @pl.when((chip == 0) | (chip == chips - 1))
+        def _():
+            plane.start_later()
+
+    else:
+        plane.start_later()
+    for a in kinds:
         finish(a)
 
     for a in kinds:
@@ -802,17 +814,22 @@
             to[:, e * own : (e + 1) * own] = qkv_box[e, :, m * own : (m + 1) * own].astype(F32)
 
 
-def last_exchange(small, qkv, out, collective_id):
+def last_exchange(small, qkv, out, after, collective_id):
     groups, seqs = lax.axis_size("expert"), lax.axis_size("dp")
     total = groups * seqs
     block, width = out.shape
     vmem = pl.BlockSpec(memory_space=pltpu.VMEM)
     dma = pltpu.SemaphoreType.DMA
     matrix = jax.ShapeDtypeStruct((block, width), F32)
+    held = len(after)
+
+    def kernel(*refs):
+        last_body(groups, seqs, *refs[:3], *refs[3 + held :])
+
     return pl.pallas_call(
-        functools.partial(last_body, groups, seqs),
+        kernel,
         out_shape=[jax.ShapeDtypeStruct(small.shape[1:], F32)] + [matrix] * 4,
-        in_specs=[vmem] * 3,
+        in_specs=[vmem] * 3 + [pl.BlockSpec(memory_space=pl.ANY)] * held,
         out_specs=[vmem] * 5,
         scratch_shapes=[
             pltpu.VMEM(small.shape, F32),
@@ -825,7 +842,7 @@
         ),
         cost_estimate=cost_of(25),
         name="last_exchange",
-    )(small, qkv, out)
+    )(small, qkv, out, *after)
 
 
 def exchange_body(count, spread, same, reduce, plane, x_ref, o_ref, box, send, recv):
@@ -1340,50 +1357,56 @@
     )(x, g_all, w_gate, w_up, w_down, *near)
 
 
-class ExpertSum:
-    def __init__(self, size, ref, out, first, mid, own, near, load, send, recv):
+class Blocks:
+    def __init__(self, ref, size, half_stride, owner_stride):
         self.me, self.dp = lax.axis_index("expert"), lax.axis_index("dp")
-        self.size, self.ref, self.out = size, ref, out
-        self.first, self.mid, self.own, self.near = first, mid, own, near
-        self.load_sem, self.send, self.recv = load, send, recv
+        self.ref, self.size = ref, size
+        self.half_stride, self.owner_stride = half_stride, owner_stride
         x, y = flipped(self.dp, 1), flipped(self.dp, 2)
         self.owners = (self.dp, x, y, flipped(x, 2))
-        self.stride = ref.shape[0] // 2
+
+    def piece(self, half, q):
+        start = half * self.half_stride + self.owners[q] * self.owner_stride
+        return self.ref.at[pl.ds(pl.multiple_of(start, self.size), self.size)]
+
+    def remote(self, src, dst, send, recv, flip):
+        return pltpu.make_async_remote_copy(
+            src_ref=src, dst_ref=dst, send_sem=send, recv_sem=recv,
+            device_id=(flipped(self.dp, flip), self.me), device_id_type=MESH,
+        )
+
+
+class SumEarly:
+    def __init__(self, blocks, first, mid, near_out, mid_out, load, send, recv):
+        self.me, self.dp = blocks.me, blocks.dp
+        self.blocks, self.first, self.mid = blocks, first, mid
+        self.near_out, self.mid_out = near_out, mid_out
+        self.load_sem, self.send, self.recv = load, send, recv
 
     def busy(self):
         return True
 
     greet = Plane.greet
 
-    def piece(self, e, q):
-        return self.ref.at[
-            pl.ds(pl.multiple_of(e * self.stride + self.owners[q] * self.size, self.size), self.size)
+    def copy(self, i):
+        b = self.blocks
+        src, dst = (
+            (b.piece(0, 3), self.first.at[0]),
+            (b.piece(1, 3), self.first.at[1]),
+            (b.piece(0, 1), self.near_out.at[0]),
+            (b.piece(1, 2), self.near_out.at[1]),
+        )[i]
+        return b.remote(src, dst, self.send.at[i], self.recv.at[i], i % 2 + 1)
+
+    def loads(self):
+        b = self.blocks
+        return [
+            pltpu.make_async_copy(b.piece(0, 2), self.mid.at[0], self.load_sem.at[0]),
+            pltpu.make_async_copy(b.piece(1, 1), self.mid.at[1], self.load_sem.at[1]),
         ]
 
-    def copy(self, i):
-        src, dst, flip = (
-            (self.piece(0, 3), self.first.at[0], 1),
-            (self.piece(1, 3), self.first.at[1], 2),
-            (self.piece(0, 1), self.near.at[0, 0], 1),
-            (self.piece(1, 2), self.near.at[1, 1], 2),
-            (self.mid.at[1], self.near.at[0, 1], 1),
-            (self.mid.at[0], self.near.at[1, 0], 2),
-        )[i]
-        return pltpu.make_async_remote_copy(
-            src_ref=src, dst_ref=dst, send_sem=self.send.at[i], recv_sem=self.recv.at[i],
-            device_id=(flipped(self.dp, flip), self.me), device_id_type=MESH,
-        )
-
-    def loads(self):
-        return [
-            pltpu.make_async_copy(src, dst, self.load_sem.at[i])
-            for i, (src, dst) in enumerate(
-                (
-                    (self.piece(0, 2), self.mid.at[0]), (self.piece(1, 1), self.mid.at[1]),
-                    (self.piece(0, 0), self.own.at[0]), (self.piece(1, 0), self.own.at[1]),
-                )
-            )
-        ]
+    def keep(self):
+        return pltpu.make_async_copy(self.mid, self.mid_out, self.load_sem.at[2])
 
     def start(self):
         for i in range(4):
@@ -1391,7 +1414,7 @@
         for copy in self.loads():
             copy.start()
 
-    def relay(self):
+    def start_later(self):
         for copy in self.loads():
             copy.wait()
         for i in range(2):
@@ -1403,36 +1426,90 @@
                 self.mid[i, here] = value.astype(BF16)
                 return carry
 
-            lax.fori_loop(0, self.size // 16, body, 0)
-        for i in (4, 5):
+            lax.fori_loop(0, self.blocks.size // 16, body, 0)
+        self.keep().start()
+
+    def finish(self):
+        for i in range(4):
+            if i >= 2:
+                self.copy(i).wait_recv()
+            self.copy(i).wait_send()
+        self.keep().wait()
+
+
+class SumLate:
+    def __init__(self, blocks, mid_ref, near_ref, late, near, own, out, load, send, recv):
+        self.blocks, self.mid_ref, self.near_ref = blocks, mid_ref, near_ref
+        self.late, self.near, self.own, self.out = late, near, own, out
+        self.load_sem, self.send, self.recv = load, send, recv
+
+    def copy(self, i):
+        return self.blocks.remote(
+            self.mid_ref.at[1 - i], self.late.at[1 - i], self.send.at[i], self.recv.at[i], i + 1
+        )
+
+    def loads(self):
+        b = self.blocks
+        return [
+            pltpu.make_async_copy(b.piece(0, 0), self.own.at[0], self.load_sem.at[0]),
+            pltpu.make_async_copy(b.piece(1, 0), self.own.at[1], self.load_sem.at[1]),
+            pltpu.make_async_copy(self.near_ref, self.near, self.load_sem.at[2]),
+        ]
+
+    def start(self):
+        for i in range(2):
             self.copy(i).start()
+        for copy in self.loads():
+            copy.start()
+
+    def start_later(self):
+        pass
 
     def finish(self):
-        for i in range(2, 6):
-            self.copy(i).wait_recv()
-        for e in range(2):
-
-            def body(t, carry, e=e):
+        for copy in self.loads():
+            copy.wait()
+        for i in range(2):
+            self.copy(i).wait()
+        for half in range(2):
+
+            def body(t, carry, half=half):
                 here = pl.ds(pl.multiple_of(t * 16, 16), 16)
-                value = self.own[e, here].astype(F32)
-                for side in range(2):
-                    value = value + self.near[side, e, here].astype(F32)
-                self.own[e, here] = value.astype(BF16)
+                value = self.own[half, here].astype(F32) + self.near[half, here].astype(F32)
+                value = value + self.late[half, here].astype(F32)
+                self.out[half, here] = value.astype(BF16)
                 return carry
 
-            lax.fori_loop(0, self.size // 16, body, 0)
-        keep = pltpu.make_async_copy(self.own, self.out, self.load_sem.at[0])
-        keep.start()
-        for i in range(6):
-            self.copy(i).wait_send()
-        keep.wait()
+            lax.fori_loop(0, self.blocks.size // 16, body, 0)
+
+
+class Several:
+    def __init__(self, parts):
+        self.me, self.dp = lax.axis_index("expert"), lax.axis_index("dp")
+        self.parts = parts
+
+    def busy(self):
+        return True
+
+    greet = Plane.greet
+
+    def start(self):
+        for part in self.parts:
+            part.start()
+
+    def start_later(self):
+        for part in self.parts:
+            part.start_later()
+
+    def finish(self):
+        for part in self.parts:
+            part.finish()
 
 
 def expert_second_body(
     groups, seqs, rows, width, ff, experts, parts,
-    sg_ref, su_ref, tail_ref, f_ref, gate_ref, up_ref, down_ref, near_refs, grad_out, down_out, o_ref,
+    sg_ref, su_ref, tail_ref, f_ref, gate_ref, up_ref, down_ref, near_refs, grad_out, near_out, mid_out, o_ref,
     wg, wu, sg, su, tail_buf, f_buf, stage, acc, pair_in, inbox, last,
-    first, mid, own_block, near_buf,
+    first, mid,
     in_sem, w_sem, stage_sem, pair_send, pair_recv, hop_send, hop_recv, last_recv,
     sum_load, sum_send, sum_recv,
 ):
@@ -1473,9 +1550,8 @@
                 )
     for copy in loads[:3] + weights + loads[3:]:
         copy.start()
-    total = ExpertSum(
-        ff // seqs, down_ref, down_out, first, mid, own_block, near_buf, sum_load, sum_send, sum_recv
-    )
+    blocks = Blocks(down_ref, ff // seqs, ff, ff // seqs)
+    total = SumEarly(blocks, first, mid, near_out, mid_out, sum_load, sum_send, sum_recv)
     line_greet(me, dp, chip, chips, total)
     total.start()
     for copy in loads[:3]:
@@ -1613,7 +1689,7 @@
                 forward(goal(j))
 
         if j == min(1, chips - 1):
-            total.relay()
+            total.start_later()
         for t in range(j * tiles // chips, (j + 1) * tiles // chips):
             grad_tile(t)
 
@@ -1680,10 +1756,11 @@
         out_shape=[
             jax.ShapeDtypeStruct((width, experts * ff), BF16),
             jax.ShapeDtypeStruct((2, size, width), BF16),
+            jax.ShapeDtypeStruct((2, size, width), BF16),
             jax.ShapeDtypeStruct((rows, wide), F32),
         ],
         in_specs=[anywhere] * (7 + n),
-        out_specs=[anywhere, anywhere, pl.BlockSpec(memory_space=pltpu.VMEM)],
+        out_specs=[anywhere] * 3 + [pl.BlockSpec(memory_space=pltpu.VMEM)],
         scratch_shapes=[
             pltpu.VMEM((width, experts * ff), BF16),
             pltpu.VMEM((width, experts * ff), BF16),
@@ -1695,10 +1772,10 @@
             pltpu.VMEM((chips, rows, wide), BF16),
             pltpu.VMEM((chips, rows, wide), BF16),
             pltpu.VMEM((rows, wide), BF16),
-            block, block, block, pltpu.VMEM((2, 2, size, width), BF16),
+            block, block,
             dma((4,)), dma((2, experts, 4)), dma((2,)), dma((chips,)), dma((chips,)),
             dma((chips, parts)), dma((chips, parts)), dma((parts,)),
-            dma((4,)), dma((6,)), dma((6,)),
+            dma((3,)), dma((4,)), dma((4,)),
         ],
         compiler_params=pltpu.CompilerParams(
             collective_id=collective_id, has_side_effects=True, vmem_limit_bytes=60 * 1024 * 1024
@@ -1709,8 +1786,10 @@
 
 
 def gather_fill_body(
-    groups, rows, parts, x_ref, f_ref, su_ref, hid_ref, wd_ref, o_ref, grad_out, y_out,
-    f_buf, su, hid, wd, stage, in_sem, stage_sem, own_sem, send, recv, pair_send, pair_recv,
+    groups, seqs, ff, rows, parts, x_ref, f_ref, su_ref, hid_ref, wd_ref, down_ref, mid_ref, near_ref,
+    o_ref, grad_out, y_out, down_out,
+    f_buf, su, hid, wd, stage, late, near, own_block, in_sem, stage_sem, sum_load, sum_send, sum_recv,
+    own_sem, send, recv, pair_send, pair_recv,
 ):
     chips = groups // 2
     length, width = f_buf.shape
@@ -1751,6 +1830,10 @@
         out_copy(t).start()
 
     turns = max(chips - 1, 1)
+    rest = SumLate(
+        Blocks(down_ref, ff // seqs, ff, ff // seqs), mid_ref, near_ref, late, near, own_block, down_out,
+        sum_load, sum_send, sum_recv,
+    )
 
     def work(k):
         if k < turns:
@@ -1758,40 +1841,47 @@
                 tile(t)
 
     gather_body(
-        groups, rows, parts, Plane((), (), (), (), None, None), x_ref, o_ref,
+        groups, rows, parts, Several([rest]), x_ref, o_ref,
         own_sem, send, recv, pair_send, pair_recv, work=work,
     )
     for t in range(total - 2, total):
         out_copy(t).wait()
 
 
-def gather_fill(x, ffn_all, su, hid, wd, collective_id, parts=4):
-    groups = lax.axis_size("expert")
+def gather_fill(x, ffn_all, su, hid, wd, d_down, mid, near, ff, collective_id, parts=4):
+    groups, seqs = lax.axis_size("expert"), lax.axis_size("dp")
     rows, width = x.shape
     length, hidden = su.shape
-    anywhere = pl.BlockSpec(memory_space=pl.ANY)
+    anywhere, vmem = pl.BlockSpec(memory_space=pl.ANY), pl.BlockSpec(memory_space=pltpu.VMEM)
     dma = pltpu.SemaphoreType.DMA
     line = dma((2, groups // 2, parts))
     tokens = jax.ShapeDtypeStruct((length, width), BF16)
     return pl.pallas_call(
-        functools.partial(gather_fill_body, groups, rows, parts),
-        out_shape=[tokens, jax.ShapeDtypeStruct((width, hidden), BF16), tokens],
-        in_specs=[anywhere] * 5,
-        out_specs=[anywhere] * 3,
+        functools.partial(gather_fill_body, groups, seqs, ff, rows, parts),
+        out_shape=[
+            tokens, jax.ShapeDtypeStruct((width, hidden), BF16), tokens,
+            jax.ShapeDtypeStruct(mid.shape, BF16),
+        ],
+        in_specs=[anywhere] * 8,
+        out_specs=[anywhere] * 3 + [vmem],
         scratch_shapes=[
             pltpu.VMEM((length, width), BF16),
             pltpu.VMEM((length, hidden), BF16),
             pltpu.VMEM((length, hidden), BF16),
             pltpu.VMEM((hidden, width), BF16),
             pltpu.VMEM((2, 256, max(hidden, width)), BF16),
-            dma((4,)), dma((2,)), dma, line, line, line, line,
+            pltpu.VMEM(mid.shape, BF16),
+            pltpu.VMEM(mid.shape, BF16),
+            pltpu.VMEM(mid.shape, BF16),
+            dma((4,)), dma((2,)), dma((3,)), dma((2,)), dma((2,)),
+            dma, line, line, line, line,
         ],
         compiler_params=pltpu.CompilerParams(
             collective_id=collective_id, has_side_effects=True, vmem_limit_bytes=VMEM_LIMIT
         ),
         cost_estimate=cost_of(45),
         name="gather_fill",
-    )(x, ffn_all, su, hid, wd)
+    )(x, ffn_all, su, hid, wd, d_down, mid, near)
 
 
 class Opening:
@@ -1799,15 +1889,12 @@
         self.sends, self.arrived, self.wholes = sends, arrived, wholes
 
     def start(self):
-        for i in (0, 1):
-            self.sends.copy(i).start()
+        pass
 
     def start_mid(self):
         self.arrived()
         for whole in self.wholes:
             whole.start()
-        for i in (2, 3):
-            self.sends.copy(i).start()
 
     def start_later(self):
         for whole in self.wholes:
@@ -1880,9 +1967,6 @@
         device_id=device(moved), device_id_type=MESH,
     )
     stay = pltpu.make_async_copy(out_ref, out_to, out_sem.at[0])
-    for copy in spread:
-        copy.start()
-
     @pl.when(moved != mine)
     def _():
         away.start()
@@ -1891,14 +1975,19 @@
     def _():
         stay.start()
 
+    sends = Plane(
+        [(0, 0, 1, 1), (0, 0, 1, 2), (0, 1, 1, 1), (0, 1, 1, 2)], (), [gate_ref], gate_refs,
+        plane_send, plane_recv,
+    )
+    sends.start()
+    for copy in spread:
+        copy.start()
     for copy in own:
         copy.start()
     box[mine] = small_ref[...]
     out_small = pltpu.make_async_copy(box, small_to, small_sem)
 
     def arrived():
-        lax.fori_loop(1, total, wait, 0)
-        out_small.start()
         for copy in own + spread:
             copy.wait()
 
@@ -1910,10 +1999,6 @@
         def _():
             stay.wait()
 
-    sends = Plane(
-        [(0, 0, 1, 1), (0, 0, 1, 2), (0, 1, 1, 1), (0, 1, 1, 2)], (), [gate_ref], gate_refs,
-        plane_send, plane_recv,
-    )
     wholes = [
         Whole(a, b, whole_own.at[i], whole_send.at[i], whole_recv.at[i])
         for i, (a, b) in enumerate(((spread_to, qkv_to), (out_to, wo_to)))
@@ -1922,6 +2007,8 @@
         groups, rows, parts, Opening(sends, arrived, wholes), x_ref, x_to,
         keep_sem, line_send, line_recv, pair_send, pair_recv, greet=False,
     )
+    lax.fori_loop(1, total, wait, 0)
+    out_small.start()
     out_small.wait()
 
 
@@ -2150,7 +2237,7 @@
             jnp.concatenate([ffn_low, extra], axis=1), g_all, w_gate, w_up, w_down,
             gate_near + up_near, 9,
         )
-        d_gate_w, own_down, d_rows = expert_second(
+        d_gate_w, down_near, down_mid, d_rows = expert_second(
             d_gate, d_up, tail, ffn_all, d_down, w_gate, w_up, gate_near + up_near, 13
         )
         d_weight = d_rows[:, width : width + LANES]
@@ -2204,7 +2291,7 @@
     if not fused:
         own_down = lax.psum_scatter(d_down, "dp", scatter_dimension=1, tiled=True)
         d_gate_w = dot_tn(ffn_all, d_gate).astype(BF16)
-    own_gate = scatter_in(d_gate_w)
+    own_gate = to_experts(scatter_in(d_gate_w))
     d_router_prob = d_weight * chosen_mask
 
     d_logits = (
@@ -2215,8 +2302,9 @@
     d_after_norm, d_gain_ffn = norm_back(after_attn, inv_ffn, g_ffn, d_normed_ffn)
     d_after = g_low.astype(F32) + d_after_norm
     if fused:
-        d_after_all, d_up_w, y_part = gather_fill(
-            d_after.astype(BF16), ffn_all, d_up, hidden_w, wd.reshape(local_experts * ff, width), 11
+        d_after_all, d_up_w, y_part, own_down = gather_fill(
+            d_after.astype(BF16), ffn_all, d_up, hidden_w, wd.reshape(local_experts * ff, width),
+            d_down, down_mid, down_near, ff, 11,
         )
     else:
         d_after_all = line_gather(d_after.astype(BF16), 16)
@@ -2280,7 +2368,10 @@
     )
     small_grad = small_grad.reshape(total, small_rows, 128)
     if own % 128 == 0:
-        small_grad, *matrices = last_exchange(small_grad, own_qkv, own_out, 8)
+        output, input_grad = (a.reshape(1, rows, width) for a in (output, input_grad))
+        small_grad, *matrices = last_exchange(
+            small_grad, own_qkv, own_out, [output, input_grad], 8
+        )
     else:
         small_grad = exchange(small_grad, 8, spread=True, reduce=True)
         own_qkv = exchange(own_qkv.reshape(groups, block, 3 * own), 7)
@@ -2288,7 +2379,7 @@
         own_out = lax.ppermute(own_out, ("dp", "expert"), [(b, a) for a, b in moves])
         matrices = [*own_qkv.reshape(3, block, width).astype(F32), own_out.astype(F32)]
     small_grad = small_grad.reshape(-1)
-    expert_owned = [to_experts(own_gate), to_experts(own_up), own_down.astype(F32)]
+    expert_owned = [own_gate, to_experts(own_up), own_down.astype(F32)]
     return (
         output.reshape(1, rows, width),
         input_grad.reshape(1, rows, width),

time: 638 us -> 626 us (0.981)
    pallas_call x1, Pallas kernels: 76.5 us -> 58.2 us  [expert_second(): pl.pallas_call(kernel, out_shape=[jax.ShapeDtypeStruct((width, experts *...]
    pallas_call x2, Pallas kernels: 89.7 us -> 102 us  [the longest x1 54.6 us: gather_fill(): pl.pallas_call(functools.partial(gather_fill_body, groups, seqs, ff, rows...]
    unnamed x167 -> x83, local copies, waits for them, and re-layouts: 17.3 us -> 15 us
  transfers between devices with their start and end apart: 5 -> 5, of which waited for: 2 -> 2; matrix products, arithmetic and copies ran while one was open for 13% -> 14% of each run, Pallas kernels for 37% -> 40%
where the time goes in v5:
time: 626 us; the launch traced here: 619 us
  Pallas kernels  483 us (77%)
  matrix products  40.1 us (6%)
  other arithmetic  37.1 us (6%)
  local copies, waits for them, and re-layouts  30.6 us (5%)
  between operations  14.7 us (2%)
  starting transfers between devices  7.05 us (1%)
    pallas_call x1, Pallas kernels, opening(): pl.pallas_call(kernel, out_shape=[jax.ShapeDtypeStruct((groups * rows, wi...  97 us
    pallas_call x1, Pallas kernels, expert_first(): pl.pallas_call(kernel, out_shape=[jax.ShapeDtypeStruct((length, width), B...  81.2 us
    pallas_call x1, Pallas kernels, joint_reduce(): pl.pallas_call(kernel, out_shape=[jax.ShapeDtypeStruct((rows, width), F32...  77.8 us
    pallas_call x3, Pallas kernels, run(): pl.pallas_call(kernel, out_shape=[out] + targets + whole_out + [jax.Shape...  66.4 us
    pallas_call x1, Pallas kernels, expert_second(): pl.pallas_call(kernel, out_shape=[jax.ShapeDtypeStruct((width, experts *...  58.2 us
    pallas_call x1, Pallas kernels, gather_fill(): pl.pallas_call(functools.partial(gather_fill_body, groups, seqs, ff, rows...  54.6 us
    pallas_call x1, Pallas kernels, last_exchange(): pl.pallas_call(kernel, out_shape=[jax.ShapeDtypeStruct(small.shape[1:], F...  47.5 us
    unnamed x83, local copies, waits for them, and re-layouts  15 us
  transfers between devices with their start and end apart: 5, of which 2 were waited for; matrix products, arithmetic and copies ran while one was open for 14% of the time, Pallas kernels for 40%

profile of v5, /device:TPU:5, one launch (start us, length us, event | category | flops | bytes accessed | tf_op | source)
XLA Modules:
  0.0 618.5 jit_solution(16658012976618110347)
XLA Ops:
  7.2 1.9 copy.63
  10.0 3.3 concatenate.39
  13.3 97.0 %opening.1 = (bf16[1024,2048]{1,0:T(8,128)(2,1)}, bf16[32,16,128]{2,1,0:T(8,128)(2,1)}, bf16[2048,768]{1,0:T(8,128)(2,1)}, bf16[256,2048]{1,0:T(8,128)(2,1)}, bf...) custom-call(bf16[128,2048]{1,0:T(8,128)(2,1)} %bitcast.160, ...), custom_call_target="tpu_custom_call", output_to_operand_aliasing={{10}: (7, {})} | custom-call | bytes 240000000 | tf_op jit(solution)/shard_map/opening/pallas_call | solution.py:2030
  110.4 1.3 collective-permute-start.1
  111.6 5.6 collective-permute-start
  117.4 3.1 fusion
  120.7 8.8 %fusion.10 = f32[1024,768]{0,1:T(8,128)} fusion(bf16[2048,768]{1,0:T(8,128)(2,1)} %get-tuple-element.55, bf16[1024,2048]{1,0:T(8,128)(2,1)} %get-tuple-element.53, f32[2048]{0:T(1024)S(1)} %reshape.281, f32[1024]{0:T(1024)S(1)} %add_rsqrt_fusion.1), kind=kOutput, calls=%fused_computation.47 | convolution fusion | flops 3229614080 | bytes 10498048 | tf_op jit(solution)/shard_map/dot_general | solution.py:23
  130.4 2.2 slice.329
  132.5 1.7 multiply_reduce_fusion.6
  134.9 8.0 %exchange.2 = f32[16,128]{1,0:T(8,128)} custom-call(f32[1,16,128]{2,1,0:T(8,128)} %reshape.267.refs_0_), custom_call_target="tpu_custom_call" | custom-call | bytes 24000000 | tf_op jit(solution)/shard_map/exchange/pallas_call | solution.py:936
  142.9 1.0 multiply_cosine_fusion
  144.8 1.8 multiply_multiply_fusion
  152.9 3.3 convolution_convert_fusion.refs_0_
  156.2 1.3 collective-permute-done.1.refs_4_.refs_11_.refs_12_.refs_13_.refs_14_
  157.5 4.9 collective-permute-done.refs_3_.refs_13_.refs_14_.refs_15_.refs_16_
  162.3 50.0 %line_reduce.1 = (f32[128,2048]{1,0:T(8,128)}, bf16[1,512,1024]{2,1,0:T(8,128)(2,1)}, bf16[1,512,1024]{2,1,0:T(8,128)(2,1)}, bf16[1,512,1024]{2,1,0:T(8,128)(2,1)}, bf16[1,512,1024]{2,1,0:T(8,128)(2,1)}) custom-call(bf16[1024,2048]{1,0:T(8,128)(2,1)} %convolution_convert_fusion.refs_0_, bf16[1,512,1024]{2,1,0:T(8,128)(2,1)} %get-tuple-element.57.refs_1_.refs_7_.refs_9_, ...), custom_call_target="tpu_custom_call" | custom-call | bytes 120000000 | tf_op jit(solution)/shard_map/line_reduce/pallas_call | solution.py:936
  212.3 1.5 multiply_reduce_fusion.4
  214.8 1.0 concatenate.45.refs_0_
  215.7 81.2 %expert_first.1 = (bf16[1024,2048]{1,0:T(8,128)(2,1)}, bf16[1024,2048]{1,0:T(8,128)(2,1)}, bf16[1024,2048]{1,0:T(8,128)(2,1)}, bf16[1024,2048]{1,0:T(8,128)(2,1)...) custom-call(bf16[128,2176]{1,0:T(8,128)(2,1)} %concatenate.45.refs_0_, ...), custom_call_target="tpu_custom_call" | custom-call | bytes 210000000 | tf_op jit(solution)/shard_map/expert_first/pallas_call | solution.py:1326
  296.9 58.2 %expert_second.1 = (bf16[2048,2048]{1,0:T(8,128)(2,1)}, bf16[2,256,2048]{2,1,0:T(8,128)(2,1)}, bf16[2,256,2048]{2,1,0:T(8,128)(2,1)}, f32[128,2176]{1,0:T(8,128)}) custom-call(bf16[1024,2048]{1,0:T(8,128)(2,1)} %get-tuple-element.68.refs_0_, bf16[1024,2048]{1,0:T(8,128)(2,1)} %get-tuple-element.69.refs_1_.su_ref, ...), custom_call_target="tpu_custom_call" | custom-call | bytes 195000000 | tf_op jit(solution)/shard_map/expert_second/pallas_call | solution.py:1754
  355.2 1.1 multiply_reduce_fusion.7
  356.3 1.9 multiply_reduce_fusion.2
  358.2 2.8 fusion.75
  361.0 54.6 %gather_fill.1 = (bf16[1024,2048]{1,0:T(8,128)(2,1)}, bf16[2048,2048]{1,0:T(8,128)(2,1)}, bf16[1024,2048]{1,0:T(8,128)(2,1)}, bf16[2,256,2048]{2,1,0:T(8,128)(2,1)}) custom-call(bf16[128,2048]{1,0:T(8,128)(2,1)} %get-tuple-element.162.x_ref, bf16[1024,2048]{1,0:T(8,128)(2,1)} %get-tuple-element.71.refs_3_.f_ref, ...), custom_call_target="tpu_custom_call" | custom-call | bytes 135000000 | tf_op jit(solution)/shard_map/gather_fill/pallas_call | solution.py:1859
  415.7 1.3 fusion.80
  417.7 4.3 convert_element_type.166
  422.0 1.3 convolution_convert_fusion.4
  423.3 1.2 copy-done.3
  425.5 1.1 multiply_convert_fusion
  428.9 1.1 multiply_convert_fusion.1
  432.9 1.3 copy-done.1
  435.3 8.5 %exchange.3 = f32[16,128]{1,0:T(8,128)} custom-call(f32[1,16,128]{2,1,0:T(8,128)} %reshape.272.refs_0_), custom_call_target="tpu_custom_call" | custom-call | bytes 24000000 | tf_op jit(solution)/shard_map/exchange/pallas_call | solution.py:936
  444.9 2.6 fusion.36
  447.5 3.4 convolution_convert_fusion.3.refs_3_
  451.9 1.5 copy-done.4
  454.3 1.3 copy-done.34
  455.6 5.0 convolution_convert_fusion.1.refs_0_
  460.6 5.6 convolution_convert_fusion.2.refs_2_
  466.2 1.7 slice_bitcast_fusion.3
  467.9 2.3 maximum_convert_fusion.refs_4_
  470.2 77.8 %joint_reduce.1 = (f32[128,2048]{1,0:T(8,128)}, f32[128,2048]{1,0:T(8,128)}, bf16[512,768]{1,0:T(8,128)(2,1)}, bf16[64,2048]{1,0:T(8,128)(2,1)}) custom-call(bf16[1024,2048]{1,0:T(8,128)(2,1)} %convolution_convert_fusion.1.refs_0_, bf16[1024,2048]{1,0:T(8,128)(2,1)} %get-tuple-element.79.refs_1_, bf16[2048,768]{1,0:T(8,128)(2,1)} %convolution_convert_fusion.2.refs_2_, ...), custom_call_target="tpu_custom_call" | custom-call | bytes 210000000 | tf_op jit(solution)/shard_map/joint_reduce/pallas_call | solution.py:709
  548.0 1.6 fusion.22
  550.5 2.3 add_bitcast_fusion.refs_3_
  552.9 1.3 fusion.20.refs_4_
  554.1 47.5 %last_exchange.1 = (f32[16,128]{1,0:T(8,128)}, f32[64,2048]{1,0:T(8,128)}, f32[64,2048]{1,0:T(8,128)}, f32[64,2048]{1,0:T(8,128)}, f32[64,2048]{1,0:T(8,128)}) custom-call(f32[32,16,128]{2,1,0:T(8,128)} %bitcast.163, bf16[512,768]{1,0:T(8,128)(2,1)} %get-tuple-element.83.refs_1_, bf16[64,2048]{1,0:T(8,128)(2,1)} %get-tuple-element.84.refs_2_, ...), custom_call_target="tpu_custom_call" | custom-call | bytes 75000000 | tf_op jit(solution)/shard_map/last_exchange/pallas_call | solution.py:829
  603.1 1.4 fusion.78
  604.5 1.7 slice_bitcast_fusion.1
  606.3 2.3 maximum_convert_fusion.1
  (154 shorter events, 27.2 us)
Async XLA Ops:
  7.2 208.5 %all-gather.2.cloned.1.call-start = ((), (), s32[]{:S(2)}) async-start(), calls=%async_computation.2 | async-start | bytes 4718592 | tf_op jit(solution)/shard_map/all_gather | solution.py:2183
  110.4 10.1 %copy-start.30 = (bf16[32,16,128]{2,1,0:T(8,128)(2,1)S(1)}, bf16[32,16,128]{2,1,0:T(8,128)(2,1)}, u32[]{:S(2)}) copy-start(bf16[32,16,128]{2,1,0:T(8,128)(2,1)} %get-tuple-element.54) | copy-start | bytes 393220
  110.4 47.1 %collective-permute-start.1 = (bf16[2,512,1024]{2,1,0:T(8,128)(2,1)}, bf16[2,512,1024]{2,1,0:T(8,128)(2,1)S(1)}, u32[]{:S(2)}, u32[]{:S(2)}) collective-permute-start(bf16[2,512,1024]{2,1,0:T(8,128)(2,1)} %refs_5_.3), channel_id=1, source_target_pairs={{0,8},{8,0},{16,24},{24,16},{1,9},{9,1},{17,25},{25,17},{2,10},{10... | collective-permute-start | bytes 6291464 | tf_op jit(solution)/shard_map/ppermute | solution.py:2062
  111.6 50.7 %collective-permute-start = (bf16[2,512,1024]{2,1,0:T(8,128)(2,1)}, bf16[2,512,1024]{2,1,0:T(8,128)(2,1)}, u32[]{:S(2)}, u32[]{:S(2)}) collective-permute-start(bf16[2,512,1024]{2,1,0:T(8,128)(2,1)} %refs_5_.3), channel_id=1, source_target_pairs={{0,16},{8,24},{16,0},{24,8},{1,17},{9,25},{17,1},{25,9},{2,18},{10... | collective-permute-start | bytes 6291464 | tf_op jit(solution)/shard_map/ppermute | solution.py:2062
  117.3 348.9 %reduce-scatter.3.cloned.1.call-start = ((), (), s32[]{:S(2)}) async-start(), calls=%async_computation.3 | async-start | bytes 10485760 | tf_op jit(solution)/shard_map/reduce_scatter | solution.py:2286
  120.7 8.8 %copy-start.31 = (s32[1,128,8]{1,2,0:T(8,128)S(1)}, s32[1,128,8]{1,2,0:T(8,128)}, u32[]{:S(2)}) copy-start(s32[1,128,8]{1,2,0:T(8,128)} %param.16) | copy-start | bytes 12292
  144.0 2.7 copy-start.11
  144.0 2.7 copy-start.13
  147.4 1.6 copy-start.18
  148.1 2.0 copy-start.2
  148.9 2.6 copy-start.5
  148.9 1.4 copy-start.22
  151.5 0.8 copy-start.28
  151.5 1.3 copy-start.20
  152.3 10.1 %copy-start.29 = (bf16[1024,128]{0,1:T(8,128)(2,1)}, bf16[1024,128]{0,1:T(8,128)(2,1)S(1)}, u32[]{:S(2)}) copy-start(bf16[1024,128]{0,1:T(8,128)(2,1)S(1)} %convolution_convert_fusion.6) | copy-start | bytes 786436
  157.5 4.9 copy-start
  162.3 50.0 %copy-start.9 = (bf16[1,128,2048]{2,1,0:T(8,128)(2,1)S(1)}, bf16[1,128,2048]{2,1,0:T(8,128)(2,1)}, u32[]{:S(2)}) copy-start(bf16[1,128,2048]{2,1,0:T(8,128)(2,1)} %param.15) | copy-start | bytes 1572868
  355.1 3.1 copy-start.8
  355.2 249.4 %reduce-scatter.5.cloned.1.call-start = ((), (), s32[]{:S(2)}) async-start(), calls=%async_computation.4 | async-start | bytes 10485760 | tf_op jit(solution)/shard_map/reduce_scatter | solution.py:2286
  417.6 4.4 copy-start.21
  417.7 4.3 copy-start.32
  422.0 2.5 copy-start.3
  422.0 2.6 copy-start.23
  424.6 2.5 copy-start.35
  425.5 1.1 copy-start.19
  425.5 2.4 copy-start.6
  430.4 1.8 copy-start.12
  430.5 1.8 copy-start.14
  432.3 1.9 copy-start.1
  444.1 3.5 copy-start.33
  447.5 3.5 copy-start.7
  447.5 3.4 copy-start.36
  451.0 2.4 copy-start.4
  453.4 2.2 copy-start.34
  455.6 5.0 copy-start.15
  470.2 77.8 %copy-start.10 = (bf16[1,128,2048]{2,1,0:T(8,128)(2,1)S(1)}, bf16[1,128,2048]{2,1,0:T(8,128)(2,1)}, u32[]{:S(2)}) copy-start(bf16[1,128,2048]{2,1,0:T(8,128)(2,1)} %param.15) | copy-start | bytes 1572868
  548.0 4.9 copy-start.16
  549.8 3.1 copy-start.17
  606.2 2.3 copy-start.27
  606.2 3.1 copy-start.26
  606.3 3.9 copy-start.25
  606.3 4.7 copy-start.24
Sparse Core Ops, SparseCore 0:
  117.4 47.0 all-gather.1
  355.3 110.4 reduce-scatter.2
  469.2 117.9 reduce-scatter.4

commit v6 on v5

--- a/solution.py
+++ b/solution.py
@@ -550,11 +550,11 @@
             def _(a=a, near=near):
                 forward(a, near, 1)
 
-        if a == 0 and len(p_refs) > 1:
-
-            @pl.when((chip > 0) & (chip < chips - 1))
-            def _():
-                plane.start_later()
+            if a == 0 and j == (chips - 1) // 2:
+
+                @pl.when((chip > 0) & (chip < chips - 1))
+                def _():
+                    plane.start_later()
 
     if len(p_refs) > 1:
 
@@ -2012,7 +2012,7 @@
     out_small.wait()
 
 
-def opening(x, small, w_out, w_query, w_key, w_value, w_gate, copies, slab, carry, collective_id, parts=4):
+def opening(x, small, w_out, w_query, w_key, w_value, w_gate, copies, slab, collective_id, parts=4):
     groups, seqs = lax.axis_size("expert"), lax.axis_size("dp")
     total = groups * seqs
     block, width = w_query.shape
@@ -2020,8 +2020,8 @@
     gate = jax.ShapeDtypeStruct((1,) + w_gate.shape[1:], BF16)
 
     def kernel(*refs):
-        ins, refs = refs[:7], refs[8:]
-        outs, gates, rest = refs[:6], refs[6:10], refs[11:]
+        ins, refs = refs[:7], refs[7:]
+        outs, gates, rest = refs[:6], refs[6:10], refs[10:]
         opening_body(groups, seqs, copies, slab, rows, parts, gates, *ins, *outs, *rest)
 
     vmem, anywhere = pl.BlockSpec(memory_space=pltpu.VMEM), pl.BlockSpec(memory_space=pl.ANY)
@@ -2037,11 +2037,9 @@
             jax.ShapeDtypeStruct((block, width), BF16),
             jax.ShapeDtypeStruct((groups * block, 3 * slab), BF16),
         ]
-        + [gate] * 4
-        + [jax.ShapeDtypeStruct(carry.shape, carry.dtype)],
-        in_specs=[anywhere, vmem] + [anywhere] * 6,
-        out_specs=[anywhere] * 11,
-        input_output_aliases={7: 10},
+        + [gate] * 4,
+        in_specs=[anywhere, vmem] + [anywhere] * 5,
+        out_specs=[anywhere] * 10,
         scratch_shapes=[pltpu.VMEM((total,) + small.shape, small.dtype)]
         + [dma((total,)), dma((total,)), dma((2,)), dma((3,)), dma((groups, 3)), dma((groups, 3)), dma]
         + [dma((4,)), dma((4,)), dma((2,)), dma((2, 4)), dma((2, 4))]
@@ -2049,7 +2047,7 @@
         compiler_params=pltpu.CompilerParams(collective_id=collective_id, has_side_effects=True),
         cost_estimate=cost_of(80),
         name="opening",
-    )(x, small, w_out, w_query, w_key, w_value, w_gate, carry)
+    )(x, small, w_out, w_query, w_key, w_value, w_gate)
 
 
 def both(array, start=0, size=None):
@@ -2151,9 +2149,9 @@
         [w_router.reshape(-1), gain_attn, gain_query, gain_key, gain_ffn,
          jnp.zeros((small_rows * 128 - small_size,), BF16)]
     )
-    x_all, small_all, w_qkv, w_o, _, _, gate0_x, gate0_y, gate1_x, gate1_y, g_low = opening(
+    x_all, small_all, w_qkv, w_o, _, _, gate0_x, gate0_y, gate1_x, gate1_y = opening(
         x_low, small.reshape(small_rows, 128), w_out, w_query, w_key, w_value, w_gate, copies, slab,
-        g_low, 1,
+        1,
     )
     small_all = small_all.reshape(seqs * groups, small_rows * 128)
     split = block * all_experts

time: 626 us -> 624 us (level)
    unnamed x83 -> x82, local copies, waits for them, and re-layouts: 15 us -> 13.1 us
where the time goes in v6:
time: 624 us; the launch traced here: 617 us
  Pallas kernels  483 us (77%)
  matrix products  40.2 us (6%)
  other arithmetic  37 us (6%)
  local copies, waits for them, and re-layouts  28.7 us (5%)
  between operations  14.7 us (2%)
  starting transfers between devices  7.05 us (1%)
    pallas_call x1, Pallas kernels, opening(): pl.pallas_call(kernel, out_shape=[jax.ShapeDtypeStruct((groups * rows, wi...  97 us
    pallas_call x1, Pallas kernels, expert_first(): pl.pallas_call(kernel, out_shape=[jax.ShapeDtypeStruct((length, width), B...  81.1 us
    pallas_call x1, Pallas kernels, joint_reduce(): pl.pallas_call(kernel, out_shape=[jax.ShapeDtypeStruct((rows, width), F32...  77.7 us
    pallas_call x3, Pallas kernels, run(): pl.pallas_call(kernel, out_shape=[out] + targets + whole_out + [jax.Shape...  66.3 us
    pallas_call x1, Pallas kernels, expert_second(): pl.pallas_call(kernel, out_shape=[jax.ShapeDtypeStruct((width, experts *...  58.3 us
    pallas_call x1, Pallas kernels, gather_fill(): pl.pallas_call(functools.partial(gather_fill_body, groups, seqs, ff, rows...  54.8 us
    pallas_call x1, Pallas kernels, last_exchange(): pl.pallas_call(kernel, out_shape=[jax.ShapeDtypeStruct(small.shape[1:], F...  47.6 us
    dot_general x7, matrix products, dot(): return jnp.dot(left, right, preferred_element_type=F32)  14.8 us
  transfers between devices with their start and end apart: 5, of which 2 were waited for; matrix products, arithmetic and copies ran while one was open for 14% of the time, Pallas kernels for 40%

profile of v6, /device:TPU:5, one launch (start us, length us, event | category | flops | bytes accessed | tf_op | source)
XLA Modules:
  0.0 616.8 jit_solution(16499244677577264611)
XLA Ops:
  8.1 3.3 concatenate.39
  11.4 97.0 %opening.1 = (bf16[1024,2048]{1,0:T(8,128)(2,1)}, bf16[32,16,128]{2,1,0:T(8,128)(2,1)}, bf16[2048,768]{1,0:T(8,128)(2,1)}, bf16[256,2048]{1,0:T(8,128)(2,1)}, bf...) custom-call(bf16[128,2048]{1,0:T(8,128)(2,1)} %bitcast.163, ...), custom_call_target="tpu_custom_call" | custom-call | bytes 240000000 | tf_op jit(solution)/shard_map/opening/pallas_call | solution.py:2030
  108.5 1.3 collective-permute-start.1
  109.8 5.6 collective-permute-start
  115.5 3.1 fusion
  118.8 8.8 %fusion.10 = f32[1024,768]{0,1:T(8,128)} fusion(bf16[2048,768]{1,0:T(8,128)(2,1)} %get-tuple-element.54, bf16[1024,2048]{1,0:T(8,128)(2,1)} %get-tuple-element.52, f32[2048]{0:T(1024)S(1)} %reshape.281, f32[1024]{0:T(1024)S(1)} %add_rsqrt_fusion.1), kind=kOutput, calls=%fused_computation.47 | convolution fusion | flops 3229614080 | bytes 10498048 | tf_op jit(solution)/shard_map/dot_general | solution.py:23
  128.5 2.2 slice.329
  130.6 1.7 multiply_reduce_fusion.6
  133.0 8.0 %exchange.2 = f32[16,128]{1,0:T(8,128)} custom-call(f32[1,16,128]{2,1,0:T(8,128)} %reshape.266.refs_0_), custom_call_target="tpu_custom_call" | custom-call | bytes 24000000 | tf_op jit(solution)/shard_map/exchange/pallas_call | solution.py:936
  141.0 1.0 multiply_cosine_fusion
  142.9 1.8 multiply_multiply_fusion
  151.0 3.3 convolution_convert_fusion.refs_0_
  154.3 1.3 collective-permute-done.1.refs_4_.refs_11_.refs_12_.refs_13_.refs_14_
  155.6 4.9 collective-permute-done.refs_3_.refs_13_.refs_14_.refs_15_.refs_16_
  160.5 50.0 %line_reduce.1 = (f32[128,2048]{1,0:T(8,128)}, bf16[1,512,1024]{2,1,0:T(8,128)(2,1)}, bf16[1,512,1024]{2,1,0:T(8,128)(2,1)}, bf16[1,512,1024]{2,1,0:T(8,128)(2,1)}, bf16[1,512,1024]{2,1,0:T(8,128)(2,1)}) custom-call(bf16[1024,2048]{1,0:T(8,128)(2,1)} %convolution_convert_fusion.refs_0_, bf16[1,512,1024]{2,1,0:T(8,128)(2,1)} %get-tuple-element.56.refs_1_.refs_7_.refs_9_, ...), custom_call_target="tpu_custom_call" | custom-call | bytes 120000000 | tf_op jit(solution)/shard_map/line_reduce/pallas_call | solution.py:936
  210.5 1.5 multiply_reduce_fusion.4
  212.9 1.0 concatenate.45.refs_0_
  213.9 81.1 %expert_first.1 = (bf16[1024,2048]{1,0:T(8,128)(2,1)}, bf16[1024,2048]{1,0:T(8,128)(2,1)}, bf16[1024,2048]{1,0:T(8,128)(2,1)}, bf16[1024,2048]{1,0:T(8,128)(2,1)...) custom-call(bf16[128,2176]{1,0:T(8,128)(2,1)} %concatenate.45.refs_0_, ...), custom_call_target="tpu_custom_call" | custom-call | bytes 210000000 | tf_op jit(solution)/shard_map/expert_first/pallas_call | solution.py:1326
  295.1 58.3 %expert_second.1 = (bf16[2048,2048]{1,0:T(8,128)(2,1)}, bf16[2,256,2048]{2,1,0:T(8,128)(2,1)}, bf16[2,256,2048]{2,1,0:T(8,128)(2,1)}, f32[128,2176]{1,0:T(8,128)}) custom-call(bf16[1024,2048]{1,0:T(8,128)(2,1)} %get-tuple-element.66.refs_0_, bf16[1024,2048]{1,0:T(8,128)(2,1)} %get-tuple-element.67.refs_1_.su_ref, ...), custom_call_target="tpu_custom_call" | custom-call | bytes 195000000 | tf_op jit(solution)/shard_map/expert_second/pallas_call | solution.py:1754
  353.5 1.1 multiply_reduce_fusion.7
  354.6 1.9 multiply_reduce_fusion.2
  356.5 2.8 fusion.75
  359.2 54.8 %gather_fill.1 = (bf16[1024,2048]{1,0:T(8,128)(2,1)}, bf16[2048,2048]{1,0:T(8,128)(2,1)}, bf16[1024,2048]{1,0:T(8,128)(2,1)}, bf16[2,256,2048]{2,1,0:T(8,128)(2,1)}) custom-call(bf16[128,2048]{1,0:T(8,128)(2,1)} %get-tuple-element.160.x_ref, bf16[1024,2048]{1,0:T(8,128)(2,1)} %get-tuple-element.69.refs_3_.f_ref, ...), custom_call_target="tpu_custom_call" | custom-call | bytes 135000000 | tf_op jit(solution)/shard_map/gather_fill/pallas_call | solution.py:1859
  414.1 1.3 fusion.80
  416.2 4.3 convert_element_type.166
  420.5 1.3 convolution_convert_fusion.4
  421.7 1.2 copy-done.3
  424.0 1.1 multiply_convert_fusion
  426.3 0.9 multiply_reduce_fusion.1
  427.3 1.1 multiply_convert_fusion.1
  431.3 1.3 copy-done.1
  433.8 8.3 %exchange.3 = f32[16,128]{1,0:T(8,128)} custom-call(f32[1,16,128]{2,1,0:T(8,128)} %reshape.272.refs_0_), custom_call_target="tpu_custom_call" | custom-call | bytes 24000000 | tf_op jit(solution)/shard_map/exchange/pallas_call | solution.py:936
  443.2 2.6 fusion.36
  445.8 3.4 convolution_convert_fusion.3.refs_3_
  450.1 1.5 copy-done.4
  452.5 1.3 copy-done.34
  453.8 5.0 convolution_convert_fusion.1.refs_0_
  458.8 5.6 convolution_convert_fusion.2.refs_2_
  464.5 1.7 slice_bitcast_fusion.3
  466.2 2.3 maximum_convert_fusion.refs_4_
  468.5 77.7 %joint_reduce.1 = (f32[128,2048]{1,0:T(8,128)}, f32[128,2048]{1,0:T(8,128)}, bf16[512,768]{1,0:T(8,128)(2,1)}, bf16[64,2048]{1,0:T(8,128)(2,1)}) custom-call(bf16[1024,2048]{1,0:T(8,128)(2,1)} %convolution_convert_fusion.1.refs_0_, bf16[1024,2048]{1,0:T(8,128)(2,1)} %get-tuple-element.77.refs_1_, bf16[2048,768]{1,0:T(8,128)(2,1)} %convolution_convert_fusion.2.refs_2_, ...), custom_call_target="tpu_custom_call" | custom-call | bytes 210000000 | tf_op jit(solution)/shard_map/joint_reduce/pallas_call | solution.py:709
  546.3 1.6 fusion.22
  548.8 2.3 add_bitcast_fusion.refs_3_
  551.1 1.3 fusion.20.refs_4_
  552.4 47.6 %last_exchange.1 = (f32[16,128]{1,0:T(8,128)}, f32[64,2048]{1,0:T(8,128)}, f32[64,2048]{1,0:T(8,128)}, f32[64,2048]{1,0:T(8,128)}, f32[64,2048]{1,0:T(8,128)}) custom-call(f32[32,16,128]{2,1,0:T(8,128)} %bitcast.167, bf16[512,768]{1,0:T(8,128)(2,1)} %get-tuple-element.81.refs_1_, bf16[64,2048]{1,0:T(8,128)(2,1)} %get-tuple-element.82.refs_2_, ...), custom_call_target="tpu_custom_call" | custom-call | bytes 75000000 | tf_op jit(solution)/shard_map/last_exchange/pallas_call | solution.py:829
  601.4 1.4 fusion.78
  602.8 1.7 slice_bitcast_fusion.1
  604.5 2.3 maximum_convert_fusion.1
  (153 shorter events, 26.2 us)
Async XLA Ops:
  7.2 206.7 %all-gather.3.cloned.1.call-start = ((), (), s32[]{:S(2)}) async-start(), calls=%async_computation.4 | async-start | bytes 4718592 | tf_op jit(solution)/shard_map/all_gather | solution.py:2181
  108.5 10.1 %copy-start.30 = (bf16[32,16,128]{2,1,0:T(8,128)(2,1)S(1)}, bf16[32,16,128]{2,1,0:T(8,128)(2,1)}, u32[]{:S(2)}) copy-start(bf16[32,16,128]{2,1,0:T(8,128)(2,1)} %get-tuple-element.53) | copy-start | bytes 393220
  108.5 47.1 %collective-permute-start.1 = (bf16[2,512,1024]{2,1,0:T(8,128)(2,1)}, bf16[2,512,1024]{2,1,0:T(8,128)(2,1)S(1)}, u32[]{:S(2)}, u32[]{:S(2)}) collective-permute-start(bf16[2,512,1024]{2,1,0:T(8,128)(2,1)} %refs_5_.3), channel_id=1, source_target_pairs={{0,8},{8,0},{16,24},{24,16},{1,9},{9,1},{17,25},{25,17},{2,10},{10... | collective-permute-start | bytes 6291464 | tf_op jit(solution)/shard_map/ppermute | solution.py:2060
  109.8 50.7 %collective-permute-start = (bf16[2,512,1024]{2,1,0:T(8,128)(2,1)}, bf16[2,512,1024]{2,1,0:T(8,128)(2,1)}, u32[]{:S(2)}, u32[]{:S(2)}) collective-permute-start(bf16[2,512,1024]{2,1,0:T(8,128)(2,1)} %refs_5_.3), channel_id=1, source_target_pairs={{0,16},{8,24},{16,0},{24,8},{1,17},{9,25},{17,1},{25,9},{2,18},{10... | collective-permute-start | bytes 6291464 | tf_op jit(solution)/shard_map/ppermute | solution.py:2060
  115.4 349.1 %reduce-scatter.3.cloned.1.call-start = ((), (), s32[]{:S(2)}) async-start(), calls=%async_computation.2 | async-start | bytes 10485760 | tf_op jit(solution)/shard_map/reduce_scatter | solution.py:2284
  118.8 8.8 %copy-start.31 = (s32[1,128,8]{1,2,0:T(8,128)S(1)}, s32[1,128,8]{1,2,0:T(8,128)}, u32[]{:S(2)}) copy-start(s32[1,128,8]{1,2,0:T(8,128)} %param.16) | copy-start | bytes 12292
  142.1 2.7 copy-start.10
  142.1 2.7 copy-start.12
  145.5 1.6 copy-start.18
  146.3 2.0 copy-start.2
  147.0 2.6 copy-start.5
  147.1 1.4 copy-start.22
  149.7 0.8 copy-start.28
  149.7 1.3 copy-start.20
  150.4 10.1 %copy-start.29 = (bf16[1024,128]{0,1:T(8,128)(2,1)}, bf16[1024,128]{0,1:T(8,128)(2,1)S(1)}, u32[]{:S(2)}) copy-start(bf16[1024,128]{0,1:T(8,128)(2,1)S(1)} %convolution_convert_fusion.6) | copy-start | bytes 786436
  155.6 4.9 copy-start
  160.5 50.1 %copy-start.8 = (bf16[1,128,2048]{2,1,0:T(8,128)(2,1)S(1)}, bf16[1,128,2048]{2,1,0:T(8,128)(2,1)}, u32[]{:S(2)}) copy-start(bf16[1,128,2048]{2,1,0:T(8,128)(2,1)} %param.15) | copy-start | bytes 1572868
  353.4 3.1 copy-start.17
  353.4 249.3 %reduce-scatter.5.cloned.1.call-start = ((), (), s32[]{:S(2)}) async-start(), calls=%async_computation.3 | async-start | bytes 10485760 | tf_op jit(solution)/shard_map/reduce_scatter | solution.py:2284
  416.1 4.4 copy-start.21
  416.2 4.3 copy-start.32
  420.4 2.5 copy-start.3
  420.4 2.6 copy-start.23
  423.0 2.5 copy-start.35
  423.9 1.1 copy-start.19
  424.0 2.4 copy-start.6
  428.9 1.8 copy-start.11
  428.9 1.8 copy-start.13
  430.7 1.9 copy-start.1
  442.3 3.5 copy-start.33
  445.8 3.5 copy-start.7
  445.8 3.4 copy-start.36
  449.3 2.4 copy-start.4
  451.7 2.2 copy-start.34
  453.8 5.0 copy-start.14
  468.5 77.8 %copy-start.9 = (bf16[1,128,2048]{2,1,0:T(8,128)(2,1)S(1)}, bf16[1,128,2048]{2,1,0:T(8,128)(2,1)}, u32[]{:S(2)}) copy-start(bf16[1,128,2048]{2,1,0:T(8,128)(2,1)} %param.15) | copy-start | bytes 1572868
  546.2 4.9 copy-start.15
  548.0 3.1 copy-start.16
  604.5 2.3 copy-start.27
  604.5 3.1 copy-start.26
  604.5 3.9 copy-start.25
  604.5 4.7 copy-start.24
Sparse Core Ops, SparseCore 0:
  115.5 47.0 all-gather.2
  353.6 110.4 reduce-scatter.2
  467.4 117.9 reduce-scatter.4

commit v7 on v6

--- a/solution.py
+++ b/solution.py
@@ -1807,9 +1807,19 @@
     def place(t):
         return pl.ds((t if t < grads else t - grads) * size, size)
 
-    def out_copy(t):
-        to = grad_out if t < grads else y_out
-        return pltpu.make_async_copy(stage.at[t % 2], to.at[place(t)], stage_sem.at[t % 2])
+    experts, per = hidden // ff, width // seqs // size
+
+    def out_copies(t):
+        if t >= grads:
+            return [pltpu.make_async_copy(stage.at[t % 2], y_out.at[place(t)], stage_sem.at[t % 2, 0])]
+        return [
+            pltpu.make_async_copy(
+                stage.at[t % 2, :, pl.ds(e * ff, ff)],
+                grad_out.at[t // per, e, pl.ds(t % per * size, size)],
+                stage_sem.at[t % 2, e],
+            )
+            for e in range(experts)
+        ]
 
     def tile(t):
         if t == 0:
@@ -1819,7 +1829,8 @@
             loads[2].wait()
             loads[3].wait()
         if t >= 2:
-            out_copy(t - 2).wait()
+            for copy in out_copies(t - 2):
+                copy.wait()
         for n in range(hidden // (2 * TILE)):
             cols = pl.ds(n * 2 * TILE, 2 * TILE)
             if t < grads:
@@ -1827,7 +1838,8 @@
             else:
                 value = dot(hid[place(t), :], wd[:, cols])
             stage[t % 2, :, cols] = value.astype(BF16)
-        out_copy(t).start()
+        for copy in out_copies(t):
+            copy.start()
 
     turns = max(chips - 1, 1)
     rest = SumLate(
@@ -1845,7 +1857,8 @@
         own_sem, send, recv, pair_send, pair_recv, work=work,
     )
     for t in range(total - 2, total):
-        out_copy(t).wait()
+        for copy in out_copies(t):
+            copy.wait()
 
 
 def gather_fill(x, ffn_all, su, hid, wd, d_down, mid, near, ff, collective_id, parts=4):
@@ -1859,7 +1872,7 @@
     return pl.pallas_call(
         functools.partial(gather_fill_body, groups, seqs, ff, rows, parts),
         out_shape=[
-            tokens, jax.ShapeDtypeStruct((width, hidden), BF16), tokens,
+            tokens, jax.ShapeDtypeStruct((seqs, hidden // ff, width // seqs, ff), BF16), tokens,
             jax.ShapeDtypeStruct(mid.shape, BF16),
         ],
         in_specs=[anywhere] * 8,
@@ -1873,7 +1886,7 @@
             pltpu.VMEM(mid.shape, BF16),
             pltpu.VMEM(mid.shape, BF16),
             pltpu.VMEM(mid.shape, BF16),
-            dma((4,)), dma((2,)), dma((3,)), dma((2,)), dma((2,)),
+            dma((4,)), dma((2, hidden // ff)), dma((3,)), dma((2,)), dma((2,)),
             dma, line, line, line, line,
         ],
         compiler_params=pltpu.CompilerParams(
@@ -2308,6 +2321,7 @@
         d_after_all = line_gather(d_after.astype(BF16), 16)
         d_up_w = dot_tn(ffn_all, d_up).astype(BF16)
     own_up = scatter_in(d_up_w)
+    own_up = own_up[0].astype(F32) if fused else to_experts(own_up)
     d_out_w = dot_tn(mix, d_after_all)
     d_mix = dot_nt(d_after_all, w_o).astype(BF16)
     dqs, dks, dvs = [], [], []
@@ -2377,7 +2391,7 @@
         own_out = lax.ppermute(own_out, ("dp", "expert"), [(b, a) for a, b in moves])
         matrices = [*own_qkv.reshape(3, block, width).astype(F32), own_out.astype(F32)]
     small_grad = small_grad.reshape(-1)
-    expert_owned = [own_gate, to_experts(own_up), own_down.astype(F32)]
+    expert_owned = [own_gate, own_up, own_down.astype(F32)]
     return (
         output.reshape(1, rows, width),
         input_grad.reshape(1, rows, width),

time: 624 us -> 624 us (level)
  no operation moved by 1% of the time
where the time goes in v7:
time: 624 us; the launch traced here: 617 us
  Pallas kernels  483 us (77%)
  matrix products  40.2 us (6%)
  other arithmetic  38.9 us (6%)
  local copies, waits for them, and re-layouts  27.1 us (4%)
  between operations  14.7 us (2%)
  starting transfers between devices  7.05 us (1%)
    pallas_call x1, Pallas kernels, opening(): pl.pallas_call(kernel, out_shape=[jax.ShapeDtypeStruct((groups * rows, wi...  97 us
    pallas_call x1, Pallas kernels, expert_first(): pl.pallas_call(kernel, out_shape=[jax.ShapeDtypeStruct((length, width), B...  81.1 us
    pallas_call x1, Pallas kernels, joint_reduce(): pl.pallas_call(kernel, out_shape=[jax.ShapeDtypeStruct((rows, width), F32...  77.7 us
    pallas_call x3, Pallas kernels, run(): pl.pallas_call(kernel, out_shape=[out] + targets + whole_out + [jax.Shape...  66.4 us
    pallas_call x1, Pallas kernels, expert_second(): pl.pallas_call(kernel, out_shape=[jax.ShapeDtypeStruct((width, experts *...  58.3 us
    pallas_call x1, Pallas kernels, gather_fill(): pl.pallas_call(functools.partial(gather_fill_body, groups, seqs, ff, rows...  54.9 us
    pallas_call x1, Pallas kernels, last_exchange(): pl.pallas_call(kernel, out_shape=[jax.ShapeDtypeStruct(small.shape[1:], F...  47.7 us
    dot_general x7, matrix products, dot(): return jnp.dot(left, right, preferred_element_type=F32)  14.8 us
  transfers between devices with their start and end apart: 5, of which 2 were waited for; matrix products, arithmetic and copies ran while one was open for 14% of the time, Pallas kernels for 40%

profile of v7, /device:TPU:5, one launch (start us, length us, event | category | flops | bytes accessed | tf_op | source)
XLA Modules:
  0.0 617.1 jit_solution(15138020732435687955)
XLA Ops:
  8.1 3.3 concatenate.39
  11.4 97.0 %opening.1 = (bf16[1024,2048]{1,0:T(8,128)(2,1)}, bf16[32,16,128]{2,1,0:T(8,128)(2,1)}, bf16[2048,768]{1,0:T(8,128)(2,1)}, bf16[256,2048]{1,0:T(8,128)(2,1)}, bf...) custom-call(bf16[128,2048]{1,0:T(8,128)(2,1)} %bitcast.163, ...), custom_call_target="tpu_custom_call" | custom-call | bytes 240000000 | tf_op jit(solution)/shard_map/opening/pallas_call | solution.py:2043
  108.5 1.3 collective-permute-start.1
  109.7 5.6 collective-permute-start
  115.5 3.1 fusion
  118.8 8.8 %fusion.10 = f32[1024,768]{0,1:T(8,128)} fusion(bf16[2048,768]{1,0:T(8,128)(2,1)} %get-tuple-element.54, bf16[1024,2048]{1,0:T(8,128)(2,1)} %get-tuple-element.52, f32[2048]{0:T(1024)S(1)} %reshape.283, f32[1024]{0:T(1024)S(1)} %add_rsqrt_fusion.1), kind=kOutput, calls=%fused_computation.47 | convolution fusion | flops 3229614080 | bytes 10498048 | tf_op jit(solution)/shard_map/dot_general | solution.py:23
  128.5 2.2 slice.317
  130.6 1.7 multiply_reduce_fusion.6
  133.0 8.0 %exchange.2 = f32[16,128]{1,0:T(8,128)} custom-call(f32[1,16,128]{2,1,0:T(8,128)} %reshape.268.refs_0_), custom_call_target="tpu_custom_call" | custom-call | bytes 24000000 | tf_op jit(solution)/shard_map/exchange/pallas_call | solution.py:936
  141.0 1.0 multiply_cosine_fusion
  142.9 1.8 multiply_multiply_fusion
  151.0 3.3 convolution_convert_fusion.refs_0_
  154.3 1.3 collective-permute-done.1.refs_4_.refs_11_.refs_12_.refs_13_.refs_14_
  155.6 4.9 collective-permute-done.refs_3_.refs_13_.refs_14_.refs_15_.refs_16_
  160.5 50.0 %line_reduce.1 = (f32[128,2048]{1,0:T(8,128)}, bf16[1,512,1024]{2,1,0:T(8,128)(2,1)}, bf16[1,512,1024]{2,1,0:T(8,128)(2,1)}, bf16[1,512,1024]{2,1,0:T(8,128)(2,1)}, bf16[1,512,1024]{2,1,0:T(8,128)(2,1)}) custom-call(bf16[1024,2048]{1,0:T(8,128)(2,1)} %convolution_convert_fusion.refs_0_, bf16[1,512,1024]{2,1,0:T(8,128)(2,1)} %get-tuple-element.56.refs_1_.refs_7_.refs_9_, ...), custom_call_target="tpu_custom_call" | custom-call | bytes 120000000 | tf_op jit(solution)/shard_map/line_reduce/pallas_call | solution.py:936
  210.5 1.5 multiply_reduce_fusion.4
  212.9 1.0 concatenate.45.refs_0_
  213.9 81.1 %expert_first.1 = (bf16[1024,2048]{1,0:T(8,128)(2,1)}, bf16[1024,2048]{1,0:T(8,128)(2,1)}, bf16[1024,2048]{1,0:T(8,128)(2,1)}, bf16[1024,2048]{1,0:T(8,128)(2,1)...) custom-call(bf16[128,2176]{1,0:T(8,128)(2,1)} %concatenate.45.refs_0_, ...), custom_call_target="tpu_custom_call" | custom-call | bytes 210000000 | tf_op jit(solution)/shard_map/expert_first/pallas_call | solution.py:1326
  295.0 58.3 %expert_second.1 = (bf16[2048,2048]{1,0:T(8,128)(2,1)}, bf16[2,256,2048]{2,1,0:T(8,128)(2,1)}, bf16[2,256,2048]{2,1,0:T(8,128)(2,1)}, f32[128,2176]{1,0:T(8,128)}) custom-call(bf16[1024,2048]{1,0:T(8,128)(2,1)} %get-tuple-element.66.refs_0_, bf16[1024,2048]{1,0:T(8,128)(2,1)} %get-tuple-element.67.refs_1_.su_ref, ...), custom_call_target="tpu_custom_call" | custom-call | bytes 195000000 | tf_op jit(solution)/shard_map/expert_second/pallas_call | solution.py:1754
  353.4 1.1 multiply_reduce_fusion.7
  354.5 1.9 multiply_reduce_fusion.2
  356.4 2.8 fusion.75
  359.1 54.9 %gather_fill.1 = (bf16[1024,2048]{1,0:T(8,128)(2,1)}, bf16[4,2,512,1024]{3,2,1,0:T(8,128)(2,1)}, bf16[1024,2048]{1,0:T(8,128)(2,1)}, bf16[2,256,2048]{2,1,0:T(8,128)(2,1)}) custom-call(bf16[128,2048]{1,0:T(8,128)(2,1)} %get-tuple-element.174.x_ref, bf16[1024,2048]{1,0:T(8,128)(2,1)} %get-tuple-element.69.refs_3_.f_ref, ...), custom_call_target="tpu_custom_call" | custom-call | bytes 135000000 | tf_op jit(solution)/shard_map/gather_fill/pallas_call | solution.py:1872
  414.1 1.3 fusion.80
  416.1 4.3 convert_element_type.170
  420.4 1.3 convolution_convert_fusion.4
  421.7 1.2 copy-done.3
  423.0 0.9 multiply_reduce_fusion
  424.0 1.1 multiply_convert_fusion
  426.3 0.9 multiply_reduce_fusion.1
  427.2 1.1 multiply_convert_fusion.1
  431.3 1.3 copy-done.1
  433.7 8.4 %exchange.3 = f32[16,128]{1,0:T(8,128)} custom-call(f32[1,16,128]{2,1,0:T(8,128)} %reshape.274.refs_0_), custom_call_target="tpu_custom_call" | custom-call | bytes 24000000 | tf_op jit(solution)/shard_map/exchange/pallas_call | solution.py:936
  443.2 2.6 fusion.36
  445.8 3.4 convolution_convert_fusion.3.refs_3_
  450.1 1.5 copy-done.4
  452.5 1.3 copy-done.34
  453.8 5.0 convolution_convert_fusion.1.refs_0_
  458.8 5.6 convolution_convert_fusion.2.refs_2_
  464.5 1.7 slice_bitcast_fusion.1
  466.2 2.3 maximum_convert_fusion.refs_4_
  468.5 77.7 %joint_reduce.1 = (f32[128,2048]{1,0:T(8,128)}, f32[128,2048]{1,0:T(8,128)}, bf16[512,768]{1,0:T(8,128)(2,1)}, bf16[64,2048]{1,0:T(8,128)(2,1)}) custom-call(bf16[1024,2048]{1,0:T(8,128)(2,1)} %convolution_convert_fusion.1.refs_0_, bf16[1024,2048]{1,0:T(8,128)(2,1)} %get-tuple-element.77.refs_1_, bf16[2048,768]{1,0:T(8,128)(2,1)} %convolution_convert_fusion.2.refs_2_, ...), custom_call_target="tpu_custom_call" | custom-call | bytes 210000000 | tf_op jit(solution)/shard_map/joint_reduce/pallas_call | solution.py:709
  546.2 1.6 fusion.22
  548.8 2.3 add_bitcast_fusion.refs_3_
  551.1 1.3 fusion.20.refs_4_
  552.3 47.7 %last_exchange.1 = (f32[16,128]{1,0:T(8,128)}, f32[64,2048]{1,0:T(8,128)}, f32[64,2048]{1,0:T(8,128)}, f32[64,2048]{1,0:T(8,128)}, f32[64,2048]{1,0:T(8,128)}) custom-call(f32[32,16,128]{2,1,0:T(8,128)} %bitcast.167, bf16[512,768]{1,0:T(8,128)(2,1)} %get-tuple-element.81.refs_1_, bf16[64,2048]{1,0:T(8,128)(2,1)} %get-tuple-element.82.refs_2_, ...), custom_call_target="tpu_custom_call" | custom-call | bytes 75000000 | tf_op jit(solution)/shard_map/last_exchange/pallas_call | solution.py:829
  601.6 1.4 fusion.78
  603.0 4.2 bitcast_convert_fusion
  (152 shorter events, 25.4 us)
Async XLA Ops:
  7.2 206.7 %all-gather.3.cloned.1.call-start = ((), (), s32[]{:S(2)}) async-start(), calls=%async_computation.3 | async-start | bytes 4718592 | tf_op jit(solution)/shard_map/all_gather | solution.py:2194
  108.5 10.1 %copy-start.30 = (bf16[32,16,128]{2,1,0:T(8,128)(2,1)S(1)}, bf16[32,16,128]{2,1,0:T(8,128)(2,1)}, u32[]{:S(2)}) copy-start(bf16[32,16,128]{2,1,0:T(8,128)(2,1)} %get-tuple-element.53) | copy-start | bytes 393220
  108.5 47.1 %collective-permute-start.1 = (bf16[2,512,1024]{2,1,0:T(8,128)(2,1)}, bf16[2,512,1024]{2,1,0:T(8,128)(2,1)S(1)}, u32[]{:S(2)}, u32[]{:S(2)}) collective-permute-start(bf16[2,512,1024]{2,1,0:T(8,128)(2,1)} %refs_5_.3), channel_id=1, source_target_pairs={{0,8},{8,0},{16,24},{24,16},{1,9},{9,1},{17,25},{25,17},{2,10},{10... | collective-permute-start | bytes 6291464 | tf_op jit(solution)/shard_map/ppermute | solution.py:2073
  109.7 50.7 %collective-permute-start = (bf16[2,512,1024]{2,1,0:T(8,128)(2,1)}, bf16[2,512,1024]{2,1,0:T(8,128)(2,1)}, u32[]{:S(2)}, u32[]{:S(2)}) collective-permute-start(bf16[2,512,1024]{2,1,0:T(8,128)(2,1)} %refs_5_.3), channel_id=1, source_target_pairs={{0,16},{8,24},{16,0},{24,8},{1,17},{9,25},{17,1},{25,9},{2,18},{10... | collective-permute-start | bytes 6291464 | tf_op jit(solution)/shard_map/ppermute | solution.py:2073
  115.4 349.1 %reduce-scatter.5.cloned.1.call-start = ((), (), s32[]{:S(2)}) async-start(), calls=%async_computation.2 | async-start | bytes 10485760 | tf_op jit(solution)/shard_map/reduce_scatter | solution.py:2297
  118.8 8.8 %copy-start.31 = (s32[1,128,8]{1,2,0:T(8,128)S(1)}, s32[1,128,8]{1,2,0:T(8,128)}, u32[]{:S(2)}) copy-start(s32[1,128,8]{1,2,0:T(8,128)} %param.16) | copy-start | bytes 12292
  142.1 2.7 copy-start.10
  142.1 2.7 copy-start.12
  145.5 1.6 copy-start.18
  146.3 2.0 copy-start.2
  147.0 2.6 copy-start.5
  147.1 1.4 copy-start.22
  149.7 0.8 copy-start.28
  149.7 1.3 copy-start.20
  150.4 10.0 %copy-start.29 = (bf16[1024,128]{0,1:T(8,128)(2,1)}, bf16[1024,128]{0,1:T(8,128)(2,1)S(1)}, u32[]{:S(2)}) copy-start(bf16[1024,128]{0,1:T(8,128)(2,1)S(1)} %convolution_convert_fusion.6) | copy-start | bytes 786436
  155.6 4.9 copy-start
  160.5 50.1 %copy-start.8 = (bf16[1,128,2048]{2,1,0:T(8,128)(2,1)S(1)}, bf16[1,128,2048]{2,1,0:T(8,128)(2,1)}, u32[]{:S(2)}) copy-start(bf16[1,128,2048]{2,1,0:T(8,128)(2,1)} %param.15) | copy-start | bytes 1572868
  353.3 3.1 copy-start.17
  353.3 249.7 %reduce-scatter.7.cloned.1.call-start = ((), (), s32[]{:S(2)}) async-start(), calls=%async_computation.4 | async-start | bytes 10485760
  416.1 4.4 copy-start.21
  416.1 4.3 copy-start.32
  420.4 2.5 copy-start.3
  420.4 2.6 copy-start.23
  423.0 2.5 copy-start.35
  423.9 1.1 copy-start.19
  423.9 2.4 copy-start.6
  428.8 1.8 copy-start.11
  428.9 1.8 copy-start.13
  430.7 1.9 copy-start.1
  442.3 3.5 copy-start.33
  445.8 3.5 copy-start.7
  445.8 3.4 copy-start.36
  449.2 2.4 copy-start.4
  451.6 2.2 copy-start.34
  453.8 5.0 copy-start.14
  468.5 77.7 %copy-start.9 = (bf16[1,128,2048]{2,1,0:T(8,128)(2,1)S(1)}, bf16[1,128,2048]{2,1,0:T(8,128)(2,1)}, u32[]{:S(2)}) copy-start(bf16[1,128,2048]{2,1,0:T(8,128)(2,1)} %param.15) | copy-start | bytes 1572868
  546.2 4.9 copy-start.15
  548.0 3.1 copy-start.16
  600.1 7.1 %copy-start.27 = (f32[64,2048]{1,0:T(8,128)S(1)}, f32[64,2048]{1,0:T(8,128)}, u32[]{:S(2)}) copy-start(f32[64,2048]{1,0:T(8,128)} %get-tuple-element.245) | copy-start | bytes 1572868
  600.1 7.9 %copy-start.26 = (f32[64,2048]{1,0:T(8,128)S(1)}, f32[64,2048]{1,0:T(8,128)}, u32[]{:S(2)}) copy-start(f32[64,2048]{1,0:T(8,128)} %get-tuple-element.246) | copy-start | bytes 1572868
  603.0 5.8 copy-start.25
  603.0 6.6 %copy-start.24 = (f32[64,2048]{1,0:T(8,128)S(1)}, f32[64,2048]{1,0:T(8,128)}, u32[]{:S(2)}) copy-start(f32[64,2048]{1,0:T(8,128)} %get-tuple-element.248) | copy-start | bytes 1572868
Sparse Core Ops, SparseCore 0:
  115.5 47.0 all-gather.2
  353.4 110.4 reduce-scatter.4
  467.3 117.9 reduce-scatter.6
